TPU v7x, 32 devices: a whole 2x2x4 slice. The times are simulated.
32 devices in a mesh: case: 2 (over y), dom: 8 (over z, x), sub: 2 (over core).
Axes of the slice: x: 2, y: 2, z: 4, core: 2. Of those that a mesh axis runs over, the one named last changes fastest.
Arguments:
- states: float32 [19, 65536], P(None, ('case', 'dom', 'sub')), parts along dimension 1, may hold values from -0.9 to 2, as said below
- send_node: int32 [32, 4, 512], P(('case', 'dom', 'sub')), parts along dimension 0, may hold values from 0 to 2047
- send_count: int32 [32, 4], P(('case', 'dom', 'sub')), parts along dimension 0, may hold values from 1 to 512, as said below
- recv_row: int32 [32, 4, 512], P(('case', 'dom', 'sub')), parts along dimension 0, may hold values from 0 to 1023
- columns: int32 [128, 8], P(('case', 'dom'), 'sub'), parts along dimension 0, may hold values from 0 to 11
- tile_values: float32 [128, 8, 128, 128], P(('case', 'dom'), 'sub'), parts along dimension 0, may hold values from -0.109375 to 0.109375
- diagonal: float32 [16384], P(('case', 'dom')), parts along dimension 0, may hold values from 2.5 to 4
Outputs:
- new_states: float32 [19, 65536], P(None, ('case', 'dom', 'sub')), parts along dimension 1
- potential: float32 [16384], P(('case', 'dom')), parts along dimension 0
- residual: float32 [16384], P(('case', 'dom')), parts along dimension 0
There are 2 independent parts, one for each index of `case`. A program takes and returns all parts, laid end to end along the dimension named above; each array names one. Nothing has to cross between parts.
Inputs may be any that keep to these rules, and one draw needn't show every extreme that they name: `states`: row 0 lies in -0.9 to 0.4, rows 1 to 13 in 0.001 to 0.999, rows 14 to 18 are positive. `send_count`: every device has one peer with exactly 512 live slots.
All inputs are finite; a program needn't handle non-finite values.
Results may differ from a plain program's by a relative error of at most 0.0001.
Values sent between devices are 32-bit elements; how exact they have to be, the bound alone decides.
No kernel may reach another device: no remote copies, remote signals or barrier semaphores. Data moves between devices by JAX's collectives and lax.ppermute only.
A program may use at most 64 MiB of HBM per device.

v0:
```python
import jax
import jax.numpy as jnp
from jax import lax
from jax.sharding import PartitionSpec as P

HALO = 2
SWEEPS = 3
STEPS = 2


TIME_STEP = 0.02
NERNST_SCALE = 0.267
SODIUM_OUT = 1.4
POTASSIUM_OUT = 0.054
CALCIUM_OUT = 2000.0
COND_SODIUM = 8.0
COND_CALCIUM = 1.0
COND_TRANSIENT = 0.3
COND_RAPID = 0.2
COND_SLOW = 0.3
COND_INWARD = 2.0
COND_RELEASE = 3.0
MEMBRANE_RATE = 2.0
TORSO_COUPLING = 0.5
FEEDBACK_RATE = 5.0
CHEB_THETA = 1.0
CHEB_DELTA = 0.5
GATE_MIDPOINT = [-0.56, -0.7, -0.7, -0.08, -0.2, -0.3, 0.2, -0.28, -0.26, -0.88, 0.05, -0.8, -0.5]
GATE_STEEPNESS = [
    0.09,
    -0.07,
    -0.07,
    0.07,
    -0.07,
    -0.09,
    0.06,
    -0.05,
    0.07,
    -0.24,
    0.14,
    -0.1,
    0.08,
]
TIME_BASE = [0.02, 0.3, 1.0, 0.1, 2.0, 0.5, 0.1, 1.0, 1.0, 0.5, 1.0, 0.05, 0.2]
TIME_PEAK = [0.1, 1.0, 3.0, 0.5, 5.0, 2.0, 0.3, 5.0, 3.0, 2.0, 4.0, 0.1, 1.0]


def padded_2(block, sides, width):
    for axis, dim in sides:
        count = lax.axis_size(axis)
        forward = [(i, i + 1) for i in range(count - 1)]
        backward = [(target, source) for source, target in forward]
        low = lax.ppermute(
            lax.slice_in_dim(block, block.shape[dim] - width, None, axis=dim), axis, forward
        )
        high = lax.ppermute(lax.slice_in_dim(block, 0, width, axis=dim), axis, backward)
        block = jnp.concatenate([low, block, high], axis=dim)
    return block


def ionic(states):
    voltage = states[0]
    gating = states[1:14]
    sodium = states[14]
    potassium = states[15]
    calcium = states[16]
    reticulum = states[17]
    subspace = states[18]
    midpoint = jnp.array(GATE_MIDPOINT, jnp.float32)[:, None]
    steepness = jnp.array(GATE_STEEPNESS, jnp.float32)[:, None]
    time_base = jnp.array(TIME_BASE, jnp.float32)[:, None]
    time_peak = jnp.array(TIME_PEAK, jnp.float32)[:, None]
    shifted = voltage[None, :] - midpoint
    steady = jax.nn.sigmoid(shifted / steepness)
    time_const = time_base + time_peak * jnp.exp(-jnp.square(shifted / 0.3))
    gating = steady + (gating - steady) * jnp.exp(-TIME_STEP / time_const)
    sodium_rev = NERNST_SCALE * jnp.log(SODIUM_OUT / sodium)
    potassium_rev = NERNST_SCALE * jnp.log(POTASSIUM_OUT / potassium)
    calcium_rev = 0.5 * NERNST_SCALE * jnp.log(CALCIUM_OUT / subspace)
    sodium_flow = COND_SODIUM * gating[0] ** 3 * gating[1] * gating[2] * (voltage - sodium_rev)
    calcium_flow = COND_CALCIUM * gating[3] * gating[4] * gating[5] * (voltage - calcium_rev)
    potassium_cond = (
        COND_TRANSIENT * gating[6] * gating[7]
        + COND_RAPID * gating[8] * gating[9]
        + COND_SLOW * gating[10] ** 2
        + COND_INWARD * gating[11]
    )
    potassium_flow = potassium_cond * (voltage - potassium_rev)
    current = sodium_flow + calcium_flow + potassium_flow
    release = COND_RELEASE * gating[12] * (reticulum - subspace) / (reticulum + subspace)
    sodium = sodium * jnp.exp(-0.5 * TIME_STEP * sodium_flow)
    potassium = potassium * jnp.exp(-0.5 * TIME_STEP * potassium_flow)
    calcium = calcium * jnp.exp(-0.5 * TIME_STEP * calcium_flow)
    subspace = subspace * jnp.exp(TIME_STEP * (release - 0.5 * calcium_flow))
    reticulum = reticulum * jnp.exp(-TIME_STEP * release)
    voltage = voltage - TIME_STEP * MEMBRANE_RATE * current
    stacked = jnp.concatenate(
        [
            voltage[None],
            gating,
            sodium[None],
            potassium[None],
            calcium[None],
            reticulum[None],
            subspace[None],
        ],
        axis=0,
    )
    return (stacked, current)


def apply_operator(field, columns, tile_values, diagonal):
    block = tile_values.shape[-1]
    padded = padded_2(field, (("dom", 0),), HALO * block)
    blocks = padded.reshape(-1, block)
    picked = blocks[columns]
    partial_value = jnp.einsum(
        "rkab,rkb->ra", tile_values, picked, precision=lax.Precision.HIGHEST
    ).reshape(-1)
    return diagonal * field + lax.psum(partial_value, "sub")


def on_device(states, send_node, send_count, recv_row, columns, tile_values, diagonal):
    peer_count = send_node.shape[1]
    slot_count = send_node.shape[2]
    chain_size = lax.axis_size("dom")
    position = lax.axis_index("dom")
    node_count = states.shape[1]
    torso_rows = diagonal.shape[0]
    offsets = jnp.array([0, 1, chain_size - 1, chain_size // 2][:peer_count], jnp.int32)
    chain_ids = jnp.arange(chain_size, dtype=jnp.int32)
    send_map = (chain_ids[:, None] == ((position + offsets) % chain_size)[None, :]).astype(
        jnp.float32
    )
    back_map = (
        chain_ids[:, None] == ((position - offsets + chain_size) % chain_size)[None, :]
    ).astype(jnp.float32)
    slot_live = jnp.arange(slot_count, dtype=jnp.int32)[None, :] < send_count[0][:, None]
    node_slots = send_node[0]
    land_rows = recv_row[0].reshape(-1)
    flat_nodes = node_slots.reshape(-1)
    sigma = CHEB_THETA / CHEB_DELTA
    estimate = jnp.zeros((torso_rows,), jnp.float32)
    residual = estimate
    for time_step in range(STEPS):
        states, current = ionic(states)
        outgoing = jnp.where(slot_live, current[node_slots], 0.0)
        padded_out = jnp.dot(send_map, outgoing, precision=lax.Precision.HIGHEST)
        received = lax.all_to_all(padded_out, "dom", split_axis=0, concat_axis=0, tiled=True)
        incoming = jnp.dot(back_map.T, received, precision=lax.Precision.HIGHEST)
        gathered = jnp.zeros((torso_rows,), jnp.float32).at[land_rows].add(incoming.reshape(-1))
        forcing = TORSO_COUPLING * lax.psum(gathered, "sub")
        estimate = jnp.zeros((torso_rows,), jnp.float32)
        residual = forcing
        ratio = 1.0 / sigma
        direction = residual / (CHEB_THETA * diagonal)
        for sweep_idx in range(SWEEPS):
            estimate = estimate + direction
            residual = residual - apply_operator(direction, columns, tile_values, diagonal)
            if sweep_idx + 1 < SWEEPS:
                ratio_next = 1.0 / (2.0 * sigma - ratio)
                direction = ratio_next * ratio * direction + 2.0 * ratio_next / CHEB_DELTA * (
                    residual / diagonal
                )
                ratio = ratio_next
        values_back = estimate[land_rows].reshape(peer_count, slot_count)
        padded_back = jnp.dot(back_map, values_back, precision=lax.Precision.HIGHEST)
        received_back = lax.all_to_all(padded_back, "dom", split_axis=0, concat_axis=0, tiled=True)
        returned = jnp.dot(send_map.T, received_back, precision=lax.Precision.HIGHEST)
        returned = jnp.where(slot_live, returned, 0.0)
        feedback = jnp.zeros((node_count,), jnp.float32).at[flat_nodes].add(returned.reshape(-1))
        states = states.at[0].add(TIME_STEP * FEEDBACK_RATE * feedback)
    return (states, estimate, residual)


def solution(mesh):
    placed = (
        P(None, ("case", "dom", "sub")),
        P(("case", "dom", "sub"), None, None),
        P(("case", "dom", "sub"), None),
        P(("case", "dom", "sub"), None, None),
        P(("case", "dom"), "sub"),
        P(("case", "dom"), "sub", None, None),
        P(("case", "dom")),
    )
    return jax.shard_map(
        on_device,
        mesh=mesh,
        in_specs=placed,
        out_specs=(P(None, ("case", "dom", "sub")), P(("case", "dom")), P(("case", "dom"))),
        check_vma=False,
    )
```

profile of v0, /device:TPU:0, one launch (start us, length us, event | category | flops | bytes accessed | tf_op | source)
XLA Modules:
  0.0 219.1 jit_solution(3592502420498391976)
XLA Ops:
  5.7 11.8 %gather_fusion = f32[2048]{0:T(1024)S(1)} fusion(f32[2048]{0:T(1024)S(1)} %fusion.44, s32[2048]{0:T(1024)S(1)} %broadcast_clamp_fusion.1), kind=kCustom, calls=%fused_computation | custom fusion | bytes 24576 | tf_op jit(solution)/shard_map/gather | solution.py:147
  18.4 7.3 %all-to-all-start = ((f32[8,1,512]{2,1,0:T(1,128)}), f32[8,1,512]{2,1,0:T(1,128)S(1)}, u32[]{:S(2)}, u32[]{:S(2)}) async-start(f32[8,1,512]{2,1,0:T(1,128)} %copy.21), calls=%async_computation | async-start | bytes 32768 | tf_op jit(solution)/shard_map/all_to_all | solution.py:149
  25.9 6.3 %all-to-all-done = f32[8,1,512]{2,1,0:T(1,128)S(1)} async-done(((f32[8,1,512]{2,1,0:T(1,128)}), f32[8,1,512]{2,1,0:T(1,128)S(1)}, u32[]{:S(2)}, u32[]{:S(2)}) %all-to-all-start) | async-done | bytes 16416 | tf_op jit(solution)/shard_map/all_to_all | solution.py:149
  32.4 14.7 %scatter_custom_fusion = f32[1024]{0:T(1024)S(1)} fusion(s32[2048]{0:T(1024)S(1)} %bitcast.163, f32[2048]{0:T(1024)S(1)} %bitcast.184, f32[]{:T(128)} %constant.128.clone.1), kind=kCustom, calls=%fused_computation.181 | custom fusion | flops 2048 | bytes 4100 | tf_op jit(solution)/shard_map/scatter-add | solution.py:151
  47.1 2.5 %psum.49 = f32[1024]{0:T(1024)S(1)} all-reduce(f32[1024]{0:T(1024)S(1)} %scatter_custom_fusion), channel_id=1, replica_groups=mesh['case'=2,'dom'=8,'sub'=2] {'sub'}, use_global_device_ids=true, to_apply=%region_1.2 | all-reduce | flops 1024 | bytes 8192 | tf_op jit(solution)/shard_map/psum | solution.py:152
  53.3 4.1 %collective-permute-done.1 = f32[256]{0:T(256)S(1)} collective-permute-done((f32[256]{0:T(256)S(1)}, f32[256]{0:T(256)S(1)}, u32[]{:S(2)}, u32[]{:S(2)}) %collective-permute-start.1) | collective-permute-done | bytes 1056 | tf_op jit(solution)/shard_map/ppermute | solution.py:56
  62.4 4.2 %collective-permute-start.2 = (f32[256]{0:T(256)S(1)}, f32[256]{0:T(256)S(1)}, u32[]{:S(2)}, u32[]{:S(2)}) collective-permute-start(f32[256]{0:T(256)S(1)} %get-tuple-element.68), channel_id=1, source_target_pairs={{0,2},{2,4},{4,6},{6,8},{8,10},{10,12},{12,14},{1,3},{3,5},{5,7},{... | collective-permute-start | bytes 3080 | tf_op jit(solution)/shard_map/ppermute | solution.py:53
  67.9 4.1 %collective-permute-done.3 = f32[256]{0:T(256)S(1)} collective-permute-done((f32[256]{0:T(256)S(1)}, f32[256]{0:T(256)S(1)}, u32[]{:S(2)}, u32[]{:S(2)}) %collective-permute-start.3) | collective-permute-done | bytes 1056 | tf_op jit(solution)/shard_map/ppermute | solution.py:56
  77.0 8.6 %gather_fusion.3 = f32[2048]{0:T(1024)S(1)} fusion(f32[1024]{0:T(1024)S(1)} %add_add_fusion.1, s32[2048]{0:T(1024)S(1)} %broadcast_clamp_fusion), kind=kCustom, calls=%fused_computation.3 | custom fusion | bytes 24576 | tf_op jit(solution)/shard_map/gather | solution.py:166
  86.4 3.3 %all-to-all-start.1 = ((f32[8,1,512]{2,1,0:T(1,128)}), f32[8,1,512]{2,1,0:T(1,128)S(1)}, u32[]{:S(2)}, u32[]{:S(2)}) async-start(f32[8,1,512]{2,1,0:T(1,128)} %copy.23), calls=%async_computation.1 | async-start | bytes 32768 | tf_op jit(solution)/shard_map/all_to_all | solution.py:168
  89.7 6.5 %all-to-all-done.1 = f32[8,1,512]{2,1,0:T(1,128)S(1)} async-done(((f32[8,1,512]{2,1,0:T(1,128)}), f32[8,1,512]{2,1,0:T(1,128)S(1)}, u32[]{:S(2)}, u32[]{:S(2)}) %all-to-all-start.1) | async-done | bytes 16416 | tf_op jit(solution)/shard_map/all_to_all | solution.py:168
  96.4 11.3 %scatter_custom_fusion.1 = f32[2048]{0:T(1024)S(1)} fusion(s32[2048]{0:T(1024)S(1)} %bitcast.180, f32[2048]{0:T(1024)S(1)} %bitcast.185, f32[]{:T(128)} %constant.128.clone.1), kind=kCustom, calls=%fused_computation.171 | custom fusion | flops 2048 | bytes 8196 | tf_op jit(solution)/shard_map/scatter-add | solution.py:171
  108.2 11.8 %gather_fusion.4 = f32[2048]{0:T(1024)S(1)} fusion(f32[2048]{0:T(1024)S(1)} %fusion.53, s32[2048]{0:T(1024)S(1)} %broadcast_clamp_fusion.1), kind=kCustom, calls=%fused_computation.4 | custom fusion | bytes 24576 | tf_op jit(solution)/shard_map/gather | solution.py:147
  120.3 8.9 %all_to_all.48 = f32[8,1,512]{2,1,0:T(1,128)S(1)} all-to-all(f32[8,1,512]{2,1,0:T(1,128)S(1)} %copy.24), channel_id=1, replica_groups=mesh['case'=2,'dom'=8,'sub'=2] {'dom'}, dimensions={0} | all-to-all | bytes 32768 | tf_op jit(solution)/shard_map/all_to_all | solution.py:149
  129.4 14.7 %scatter_custom_fusion.2 = f32[1024]{0:T(1024)S(1)} fusion(s32[2048]{0:T(1024)S(1)} %bitcast.165, f32[2048]{0:T(1024)S(1)} %bitcast.183, f32[]{:T(128)} %constant.128.clone.1), kind=kCustom, calls=%fused_computation.179 | custom fusion | flops 2048 | bytes 4100 | tf_op jit(solution)/shard_map/scatter-add | solution.py:151
  144.1 2.5 %psum.52 = f32[1024]{0:T(1024)S(1)} all-reduce(f32[1024]{0:T(1024)S(1)} %scatter_custom_fusion.2), channel_id=1, replica_groups=mesh['case'=2,'dom'=8,'sub'=2] {'sub'}, use_global_device_ids=true, to_apply=%region_6.7 | all-reduce | flops 1024 | bytes 8192 | tf_op jit(solution)/shard_map/psum | solution.py:152
  150.3 4.2 %collective-permute-done.5 = f32[256]{0:T(256)S(1)} collective-permute-done((f32[256]{0:T(256)S(1)}, f32[256]{0:T(256)S(1)}, u32[]{:S(2)}, u32[]{:S(2)}) %collective-permute-start.5) | collective-permute-done | bytes 1056 | tf_op jit(solution)/shard_map/ppermute | solution.py:56
  159.3 4.2 %collective-permute-start.6 = (f32[256]{0:T(256)S(1)}, f32[256]{0:T(256)S(1)}, u32[]{:S(2)}, u32[]{:S(2)}) collective-permute-start(f32[256]{0:T(256)S(1)} %get-tuple-element.64), channel_id=1, source_target_pairs={{0,2},{2,4},{4,6},{6,8},{8,10},{10,12},{12,14},{1,3},{3,5},{5,7},{... | collective-permute-start | bytes 3080 | tf_op jit(solution)/shard_map/ppermute | solution.py:53
  164.9 4.2 %collective-permute-done.7 = f32[256]{0:T(256)S(1)} collective-permute-done((f32[256]{0:T(256)S(1)}, f32[256]{0:T(256)S(1)}, u32[]{:S(2)}, u32[]{:S(2)}) %collective-permute-start.7) | collective-permute-done | bytes 1056 | tf_op jit(solution)/shard_map/ppermute | solution.py:56
  173.9 2.8 %collective-permute-start.8 = (f32[256]{0:T(256)S(1)}, f32[256]{0:T(256)S(1)}, u32[]{:S(2)}, u32[]{:S(2)}) collective-permute-start(f32[256]{0:T(256)S(1)} %get-tuple-element.62), channel_id=1, source_target_pairs={{0,2},{2,4},{4,6},{6,8},{8,10},{10,12},{12,14},{1,3},{3,5},{5,7},{... | collective-permute-start | bytes 3080 | tf_op jit(solution)/shard_map/ppermute | solution.py:53
  178.1 4.2 %collective-permute-done.9 = f32[256]{0:T(256)S(1)} collective-permute-done((f32[256]{0:T(256)S(1)}, f32[256]{0:T(256)S(1)}, u32[]{:S(2)}, u32[]{:S(2)}) %collective-permute-start.9) | collective-permute-done | bytes 1056 | tf_op jit(solution)/shard_map/ppermute | solution.py:56
  187.7 8.6 %gather_fusion.7 = f32[2048]{0:T(1024)S(1)} fusion(f32[1024]{0:T(1024)S(1)} %get-tuple-element.61, s32[2048]{0:T(1024)S(1)} %broadcast_clamp_fusion), kind=kCustom, calls=%fused_computation.7 | custom fusion | bytes 24576 | tf_op jit(solution)/shard_map/gather | solution.py:166
  196.4 9.7 %all_to_all.49 = f32[8,1,512]{2,1,0:T(1,128)S(1)} all-to-all(f32[8,1,512]{2,1,0:T(1,128)S(1)} %copy.25), channel_id=1, replica_groups=mesh['case'=2,'dom'=8,'sub'=2] {'dom'}, dimensions={0} | all-to-all | bytes 32768 | tf_op jit(solution)/shard_map/all_to_all | solution.py:168
  206.4 11.3 %scatter_custom_fusion.3 = f32[2048]{0:T(1024)S(1)} fusion(s32[2048]{0:T(1024)S(1)} %bitcast.181, f32[2048]{0:T(1024)S(1)} %bitcast.182, f32[]{:T(128)} %constant.128.clone.1), kind=kCustom, calls=%fused_computation.169 | custom fusion | flops 2048 | bytes 8196 | tf_op jit(solution)/shard_map/scatter-add | solution.py:171
  (124 shorter events, 46.2 us)
Async XLA Ops:
  0.6 57.4 %copy-start = (f32[8,4,128,128]{3,2,1,0:T(8,128)S(1)}, f32[8,4,128,128]{3,2,1,0:T(8,128)}, u32[]{:S(2)}) copy-start(f32[8,4,128,128]{3,2,1,0:T(8,128)} %param.25) | copy-start | bytes 6291460
  5.6 11.9 %copy-start.12 = (s32[1,4]{1,0:T(1,128)S(1)}, s32[1,4]{1,0:T(1,128)}, u32[]{:S(2)}) copy-start(s32[1,4]{1,0:T(1,128)} %param.22) | copy-start | bytes 52
  5.6 20.0 %copy-start.7 = (s32[8,4]{0,1:T(4,128)S(1)}, s32[8,4]{0,1:T(4,128)}, u32[]{:S(2)}) copy-start(s32[8,4]{0,1:T(4,128)} %param.24) | copy-start | bytes 388
  5.7 20.0 %copy-start.6 = (s32[1,4,512]{2,1,0:T(4,128)S(1)}, s32[1,4,512]{2,1,0:T(4,128)}, u32[]{:S(2)}) copy-start(s32[1,4,512]{2,1,0:T(4,128)} %param.23) | copy-start | bytes 24580
  5.7 20.0 %copy-start.13 = (s32[4]{0:T(128)S(1)}, s32[4]{0:T(128)}, u32[]{:S(2)}) copy-start(s32[4]{0:T(128)} %constant.159) | copy-start | bytes 52
  5.7 43.9 %copy-start.3 = (f32[1024]{0:T(1024)S(1)}, f32[1024]{0:T(1024)}, u32[]{:S(2)}) copy-start(f32[1024]{0:T(1024)} %param.26) | copy-start | bytes 12292
  17.5 50.4 %copy-start.5 = (s32[1,4,512]{2,1,0:T(4,128)S(1)}, s32[1,4,512]{2,1,0:T(4,128)}, u32[]{:S(2)}) copy-start(s32[1,4,512]{2,1,0:T(4,128)} %param.21) | copy-start | bytes 24580
  18.4 13.8 %all-to-all-start = ((f32[8,1,512]{2,1,0:T(1,128)}), f32[8,1,512]{2,1,0:T(1,128)S(1)}, u32[]{:S(2)}, u32[]{:S(2)}) async-start(f32[8,1,512]{2,1,0:T(1,128)} %copy.21), calls=%async_computation | async-start | bytes 32768 | tf_op jit(solution)/shard_map/all_to_all | solution.py:149
  49.6 3.7 %collective-permute-start = (f32[256]{0:T(256)S(1)}, f32[256]{0:T(256)S(1)}, u32[]{:S(2)}, u32[]{:S(2)}) collective-permute-start(f32[256]{0:T(256)S(1)} %get-tuple-element.70), channel_id=1, source_target_pairs={{0,2},{2,4},{4,6},{6,8},{8,10},{10,12},{12,14},{1,3},{3,5},{5,7},{... | collective-permute-start | bytes 3080 | tf_op jit(solution)/shard_map/ppermute | solution.py:53
  52.0 5.5 %collective-permute-start.1 = (f32[256]{0:T(256)S(1)}, f32[256]{0:T(256)S(1)}, u32[]{:S(2)}, u32[]{:S(2)}) collective-permute-start(f32[256]{0:T(256)S(1)} %get-tuple-element.71), channel_id=1, source_target_pairs={{2,0},{4,2},{6,4},{8,6},{10,8},{12,10},{14,12},{3,1},{5,3},{7,5},{... | collective-permute-start | bytes 3080 | tf_op jit(solution)/shard_map/ppermute | solution.py:56
  62.4 5.6 %collective-permute-start.2 = (f32[256]{0:T(256)S(1)}, f32[256]{0:T(256)S(1)}, u32[]{:S(2)}, u32[]{:S(2)}) collective-permute-start(f32[256]{0:T(256)S(1)} %get-tuple-element.68), channel_id=1, source_target_pairs={{0,2},{2,4},{4,6},{6,8},{8,10},{10,12},{12,14},{1,3},{3,5},{5,7},{... | collective-permute-start | bytes 3080 | tf_op jit(solution)/shard_map/ppermute | solution.py:53
  66.6 5.5 %collective-permute-start.3 = (f32[256]{0:T(256)S(1)}, f32[256]{0:T(256)S(1)}, u32[]{:S(2)}, u32[]{:S(2)}) collective-permute-start(f32[256]{0:T(256)S(1)} %get-tuple-element.69), channel_id=1, source_target_pairs={{2,0},{4,2},{6,4},{8,6},{10,8},{12,10},{14,12},{3,1},{5,3},{7,5},{... | collective-permute-start | bytes 3080 | tf_op jit(solution)/shard_map/ppermute | solution.py:56
  76.9 30.8 %copy-start.2 = (f32[19,2048]{1,0:T(8,128)S(1)}, f32[19,2048]{1,0:T(8,128)}, u32[]{:S(2)}) copy-start(f32[19,2048]{1,0:T(8,128)} %param.20) | copy-start | bytes 466948
  76.9 30.8 %copy-start.8 = (f32[13]{0:T(128)S(1)}, f32[13]{0:T(128)}, u32[]{:S(2)}) copy-start(f32[13]{0:T(128)} %constant.158) | copy-start | bytes 160
  77.0 30.8 %copy-start.9 = (f32[13]{0:T(128)S(1)}, f32[13]{0:T(128)}, u32[]{:S(2)}) copy-start(f32[13]{0:T(128)} %constant.156) | copy-start | bytes 160
  77.0 30.8 %copy-start.10 = (f32[13]{0:T(128)S(1)}, f32[13]{0:T(128)}, u32[]{:S(2)}) copy-start(f32[13]{0:T(128)} %constant.150.clone) | copy-start | bytes 160
  77.0 30.8 %copy-start.11 = (f32[13]{0:T(128)S(1)}, f32[13]{0:T(128)}, u32[]{:S(2)}) copy-start(f32[13]{0:T(128)} %constant.149.clone) | copy-start | bytes 160
  86.4 9.9 %all-to-all-start.1 = ((f32[8,1,512]{2,1,0:T(1,128)}), f32[8,1,512]{2,1,0:T(1,128)S(1)}, u32[]{:S(2)}, u32[]{:S(2)}) async-start(f32[8,1,512]{2,1,0:T(1,128)} %copy.23), calls=%async_computation.1 | async-start | bytes 32768 | tf_op jit(solution)/shard_map/all_to_all | solution.py:168
  146.6 3.7 %collective-permute-start.4 = (f32[256]{0:T(256)S(1)}, f32[256]{0:T(256)S(1)}, u32[]{:S(2)}, u32[]{:S(2)}) collective-permute-start(f32[256]{0:T(256)S(1)} %get-tuple-element.66), channel_id=1, source_target_pairs={{0,2},{2,4},{4,6},{6,8},{8,10},{10,12},{12,14},{1,3},{3,5},{5,7},{... | collective-permute-start | bytes 3080 | tf_op jit(solution)/shard_map/ppermute | solution.py:53
  149.0 5.5 %collective-permute-start.5 = (f32[256]{0:T(256)S(1)}, f32[256]{0:T(256)S(1)}, u32[]{:S(2)}, u32[]{:S(2)}) collective-permute-start(f32[256]{0:T(256)S(1)} %get-tuple-element.67), channel_id=1, source_target_pairs={{2,0},{4,2},{6,4},{8,6},{10,8},{12,10},{14,12},{3,1},{5,3},{7,5},{... | collective-permute-start | bytes 3080 | tf_op jit(solution)/shard_map/ppermute | solution.py:56
  159.3 5.5 %collective-permute-start.6 = (f32[256]{0:T(256)S(1)}, f32[256]{0:T(256)S(1)}, u32[]{:S(2)}, u32[]{:S(2)}) collective-permute-start(f32[256]{0:T(256)S(1)} %get-tuple-element.64), channel_id=1, source_target_pairs={{0,2},{2,4},{4,6},{6,8},{8,10},{10,12},{12,14},{1,3},{3,5},{5,7},{... | collective-permute-start | bytes 3080 | tf_op jit(solution)/shard_map/ppermute | solution.py:53
  163.6 5.5 %collective-permute-start.7 = (f32[256]{0:T(256)S(1)}, f32[256]{0:T(256)S(1)}, u32[]{:S(2)}, u32[]{:S(2)}) collective-permute-start(f32[256]{0:T(256)S(1)} %get-tuple-element.65), channel_id=1, source_target_pairs={{2,0},{4,2},{6,4},{8,6},{10,8},{12,10},{14,12},{3,1},{5,3},{7,5},{... | collective-permute-start | bytes 3080 | tf_op jit(solution)/shard_map/ppermute | solution.py:56
  173.9 4.1 %collective-permute-start.8 = (f32[256]{0:T(256)S(1)}, f32[256]{0:T(256)S(1)}, u32[]{:S(2)}, u32[]{:S(2)}) collective-permute-start(f32[256]{0:T(256)S(1)} %get-tuple-element.62), channel_id=1, source_target_pairs={{0,2},{2,4},{4,6},{6,8},{8,10},{10,12},{12,14},{1,3},{3,5},{5,7},{... | collective-permute-start | bytes 3080 | tf_op jit(solution)/shard_map/ppermute | solution.py:53
  176.7 5.5 %collective-permute-start.9 = (f32[256]{0:T(256)S(1)}, f32[256]{0:T(256)S(1)}, u32[]{:S(2)}, u32[]{:S(2)}) collective-permute-start(f32[256]{0:T(256)S(1)} %get-tuple-element.63), channel_id=1, source_target_pairs={{2,0},{4,2},{6,4},{8,6},{10,8},{12,10},{14,12},{3,1},{5,3},{7,5},{... | collective-permute-start | bytes 3080 | tf_op jit(solution)/shard_map/ppermute | solution.py:56
  (3 other events, 21.2 us)
where the time goes:
time: 220 us; the launch traced here: 219 us
  other arithmetic  57.3 us (26%)
  local copies, waits for them, and re-layouts  47.4 us (22%)
  blocking collectives  35.9 us (16%)
  waiting for transfers between devices  33.5 us (15%)
  starting transfers between devices  33.2 us (15%)
  matrix products  10.5 us (5%)
    scatter-add x2, other arithmetic, on_device(): jnp.zeros((torso_rows,), jnp.float32).at[land_rows]  29.3 us
    gather x4, local copies, waits for them, and re-layouts, on_device(): outgoing = jnp.where(slot_live, current[node_slots], 0.0)  23.6 us
    scatter-add x2, other arithmetic, on_device(): jnp.zeros((node_count,), jnp.float32).at[flat_nodes]  22.6 us
    ppermute x5, waiting for transfers between devices, padded_2(): lax.ppermute(lax.slice_in_dim(block, 0, width, axis=dim), axis, backward)  20.7 us
    gather x2, local copies, waits for them, and re-layouts, on_device(): values_back = estimate[land_rows].reshape(peer_count, slot_count)  17.2 us
    ppermute x5, starting transfers between devices, padded_2(): lax.ppermute(lax.slice_in_dim(block, block.shape[dim] - width, None, axis...  16.1 us
    psum x5, blocking collectives, apply_operator(): return diagonal * field + lax.psum(partial_value, 'sub')  12.3 us
    all_to_all x1, blocking collectives, on_device(): lax.all_to_all(padded_back, 'dom', split_axis=0, concat_axis=0, tiled=True)  9.75 us
  transfers between devices with their start and end apart: 12, of which 7 were waited for; matrix products, arithmetic and copies ran while one was open for 0% of the time, Pallas kernels for 0%

commit v1 on v0

v1 whole, which is shorter than its diff:
```python
import functools

import jax
import jax.numpy as jnp
from jax import lax
from jax.experimental import pallas as pl
from jax.experimental.pallas import tpu as pltpu
from jax.sharding import PartitionSpec as P

HALO = 2
SWEEPS = 3
LANES = 128

TIME_STEP = 0.02
NERNST_SCALE = 0.267
SODIUM_OUT = 1.4
POTASSIUM_OUT = 0.054
CALCIUM_OUT = 2000.0
COND_SODIUM = 8.0
COND_CALCIUM = 1.0
COND_TRANSIENT = 0.3
COND_RAPID = 0.2
COND_SLOW = 0.3
COND_INWARD = 2.0
COND_RELEASE = 3.0
MEMBRANE_RATE = 2.0
TORSO_COUPLING = 0.5
FEEDBACK_RATE = 5.0
CHEB_THETA = 1.0
CHEB_DELTA = 0.5
GATE_MIDPOINT = [-0.56, -0.7, -0.7, -0.08, -0.2, -0.3, 0.2, -0.28, -0.26, -0.88, 0.05, -0.8, -0.5]
GATE_STEEPNESS = [0.09, -0.07, -0.07, 0.07, -0.07, -0.09, 0.06, -0.05, 0.07, -0.24, 0.14, -0.1, 0.08]
TIME_BASE = [0.02, 0.3, 1.0, 0.1, 2.0, 0.5, 0.1, 1.0, 1.0, 0.5, 1.0, 0.05, 0.2]
TIME_PEAK = [0.1, 1.0, 3.0, 0.5, 5.0, 2.0, 0.3, 5.0, 3.0, 2.0, 4.0, 0.1, 1.0]

SIGMA = CHEB_THETA / CHEB_DELTA
KEEP, PULL = [], []
_ratio = 1.0 / SIGMA
for _ in range(SWEEPS - 1):
    _next = 1.0 / (2.0 * SIGMA - _ratio)
    KEEP.append(_next * _ratio)
    PULL.append(2.0 * _next / CHEB_DELTA)
    _ratio = _next

VMEM = pl.BlockSpec(memory_space=pltpu.VMEM)
SMEM = pl.BlockSpec(memory_space=pltpu.SMEM)
F32 = jnp.float32


def call(kernel, outs, scratch=(), limit=16, cost=4_000_000):
    return functools.partial(
        pl.pallas_call,
        kernel,
        out_shape=outs,
        out_specs=jax.tree.map(lambda _: VMEM, outs),
        scratch_shapes=list(scratch),
        compiler_params=pltpu.CompilerParams(vmem_limit_bytes=limit << 20),
        cost_estimate=pl.CostEstimate(flops=cost, bytes_accessed=1 << 18, transcendentals=0),
    )


def ionic_rows(rows):
    voltage, gating = rows[0], rows[1:14]
    sodium, potassium, calcium, reticulum, subspace = rows[14:19]
    moved = []
    for i, gate in enumerate(gating):
        shifted = voltage - GATE_MIDPOINT[i]
        steady = jax.nn.sigmoid(shifted / GATE_STEEPNESS[i])
        time_const = TIME_BASE[i] + TIME_PEAK[i] * jnp.exp(-jnp.square(shifted / 0.3))
        moved.append(steady + (gate - steady) * jnp.exp(-TIME_STEP / time_const))
    g = moved
    sodium_rev = NERNST_SCALE * jnp.log(SODIUM_OUT / sodium)
    potassium_rev = NERNST_SCALE * jnp.log(POTASSIUM_OUT / potassium)
    calcium_rev = 0.5 * NERNST_SCALE * jnp.log(CALCIUM_OUT / subspace)
    sodium_flow = COND_SODIUM * (g[0] * g[0] * g[0]) * g[1] * g[2] * (voltage - sodium_rev)
    calcium_flow = COND_CALCIUM * g[3] * g[4] * g[5] * (voltage - calcium_rev)
    potassium_cond = (
        COND_TRANSIENT * g[6] * g[7]
        + COND_RAPID * g[8] * g[9]
        + COND_SLOW * (g[10] * g[10])
        + COND_INWARD * g[11]
    )
    potassium_flow = potassium_cond * (voltage - potassium_rev)
    current = sodium_flow + calcium_flow + potassium_flow
    release = COND_RELEASE * g[12] * (reticulum - subspace) / (reticulum + subspace)
    sodium = sodium * jnp.exp(-0.5 * TIME_STEP * sodium_flow)
    potassium = potassium * jnp.exp(-0.5 * TIME_STEP * potassium_flow)
    calcium = calcium * jnp.exp(-0.5 * TIME_STEP * calcium_flow)
    subspace = subspace * jnp.exp(TIME_STEP * (release - 0.5 * calcium_flow))
    reticulum = reticulum * jnp.exp(-TIME_STEP * release)
    voltage = voltage - TIME_STEP * MEMBRANE_RATE * current
    return [voltage, *moved, sodium, potassium, calcium, reticulum, subspace], current


def pairs_of(index):
    chunks = [index[:, k : k + LANES] for k in range(0, index.shape[1], LANES)]
    return [jnp.concatenate(chunks[k : k + 2], axis=0) for k in range(0, len(chunks), 2)]


def gather(source, rows, index):
    peers = index.shape[0]
    out = []
    for pair in pairs_of(index):
        high, low = pair >> 7, pair & (LANES - 1)
        total = jnp.zeros(pair.shape, F32)
        for h in range(rows):
            picked = jnp.take_along_axis(source(h), low, axis=1)
            total = jnp.where(high == h, picked, total)
        out += [total[:peers], total[peers:]]
    return jnp.concatenate(out, axis=1)


def scatter(values, index, rows):
    slots = values.shape[1]
    high, low = index >> 7, index & (LANES - 1)
    first = values.astype(jnp.bfloat16).astype(F32)
    rest = values - first
    second = rest.astype(jnp.bfloat16).astype(F32)
    third = rest - second
    mine = lax.broadcasted_iota(jnp.int32, (rows, slots), 0) == high
    left = jnp.concatenate([jnp.where(mine, part, 0.0) for part in (first, second, third)], axis=0)
    spread = lax.broadcasted_iota(jnp.int32, (LANES, slots), 0) == low
    right = jnp.where(spread, 1.0, 0.0).astype(jnp.bfloat16)
    sums = lax.dot_general(
        left.astype(jnp.bfloat16), right, (((1,), (1,)), ((), ())), preferred_element_type=F32
    )
    return sums[:rows] + sums[rows : 2 * rows] + sums[2 * rows :]


def spread_current(current, nodes, maps, chain, torso, shares_ref, place_ref):
    slots = maps.shape[1]
    peers = maps.shape[0]
    outgoing = gather(
        lambda h: jnp.broadcast_to(current[h : h + 1], (2 * peers, LANES)), current.shape[0], nodes
    )
    shares_ref[...] = jnp.zeros_like(shares_ref)
    for o in range(peers):
        share = scatter(outgoing[o : o + 1], jnp.where(nodes[o : o + 1] < 0, -1, maps[o : o + 1]), torso)
        at = pl.ds(pl.multiple_of(place_ref[o] * torso, 8), torso)
        shares_ref[at, :] = shares_ref[at, :] + share
    del slots


def feedback_of(estimates, nodes, maps, heart):
    peers = nodes.shape[0]
    torso = estimates[0].shape[0]

    def source(h):
        rows = [estimate[h : h + 1] for estimate in estimates]
        return jnp.concatenate(rows * 2, axis=0)

    live = jnp.where(nodes < 0, -1, maps)
    returned = gather(source, torso, live)
    total = jnp.zeros((heart, LANES), F32)
    for o in range(peers):
        total = total + scatter(returned[o : o + 1], nodes[o : o + 1], heart)
    return total


def product(own_ref, other_ref, own_cols, other_cols, window_ref, out_ref):
    tiles, slots = own_ref.shape[0], own_ref.shape[1]
    eye = lax.broadcasted_iota(jnp.int32, (LANES, LANES), 0) == lax.broadcasted_iota(
        jnp.int32, (LANES, LANES), 1
    )

    def row(t, carry):
        total = None
        for ref, cols in ((own_ref, own_cols), (other_ref, other_cols)):
            for k in range(slots):
                term = ref[t, k] * window_ref[pl.ds(cols[t, k], 1), :]
                total = term if total is None else total + term
        column = jnp.sum(total, axis=1, keepdims=True)
        out_ref[pl.ds(t, 1), :] = jnp.sum(jnp.where(eye, column, 0.0), axis=0, keepdims=True)
        return carry

    lax.fori_loop(0, tiles, row, 0)


def first_ionic(states_ref, out_ref, current_ref):
    chunks = out_ref.shape[1]
    for k in range(chunks):
        out_ref[:, k, :] = states_ref[:, k * LANES : (k + 1) * LANES]
    rows, current = ionic_rows([out_ref[i] for i in range(out_ref.shape[0])])
    for i, row in enumerate(rows):
        out_ref[i] = row
    current_ref[...] = current


def first_shares(chain, torso, place_ref, current_ref, nodes_ref, maps_ref, shares_ref):
    spread_current(
        current_ref[...], nodes_ref[...], maps_ref[...], chain, torso, shares_ref, place_ref
    )


def next_shares(
    chain, torso, place_ref, states_ref, e0, e1, e2, e3, nodes_ref, maps_ref, out_ref, shares_ref
):
    nodes, maps = nodes_ref[...], maps_ref[...]
    feedback = feedback_of([e[...] for e in (e0, e1, e2, e3)], nodes, maps, states_ref.shape[1])
    rows = [states_ref[i] for i in range(states_ref.shape[0])]
    rows[0] = rows[0] + TIME_STEP * FEEDBACK_RATE * feedback
    rows, current = ionic_rows(rows)
    for i, row in enumerate(rows):
        out_ref[i] = row
    spread_current(current, nodes, maps, chain, torso, shares_ref, place_ref)


def last_feedback(states_ref, e0, e1, e2, e3, nodes_ref, maps_ref, out_ref, dense_ref):
    nodes, maps = nodes_ref[...], maps_ref[...]
    feedback = feedback_of([e[...] for e in (e0, e1, e2, e3)], nodes, maps, states_ref.shape[1])
    dense_ref[...] = states_ref[...]
    dense_ref[0] = states_ref[0] + TIME_STEP * FEEDBACK_RATE * feedback
    for k in range(states_ref.shape[1]):
        out_ref[:, k * LANES : (k + 1) * LANES] = dense_ref[:, k, :]


def sweep_one(
    chain, place_ref, own_cols, other_cols, own_ref, other_ref, forcing_ref, diag_ref,
    residual_ref, direction_ref, estimate_ref, window_ref, product_ref,
):
    torso = residual_ref.shape[0]
    here = place_ref[0]
    before = forcing_ref[pl.ds(pl.multiple_of(jnp.maximum(here - 1, 0) * torso, 8), torso), :]
    after = forcing_ref[pl.ds(pl.multiple_of(jnp.minimum(here + 1, chain - 1) * torso, 8), torso), :]
    own = forcing_ref[pl.ds(pl.multiple_of(here * torso, 8), torso), :]
    before = jnp.where(here > 0, before[torso - HALO :], 0.0)
    after = jnp.where(here < chain - 1, after[:HALO], 0.0)
    diag = diag_ref[HALO : HALO + torso]
    residual = TORSO_COUPLING * own
    direction = residual / (CHEB_THETA * diag)
    window_ref[0:HALO] = TORSO_COUPLING * before / (CHEB_THETA * diag_ref[0:HALO])
    window_ref[HALO : HALO + torso] = direction
    window_ref[HALO + torso : 2 * HALO + torso] = (
        TORSO_COUPLING * after / (CHEB_THETA * diag_ref[HALO + torso : 2 * HALO + torso])
    )
    product(own_ref, other_ref, own_cols, other_cols, window_ref, product_ref)
    residual = residual - (diag * direction + product_ref[...])
    estimate = direction
    direction = KEEP[0] * direction + PULL[0] * (residual / diag)
    residual_ref[...] = residual
    direction_ref[...] = direction
    estimate_ref[...] = estimate + direction


def sweep_two(
    own_cols, other_cols, own_ref, other_ref, before_ref, after_ref, direction_in, residual_in,
    estimate_in, diag_ref, residual_ref, direction_ref, estimate_ref, window_ref, product_ref,
):
    torso = residual_ref.shape[0]
    diag = diag_ref[HALO : HALO + torso]
    direction = direction_in[...]
    window_ref[0:HALO] = before_ref[...]
    window_ref[HALO : HALO + torso] = direction
    window_ref[HALO + torso : 2 * HALO + torso] = after_ref[...]
    product(own_ref, other_ref, own_cols, other_cols, window_ref, product_ref)
    residual = residual_in[...] - (diag * direction + product_ref[...])
    direction = KEEP[1] * direction + PULL[1] * (residual / diag)
    residual_ref[...] = residual
    direction_ref[...] = direction
    estimate_ref[...] = estimate_in[...] + direction


def last_residual(
    own_cols, other_cols, own_ref, other_ref, before_ref, after_ref, direction_in, residual_in,
    diag_ref, residual_ref, window_ref, product_ref,
):
    torso = residual_ref.shape[0]
    diag = diag_ref[HALO : HALO + torso]
    direction = direction_in[...]
    window_ref[0:HALO] = before_ref[...]
    window_ref[HALO : HALO + torso] = direction
    window_ref[HALO + torso : 2 * HALO + torso] = after_ref[...]
    product(own_ref, other_ref, own_cols, other_cols, window_ref, product_ref)
    residual_ref[...] = residual_in[...] - (diag * direction + product_ref[...])


def on_device(states, send_node, send_count, recv_row, columns, tile_values, diagonal):
    chain = lax.axis_size("dom")
    here = lax.axis_index("dom")
    peers, slots = send_node.shape[1:]
    node_count = states.shape[1]
    heart = node_count // LANES
    torso = diagonal.shape[0] // LANES
    offsets = [0, 1, chain - 1, chain // 2]
    place = ((here + jnp.array(offsets, jnp.int32)) % chain).astype(jnp.int32)

    def from_peer(value, offset):
        return lax.ppermute(value, "dom", [((i + offset) % chain, i) for i in range(chain)])

    def from_neighbour(value, offset):
        pairs = [(i + offset, i) for i in range(chain) if 0 <= i + offset < chain]
        return lax.ppermute(value, "dom", pairs)

    def shape(*dims):
        return jax.ShapeDtypeStruct(dims, F32)

    edge = HALO * LANES
    flip = [(0, 1), (1, 0)]
    rows_out = recv_row[0].astype(F32)
    got_after = from_peer(jnp.concatenate([rows_out[1], diagonal[:edge]]), 1)
    got_before = from_peer(jnp.concatenate([rows_out[2], diagonal[-edge:]]), chain - 1)
    got_far = from_peer(rows_out[3], chain // 2)
    other_tiles = lax.ppermute(tile_values, "sub", flip)
    other_cols = lax.ppermute(columns, "sub", flip)
    maps = jnp.stack([rows_out[0], got_after[:slots], got_before[:slots], got_far]).astype(jnp.int32)
    diag = jnp.concatenate([got_before[slots:], diagonal, got_after[slots:]]).reshape(-1, LANES)
    live = jnp.arange(slots, dtype=jnp.int32)[None, :] < send_count[0][:, None]
    nodes = jnp.where(live, send_node[0], -1)

    dense = shape(states.shape[0], heart, LANES)
    field = shape(torso, LANES)
    part = shape(chain * torso, LANES)
    work = (pltpu.VMEM((torso + 2 * HALO + 4, LANES), F32), pltpu.VMEM((torso, LANES), F32))

    states, current = call(first_ionic, (dense, shape(heart, LANES)))(in_specs=[VMEM])(states)
    shares = call(functools.partial(first_shares, chain, torso), part)(
        in_specs=[SMEM] + [VMEM] * 3
    )(place, current, nodes, maps)
    for time_step in range(2):
        last = time_step == 1
        forcing = lax.psum(shares, ("dom", "sub"))
        residual, direction, estimate = call(
            functools.partial(sweep_one, chain), (field,) * 3, work
        )(in_specs=[SMEM] * 3 + [VMEM] * 4)(
            place, columns, other_cols, tile_values, other_tiles, forcing, diag
        )
        before = from_neighbour(direction[-HALO:], -1)
        after = from_neighbour(direction[:HALO], 1)
        residual, direction, estimate = call(sweep_two, (field,) * 3, work)(
            in_specs=[SMEM] * 2 + [VMEM] * 8
        )(
            columns, other_cols, tile_values, other_tiles, before, after, direction, residual,
            estimate, diag,
        )
        estimates = [estimate] + [from_peer(estimate, offset) for offset in offsets[1:]]
        if not last:
            states, shares = call(
                functools.partial(next_shares, chain, torso), (dense, part)
            )(in_specs=[SMEM] + [VMEM] * 7)(place, states, *estimates, nodes, maps)
            continue
        before = from_neighbour(direction[-HALO:], -1)
        after = from_neighbour(direction[:HALO], 1)
        residual = call(last_residual, field, work)(in_specs=[SMEM] * 2 + [VMEM] * 7)(
            columns, other_cols, tile_values, other_tiles, before, after, direction, residual, diag
        )
        new_states = call(
            last_feedback, shape(19, node_count), (pltpu.VMEM(dense.shape, F32),)
        )(in_specs=[VMEM] * 7)(states, *estimates, nodes, maps)
    return new_states, estimate.reshape(-1), residual.reshape(-1)


def solution(mesh):
    placed = (
        P(None, ("case", "dom", "sub")),
        P(("case", "dom", "sub"), None, None),
        P(("case", "dom", "sub"), None),
        P(("case", "dom", "sub"), None, None),
        P(("case", "dom"), "sub"),
        P(("case", "dom"), "sub", None, None),
        P(("case", "dom")),
    )
    return jax.shard_map(
        on_device,
        mesh=mesh,
        in_specs=placed,
        out_specs=(P(None, ("case", "dom", "sub")), P(("case", "dom")), P(("case", "dom"))),
        check_vma=False,
    )
```

time: 220 us -> 188 us (0.85)
  blocking collectives: 35.9 us -> 117 us
  other arithmetic: 57.3 us -> 2.9 us
  local copies, waits for them, and re-layouts: 47.4 us -> 10.2 us
  waiting for transfers between devices: 33.5 us -> 8.37 us
  Pallas kernels: 0 us -> 13.9 us
  matrix products: 10.5 us -> 0 us
    psum x7 -> x2, blocking collectives: 17.3 us -> 117 us  [on_device(): forcing = lax.psum(shares, ('dom', 'sub'))]
    scatter-add x4 -> x0, other arithmetic: 52 us -> none  [the longest x2 29.3 us: on_device(): jnp.zeros((torso_rows,), jnp.float32).at[land_rows]]
    gather x11 -> x0, local copies, waits for them, and re-layouts: 43.6 us -> none  [the longest x4 23.6 us: on_device(): outgoing = jnp.where(slot_live, current[node_slots], 0.0)]
    all_to_all x2 -> x0, blocking collectives: 18.7 us -> none  [the longest x1 9.75 us: on_device(): lax.all_to_all(padded_back, 'dom', split_axis=0, concat_axis=0, tiled=True)]
    pallas_call x0 -> x9, Pallas kernels: none -> 13.9 us  [the longest x2 4.64 us: on_device(): call(sweep_two, (field,) * 3, work)(in_specs=[SMEM] * 2 + [VMEM] * 8)]
    all_to_all x2 -> x0, waiting for transfers between devices: 12.8 us -> none  [the longest x1 6.49 us: on_device(): lax.all_to_all(padded_back, 'dom', split_axis=0, concat_axis=0, tiled=True)]
    ppermute x10 -> x17, waiting for transfers between devices: 20.7 us -> 8.37 us  [the longest x9 4.54 us: from_peer(): lax.ppermute(value, 'dom', [((i + offset) % chain, i) for i in range(chai...]
    ppermute x10 -> x17, starting transfers between devices: 22.6 us -> 33.5 us  [the longest x6 17.5 us: from_neighbour(): return lax.ppermute(value, 'dom', pairs)]
  transfers between devices with their start and end apart: 12 -> 17, of which waited for: 7 -> 5; matrix products, arithmetic and copies ran while one was open for 0% -> 2% of each run, Pallas kernels for 0% -> 2%
where the time goes in v1:
time: 188 us; the launch traced here: 187 us
  blocking collectives  117 us (62%)
  starting transfers between devices  33.5 us (18%)
  Pallas kernels  13.9 us (7%)
  local copies, waits for them, and re-layouts  10.2 us (5%)
  waiting for transfers between devices  8.37 us (4%)
  other arithmetic  2.9 us (2%)
    psum x2, blocking collectives, on_device(): forcing = lax.psum(shares, ('dom', 'sub'))  117 us
    ppermute x6, starting transfers between devices, from_neighbour(): return lax.ppermute(value, 'dom', pairs)  17.5 us
    ppermute x9, starting transfers between devices, from_peer(): lax.ppermute(value, 'dom', [((i + offset) % chain, i) for i in range(chai...  15.4 us
    unnamed x17, local copies, waits for them, and re-layouts  9.41 us
    pallas_call x2, Pallas kernels, on_device(): call(sweep_two, (field,) * 3, work)(in_specs=[SMEM] * 2 + [VMEM] * 8)  4.64 us
    ppermute x9, waiting for transfers between devices, from_peer(): lax.ppermute(value, 'dom', [((i + offset) % chain, i) for i in range(chai...  4.54 us
    ppermute x6, waiting for transfers between devices, from_neighbour(): return lax.ppermute(value, 'dom', pairs)  3.82 us
  transfers between devices with their start and end apart: 17, of which 5 were waited for; matrix products, arithmetic and copies ran while one was open for 2% of the time, Pallas kernels for 2%

profile of v1, /device:TPU:0, one launch (start us, length us, event | category | flops | bytes accessed | tf_op | source)
XLA Modules:
  0.0 187.1 jit_solution(3438478135832459773)
XLA Ops:
  1.9 3.7 %collective-permute-start.4 = (f32[512]{0:T(512)S(1)}, f32[512]{0:T(512)S(1)}, u32[]{:S(2)}, u32[]{:S(2)}) collective-permute-start(f32[512]{0:T(512)S(1)} %bitcast.21), channel_id=1, source_target_pairs={{8,0},{10,2},{12,4},{14,6},{0,8},{2,10},{4,12},{6,14},{9,1},{11,3}... | collective-permute-start | bytes 6152 | tf_op jit(solution)/shard_map/ppermute | solution.py:288
  6.3 2.3 %collective-permute-start.2 = (f32[768]{0:T(1024)S(1)}, f32[768]{0:T(1024)S(1)}, u32[]{:S(2)}, u32[]{:S(2)}) collective-permute-start(f32[768]{0:T(1024)S(1)} %pad_maximum_fusion), channel_id=1, source_target_pairs={{2,0},{4,2},{6,4},{8,6},{10,8},{12,10},{14,12},{0,14},{3,1},{5,3},... | collective-permute-start | bytes 9224 | tf_op jit(solution)/shard_map/ppermute | solution.py:288
  12.0 2.9 %collective-permute-done.3 = f32[768]{0:T(1024)S(1)} collective-permute-done((f32[768]{0:T(1024)S(1)}, f32[768]{0:T(1024)S(1)}, u32[]{:S(2)}, u32[]{:S(2)}) %collective-permute-start.3) | collective-permute-done | bytes 3104 | tf_op jit(solution)/shard_map/ppermute | solution.py:288
  16.6 59.4 %psum.14.forcing_ref = f32[64,128]{1,0:T(8,128)S(1)} all-reduce(f32[64,128]{1,0:T(8,128)S(1)} %shard_map.104), channel_id=1, replica_groups=mesh['case'=2,'dom'=8,'sub'=2] {'dom','sub'}, use_global_device_ids=true, to_apply=%region_0.1 | all-reduce | flops 8192 | bytes 65536 | tf_op jit(solution)/shard_map/psum | solution.py:321
  76.0 1.3 copy-done.2
  77.3 1.6 copy-done
  78.9 1.6 copy-done.3
  80.5 1.7 shard_map.105
  83.5 4.5 %collective-permute-start.5 = (f32[2,128]{1,0:T(2,128)S(1)}, f32[2,128]{1,0:T(2,128)S(1)}, u32[]{:S(2)}, u32[]{:S(2)}) collective-permute-start(f32[2,128]{1,0:T(2,128)S(1)} %get-tuple-element.40), channel_id=1, source_target_pairs={{0,2},{2,4},{4,6},{6,8},{8,10},{10,12},{12,14},{1,3},{3,5},{5,7},{... | collective-permute-start | bytes 3080 | tf_op jit(solution)/shard_map/ppermute | solution.py:292
  89.4 1.6 copy-done.4
  91.0 2.4 %shard_map.106 = (f32[8,128]{1,0:T(8,128)}, f32[8,128]{1,0:T(8,128)}, f32[8,128]{1,0:T(8,128)S(1)}) custom-call(s32[8,4]{1,0:T(8,128)S(1)} %copy.13.own_cols, s32[8,4]{1,0:T(8,128)S(1)} %collective-permute-done.other_cols, f32[8,4,128,128]{3,2,1,0:T(8,128)S(1)} %copy-done.1, f32[8,4,128,128]{3,2,1,0:T(8,128)S(1)} %copy-done.4, ...), custom_call_target="tpu_custom_call" | custom-call | flops 4000000 | bytes 262144 | tf_op jit(solution)/shard_map/pallas_call | solution.py:329
  93.3 2.3 %collective-permute-start.8 = (f32[8,128]{1,0:T(8,128)S(1)}, f32[8,128]{1,0:T(8,128)S(1)}, u32[]{:S(2)}, u32[]{:S(2)}) collective-permute-start(f32[8,128]{1,0:T(8,128)S(1)} %get-tuple-element.22.e0), channel_id=1, source_target_pairs={{14,0},{0,2},{2,4},{4,6},{6,8},{8,10},{10,12},{12,14},{15,1},{1,3}... | collective-permute-start | bytes 12296 | tf_op jit(solution)/shard_map/ppermute | solution.py:288
  95.6 2.5 %collective-permute-start.7 = (f32[8,128]{1,0:T(8,128)S(1)}, f32[8,128]{1,0:T(8,128)S(1)}, u32[]{:S(2)}, u32[]{:S(2)}) collective-permute-start(f32[8,128]{1,0:T(8,128)S(1)} %get-tuple-element.22.e0), channel_id=1, source_target_pairs={{2,0},{4,2},{6,4},{8,6},{10,8},{12,10},{14,12},{0,14},{3,1},{5,3},... | collective-permute-start | bytes 12296 | tf_op jit(solution)/shard_map/ppermute | solution.py:288
  98.0 1.6 collective-permute-done.8.e2
  99.6 1.5 shard_map.107
  101.1 58.0 %psum.15.forcing_ref = f32[64,128]{1,0:T(8,128)S(1)} all-reduce(f32[64,128]{1,0:T(8,128)S(1)} %get-tuple-element.24), channel_id=1, replica_groups=mesh['case'=2,'dom'=8,'sub'=2] {'dom','sub'}, use_global_device_ids=true, to_apply=%region_1.2 | all-reduce | flops 8192 | bytes 65536 | tf_op jit(solution)/shard_map/psum | solution.py:321
  159.1 1.6 copy-done.5
  160.7 1.7 shard_map.108
  163.7 4.5 %collective-permute-start.10 = (f32[2,128]{1,0:T(2,128)S(1)}, f32[2,128]{1,0:T(2,128)S(1)}, u32[]{:S(2)}, u32[]{:S(2)}) collective-permute-start(f32[2,128]{1,0:T(2,128)S(1)} %get-tuple-element.38), channel_id=1, source_target_pairs={{0,2},{2,4},{4,6},{6,8},{8,10},{10,12},{12,14},{1,3},{3,5},{5,7},{... | collective-permute-start | bytes 3080 | tf_op jit(solution)/shard_map/ppermute | solution.py:292
  169.6 2.3 %shard_map.109 = (f32[8,128]{1,0:T(8,128)S(1)}, f32[8,128]{1,0:T(8,128)S(1)}, f32[8,128]{1,0:T(8,128)}) custom-call(s32[8,4]{1,0:T(8,128)S(1)} %copy.13.own_cols, s32[8,4]{1,0:T(8,128)S(1)} %collective-permute-done.other_cols, f32[8,4,128,128]{3,2,1,0:T(8,128)S(1)} %copy-done.1, f32[8,4,128,128]{3,2,1,0:T(8,128)S(1)} %copy-done.5, ...), custom_call_target="tpu_custom_call" | custom-call | flops 4000000 | bytes 262144 | tf_op jit(solution)/shard_map/pallas_call | solution.py:329
  171.9 2.3 %collective-permute-start.13 = (f32[8,128]{1,0:T(8,128)}, f32[8,128]{1,0:T(8,128)S(1)}, u32[]{:S(2)}, u32[]{:S(2)}) collective-permute-start(f32[8,128]{1,0:T(8,128)} %get-tuple-element.28.e0), channel_id=1, source_target_pairs={{14,0},{0,2},{2,4},{4,6},{6,8},{8,10},{10,12},{12,14},{15,1},{1,3}... | collective-permute-start | bytes 12296 | tf_op jit(solution)/shard_map/ppermute | solution.py:288
  174.1 2.5 %collective-permute-start.12 = (f32[8,128]{1,0:T(8,128)}, f32[8,128]{1,0:T(8,128)S(1)}, u32[]{:S(2)}, u32[]{:S(2)}) collective-permute-start(f32[8,128]{1,0:T(8,128)} %get-tuple-element.28.e0), channel_id=1, source_target_pairs={{2,0},{4,2},{6,4},{8,6},{10,8},{12,10},{14,12},{0,14},{3,1},{5,3},... | collective-permute-start | bytes 12296 | tf_op jit(solution)/shard_map/ppermute | solution.py:288
  177.9 4.5 %collective-permute-start.15 = (f32[2,128]{1,0:T(2,128)S(1)}, f32[2,128]{1,0:T(2,128)S(1)}, u32[]{:S(2)}, u32[]{:S(2)}) collective-permute-start(f32[2,128]{1,0:T(2,128)S(1)} %get-tuple-element.36), channel_id=1, source_target_pairs={{0,2},{2,4},{4,6},{6,8},{8,10},{10,12},{12,14},{1,3},{3,5},{5,7},{... | collective-permute-start | bytes 3080 | tf_op jit(solution)/shard_map/ppermute | solution.py:292
  183.7 2.3 %shard_map.111 = f32[8,128]{1,0:T(8,128)} custom-call(s32[8,4]{1,0:T(8,128)S(1)} %copy.13.own_cols, s32[8,4]{1,0:T(8,128)S(1)} %collective-permute-done.other_cols, f32[8,4,128,128]{3,2,1,0:T(8,128)S(1)} %copy-done.1, f32[8,4,128,128]{3,2,1,0:T(8,128)S(1)} %copy-done.5, f32[2,128]{1,0:T(2,128)S(1)} %collective-permute-done.15.before_ref, ...), custom_call_target="tpu_custom_call" | custom-call | flops 4000000 | bytes 262144 | tf_op jit(solution)/shard_map/pallas_call | solution.py:343
  (54 shorter events, 15.8 us)
Async XLA Ops:
  0.6 75.4 %collective-permute-start.1 = (f32[8,4,128,128]{3,2,1,0:T(8,128)}, f32[8,4,128,128]{3,2,1,0:T(8,128)S(1)}, u32[]{:S(2)}, u32[]{:S(2)}) collective-permute-start(f32[8,4,128,128]{3,2,1,0:T(8,128)} %own_ref.9), channel_id=1, source_target_pairs={{0,1},{1,0},{2,3},{3,2},{4,5},{5,4},{6,7},{7,6},{8,9},{9,8},{10,11... | collective-permute-start | bytes 6291464 | tf_op jit(solution)/shard_map/ppermute | solution.py:303
  1.9 13.1 %collective-permute-start.4 = (f32[512]{0:T(512)S(1)}, f32[512]{0:T(512)S(1)}, u32[]{:S(2)}, u32[]{:S(2)}) collective-permute-start(f32[512]{0:T(512)S(1)} %bitcast.21), channel_id=1, source_target_pairs={{8,0},{10,2},{12,4},{14,6},{0,8},{2,10},{4,12},{6,14},{9,1},{11,3}... | collective-permute-start | bytes 6152 | tf_op jit(solution)/shard_map/ppermute | solution.py:288
  6.3 5.7 %collective-permute-start.2 = (f32[768]{0:T(1024)S(1)}, f32[768]{0:T(1024)S(1)}, u32[]{:S(2)}, u32[]{:S(2)}) collective-permute-start(f32[768]{0:T(1024)S(1)} %pad_maximum_fusion), channel_id=1, source_target_pairs={{2,0},{4,2},{6,4},{8,6},{10,8},{12,10},{14,12},{0,14},{3,1},{5,3},... | collective-permute-start | bytes 9224 | tf_op jit(solution)/shard_map/ppermute | solution.py:288
  8.6 6.3 %collective-permute-start.3 = (f32[768]{0:T(1024)S(1)}, f32[768]{0:T(1024)S(1)}, u32[]{:S(2)}, u32[]{:S(2)}) collective-permute-start(f32[768]{0:T(1024)S(1)} %pad_maximum_fusion.1), channel_id=1, source_target_pairs={{14,0},{0,2},{2,4},{4,6},{6,8},{8,10},{10,12},{12,14},{15,1},{1,3}... | collective-permute-start | bytes 9224 | tf_op jit(solution)/shard_map/ppermute | solution.py:288
  9.4 66.6 %collective-permute-start = (s32[8,4]{1,0:T(8,128)S(1)}, s32[8,4]{1,0:T(8,128)S(1)}, u32[]{:S(2)}, u32[]{:S(2)}) collective-permute-start(s32[8,4]{1,0:T(8,128)S(1)} %copy.13.own_cols), channel_id=1, source_target_pairs={{0,1},{1,0},{2,3},{3,2},{4,5},{5,4},{6,7},{7,6},{8,9},{9,8},{10,11... | collective-permute-start | bytes 392 | tf_op jit(solution)/shard_map/ppermute | solution.py:304
  76.0 1.4 copy-start.2
  77.3 1.6 copy-start
  78.9 1.6 copy-start.3
  80.5 8.8 %copy-start.1 = (f32[8,4,128,128]{3,2,1,0:T(8,128)S(1)}, f32[8,4,128,128]{3,2,1,0:T(8,128)}, u32[]{:S(2)}) copy-start(f32[8,4,128,128]{3,2,1,0:T(8,128)} %own_ref.9) | copy-start | bytes 6291460
  82.2 5.9 %collective-permute-start.6 = (f32[2,128]{1,0:T(2,128)S(1)}, f32[2,128]{1,0:T(2,128)S(1)}, u32[]{:S(2)}, u32[]{:S(2)}) collective-permute-start(f32[2,128]{1,0:T(2,128)S(1)} %get-tuple-element.39), channel_id=1, source_target_pairs={{2,0},{4,2},{6,4},{8,6},{10,8},{12,10},{14,12},{3,1},{5,3},{7,5},{... | collective-permute-start | bytes 3080 | tf_op jit(solution)/shard_map/ppermute | solution.py:292
  83.5 5.8 %collective-permute-start.5 = (f32[2,128]{1,0:T(2,128)S(1)}, f32[2,128]{1,0:T(2,128)S(1)}, u32[]{:S(2)}, u32[]{:S(2)}) collective-permute-start(f32[2,128]{1,0:T(2,128)S(1)} %get-tuple-element.40), channel_id=1, source_target_pairs={{0,2},{2,4},{4,6},{6,8},{8,10},{10,12},{12,14},{1,3},{3,5},{5,7},{... | collective-permute-start | bytes 3080 | tf_op jit(solution)/shard_map/ppermute | solution.py:292
  89.4 1.6 copy-start.4
  93.3 4.7 %collective-permute-start.9 = (f32[8,128]{1,0:T(8,128)S(1)}, f32[8,128]{1,0:T(8,128)S(1)}, u32[]{:S(2)}, u32[]{:S(2)}) collective-permute-start(f32[8,128]{1,0:T(8,128)S(1)} %get-tuple-element.22.e0), channel_id=1, source_target_pairs={{8,0},{10,2},{12,4},{14,6},{0,8},{2,10},{4,12},{6,14},{9,1},{11,3}... | collective-permute-start | bytes 12296 | tf_op jit(solution)/shard_map/ppermute | solution.py:288
  93.3 6.3 %collective-permute-start.8 = (f32[8,128]{1,0:T(8,128)S(1)}, f32[8,128]{1,0:T(8,128)S(1)}, u32[]{:S(2)}, u32[]{:S(2)}) collective-permute-start(f32[8,128]{1,0:T(8,128)S(1)} %get-tuple-element.22.e0), channel_id=1, source_target_pairs={{14,0},{0,2},{2,4},{4,6},{6,8},{8,10},{10,12},{12,14},{15,1},{1,3}... | collective-permute-start | bytes 12296 | tf_op jit(solution)/shard_map/ppermute | solution.py:288
  95.6 4.0 %collective-permute-start.7 = (f32[8,128]{1,0:T(8,128)S(1)}, f32[8,128]{1,0:T(8,128)S(1)}, u32[]{:S(2)}, u32[]{:S(2)}) collective-permute-start(f32[8,128]{1,0:T(8,128)S(1)} %get-tuple-element.22.e0), channel_id=1, source_target_pairs={{2,0},{4,2},{6,4},{8,6},{10,8},{12,10},{14,12},{0,14},{3,1},{5,3},... | collective-permute-start | bytes 12296 | tf_op jit(solution)/shard_map/ppermute | solution.py:288
  159.1 1.6 copy-start.5
  162.4 5.9 %collective-permute-start.11 = (f32[2,128]{1,0:T(2,128)S(1)}, f32[2,128]{1,0:T(2,128)S(1)}, u32[]{:S(2)}, u32[]{:S(2)}) collective-permute-start(f32[2,128]{1,0:T(2,128)S(1)} %get-tuple-element.37), channel_id=1, source_target_pairs={{2,0},{4,2},{6,4},{8,6},{10,8},{12,10},{14,12},{3,1},{5,3},{7,5},{... | collective-permute-start | bytes 3080 | tf_op jit(solution)/shard_map/ppermute | solution.py:292
  163.7 5.8 %collective-permute-start.10 = (f32[2,128]{1,0:T(2,128)S(1)}, f32[2,128]{1,0:T(2,128)S(1)}, u32[]{:S(2)}, u32[]{:S(2)}) collective-permute-start(f32[2,128]{1,0:T(2,128)S(1)} %get-tuple-element.38), channel_id=1, source_target_pairs={{0,2},{2,4},{4,6},{6,8},{8,10},{10,12},{12,14},{1,3},{3,5},{5,7},{... | collective-permute-start | bytes 3080 | tf_op jit(solution)/shard_map/ppermute | solution.py:292
  171.9 14.1 %collective-permute-start.14 = (f32[8,128]{1,0:T(8,128)}, f32[8,128]{1,0:T(8,128)S(1)}, u32[]{:S(2)}, u32[]{:S(2)}) collective-permute-start(f32[8,128]{1,0:T(8,128)} %get-tuple-element.28.e0), channel_id=1, source_target_pairs={{8,0},{10,2},{12,4},{14,6},{0,8},{2,10},{4,12},{6,14},{9,1},{11,3}... | collective-permute-start | bytes 12296 | tf_op jit(solution)/shard_map/ppermute | solution.py:288
  171.9 14.1 %collective-permute-start.13 = (f32[8,128]{1,0:T(8,128)}, f32[8,128]{1,0:T(8,128)S(1)}, u32[]{:S(2)}, u32[]{:S(2)}) collective-permute-start(f32[8,128]{1,0:T(8,128)} %get-tuple-element.28.e0), channel_id=1, source_target_pairs={{14,0},{0,2},{2,4},{4,6},{6,8},{8,10},{10,12},{12,14},{15,1},{1,3}... | collective-permute-start | bytes 12296 | tf_op jit(solution)/shard_map/ppermute | solution.py:288
  174.1 11.9 %collective-permute-start.12 = (f32[8,128]{1,0:T(8,128)}, f32[8,128]{1,0:T(8,128)S(1)}, u32[]{:S(2)}, u32[]{:S(2)}) collective-permute-start(f32[8,128]{1,0:T(8,128)} %get-tuple-element.28.e0), channel_id=1, source_target_pairs={{2,0},{4,2},{6,4},{8,6},{10,8},{12,10},{14,12},{0,14},{3,1},{5,3},... | collective-permute-start | bytes 12296 | tf_op jit(solution)/shard_map/ppermute | solution.py:288
  176.6 5.8 %collective-permute-start.16 = (f32[2,128]{1,0:T(2,128)S(1)}, f32[2,128]{1,0:T(2,128)S(1)}, u32[]{:S(2)}, u32[]{:S(2)}) collective-permute-start(f32[2,128]{1,0:T(2,128)S(1)} %get-tuple-element.35), channel_id=1, source_target_pairs={{2,0},{4,2},{6,4},{8,6},{10,8},{12,10},{14,12},{3,1},{5,3},{7,5},{... | collective-permute-start | bytes 3080 | tf_op jit(solution)/shard_map/ppermute | solution.py:292
  177.9 5.8 %collective-permute-start.15 = (f32[2,128]{1,0:T(2,128)S(1)}, f32[2,128]{1,0:T(2,128)S(1)}, u32[]{:S(2)}, u32[]{:S(2)}) collective-permute-start(f32[2,128]{1,0:T(2,128)S(1)} %get-tuple-element.36), channel_id=1, source_target_pairs={{0,2},{2,4},{4,6},{6,8},{8,10},{10,12},{12,14},{1,3},{3,5},{5,7},{... | collective-permute-start | bytes 3080 | tf_op jit(solution)/shard_map/ppermute | solution.py:292
  183.7 2.3 %copy-start.7 = (f32[8,128]{1,0:T(8,128)S(1)}, f32[8,128]{1,0:T(8,128)}, u32[]{:S(2)}) copy-start(f32[8,128]{1,0:T(8,128)} %get-tuple-element.28.e0) | copy-start | bytes 12292
  (1 other events, 0.9 us)

commit v2 on v1

--- a/solution.py
+++ b/solution.py
@@ -127,18 +127,35 @@
     return sums[:rows] + sums[rows : 2 * rows] + sums[2 * rows :]
 
 
-def spread_current(current, nodes, maps, chain, torso, shares_ref, place_ref):
-    slots = maps.shape[1]
+def spread_current(current, nodes, maps, chain, torso, shares_ref, blocks_ref):
     peers = maps.shape[0]
+    copies = blocks_ref.shape[0] // chain
     outgoing = gather(
         lambda h: jnp.broadcast_to(current[h : h + 1], (2 * peers, LANES)), current.shape[0], nodes
     )
     shares_ref[...] = jnp.zeros_like(shares_ref)
-    for o in range(peers):
-        share = scatter(outgoing[o : o + 1], jnp.where(nodes[o : o + 1] < 0, -1, maps[o : o + 1]), torso)
-        at = pl.ds(pl.multiple_of(place_ref[o] * torso, 8), torso)
+    here = lax.axis_index("dom")
+    for o, offset in enumerate(peer_offsets(chain)):
+        share = scatter(outgoing[o : o + 1], maps[o : o + 1], torso)
+        at = pl.ds(pl.multiple_of((lax.rem(here + offset, chain) + 1) * torso, 8), torso)
         shares_ref[at, :] = shares_ref[at, :] + share
-    del slots
+
+    def block(q, carry):
+        before, own, after = (
+            shares_ref[pl.ds(pl.multiple_of((q + k) * torso, 8), torso), :] for k in range(3)
+        )
+        filler = jnp.zeros((torso - 2 * HALO, LANES), F32)
+        rims = jnp.concatenate([before[torso - HALO :], after[:HALO], filler], axis=0)
+        for k in range(copies):
+            blocks_ref[q * copies + k, 0:torso] = own
+            blocks_ref[q * copies + k, torso : 2 * torso] = rims
+        return carry
+
+    lax.fori_loop(0, chain, block, 0)
+
+
+def peer_offsets(chain):
+    return [0, 1, chain - 1, chain // 2]
 
 
 def feedback_of(estimates, nodes, maps, heart):
@@ -149,8 +166,7 @@
         rows = [estimate[h : h + 1] for estimate in estimates]
         return jnp.concatenate(rows * 2, axis=0)
 
-    live = jnp.where(nodes < 0, -1, maps)
-    returned = gather(source, torso, live)
+    returned = gather(source, torso, maps)
     total = jnp.zeros((heart, LANES), F32)
     for o in range(peers):
         total = total + scatter(returned[o : o + 1], nodes[o : o + 1], heart)
@@ -162,18 +178,30 @@
     eye = lax.broadcasted_iota(jnp.int32, (LANES, LANES), 0) == lax.broadcasted_iota(
         jnp.int32, (LANES, LANES), 1
     )
-
-    def row(t, carry):
+    for t in range(tiles):
         total = None
         for ref, cols in ((own_ref, own_cols), (other_ref, other_cols)):
             for k in range(slots):
-                term = ref[t, k] * window_ref[pl.ds(cols[t, k], 1), :]
+                term = ref[t, k] * window_ref[pl.ds(cols[k, t], 1), :]
                 total = term if total is None else total + term
         column = jnp.sum(total, axis=1, keepdims=True)
-        out_ref[pl.ds(t, 1), :] = jnp.sum(jnp.where(eye, column, 0.0), axis=0, keepdims=True)
-        return carry
-
-    lax.fori_loop(0, tiles, row, 0)
+        out_ref[t : t + 1, :] = jnp.sum(jnp.where(eye, column, 0.0), axis=0, keepdims=True)
+
+
+def prepare(count_ref, node_ref, row_ref, diag_ref, nodes_ref, prev_ref, next_ref, far_ref):
+    peers, slots = nodes_ref.shape
+    torso = diag_ref.shape[0]
+    slot = lax.broadcasted_iota(jnp.int32, (1, slots), 1)
+    for o in range(peers):
+        nodes_ref[o : o + 1] = jnp.where(slot < count_ref[0, o], node_ref[0, o : o + 1], -1)
+    rows = [row_ref[0, o : o + 1].astype(F32) for o in range(peers)]
+    prev_ref[:, 0:slots] = rows[1]
+    next_ref[:, 0:slots] = rows[2]
+    far_ref[...] = rows[3]
+    for k in range(HALO):
+        at = slice(slots + k * LANES, slots + (k + 1) * LANES)
+        prev_ref[:, at] = diag_ref[k : k + 1]
+        next_ref[:, at] = diag_ref[torso - HALO + k : torso - HALO + k + 1]
 
 
 def first_ionic(states_ref, out_ref, current_ref):
@@ -186,28 +214,44 @@
     current_ref[...] = current
 
 
-def first_shares(chain, torso, place_ref, current_ref, nodes_ref, maps_ref, shares_ref):
-    spread_current(
-        current_ref[...], nodes_ref[...], maps_ref[...], chain, torso, shares_ref, place_ref
-    )
+def first_shares(
+    chain, current_ref, nodes_ref, row_ref, after_ref, before_ref, far_ref, diag_ref,
+    maps_ref, wide_ref, blocks_ref, shares_ref,
+):
+    nodes = nodes_ref[...]
+    slots = nodes.shape[1]
+    torso = diag_ref.shape[0]
+    rows = [after_ref[:, 0:slots], before_ref[:, 0:slots], far_ref[...]]
+    rows = [row_ref[0, 0:1]] + [row.astype(jnp.int32) for row in rows]
+    maps = jnp.where(nodes < 0, -1, jnp.concatenate(rows, axis=0))
+    maps_ref[...] = maps
+    wide_ref[HALO : HALO + torso] = diag_ref[...]
+    for k in range(HALO):
+        at = slice(slots + k * LANES, slots + (k + 1) * LANES)
+        wide_ref[k : k + 1] = before_ref[:, at]
+        wide_ref[HALO + torso + k : HALO + torso + k + 1] = after_ref[:, at]
+    spread_current(current_ref[...], nodes, maps, chain, torso, shares_ref, blocks_ref)
 
 
 def next_shares(
-    chain, torso, place_ref, states_ref, e0, e1, e2, e3, nodes_ref, maps_ref, out_ref, shares_ref
+    chain, states_ref, e0, e1, e2, e3, nodes_ref, maps_ref, out_ref, blocks_ref, shares_ref
 ):
     nodes, maps = nodes_ref[...], maps_ref[...]
+    torso = e0.shape[0]
     feedback = feedback_of([e[...] for e in (e0, e1, e2, e3)], nodes, maps, states_ref.shape[1])
     rows = [states_ref[i] for i in range(states_ref.shape[0])]
     rows[0] = rows[0] + TIME_STEP * FEEDBACK_RATE * feedback
     rows, current = ionic_rows(rows)
     for i, row in enumerate(rows):
         out_ref[i] = row
-    spread_current(current, nodes, maps, chain, torso, shares_ref, place_ref)
+    spread_current(current, nodes, maps, chain, torso, shares_ref, blocks_ref)
 
 
 def last_feedback(states_ref, e0, e1, e2, e3, nodes_ref, maps_ref, out_ref, dense_ref):
     nodes, maps = nodes_ref[...], maps_ref[...]
-    feedback = feedback_of([e[...] for e in (e0, e1, e2, e3)], nodes, maps, states_ref.shape[1])
+    torso = e0.shape[0]
+    estimates = [e0[...], e1[0:torso], e2[0:torso], e3[...]]
+    feedback = feedback_of(estimates, nodes, maps, states_ref.shape[1])
     dense_ref[...] = states_ref[...]
     dense_ref[0] = states_ref[0] + TIME_STEP * FEEDBACK_RATE * feedback
     for k in range(states_ref.shape[1]):
@@ -215,23 +259,19 @@
 
 
 def sweep_one(
-    chain, place_ref, own_cols, other_cols, own_ref, other_ref, forcing_ref, diag_ref,
+    own_cols, other_cols, own_ref, other_ref, parts_ref, diag_ref,
     residual_ref, direction_ref, estimate_ref, window_ref, product_ref,
 ):
     torso = residual_ref.shape[0]
-    here = place_ref[0]
-    before = forcing_ref[pl.ds(pl.multiple_of(jnp.maximum(here - 1, 0) * torso, 8), torso), :]
-    after = forcing_ref[pl.ds(pl.multiple_of(jnp.minimum(here + 1, chain - 1) * torso, 8), torso), :]
-    own = forcing_ref[pl.ds(pl.multiple_of(here * torso, 8), torso), :]
-    before = jnp.where(here > 0, before[torso - HALO :], 0.0)
-    after = jnp.where(here < chain - 1, after[:HALO], 0.0)
+    forcing = TORSO_COUPLING * jnp.sum(parts_ref[...], axis=0)
     diag = diag_ref[HALO : HALO + torso]
-    residual = TORSO_COUPLING * own
+    residual = forcing[0:torso]
     direction = residual / (CHEB_THETA * diag)
-    window_ref[0:HALO] = TORSO_COUPLING * before / (CHEB_THETA * diag_ref[0:HALO])
+    before, after = forcing[torso : torso + HALO], forcing[torso + HALO : torso + 2 * HALO]
+    window_ref[0:HALO] = before / (CHEB_THETA * diag_ref[0:HALO])
     window_ref[HALO : HALO + torso] = direction
     window_ref[HALO + torso : 2 * HALO + torso] = (
-        TORSO_COUPLING * after / (CHEB_THETA * diag_ref[HALO + torso : 2 * HALO + torso])
+        after / (CHEB_THETA * diag_ref[HALO + torso : 2 * HALO + torso])
     )
     product(own_ref, other_ref, own_cols, other_cols, window_ref, product_ref)
     residual = residual - (diag * direction + product_ref[...])
@@ -244,7 +284,8 @@
 
 def sweep_two(
     own_cols, other_cols, own_ref, other_ref, before_ref, after_ref, direction_in, residual_in,
-    estimate_in, diag_ref, residual_ref, direction_ref, estimate_ref, window_ref, product_ref,
+    estimate_in, diag_ref, residual_ref, direction_ref, estimate_ref, prev_ref, next_ref,
+    window_ref, product_ref,
 ):
     torso = residual_ref.shape[0]
     diag = diag_ref[HALO : HALO + torso]
@@ -255,34 +296,41 @@
     product(own_ref, other_ref, own_cols, other_cols, window_ref, product_ref)
     residual = residual_in[...] - (diag * direction + product_ref[...])
     direction = KEEP[1] * direction + PULL[1] * (residual / diag)
+    estimate = estimate_in[...] + direction
     residual_ref[...] = residual
     direction_ref[...] = direction
-    estimate_ref[...] = estimate_in[...] + direction
+    estimate_ref[...] = estimate
+    prev_ref[0:torso] = estimate
+    prev_ref[torso : torso + HALO] = direction[0:HALO]
+    next_ref[0:torso] = estimate
+    next_ref[torso : torso + HALO] = direction[torso - HALO : torso]
 
 
 def last_residual(
-    own_cols, other_cols, own_ref, other_ref, before_ref, after_ref, direction_in, residual_in,
-    diag_ref, residual_ref, window_ref, product_ref,
+    chain, own_cols, other_cols, own_ref, other_ref, after_ref, before_ref, direction_in,
+    residual_in, diag_ref, residual_ref, window_ref, product_ref,
 ):
     torso = residual_ref.shape[0]
+    here = lax.axis_index("dom")
     diag = diag_ref[HALO : HALO + torso]
     direction = direction_in[...]
-    window_ref[0:HALO] = before_ref[...]
+    window_ref[0:HALO] = jnp.where(here > 0, before_ref[torso : torso + HALO], 0.0)
     window_ref[HALO : HALO + torso] = direction
-    window_ref[HALO + torso : 2 * HALO + torso] = after_ref[...]
+    window_ref[HALO + torso : 2 * HALO + torso] = jnp.where(
+        here < chain - 1, after_ref[torso : torso + HALO], 0.0
+    )
     product(own_ref, other_ref, own_cols, other_cols, window_ref, product_ref)
     residual_ref[...] = residual_in[...] - (diag * direction + product_ref[...])
 
 
 def on_device(states, send_node, send_count, recv_row, columns, tile_values, diagonal):
     chain = lax.axis_size("dom")
-    here = lax.axis_index("dom")
-    peers, slots = send_node.shape[1:]
+    pair = lax.axis_size("sub")
+    slots = send_node.shape[2]
     node_count = states.shape[1]
     heart = node_count // LANES
     torso = diagonal.shape[0] // LANES
-    offsets = [0, 1, chain - 1, chain // 2]
-    place = ((here + jnp.array(offsets, jnp.int32)) % chain).astype(jnp.int32)
+    _, _, _, far = peer_offsets(chain)
 
     def from_peer(value, offset):
         return lax.ppermute(value, "dom", [((i + offset) % chain, i) for i in range(chain)])
@@ -291,61 +339,65 @@
         pairs = [(i + offset, i) for i in range(chain) if 0 <= i + offset < chain]
         return lax.ppermute(value, "dom", pairs)
 
-    def shape(*dims):
-        return jax.ShapeDtypeStruct(dims, F32)
-
-    edge = HALO * LANES
+    def shape(*dims, dtype=F32):
+        return jax.ShapeDtypeStruct(dims, dtype)
+
+    dense = shape(states.shape[0], heart, LANES)
+    field = shape(torso, LANES)
+    wide = shape(torso + 2 * HALO, LANES)
+    packed = shape(torso + HALO, LANES)
+    table = shape(*send_node.shape[1:], dtype=jnp.int32)
+    blocks = shape(chain * pair, 2 * torso, LANES)
+    rim = shape(1, slots + HALO * LANES)
+    shares = (pltpu.VMEM(((chain + 2) * torso, LANES), F32),)
+    work = (pltpu.VMEM(wide.shape, F32), pltpu.VMEM(field.shape, F32))
+
     flip = [(0, 1), (1, 0)]
-    rows_out = recv_row[0].astype(F32)
-    got_after = from_peer(jnp.concatenate([rows_out[1], diagonal[:edge]]), 1)
-    got_before = from_peer(jnp.concatenate([rows_out[2], diagonal[-edge:]]), chain - 1)
-    got_far = from_peer(rows_out[3], chain // 2)
+    diagonal = diagonal.reshape(torso, LANES)
+    columns = columns.T
+    nodes, to_prev, to_next, to_far = call(prepare, (table, rim, rim, shape(1, slots)))(
+        in_specs=[SMEM] + [VMEM] * 3
+    )(send_count, send_node, recv_row, diagonal)
+    got_after = from_peer(to_prev, 1)
+    got_before = from_peer(to_next, chain - 1)
+    got_far = from_peer(to_far, far)
     other_tiles = lax.ppermute(tile_values, "sub", flip)
     other_cols = lax.ppermute(columns, "sub", flip)
-    maps = jnp.stack([rows_out[0], got_after[:slots], got_before[:slots], got_far]).astype(jnp.int32)
-    diag = jnp.concatenate([got_before[slots:], diagonal, got_after[slots:]]).reshape(-1, LANES)
-    live = jnp.arange(slots, dtype=jnp.int32)[None, :] < send_count[0][:, None]
-    nodes = jnp.where(live, send_node[0], -1)
-
-    dense = shape(states.shape[0], heart, LANES)
-    field = shape(torso, LANES)
-    part = shape(chain * torso, LANES)
-    work = (pltpu.VMEM((torso + 2 * HALO + 4, LANES), F32), pltpu.VMEM((torso, LANES), F32))
 
     states, current = call(first_ionic, (dense, shape(heart, LANES)))(in_specs=[VMEM])(states)
-    shares = call(functools.partial(first_shares, chain, torso), part)(
-        in_specs=[SMEM] + [VMEM] * 3
-    )(place, current, nodes, maps)
+    maps, diag, parts = call(
+        functools.partial(first_shares, chain), (table, wide, blocks), shares
+    )(in_specs=[VMEM] * 7)(current, nodes, recv_row, got_after, got_before, got_far, diagonal)
     for time_step in range(2):
-        last = time_step == 1
-        forcing = lax.psum(shares, ("dom", "sub"))
-        residual, direction, estimate = call(
-            functools.partial(sweep_one, chain), (field,) * 3, work
-        )(in_specs=[SMEM] * 3 + [VMEM] * 4)(
-            place, columns, other_cols, tile_values, other_tiles, forcing, diag
-        )
+        parts = lax.all_to_all(parts, ("dom", "sub"), split_axis=0, concat_axis=0, tiled=True)
+        residual, direction, estimate = call(sweep_one, (field,) * 3, work)(
+            in_specs=[SMEM] * 2 + [VMEM] * 4
+        )(columns, other_cols, tile_values, other_tiles, parts, diag)
         before = from_neighbour(direction[-HALO:], -1)
         after = from_neighbour(direction[:HALO], 1)
-        residual, direction, estimate = call(sweep_two, (field,) * 3, work)(
-            in_specs=[SMEM] * 2 + [VMEM] * 8
-        )(
+        residual, direction, estimate, to_prev, to_next = call(
+            sweep_two, (field,) * 3 + (packed,) * 2, work
+        )(in_specs=[SMEM] * 2 + [VMEM] * 8)(
             columns, other_cols, tile_values, other_tiles, before, after, direction, residual,
             estimate, diag,
         )
-        estimates = [estimate] + [from_peer(estimate, offset) for offset in offsets[1:]]
-        if not last:
-            states, shares = call(
-                functools.partial(next_shares, chain, torso), (dense, part)
-            )(in_specs=[SMEM] + [VMEM] * 7)(place, states, *estimates, nodes, maps)
+        got_far = from_peer(estimate, far)
+        if time_step == 0:
+            got_after, got_before = from_peer(estimate, 1), from_peer(estimate, chain - 1)
+            states, parts = call(
+                functools.partial(next_shares, chain), (dense, blocks), shares
+            )(in_specs=[VMEM] * 7)(states, estimate, got_after, got_before, got_far, nodes, maps)
             continue
-        before = from_neighbour(direction[-HALO:], -1)
-        after = from_neighbour(direction[:HALO], 1)
-        residual = call(last_residual, field, work)(in_specs=[SMEM] * 2 + [VMEM] * 7)(
-            columns, other_cols, tile_values, other_tiles, before, after, direction, residual, diag
+        got_after, got_before = from_peer(to_prev, 1), from_peer(to_next, chain - 1)
+        residual = call(functools.partial(last_residual, chain), field, work)(
+            in_specs=[SMEM] * 2 + [VMEM] * 7
+        )(
+            columns, other_cols, tile_values, other_tiles, got_after, got_before, direction,
+            residual, diag,
         )
         new_states = call(
-            last_feedback, shape(19, node_count), (pltpu.VMEM(dense.shape, F32),)
-        )(in_specs=[VMEM] * 7)(states, *estimates, nodes, maps)
+            last_feedback, shape(*dense.shape[:1], node_count), (pltpu.VMEM(dense.shape, F32),)
+        )(in_specs=[VMEM] * 7)(states, estimate, got_after, got_before, got_far, nodes, maps)
     return new_states, estimate.reshape(-1), residual.reshape(-1)
 
 

time: 188 us -> 88.7 us (0.47)
  blocking collectives: 117 us -> 13.8 us
  waiting for transfers between devices: 8.37 us -> 21.1 us
  Pallas kernels: 13.9 us -> 11 us
  other arithmetic: 2.9 us -> 0 us
  local copies, waits for them, and re-layouts: 10.2 us -> 7.33 us
    psum x2 -> x0, blocking collectives: 117 us -> none  [on_device(): forcing = lax.psum(shares, ('dom', 'sub'))]
    all_to_all x0 -> x1, blocking collectives: none -> 13.8 us  [on_device(): lax.all_to_all(parts, ('dom', 'sub'), split_axis=0, concat_axis=0, tiled=...]
    ppermute x9, waiting for transfers between devices: 4.54 us -> 11.1 us  [from_peer(): lax.ppermute(value, 'dom', [((i + offset) % chain, i) for i in range(chai...]
    all_to_all x0 -> x1, waiting for transfers between devices: none -> 6.49 us  [on_device(): lax.all_to_all(parts, ('dom', 'sub'), split_axis=0, concat_axis=0, tiled=...]
    ppermute x6 -> x4, starting transfers between devices: 17.5 us -> 11.7 us  [from_neighbour(): return lax.ppermute(value, 'dom', pairs)]
    all_to_all x0 -> x1, starting transfers between devices: none -> 4.3 us  [on_device(): lax.all_to_all(parts, ('dom', 'sub'), split_axis=0, concat_axis=0, tiled=...]
    pallas_call x8 -> x9, Pallas kernels: 13.7 us -> 10.8 us  [the longest x2 3.32 us: on_device(): call(sweep_two, (field,) * 3 + (packed,) * 2, work)]
    unnamed x17 -> x22, local copies, waits for them, and re-layouts: 9.41 us -> 7.32 us
  transfers between devices with their start and end apart: 17 -> 16, of which waited for: 5 -> 8; matrix products, arithmetic and copies ran while one was open for 2% -> 0% of each run, Pallas kernels for 2% -> 4%
where the time goes in v2:
time: 88.7 us; the launch traced here: 88.1 us
  starting transfers between devices  34 us (38%)
  waiting for transfers between devices  21.1 us (24%)
  blocking collectives  13.8 us (16%)
  Pallas kernels  11 us (12%)
  local copies, waits for them, and re-layouts  7.33 us (8%)
    ppermute x9, starting transfers between devices, from_peer(): lax.ppermute(value, 'dom', [((i + offset) % chain, i) for i in range(chai...  17.1 us
    all_to_all x1, blocking collectives, on_device(): lax.all_to_all(parts, ('dom', 'sub'), split_axis=0, concat_axis=0, tiled=...  13.8 us
    ppermute x4, starting transfers between devices, from_neighbour(): return lax.ppermute(value, 'dom', pairs)  11.7 us
    ppermute x9, waiting for transfers between devices, from_peer(): lax.ppermute(value, 'dom', [((i + offset) % chain, i) for i in range(chai...  11.1 us
    unnamed x22, local copies, waits for them, and re-layouts  7.32 us
    all_to_all x1, waiting for transfers between devices, on_device(): lax.all_to_all(parts, ('dom', 'sub'), split_axis=0, concat_axis=0, tiled=...  6.49 us
    all_to_all x1, starting transfers between devices, on_device(): lax.all_to_all(parts, ('dom', 'sub'), split_axis=0, concat_axis=0, tiled=...  4.3 us
    pallas_call x2, Pallas kernels, on_device(): call(sweep_two, (field,) * 3 + (packed,) * 2, work)  3.32 us
  transfers between devices with their start and end apart: 16, of which 8 were waited for; matrix products, arithmetic and copies ran while one was open for 0% of the time, Pallas kernels for 4%

profile of v2, /device:TPU:0, one launch (start us, length us, event | category | flops | bytes accessed | tf_op | source)
XLA Modules:
  0.0 88.1 jit_solution(5015273200447839645)
XLA Ops:
  4.4 5.6 %collective-permute-start.2 = (f32[1,768]{1,0:T(1,128)S(1)}, f32[1,768]{1,0:T(1,128)S(1)}, u32[]{:S(2)}, u32[]{:S(2)}) collective-permute-start(f32[1,768]{1,0:T(1,128)S(1)} %get-tuple-element.29), channel_id=1, source_target_pairs={{2,0},{4,2},{6,4},{8,6},{10,8},{12,10},{14,12},{0,14},{3,1},{5,3},... | collective-permute-start | bytes 9224 | tf_op jit(solution)/shard_map/ppermute | solution.py:336
  11.2 3.3 %collective-permute-done.4.far_ref = f32[1,512]{1,0:T(1,128)S(1)} collective-permute-done((f32[1,512]{1,0:T(1,128)S(1)}, f32[1,512]{1,0:T(1,128)S(1)}, u32[]{:S(2)}, u32[]{:S(2)}) %collective-permute-start.4) | collective-permute-done | bytes 2080 | tf_op jit(solution)/shard_map/ppermute | solution.py:336
  14.5 1.8 %collective-permute-done.3.before_ref = f32[1,768]{1,0:T(1,128)S(1)} collective-permute-done((f32[1,768]{1,0:T(1,128)S(1)}, f32[1,768]{1,0:T(1,128)S(1)}, u32[]{:S(2)}, u32[]{:S(2)}) %collective-permute-start.3) | collective-permute-done | bytes 3104 | tf_op jit(solution)/shard_map/ppermute | solution.py:336
  18.8 4.3 %all-to-all-start = ((f32[16,16,128]{2,1,0:T(8,128)}), f32[16,16,128]{2,1,0:T(8,128)S(1)}, u32[]{:S(2)}, u32[]{:S(2)}) async-start(f32[16,16,128]{2,1,0:T(8,128)} %get-tuple-element.32), calls=%async_computation | async-start | bytes 262144 | tf_op jit(solution)/shard_map/all_to_all | solution.py:372
  24.5 6.5 %all-to-all-done.parts_ref = f32[16,16,128]{2,1,0:T(8,128)S(1)} async-done(((f32[16,16,128]{2,1,0:T(8,128)}), f32[16,16,128]{2,1,0:T(8,128)S(1)}, u32[]{:S(2)}, u32[]{:S(2)}) %all-to-all-start) | async-done | bytes 131104 | tf_op jit(solution)/shard_map/all_to_all | solution.py:372
  31.0 1.6 %copy-done = f32[8,4,128,128]{3,2,1,0:T(8,128)S(1)} copy-done((f32[8,4,128,128]{3,2,1,0:T(8,128)S(1)}, f32[8,4,128,128]{3,2,1,0:T(8,128)}, u32[]{:S(2)}) %copy-start) | copy-done | bytes 2097176
  34.3 1.3 %collective-permute-start.6 = (f32[2,128]{1,0:T(2,128)S(1)}, f32[2,128]{1,0:T(2,128)S(1)}, u32[]{:S(2)}, u32[]{:S(2)}) collective-permute-start(f32[2,128]{1,0:T(2,128)S(1)} %get-tuple-element.51), channel_id=1, source_target_pairs={{2,0},{4,2},{6,4},{8,6},{10,8},{12,10},{14,12},{3,1},{5,3},{7,5},{... | collective-permute-start | bytes 3080 | tf_op jit(solution)/shard_map/ppermute | solution.py:340
  35.6 4.5 %collective-permute-start.5 = (f32[2,128]{1,0:T(2,128)S(1)}, f32[2,128]{1,0:T(2,128)S(1)}, u32[]{:S(2)}, u32[]{:S(2)}) collective-permute-start(f32[2,128]{1,0:T(2,128)S(1)} %get-tuple-element.52), channel_id=1, source_target_pairs={{0,2},{2,4},{4,6},{6,8},{8,10},{10,12},{12,14},{1,3},{3,5},{5,7},{... | collective-permute-start | bytes 3080 | tf_op jit(solution)/shard_map/ppermute | solution.py:340
  40.2 1.3 %collective-permute-done.5.before_ref = f32[2,128]{1,0:T(2,128)S(1)} collective-permute-done((f32[2,128]{1,0:T(2,128)S(1)}, f32[2,128]{1,0:T(2,128)S(1)}, u32[]{:S(2)}, u32[]{:S(2)}) %collective-permute-start.5) | collective-permute-done | bytes 1056 | tf_op jit(solution)/shard_map/ppermute | solution.py:340
  41.5 1.6 %shard_map.98 = (f32[8,128]{1,0:T(8,128)}, f32[8,128]{1,0:T(8,128)}, f32[8,128]{1,0:T(8,128)S(1)}, f32[10,128]{1,0:T(8,128)}, f32[10,128]{1,0:T(8,128)}) custom-call(s32[4,8]{1,0:T(4,128)S(1)} %bitcast.6, s32[4,8]{1,0:T(4,128)S(1)} %collective-permute-done.other_cols, f32[8,4,128,128]{3,2,1,0:T(8,128)S(1)} %copy-done, ...), custom_call_target="tpu_custom_call" | custom-call | flops 4000000 | bytes 262144 | tf_op jit(solution)/shard_map/pallas_call | solution.py:378
  43.1 2.3 %collective-permute-start.9 = (f32[8,128]{1,0:T(8,128)S(1)}, f32[8,128]{1,0:T(8,128)S(1)}, u32[]{:S(2)}, u32[]{:S(2)}) collective-permute-start(f32[8,128]{1,0:T(8,128)S(1)} %get-tuple-element.37.e0), channel_id=1, source_target_pairs={{8,0},{10,2},{12,4},{14,6},{0,8},{2,10},{4,12},{6,14},{9,1},{11,3}... | collective-permute-start | bytes 12296 | tf_op jit(solution)/shard_map/ppermute | solution.py:336
  45.8 4.4 %collective-permute-start.7 = (f32[8,128]{1,0:T(8,128)S(1)}, f32[8,128]{1,0:T(8,128)S(1)}, u32[]{:S(2)}, u32[]{:S(2)}) collective-permute-start(f32[8,128]{1,0:T(8,128)S(1)} %get-tuple-element.37.e0), channel_id=1, source_target_pairs={{2,0},{4,2},{6,4},{8,6},{10,8},{12,10},{14,12},{0,14},{3,1},{5,3},... | collective-permute-start | bytes 12296 | tf_op jit(solution)/shard_map/ppermute | solution.py:336
  50.2 1.6 %collective-permute-done.8.e2 = f32[8,128]{1,0:T(8,128)S(1)} collective-permute-done((f32[8,128]{1,0:T(8,128)S(1)}, f32[8,128]{1,0:T(8,128)S(1)}, u32[]{:S(2)}, u32[]{:S(2)}) %collective-permute-start.8) | collective-permute-done | bytes 4128 | tf_op jit(solution)/shard_map/ppermute | solution.py:336
  52.8 13.8 %all_to_all.10.parts_ref = f32[16,16,128]{2,1,0:T(8,128)S(1)} all-to-all(f32[16,16,128]{2,1,0:T(8,128)S(1)} %get-tuple-element.40), channel_id=1, replica_groups=mesh['case'=2,'dom'=8,'sub'=2] {'dom','sub'}, dimensions={0} | all-to-all | bytes 262144 | tf_op jit(solution)/shard_map/all_to_all | solution.py:372
  66.7 1.1 %shard_map.100 = (f32[8,128]{1,0:T(8,128)S(1)}, f32[8,128]{1,0:T(8,128)S(1)}, f32[8,128]{1,0:T(8,128)S(1)}) custom-call(s32[4,8]{1,0:T(4,128)S(1)} %bitcast.7, s32[4,8]{1,0:T(4,128)S(1)} %collective-permute-done.other_cols, f32[8,4,128,128]{3,2,1,0:T(8,128)S(1)} %copy-done.1, f32[8,4,128,128]{3,2,1,0:T(8,128)S(1)} %collective-permute-done.1.other_ref, ...), custom_call_target="tpu_custom_call" | custom-call | flops 4000000 | bytes 262144 | tf_op jit(solution)/shard_map/pallas_call | solution.py:373
  67.8 1.3 %collective-permute-start.11 = (f32[2,128]{1,0:T(2,128)S(1)}, f32[2,128]{1,0:T(2,128)S(1)}, u32[]{:S(2)}, u32[]{:S(2)}) collective-permute-start(f32[2,128]{1,0:T(2,128)S(1)} %get-tuple-element.49), channel_id=1, source_target_pairs={{2,0},{4,2},{6,4},{8,6},{10,8},{12,10},{14,12},{3,1},{5,3},{7,5},{... | collective-permute-start | bytes 3080 | tf_op jit(solution)/shard_map/ppermute | solution.py:340
  69.1 4.5 %collective-permute-start.10 = (f32[2,128]{1,0:T(2,128)S(1)}, f32[2,128]{1,0:T(2,128)S(1)}, u32[]{:S(2)}, u32[]{:S(2)}) collective-permute-start(f32[2,128]{1,0:T(2,128)S(1)} %get-tuple-element.50), channel_id=1, source_target_pairs={{0,2},{2,4},{4,6},{6,8},{8,10},{10,12},{12,14},{1,3},{3,5},{5,7},{... | collective-permute-start | bytes 3080 | tf_op jit(solution)/shard_map/ppermute | solution.py:340
  73.6 1.3 %collective-permute-done.10.before_ref = f32[2,128]{1,0:T(2,128)S(1)} collective-permute-done((f32[2,128]{1,0:T(2,128)S(1)}, f32[2,128]{1,0:T(2,128)S(1)}, u32[]{:S(2)}, u32[]{:S(2)}) %collective-permute-start.10) | collective-permute-done | bytes 1056 | tf_op jit(solution)/shard_map/ppermute | solution.py:340
  74.9 1.7 %shard_map.101 = (f32[8,128]{1,0:T(8,128)S(1)}, f32[8,128]{1,0:T(8,128)S(1)}, f32[8,128]{1,0:T(8,128)}, f32[10,128]{1,0:T(8,128)S(1)}, f32[10,128]{1,0:T(8,128)S(1)}) custom-call(s32[4,8]{1,0:T(4,128)S(1)} %bitcast.8, s32[4,8]{1,0:T(4,128)S(1)} %collective-permute-done.other_cols, f32[8,4,128,128]{3,2,1,0:T(8,128)S(1)} %copy-done.1, ...), custom_call_target="tpu_custom_call" | custom-call | flops 4000000 | bytes 262144 | tf_op jit(solution)/shard_map/pallas_call | solution.py:378
  76.6 2.4 %collective-permute-start.12 = (f32[10,128]{1,0:T(8,128)S(1)}, f32[10,128]{1,0:T(8,128)S(1)}, u32[]{:S(2)}, u32[]{:S(2)}) collective-permute-start(f32[10,128]{1,0:T(8,128)S(1)} %get-tuple-element.45), channel_id=1, source_target_pairs={{2,0},{4,2},{6,4},{8,6},{10,8},{12,10},{14,12},{0,14},{3,1},{5,3},... | collective-permute-start | bytes 15368 | tf_op jit(solution)/shard_map/ppermute | solution.py:336
  79.0 1.9 %collective-permute-start.14 = (f32[8,128]{1,0:T(8,128)}, f32[8,128]{1,0:T(8,128)S(1)}, u32[]{:S(2)}, u32[]{:S(2)}) collective-permute-start(f32[8,128]{1,0:T(8,128)} %get-tuple-element.44.e0), channel_id=1, source_target_pairs={{8,0},{10,2},{12,4},{14,6},{0,8},{2,10},{4,12},{6,14},{9,1},{11,3}... | collective-permute-start | bytes 12296 | tf_op jit(solution)/shard_map/ppermute | solution.py:336
  80.9 4.4 %collective-permute-done.13.e2.before_ref = f32[10,128]{1,0:T(8,128)S(1)} collective-permute-done((f32[10,128]{1,0:T(8,128)S(1)}, f32[10,128]{1,0:T(8,128)S(1)}, u32[]{:S(2)}, u32[]{:S(2)}) %collective-permute-start.13) | collective-permute-done | bytes 5152 | tf_op jit(solution)/shard_map/ppermute | solution.py:336
  85.3 1.7 %shard_map.103 = f32[8,128]{1,0:T(8,128)} custom-call(s32[4,8]{1,0:T(4,128)S(1)} %bitcast.9, s32[4,8]{1,0:T(4,128)S(1)} %collective-permute-done.other_cols, f32[8,4,128,128]{3,2,1,0:T(8,128)S(1)} %copy-done.1, f32[8,4,128,128]{3,2,1,0:T(8,128)S(1)} %collective-permute-done.1.other_ref, f32[10,128]{1,0:T(8,128)S(1)} %collective-permute-done.12.e1.after_ref, ...), custom_call_target="tpu_custom_call" | custom-call | flops 4000000 | bytes 262144 | tf_op jit(solution)/shard_map/pallas_call | solution.py:392
  87.0 1.1 %shard_map.102 = f32[19,2048]{1,0:T(8,128)} custom-call(f32[19,16,128]{2,1,0:T(8,128)S(1)} %get-tuple-element.39.states_ref, f32[8,128]{1,0:T(8,128)S(1)} %copy-done.9, f32[10,128]{1,0:T(8,128)S(1)} %collective-permute-done.12.e1.after_ref, f32[10,128]{1,0:T(8,128)S(1)} %collective-permute-done.13.e2.before_ref, f32[8,128]{1,0:T(8,128)S(1)} %collective-permute-done.14.e3, ...), custom_call_target="tpu_custom_call" | custom-call | flops 4000000 | bytes 262144 | tf_op jit(solution)/shard_map/pallas_call | solution.py:398
  (43 shorter events, 12.0 us)
Async XLA Ops:
  0.6 30.4 %collective-permute-start.1 = (f32[8,4,128,128]{3,2,1,0:T(8,128)}, f32[8,4,128,128]{3,2,1,0:T(8,128)S(1)}, u32[]{:S(2)}, u32[]{:S(2)}) collective-permute-start(f32[8,4,128,128]{3,2,1,0:T(8,128)} %own_ref.9), channel_id=1, source_target_pairs={{0,1},{1,0},{2,3},{3,2},{4,5},{5,4},{6,7},{7,6},{8,9},{9,8},{10,11... | collective-permute-start | bytes 6291464 | tf_op jit(solution)/shard_map/ppermute | solution.py:364
  1.1 0.7 copy-start.4
  1.8 0.7 copy-start.6
  2.5 0.7 copy-start.8
  4.4 10.1 %collective-permute-start.2 = (f32[1,768]{1,0:T(1,128)S(1)}, f32[1,768]{1,0:T(1,128)S(1)}, u32[]{:S(2)}, u32[]{:S(2)}) collective-permute-start(f32[1,768]{1,0:T(1,128)S(1)} %get-tuple-element.29), channel_id=1, source_target_pairs={{2,0},{4,2},{6,4},{8,6},{10,8},{12,10},{14,12},{0,14},{3,1},{5,3},... | collective-permute-start | bytes 9224 | tf_op jit(solution)/shard_map/ppermute | solution.py:336
  10.0 6.3 %collective-permute-start.3 = (f32[1,768]{1,0:T(1,128)S(1)}, f32[1,768]{1,0:T(1,128)S(1)}, u32[]{:S(2)}, u32[]{:S(2)}) collective-permute-start(f32[1,768]{1,0:T(1,128)S(1)} %get-tuple-element.30), channel_id=1, source_target_pairs={{14,0},{0,2},{2,4},{4,6},{6,8},{8,10},{10,12},{12,14},{15,1},{1,3}... | collective-permute-start | bytes 9224 | tf_op jit(solution)/shard_map/ppermute | solution.py:336
  10.0 4.5 %collective-permute-start.4 = (f32[1,512]{1,0:T(1,128)S(1)}, f32[1,512]{1,0:T(1,128)S(1)}, u32[]{:S(2)}, u32[]{:S(2)}) collective-permute-start(f32[1,512]{1,0:T(1,128)S(1)} %get-tuple-element.31), channel_id=1, source_target_pairs={{8,0},{10,2},{12,4},{14,6},{0,8},{2,10},{4,12},{6,14},{9,1},{11,3}... | collective-permute-start | bytes 6152 | tf_op jit(solution)/shard_map/ppermute | solution.py:336
  10.1 0.9 %copy-start.2 = (f32[19,2048]{1,0:T(8,128)S(1)}, f32[19,2048]{1,0:T(8,128)}, u32[]{:S(2)}) copy-start(f32[19,2048]{1,0:T(8,128)} %states_ref.1) | copy-start | bytes 466948
  16.3 0.7 copy-start.5
  18.8 12.2 %all-to-all-start = ((f32[16,16,128]{2,1,0:T(8,128)}), f32[16,16,128]{2,1,0:T(8,128)S(1)}, u32[]{:S(2)}, u32[]{:S(2)}) async-start(f32[16,16,128]{2,1,0:T(8,128)} %get-tuple-element.32), calls=%async_computation | async-start | bytes 262144 | tf_op jit(solution)/shard_map/all_to_all | solution.py:372
  23.1 1.4 %collective-permute-start = (s32[4,8]{1,0:T(4,128)}, s32[4,8]{1,0:T(4,128)S(1)}, u32[]{:S(2)}, u32[]{:S(2)}) collective-permute-start(s32[4,8]{1,0:T(4,128)} %bitcast.4), channel_id=1, source_target_pairs={{0,1},{1,0},{2,3},{3,2},{4,5},{5,4},{6,7},{7,6},{8,9},{9,8},{10,11... | collective-permute-start | bytes 392 | tf_op jit(solution)/shard_map/ppermute | solution.py:365
  31.0 1.6 %copy-start = (f32[8,4,128,128]{3,2,1,0:T(8,128)S(1)}, f32[8,4,128,128]{3,2,1,0:T(8,128)}, u32[]{:S(2)}) copy-start(f32[8,4,128,128]{3,2,1,0:T(8,128)} %own_ref.9) | copy-start | bytes 6291460
  34.3 5.9 %collective-permute-start.6 = (f32[2,128]{1,0:T(2,128)S(1)}, f32[2,128]{1,0:T(2,128)S(1)}, u32[]{:S(2)}, u32[]{:S(2)}) collective-permute-start(f32[2,128]{1,0:T(2,128)S(1)} %get-tuple-element.51), channel_id=1, source_target_pairs={{2,0},{4,2},{6,4},{8,6},{10,8},{12,10},{14,12},{3,1},{5,3},{7,5},{... | collective-permute-start | bytes 3080 | tf_op jit(solution)/shard_map/ppermute | solution.py:340
  35.6 5.8 %collective-permute-start.5 = (f32[2,128]{1,0:T(2,128)S(1)}, f32[2,128]{1,0:T(2,128)S(1)}, u32[]{:S(2)}, u32[]{:S(2)}) collective-permute-start(f32[2,128]{1,0:T(2,128)S(1)} %get-tuple-element.52), channel_id=1, source_target_pairs={{0,2},{2,4},{4,6},{6,8},{8,10},{10,12},{12,14},{1,3},{3,5},{5,7},{... | collective-permute-start | bytes 3080 | tf_op jit(solution)/shard_map/ppermute | solution.py:340
  41.5 25.2 %copy-start.1 = (f32[8,4,128,128]{3,2,1,0:T(8,128)S(1)}, f32[8,4,128,128]{3,2,1,0:T(8,128)}, u32[]{:S(2)}) copy-start(f32[8,4,128,128]{3,2,1,0:T(8,128)} %own_ref.9) | copy-start | bytes 6291460
  43.1 7.1 %collective-permute-start.9 = (f32[8,128]{1,0:T(8,128)S(1)}, f32[8,128]{1,0:T(8,128)S(1)}, u32[]{:S(2)}, u32[]{:S(2)}) collective-permute-start(f32[8,128]{1,0:T(8,128)S(1)} %get-tuple-element.37.e0), channel_id=1, source_target_pairs={{8,0},{10,2},{12,4},{14,6},{0,8},{2,10},{4,12},{6,14},{9,1},{11,3}... | collective-permute-start | bytes 12296 | tf_op jit(solution)/shard_map/ppermute | solution.py:336
  45.5 6.3 %collective-permute-start.8 = (f32[8,128]{1,0:T(8,128)S(1)}, f32[8,128]{1,0:T(8,128)S(1)}, u32[]{:S(2)}, u32[]{:S(2)}) collective-permute-start(f32[8,128]{1,0:T(8,128)S(1)} %get-tuple-element.37.e0), channel_id=1, source_target_pairs={{14,0},{0,2},{2,4},{4,6},{6,8},{8,10},{10,12},{12,14},{15,1},{1,3}... | collective-permute-start | bytes 12296 | tf_op jit(solution)/shard_map/ppermute | solution.py:336
  45.8 6.0 %collective-permute-start.7 = (f32[8,128]{1,0:T(8,128)S(1)}, f32[8,128]{1,0:T(8,128)S(1)}, u32[]{:S(2)}, u32[]{:S(2)}) collective-permute-start(f32[8,128]{1,0:T(8,128)S(1)} %get-tuple-element.37.e0), channel_id=1, source_target_pairs={{2,0},{4,2},{6,4},{8,6},{10,8},{12,10},{14,12},{0,14},{3,1},{5,3},... | collective-permute-start | bytes 12296 | tf_op jit(solution)/shard_map/ppermute | solution.py:336
  67.8 5.9 %collective-permute-start.11 = (f32[2,128]{1,0:T(2,128)S(1)}, f32[2,128]{1,0:T(2,128)S(1)}, u32[]{:S(2)}, u32[]{:S(2)}) collective-permute-start(f32[2,128]{1,0:T(2,128)S(1)} %get-tuple-element.49), channel_id=1, source_target_pairs={{2,0},{4,2},{6,4},{8,6},{10,8},{12,10},{14,12},{3,1},{5,3},{7,5},{... | collective-permute-start | bytes 3080 | tf_op jit(solution)/shard_map/ppermute | solution.py:340
  69.1 5.8 %collective-permute-start.10 = (f32[2,128]{1,0:T(2,128)S(1)}, f32[2,128]{1,0:T(2,128)S(1)}, u32[]{:S(2)}, u32[]{:S(2)}) collective-permute-start(f32[2,128]{1,0:T(2,128)S(1)} %get-tuple-element.50), channel_id=1, source_target_pairs={{0,2},{2,4},{4,6},{6,8},{8,10},{10,12},{12,14},{1,3},{3,5},{5,7},{... | collective-permute-start | bytes 3080 | tf_op jit(solution)/shard_map/ppermute | solution.py:340
  76.6 4.4 %collective-permute-start.12 = (f32[10,128]{1,0:T(8,128)S(1)}, f32[10,128]{1,0:T(8,128)S(1)}, u32[]{:S(2)}, u32[]{:S(2)}) collective-permute-start(f32[10,128]{1,0:T(8,128)S(1)} %get-tuple-element.45), channel_id=1, source_target_pairs={{2,0},{4,2},{6,4},{8,6},{10,8},{12,10},{14,12},{0,14},{3,1},{5,3},... | collective-permute-start | bytes 15368 | tf_op jit(solution)/shard_map/ppermute | solution.py:336
  79.0 6.3 %collective-permute-start.13 = (f32[10,128]{1,0:T(8,128)S(1)}, f32[10,128]{1,0:T(8,128)S(1)}, u32[]{:S(2)}, u32[]{:S(2)}) collective-permute-start(f32[10,128]{1,0:T(8,128)S(1)} %get-tuple-element.46), channel_id=1, source_target_pairs={{14,0},{0,2},{2,4},{4,6},{6,8},{8,10},{10,12},{12,14},{15,1},{1,3}... | collective-permute-start | bytes 15368 | tf_op jit(solution)/shard_map/ppermute | solution.py:336
  79.0 8.0 %collective-permute-start.14 = (f32[8,128]{1,0:T(8,128)}, f32[8,128]{1,0:T(8,128)S(1)}, u32[]{:S(2)}, u32[]{:S(2)}) collective-permute-start(f32[8,128]{1,0:T(8,128)} %get-tuple-element.44.e0), channel_id=1, source_target_pairs={{8,0},{10,2},{12,4},{14,6},{0,8},{2,10},{4,12},{6,14},{9,1},{11,3}... | collective-permute-start | bytes 12296 | tf_op jit(solution)/shard_map/ppermute | solution.py:336
  85.3 1.7 %copy-start.9 = (f32[8,128]{1,0:T(8,128)S(1)}, f32[8,128]{1,0:T(8,128)}, u32[]{:S(2)}) copy-start(f32[8,128]{1,0:T(8,128)} %get-tuple-element.44.e0) | copy-start | bytes 12292
  (3 other events, 2.0 us)

commit v3 on v2

v3 whole, which is shorter than its diff:
```python
import functools

import jax
import jax.numpy as jnp
from jax import lax
from jax.experimental import pallas as pl
from jax.experimental.pallas import tpu as pltpu
from jax.sharding import PartitionSpec as P

HALO = 2
SWEEPS = 3
LANES = 128

TIME_STEP = 0.02
NERNST_SCALE = 0.267
SODIUM_OUT = 1.4
POTASSIUM_OUT = 0.054
CALCIUM_OUT = 2000.0
COND_SODIUM = 8.0
COND_CALCIUM = 1.0
COND_TRANSIENT = 0.3
COND_RAPID = 0.2
COND_SLOW = 0.3
COND_INWARD = 2.0
COND_RELEASE = 3.0
MEMBRANE_RATE = 2.0
TORSO_COUPLING = 0.5
FEEDBACK_RATE = 5.0
CHEB_THETA = 1.0
CHEB_DELTA = 0.5
GATE_MIDPOINT = [-0.56, -0.7, -0.7, -0.08, -0.2, -0.3, 0.2, -0.28, -0.26, -0.88, 0.05, -0.8, -0.5]
GATE_STEEPNESS = [0.09, -0.07, -0.07, 0.07, -0.07, -0.09, 0.06, -0.05, 0.07, -0.24, 0.14, -0.1, 0.08]
TIME_BASE = [0.02, 0.3, 1.0, 0.1, 2.0, 0.5, 0.1, 1.0, 1.0, 0.5, 1.0, 0.05, 0.2]
TIME_PEAK = [0.1, 1.0, 3.0, 0.5, 5.0, 2.0, 0.3, 5.0, 3.0, 2.0, 4.0, 0.1, 1.0]

SIGMA = CHEB_THETA / CHEB_DELTA
KEEP, PULL = [], []
_ratio = 1.0 / SIGMA
for _ in range(SWEEPS - 1):
    _next = 1.0 / (2.0 * SIGMA - _ratio)
    KEEP.append(_next * _ratio)
    PULL.append(2.0 * _next / CHEB_DELTA)
    _ratio = _next

VMEM = pl.BlockSpec(memory_space=pltpu.VMEM)
SMEM = pl.BlockSpec(memory_space=pltpu.SMEM)
HBM = pl.BlockSpec(memory_space=pltpu.HBM)
F32 = jnp.float32


def call(kernel, outs, scratch=(), limit=16, cost=4_000_000):
    return functools.partial(
        pl.pallas_call,
        kernel,
        out_shape=outs,
        out_specs=jax.tree.map(lambda _: VMEM, outs),
        scratch_shapes=list(scratch),
        compiler_params=pltpu.CompilerParams(vmem_limit_bytes=limit << 20),
        cost_estimate=pl.CostEstimate(flops=cost, bytes_accessed=1 << 18, transcendentals=0),
    )


def ionic_rows(rows):
    voltage, gating = rows[0], rows[1:14]
    sodium, potassium, calcium, reticulum, subspace = rows[14:19]
    moved = []
    for i, gate in enumerate(gating):
        shifted = voltage - GATE_MIDPOINT[i]
        steady = jax.nn.sigmoid(shifted / GATE_STEEPNESS[i])
        time_const = TIME_BASE[i] + TIME_PEAK[i] * jnp.exp(-jnp.square(shifted / 0.3))
        moved.append(steady + (gate - steady) * jnp.exp(-TIME_STEP / time_const))
    g = moved
    sodium_rev = NERNST_SCALE * jnp.log(SODIUM_OUT / sodium)
    potassium_rev = NERNST_SCALE * jnp.log(POTASSIUM_OUT / potassium)
    calcium_rev = 0.5 * NERNST_SCALE * jnp.log(CALCIUM_OUT / subspace)
    sodium_flow = COND_SODIUM * (g[0] * g[0] * g[0]) * g[1] * g[2] * (voltage - sodium_rev)
    calcium_flow = COND_CALCIUM * g[3] * g[4] * g[5] * (voltage - calcium_rev)
    potassium_cond = (
        COND_TRANSIENT * g[6] * g[7]
        + COND_RAPID * g[8] * g[9]
        + COND_SLOW * (g[10] * g[10])
        + COND_INWARD * g[11]
    )
    potassium_flow = potassium_cond * (voltage - potassium_rev)
    current = sodium_flow + calcium_flow + potassium_flow
    release = COND_RELEASE * g[12] * (reticulum - subspace) / (reticulum + subspace)
    sodium = sodium * jnp.exp(-0.5 * TIME_STEP * sodium_flow)
    potassium = potassium * jnp.exp(-0.5 * TIME_STEP * potassium_flow)
    calcium = calcium * jnp.exp(-0.5 * TIME_STEP * calcium_flow)
    subspace = subspace * jnp.exp(TIME_STEP * (release - 0.5 * calcium_flow))
    reticulum = reticulum * jnp.exp(-TIME_STEP * release)
    voltage = voltage - TIME_STEP * MEMBRANE_RATE * current
    return [voltage, *moved, sodium, potassium, calcium, reticulum, subspace], current


def pairs_of(index):
    chunks = [index[:, k : k + LANES] for k in range(0, index.shape[1], LANES)]
    return [jnp.concatenate(chunks[k : k + 2], axis=0) for k in range(0, len(chunks), 2)]


def gather(source, rows, index):
    peers = index.shape[0]
    out = []
    for pair in pairs_of(index):
        high, low = pair >> 7, pair & (LANES - 1)
        total = jnp.zeros(pair.shape, F32)
        for h in range(rows):
            picked = jnp.take_along_axis(source(h), low, axis=1)
            total = jnp.where(high == h, picked, total)
        out += [total[:peers], total[peers:]]
    return jnp.concatenate(out, axis=1)


def scatter(values, index, rows):
    slots = values.shape[1]
    high, low = index >> 7, index & (LANES - 1)
    first = values.astype(jnp.bfloat16).astype(F32)
    rest = values - first
    second = rest.astype(jnp.bfloat16).astype(F32)
    third = rest - second
    mine = lax.broadcasted_iota(jnp.int32, (rows, slots), 0) == high
    left = jnp.concatenate([jnp.where(mine, part, 0.0) for part in (first, second, third)], axis=0)
    spread = lax.broadcasted_iota(jnp.int32, (LANES, slots), 0) == low
    right = jnp.where(spread, 1.0, 0.0).astype(jnp.bfloat16)
    sums = lax.dot_general(
        left.astype(jnp.bfloat16), right, (((1,), (1,)), ((), ())), preferred_element_type=F32
    )
    return sums[:rows] + sums[rows : 2 * rows] + sums[2 * rows :]


def pick_current(current, nodes):
    rows, peers = current.shape[0], nodes.shape[0]
    return gather(
        lambda h: jnp.broadcast_to(current[h : h + 1], (2 * peers, LANES)), rows, nodes
    )


def spread_current(outgoing, maps, diag, chain, shares_ref, blocks_ref):
    torso = diag.shape[0]
    shares_ref[...] = jnp.zeros_like(shares_ref)
    here = lax.axis_index("dom")
    for o, offset in enumerate(peer_offsets(chain)):
        share = scatter(outgoing[o : o + 1], maps[o : o + 1], torso)
        at = pl.ds(pl.multiple_of((lax.rem(here + offset, chain) + 1) * torso, 8), torso)
        shares_ref[at, :] = shares_ref[at, :] + share

    def block(q, carry):
        before, own, after = (
            shares_ref[pl.ds(pl.multiple_of((q + k) * torso, 8), torso), :] for k in range(3)
        )
        blocks_ref[q, 0:torso] = own
        blocks_ref[q, torso : torso + 2 * HALO] = jnp.concatenate(
            [before[torso - HALO :], after[:HALO]], axis=0
        )
        blocks_ref[q, torso + 2 * HALO :] = jnp.concatenate(
            [
                jnp.where(q == lax.rem(here + 1, chain), diag[torso - HALO :], 0.0),
                jnp.where(q == lax.rem(here + chain - 1, chain), diag[:HALO], 0.0),
            ],
            axis=0,
        )
        return carry

    lax.fori_loop(0, chain, block, 0)


def peer_offsets(chain):
    return [0, 1, chain - 1, chain // 2]


def feedback_of(estimates, nodes, maps, heart):
    peers = nodes.shape[0]
    torso = estimates[0].shape[0]

    def source(h):
        rows = [estimate[h : h + 1] for estimate in estimates]
        return jnp.concatenate(rows * 2, axis=0)

    returned = gather(source, torso, maps)
    total = jnp.zeros((heart, LANES), F32)
    for o in range(peers):
        total = total + scatter(returned[o : o + 1], nodes[o : o + 1], heart)
    return total


def product(own_ref, other_ref, own_cols, other_cols, window_ref, out_ref):
    tiles, slots = own_ref.shape[0], own_ref.shape[1]
    eye = lax.broadcasted_iota(jnp.int32, (LANES, LANES), 0) == lax.broadcasted_iota(
        jnp.int32, (LANES, LANES), 1
    )
    for t in range(tiles):
        total = None
        for ref, cols in ((own_ref, own_cols), (other_ref, other_cols)):
            for k in range(slots):
                term = ref[t, k] * window_ref[pl.ds(cols[k, t], 1), :]
                total = term if total is None else total + term
        column = jnp.sum(total, axis=1, keepdims=True)
        out_ref[t : t + 1, :] = jnp.sum(jnp.where(eye, column, 0.0), axis=0, keepdims=True)


def fetch(pairs, sems):
    copies = [pltpu.make_async_copy(a, b, sems.at[i]) for i, (a, b) in enumerate(pairs)]
    for copy in copies:
        copy.start()
    return copies


def begin(
    count_hbm, node_hbm, row_hbm, diag_hbm, states_hbm, tiles_hbm, cols_hbm,
    nodes_ref, own_ref, diag_ref, out_ref, outgoing_ref, tiles_ref, cols_ref,
    count_ref, node_ref, row_ref, states_ref, sems,
):
    peers, slots = nodes_ref.shape
    pairs = [
        (states_hbm, states_ref), (node_hbm, node_ref), (count_hbm, count_ref),
        (row_hbm, row_ref), (diag_hbm, diag_ref), (cols_hbm, cols_ref),
        (tiles_hbm, tiles_ref),
    ]
    copies = [pltpu.make_async_copy(a, b, sems.at[i]) for i, (a, b) in enumerate(pairs)]
    for copy in copies:
        copy.start()
    for copy in copies[:3]:
        copy.wait()
    slot = lax.broadcasted_iota(jnp.int32, (1, slots), 1)
    nodes = jnp.concatenate(
        [
            jnp.where(slot < count_ref[0:1, o : o + 1], node_ref[0, o : o + 1], -1)
            for o in range(peers)
        ],
        axis=0,
    )
    nodes_ref[...] = nodes
    for k in range(out_ref.shape[1]):
        out_ref[:, k, :] = states_ref[:, k * LANES : (k + 1) * LANES]
    rows, current = ionic_rows([out_ref[i] for i in range(out_ref.shape[0])])
    for i, row in enumerate(rows):
        out_ref[i] = row
    outgoing_ref[...] = pick_current(current, nodes)
    for copy in copies[3:]:
        copy.wait()
    own_ref[...] = row_ref[0, 0:1]


def first_shares(
    chain, outgoing_ref, nodes_ref, row_ref, after_ref, before_ref, far_ref, diag_ref,
    maps_ref, blocks_ref, shares_ref,
):
    rows = [row_ref[...], after_ref[...], before_ref[...], far_ref[...]]
    maps = jnp.where(nodes_ref[...] < 0, -1, jnp.concatenate(rows, axis=0))
    maps_ref[...] = maps
    spread_current(outgoing_ref[...], maps, diag_ref[...], chain, shares_ref, blocks_ref)


def next_shares(
    chain, states_ref, e0, e1, e2, e3, nodes_ref, maps_ref, diag_ref, out_ref, blocks_ref, shares_ref
):
    nodes, maps = nodes_ref[...], maps_ref[...]
    feedback = feedback_of([e[...] for e in (e0, e1, e2, e3)], nodes, maps, states_ref.shape[1])
    rows = [states_ref[i] for i in range(states_ref.shape[0])]
    rows[0] = rows[0] + TIME_STEP * FEEDBACK_RATE * feedback
    rows, current = ionic_rows(rows)
    for i, row in enumerate(rows):
        out_ref[i] = row
    outgoing = pick_current(current, nodes)
    spread_current(outgoing, maps, diag_ref[...], chain, shares_ref, blocks_ref)


def last_feedback(states_ref, e0, e1, e2, e3, nodes_ref, maps_ref, out_ref, dense_ref):
    nodes, maps = nodes_ref[...], maps_ref[...]
    torso = e0.shape[0]
    estimates = [e0[...], e1[0:torso], e2[0:torso], e3[...]]
    feedback = feedback_of(estimates, nodes, maps, states_ref.shape[1])
    dense_ref[...] = states_ref[...]
    dense_ref[0] = states_ref[0] + TIME_STEP * FEEDBACK_RATE * feedback
    for k in range(states_ref.shape[1]):
        out_ref[:, k * LANES : (k + 1) * LANES] = dense_ref[:, k, :]


def sweep_one(
    chain, own_cols, other_cols, own_ref, other_ref, mine_ref, yours_ref, diag_ref,
    residual_ref, direction_ref, estimate_ref, window_ref, product_ref,
):
    torso = residual_ref.shape[0]
    forcing = TORSO_COUPLING * (mine_ref[...] + yours_ref[...])
    diag = diag_ref[...]
    residual = forcing[0:torso]
    direction = residual / (CHEB_THETA * diag)
    rims = [slice(torso + k * HALO, torso + (k + 1) * HALO) for k in range(4)]
    before = forcing[rims[0]] / (CHEB_THETA * mine_ref[rims[2]])
    after = forcing[rims[1]] / (CHEB_THETA * mine_ref[rims[3]])
    fill_window(chain, direction, before, after, window_ref)
    product(own_ref, other_ref, own_cols, other_cols, window_ref, product_ref)
    residual = residual - (diag * direction + product_ref[...])
    estimate = direction
    direction = KEEP[0] * direction + PULL[0] * (residual / diag)
    residual_ref[...] = residual
    direction_ref[...] = direction
    estimate_ref[...] = estimate + direction


def fill_window(chain, direction, before, after, window_ref):
    torso = direction.shape[0]
    here = lax.axis_index("dom")
    window_ref[0:HALO] = jnp.where(here > 0, before, 0.0)
    window_ref[HALO : HALO + torso] = direction
    window_ref[HALO + torso : 2 * HALO + torso] = jnp.where(here < chain - 1, after, 0.0)


def sweep_two(
    chain, last, own_cols, other_cols, own_ref, other_ref, before_ref, after_ref, direction_in,
    residual_in, estimate_in, diag_ref, *refs,
):
    estimate_ref, window_ref, product_ref = refs[0], refs[-2], refs[-1]
    torso = estimate_ref.shape[0]
    diag = diag_ref[...]
    direction = direction_in[...]
    fill_window(chain, direction, before_ref[...], after_ref[...], window_ref)
    product(own_ref, other_ref, own_cols, other_cols, window_ref, product_ref)
    residual = residual_in[...] - (diag * direction + product_ref[...])
    direction = KEEP[1] * direction + PULL[1] * (residual / diag)
    estimate = estimate_in[...] + direction
    estimate_ref[...] = estimate
    if last:
        final_ref, residual_ref, direction_ref, prev_ref, next_ref = refs[1:-2]
        final_ref[...] = estimate
        residual_ref[...] = residual
        direction_ref[...] = direction
        prev_ref[0:torso] = estimate
        prev_ref[torso : torso + HALO] = direction[0:HALO]
        next_ref[0:torso] = estimate
        next_ref[torso : torso + HALO] = direction[torso - HALO : torso]


def last_residual(
    chain, own_cols, other_cols, own_ref, other_ref, after_ref, before_ref, direction_in,
    residual_in, diag_ref, residual_ref, window_ref, product_ref,
):
    torso = residual_ref.shape[0]
    rim = slice(torso, torso + HALO)
    diag = diag_ref[...]
    direction = direction_in[...]
    fill_window(chain, direction, before_ref[rim], after_ref[rim], window_ref)
    product(own_ref, other_ref, own_cols, other_cols, window_ref, product_ref)
    residual_ref[...] = residual_in[...] - (diag * direction + product_ref[...])


def on_device(states, send_node, send_count, recv_row, columns, tile_values, diagonal):
    chain = lax.axis_size("dom")
    peers, slots = send_node.shape[1:]
    node_count = states.shape[1]
    heart = node_count // LANES
    torso = diagonal.shape[0] // LANES
    far = peer_offsets(chain)[3]

    def from_peer(value, offset):
        return lax.ppermute(value, "dom", [((i + offset) % chain, i) for i in range(chain)])

    def from_sibling(value):
        return lax.ppermute(value, "sub", [(0, 1), (1, 0)])

    def shape(*dims, dtype=F32):
        return jax.ShapeDtypeStruct(dims, dtype)

    dense = shape(states.shape[0], heart, LANES)
    field = shape(torso, LANES)
    packed = shape(torso + HALO, LANES)
    table = shape(peers, slots, dtype=jnp.int32)
    row = shape(1, slots, dtype=jnp.int32)
    blocks = shape(chain, 2 * torso, LANES)
    shares = (pltpu.VMEM(((chain + 2) * torso, LANES), F32),)
    work = (pltpu.VMEM((torso + 2 * HALO, LANES), F32), pltpu.VMEM(field.shape, F32))
    arrivals = (
        pltpu.VMEM(send_count.shape, jnp.int32),
        pltpu.VMEM(send_node.shape, jnp.int32),
        pltpu.VMEM(recv_row.shape, jnp.int32),
        pltpu.VMEM(states.shape, F32),
        pltpu.SemaphoreType.DMA((7,)),
    )

    got_after = from_peer(recv_row[0, 1:2], 1)
    got_before = from_peer(recv_row[0, 2:3], chain - 1)
    got_far = from_peer(recv_row[0, 3:4], far)
    other_tiles = from_sibling(tile_values)
    columns = columns.T
    nodes, own_rows, diag, states, outgoing, tiles, columns = call(
        begin,
        (
            table,
            row,
            field,
            dense,
            shape(peers, slots),
            shape(*tile_values.shape),
            shape(*columns.shape, dtype=jnp.int32),
        ),
        arrivals,
    )(in_specs=[HBM] * 7)(
        send_count, send_node, recv_row, diagonal.reshape(torso, LANES), states, tile_values,
        columns,
    )
    other_columns = from_sibling(columns)
    stored = (columns, other_columns, tiles, other_tiles)
    maps, parts = call(functools.partial(first_shares, chain), (table, blocks), shares)(
        in_specs=[VMEM] * 7
    )(outgoing, nodes, own_rows, got_after, got_before, got_far, diag)
    parts, stored = lax.optimization_barrier((parts, stored))
    for time_step in range(2):
        last = time_step == 1
        parts = lax.all_to_all(parts, "dom", split_axis=0, concat_axis=0, tiled=True)
        mine = jnp.sum(parts, axis=0)
        residual, direction, estimate = call(functools.partial(sweep_one, chain), (field,) * 3, work)(
            in_specs=[SMEM] * 2 + [VMEM] * 5
        )(*stored, mine, from_sibling(mine), diag)
        before = from_peer(direction[-HALO:], chain - 1)
        after = from_peer(direction[:HALO], 1)
        estimate, *rest = call(
            functools.partial(sweep_two, chain, last),
            (field,) * 4 + (packed,) * 2 if last else (field,),
            work,
        )(in_specs=[SMEM] * 2 + [VMEM] * 8)(
            *stored, before, after, direction, residual, estimate, diag
        )
        if not last:
            got_after, got_before = from_peer(estimate, 1), from_peer(estimate, chain - 1)
            got_far = from_peer(estimate, far)
            states, parts = call(
                functools.partial(next_shares, chain), (dense, blocks), shares
            )(in_specs=[VMEM] * 8)(
                states, estimate, got_after, got_before, got_far, nodes, maps, diag
            )
    potential, residual, direction, to_prev, to_next = rest
    got_after, got_before = from_peer(to_prev, 1), from_peer(to_next, chain - 1)
    got_far = from_peer(estimate, far)
    residual = call(functools.partial(last_residual, chain), field, work)(
        in_specs=[SMEM] * 2 + [VMEM] * 7
    )(*stored, got_after, got_before, direction, residual, diag)
    new_states = call(
        last_feedback, shape(*dense.shape[:1], node_count), (pltpu.VMEM(dense.shape, F32),)
    )(in_specs=[VMEM] * 7)(states, estimate, got_after, got_before, got_far, nodes, maps)
    return new_states, potential.reshape(-1), residual.reshape(-1)


def solution(mesh):
    placed = (
        P(None, ("case", "dom", "sub")),
        P(("case", "dom", "sub"), None, None),
        P(("case", "dom", "sub"), None),
        P(("case", "dom", "sub"), None, None),
        P(("case", "dom"), "sub"),
        P(("case", "dom"), "sub", None, None),
        P(("case", "dom")),
    )
    return jax.shard_map(
        on_device,
        mesh=mesh,
        in_specs=placed,
        out_specs=(P(None, ("case", "dom", "sub")), P(("case", "dom")), P(("case", "dom"))),
        check_vma=False,
    )
```

time: 88.7 us -> 84.7 us (0.955)
  starting transfers between devices: 34 us -> 17.6 us
  blocking collectives: 13.8 us -> 25.4 us
  local copies, waits for them, and re-layouts: 7.33 us -> 11.3 us
  waiting for transfers between devices: 21.1 us -> 19.1 us
  Pallas kernels: 11 us -> 10.1 us
    ppermute x6 -> x4, starting transfers between devices: 12.6 us -> 0.66 us  [from_sibling(): return lax.ppermute(value, 'sub', [(0, 1), (1, 0)])]
    all_to_all x1 -> x2, blocking collectives: 13.8 us -> 25.4 us  [on_device(): lax.all_to_all(parts, 'dom', split_axis=0, concat_axis=0, tiled=True)]
    all_to_all x1 -> x0, waiting for transfers between devices: 6.49 us -> none  [on_device(): lax.all_to_all(parts, ('dom', 'sub'), split_axis=0, concat_axis=0, tiled=...]
    ppermute x9 -> x13, waiting for transfers between devices: 11.1 us -> 16 us  [from_peer(): lax.ppermute(value, 'dom', [((i + offset) % chain, i) for i in range(chai...]
    all_to_all x1 -> x0, starting transfers between devices: 4.3 us -> none  [on_device(): lax.all_to_all(parts, ('dom', 'sub'), split_axis=0, concat_axis=0, tiled=...]
    unnamed x22 -> x20, local copies, waits for them, and re-layouts: 7.32 us -> 10.5 us
    pallas_call x7 -> x6, Pallas kernels: 7.24 us -> 6.21 us  [the longest x2 2.87 us: on_device(): call(functools.partial(sweep_two, chain, last), (field,) * 4 + (packed,)...]
    ppermute x6 -> x4, waiting for transfers between devices: 3.58 us -> 3.09 us  [from_sibling(): return lax.ppermute(value, 'sub', [(0, 1), (1, 0)])]
  transfers between devices with their start and end apart: 16 -> 17, of which waited for: 8 -> 10; matrix products, arithmetic and copies ran while one was open for 0% -> 1% of each run, Pallas kernels for 4% -> 3%
where the time goes in v3:
time: 84.7 us; the launch traced here: 84.2 us
  blocking collectives  25.4 us (30%)
  waiting for transfers between devices  19.1 us (23%)
  starting transfers between devices  17.6 us (21%)
  local copies, waits for them, and re-layouts  11.3 us (13%)
  Pallas kernels  10.1 us (12%)
    all_to_all x2, blocking collectives, on_device(): lax.all_to_all(parts, 'dom', split_axis=0, concat_axis=0, tiled=True)  25.4 us
    ppermute x13, starting transfers between devices, from_peer(): lax.ppermute(value, 'dom', [((i + offset) % chain, i) for i in range(chai...  17 us
    ppermute x13, waiting for transfers between devices, from_peer(): lax.ppermute(value, 'dom', [((i + offset) % chain, i) for i in range(chai...  16 us
    unnamed x20, local copies, waits for them, and re-layouts  10.5 us
    ppermute x4, waiting for transfers between devices, from_sibling(): return lax.ppermute(value, 'sub', [(0, 1), (1, 0)])  3.09 us
    pallas_call x2, Pallas kernels, on_device(): call(functools.partial(sweep_two, chain, last), (field,) * 4 + (packed,)...  2.87 us
    pallas_call x2, Pallas kernels, on_device(): call(functools.partial(sweep_one, chain), (field,) * 3, work)  2.23 us
    pallas_call x1, Pallas kernels, on_device(): call(functools.partial(last_residual, chain), field, work)  1.73 us
  transfers between devices with their start and end apart: 17, of which 10 were waited for; matrix products, arithmetic and copies ran while one was open for 1% of the time, Pallas kernels for 3%

profile of v3, /device:TPU:0, one launch (start us, length us, event | category | flops | bytes accessed | tf_op | source)
XLA Modules:
  0.0 84.2 jit_solution(107743717026398329)
XLA Ops:
  2.0 3.7 %collective-permute-start.2 = (s32[1,512]{1,0:T(1,128)S(1)}, s32[1,512]{1,0:T(1,128)S(1)}, u32[]{:S(2)}, u32[]{:S(2)}) collective-permute-start(s32[1,512]{1,0:T(1,128)S(1)} %get-tuple-element.59), channel_id=1, source_target_pairs={{8,0},{10,2},{12,4},{14,6},{0,8},{2,10},{4,12},{6,14},{9,1},{11,3}... | collective-permute-start | bytes 6152 | tf_op jit(solution)/shard_map/ppermute | solution.py:356
  5.6 2.3 %collective-permute-start = (s32[1,512]{1,0:T(1,128)S(1)}, s32[1,512]{1,0:T(1,128)S(1)}, u32[]{:S(2)}, u32[]{:S(2)}) collective-permute-start(s32[1,512]{1,0:T(1,128)S(1)} %get-tuple-element.60), channel_id=1, source_target_pairs={{2,0},{4,2},{6,4},{8,6},{10,8},{12,10},{14,12},{0,14},{3,1},{5,3},... | collective-permute-start | bytes 6152 | tf_op jit(solution)/shard_map/ppermute | solution.py:356
  7.9 1.6 %copy-done.3 = f32[8,4,128,128]{3,2,1,0:T(8,128)S(1)} copy-done((f32[8,4,128,128]{3,2,1,0:T(8,128)S(1)}, f32[8,4,128,128]{3,2,1,0:T(8,128)}, u32[]{:S(2)}) %copy-start.3) | copy-done | bytes 2097176
  14.6 1.3 %copy-done = f32[8,4,128,128]{3,2,1,0:T(8,128)} copy-done((f32[8,4,128,128]{3,2,1,0:T(8,128)}, f32[8,4,128,128]{3,2,1,0:T(8,128)S(1)}, u32[]{:S(2)}) %copy-start) | copy-done | bytes 2097176
  17.1 12.7 %all_to_all.10 = f32[8,16,128]{2,1,0:T(8,128)S(1)} all-to-all(f32[8,16,128]{2,1,0:T(8,128)S(1)} %get-tuple-element.43), channel_id=1, replica_groups=mesh['case'=2,'dom'=8,'sub'=2] {'dom'}, dimensions={0} | all-to-all | bytes 131072 | tf_op jit(solution)/shard_map/all_to_all | solution.py:409
  29.9 1.2 %collective-permute-done.5.yours_ref = f32[16,128]{1,0:T(8,128)S(1)} collective-permute-done((f32[16,128]{1,0:T(8,128)S(1)}, f32[16,128]{1,0:T(8,128)S(1)}, u32[]{:S(2)}, u32[]{:S(2)}) %collective-permute-start.5) | collective-permute-done | bytes 8224 | tf_op jit(solution)/shard_map/ppermute | solution.py:359
  31.1 1.6 %copy-done.1 = f32[8,4,128,128]{3,2,1,0:T(8,128)S(1)} copy-done((f32[8,4,128,128]{3,2,1,0:T(8,128)S(1)}, f32[8,4,128,128]{3,2,1,0:T(8,128)}, u32[]{:S(2)}) %copy-start.1) | copy-done | bytes 2097176
  34.7 1.2 %collective-permute-start.6 = (f32[2,128]{1,0:T(2,128)S(1)}, f32[2,128]{1,0:T(2,128)S(1)}, u32[]{:S(2)}, u32[]{:S(2)}) collective-permute-start(f32[2,128]{1,0:T(2,128)S(1)} %get-tuple-element.65), channel_id=1, source_target_pairs={{14,0},{0,2},{2,4},{4,6},{6,8},{8,10},{10,12},{12,14},{15,1},{1,3}... | collective-permute-start | bytes 3080 | tf_op jit(solution)/shard_map/ppermute | solution.py:356
  35.9 1.5 %collective-permute-done.7.after_ref = f32[2,128]{1,0:T(2,128)S(1)} collective-permute-done((f32[2,128]{1,0:T(2,128)S(1)}, f32[2,128]{1,0:T(2,128)S(1)}, u32[]{:S(2)}, u32[]{:S(2)}) %collective-permute-start.7) | collective-permute-done | bytes 1056 | tf_op jit(solution)/shard_map/ppermute | solution.py:356
  37.4 3.5 %collective-permute-done.6.before_ref = f32[2,128]{1,0:T(2,128)S(1)} collective-permute-done((f32[2,128]{1,0:T(2,128)S(1)}, f32[2,128]{1,0:T(2,128)S(1)}, u32[]{:S(2)}, u32[]{:S(2)}) %collective-permute-start.6) | collective-permute-done | bytes 1056 | tf_op jit(solution)/shard_map/ppermute | solution.py:356
  40.9 1.1 %shard_map.97.e0 = f32[8,128]{1,0:T(8,128)S(1)} custom-call(s32[4,8]{1,0:T(4,128)S(1)} %get-tuple-element.39.own_cols, s32[4,8]{1,0:T(4,128)S(1)} %collective-permute-done.3.other_cols, f32[8,4,128,128]{3,2,1,0:T(8,128)S(1)} %copy-done.1, f32[8,4,128,128]{3,2,1,0:T(8,128)S(1)} %collective-permute-done.4.other_ref, ...), custom_call_target="tpu_custom_call" | custom-call | flops 4000000 | bytes 262144 | tf_op jit(solution)/shard_map/pallas_call | solution.py:416
  42.2 4.7 %collective-permute-start.8 = (f32[8,128]{1,0:T(8,128)S(1)}, f32[8,128]{1,0:T(8,128)S(1)}, u32[]{:S(2)}, u32[]{:S(2)}) collective-permute-start(f32[8,128]{1,0:T(8,128)S(1)} %shard_map.97.e0), channel_id=1, source_target_pairs={{2,0},{4,2},{6,4},{8,6},{10,8},{12,10},{14,12},{0,14},{3,1},{5,3},... | collective-permute-start | bytes 12296 | tf_op jit(solution)/shard_map/ppermute | solution.py:356
  46.9 1.6 %collective-permute-done.9.e2 = f32[8,128]{1,0:T(8,128)S(1)} collective-permute-done((f32[8,128]{1,0:T(8,128)S(1)}, f32[8,128]{1,0:T(8,128)S(1)}, u32[]{:S(2)}, u32[]{:S(2)}) %collective-permute-start.9) | collective-permute-done | bytes 4128 | tf_op jit(solution)/shard_map/ppermute | solution.py:356
  49.5 12.7 %all_to_all.11 = f32[8,16,128]{2,1,0:T(8,128)S(1)} all-to-all(f32[8,16,128]{2,1,0:T(8,128)S(1)} %get-tuple-element.49), channel_id=1, replica_groups=mesh['case'=2,'dom'=8,'sub'=2] {'dom'}, dimensions={0} | all-to-all | bytes 131072 | tf_op jit(solution)/shard_map/all_to_all | solution.py:409
  62.3 1.2 %collective-permute-done.11.yours_ref = f32[16,128]{1,0:T(8,128)S(1)} collective-permute-done((f32[16,128]{1,0:T(8,128)S(1)}, f32[16,128]{1,0:T(8,128)S(1)}, u32[]{:S(2)}, u32[]{:S(2)}) %collective-permute-start.11) | collective-permute-done | bytes 8224 | tf_op jit(solution)/shard_map/ppermute | solution.py:359
  63.5 1.6 %copy-done.2 = f32[8,4,128,128]{3,2,1,0:T(8,128)S(1)} copy-done((f32[8,4,128,128]{3,2,1,0:T(8,128)S(1)}, f32[8,4,128,128]{3,2,1,0:T(8,128)}, u32[]{:S(2)}) %copy-start.2) | copy-done | bytes 2097176
  67.1 1.2 %collective-permute-start.12 = (f32[2,128]{1,0:T(2,128)S(1)}, f32[2,128]{1,0:T(2,128)S(1)}, u32[]{:S(2)}, u32[]{:S(2)}) collective-permute-start(f32[2,128]{1,0:T(2,128)S(1)} %get-tuple-element.63), channel_id=1, source_target_pairs={{14,0},{0,2},{2,4},{4,6},{6,8},{8,10},{10,12},{12,14},{15,1},{1,3}... | collective-permute-start | bytes 3080 | tf_op jit(solution)/shard_map/ppermute | solution.py:356
  68.3 1.5 %collective-permute-done.13.after_ref = f32[2,128]{1,0:T(2,128)S(1)} collective-permute-done((f32[2,128]{1,0:T(2,128)S(1)}, f32[2,128]{1,0:T(2,128)S(1)}, u32[]{:S(2)}, u32[]{:S(2)}) %collective-permute-start.13) | collective-permute-done | bytes 1056 | tf_op jit(solution)/shard_map/ppermute | solution.py:356
  69.8 3.5 %collective-permute-done.12.before_ref = f32[2,128]{1,0:T(2,128)S(1)} collective-permute-done((f32[2,128]{1,0:T(2,128)S(1)}, f32[2,128]{1,0:T(2,128)S(1)}, u32[]{:S(2)}, u32[]{:S(2)}) %collective-permute-start.12) | collective-permute-done | bytes 1056 | tf_op jit(solution)/shard_map/ppermute | solution.py:356
  73.3 1.7 %shard_map.100 = (f32[8,128]{1,0:T(8,128)S(1)}, f32[8,128]{1,0:T(8,128)}, f32[8,128]{1,0:T(8,128)S(1)}, f32[8,128]{1,0:T(8,128)S(1)}, f32[10,128]{1,0:T(8,128)S(1)}, /*index=5*/f32[10,128]{1,0:T(8,128)S(1)}) custom-call(s32[4,8]{1,0:T(4,128)S(1)} %get-tuple-element.39.own_cols, s32[4,8]{1,0:T(4,128)S(1)} %collective-permute-done.3.other_cols, ...), custom_call_target="tpu_custom_call" | custom-call | flops 4000000 | bytes 262144 | tf_op jit(solution)/shard_map/pallas_call | solution.py:416
  75.1 2.0 %collective-permute-start.15 = (f32[10,128]{1,0:T(8,128)S(1)}, f32[10,128]{1,0:T(8,128)S(1)}, u32[]{:S(2)}, u32[]{:S(2)}) collective-permute-start(f32[10,128]{1,0:T(8,128)S(1)} %get-tuple-element.55), channel_id=1, source_target_pairs={{14,0},{0,2},{2,4},{4,6},{6,8},{8,10},{10,12},{12,14},{15,1},{1,3}... | collective-permute-start | bytes 15368 | tf_op jit(solution)/shard_map/ppermute | solution.py:356
  77.1 1.6 %collective-permute-done.14.e1.after_ref = f32[10,128]{1,0:T(8,128)S(1)} collective-permute-done((f32[10,128]{1,0:T(8,128)S(1)}, f32[10,128]{1,0:T(8,128)S(1)}, u32[]{:S(2)}, u32[]{:S(2)}) %collective-permute-start.14) | collective-permute-done | bytes 5152 | tf_op jit(solution)/shard_map/ppermute | solution.py:356
  78.7 2.7 %collective-permute-done.15.e2.before_ref = f32[10,128]{1,0:T(8,128)S(1)} collective-permute-done((f32[10,128]{1,0:T(8,128)S(1)}, f32[10,128]{1,0:T(8,128)S(1)}, u32[]{:S(2)}, u32[]{:S(2)}) %collective-permute-start.15) | collective-permute-done | bytes 5152 | tf_op jit(solution)/shard_map/ppermute | solution.py:356
  81.4 1.7 %shard_map.102 = f32[8,128]{1,0:T(8,128)} custom-call(s32[4,8]{1,0:T(4,128)S(1)} %get-tuple-element.39.own_cols, s32[4,8]{1,0:T(4,128)S(1)} %collective-permute-done.3.other_cols, f32[8,4,128,128]{3,2,1,0:T(8,128)S(1)} %copy-done.2, f32[8,4,128,128]{3,2,1,0:T(8,128)S(1)} %collective-permute-done.4.other_ref, ...), custom_call_target="tpu_custom_call" | custom-call | flops 4000000 | bytes 262144 | tf_op jit(solution)/shard_map/pallas_call | solution.py:434
  (46 shorter events, 14.0 us)
Async XLA Ops:
  0.6 16.5 %collective-permute-start.4 = (f32[8,4,128,128]{3,2,1,0:T(8,128)}, f32[8,4,128,128]{3,2,1,0:T(8,128)S(1)}, u32[]{:S(2)}, u32[]{:S(2)}) collective-permute-start(f32[8,4,128,128]{3,2,1,0:T(8,128)} %tiles_hbm.1), channel_id=1, source_target_pairs={{0,1},{1,0},{2,3},{3,2},{4,5},{5,4},{6,7},{7,6},{8,9},{9,8},{10,11... | collective-permute-start | bytes 6291464 | tf_op jit(solution)/shard_map/ppermute | solution.py:359
  2.0 14.0 %collective-permute-start.2 = (s32[1,512]{1,0:T(1,128)S(1)}, s32[1,512]{1,0:T(1,128)S(1)}, u32[]{:S(2)}, u32[]{:S(2)}) collective-permute-start(s32[1,512]{1,0:T(1,128)S(1)} %get-tuple-element.59), channel_id=1, source_target_pairs={{8,0},{10,2},{12,4},{14,6},{0,8},{2,10},{4,12},{6,14},{9,1},{11,3}... | collective-permute-start | bytes 6152 | tf_op jit(solution)/shard_map/ppermute | solution.py:356
  5.6 10.3 %collective-permute-start = (s32[1,512]{1,0:T(1,128)S(1)}, s32[1,512]{1,0:T(1,128)S(1)}, u32[]{:S(2)}, u32[]{:S(2)}) collective-permute-start(s32[1,512]{1,0:T(1,128)S(1)} %get-tuple-element.60), channel_id=1, source_target_pairs={{2,0},{4,2},{6,4},{8,6},{10,8},{12,10},{14,12},{0,14},{3,1},{5,3},... | collective-permute-start | bytes 6152 | tf_op jit(solution)/shard_map/ppermute | solution.py:356
  7.9 8.1 %collective-permute-start.1 = (s32[1,512]{1,0:T(1,128)S(1)}, s32[1,512]{1,0:T(1,128)S(1)}, u32[]{:S(2)}, u32[]{:S(2)}) collective-permute-start(s32[1,512]{1,0:T(1,128)S(1)} %get-tuple-element.61), channel_id=1, source_target_pairs={{14,0},{0,2},{2,4},{4,6},{6,8},{8,10},{10,12},{12,14},{15,1},{1,3}... | collective-permute-start | bytes 6152 | tf_op jit(solution)/shard_map/ppermute | solution.py:356
  7.9 1.6 %copy-start.3 = (f32[8,4,128,128]{3,2,1,0:T(8,128)S(1)}, f32[8,4,128,128]{3,2,1,0:T(8,128)}, u32[]{:S(2)}) copy-start(f32[8,4,128,128]{3,2,1,0:T(8,128)} %tiles_hbm.1) | copy-start | bytes 6291460
  9.5 0.9 %copy-start.4 = (f32[19,2048]{1,0:T(8,128)S(1)}, f32[19,2048]{1,0:T(8,128)}, u32[]{:S(2)}) copy-start(f32[19,2048]{1,0:T(8,128)} %states_hbm.1) | copy-start | bytes 466948
  10.4 0.7 copy-start.5
  11.1 0.7 copy-start.6
  14.6 1.4 %copy-start = (f32[8,4,128,128]{3,2,1,0:T(8,128)}, f32[8,4,128,128]{3,2,1,0:T(8,128)S(1)}, u32[]{:S(2)}) copy-start(f32[8,4,128,128]{3,2,1,0:T(8,128)S(1)} %get-tuple-element.41.own_ref) | copy-start | bytes 6291460
  16.0 1.2 %collective-permute-start.3 = (s32[4,8]{1,0:T(4,128)S(1)}, s32[4,8]{1,0:T(4,128)S(1)}, u32[]{:S(2)}, u32[]{:S(2)}) collective-permute-start(s32[4,8]{1,0:T(4,128)S(1)} %get-tuple-element.39.own_cols), channel_id=1, source_target_pairs={{0,1},{1,0},{2,3},{3,2},{4,5},{5,4},{6,7},{7,6},{8,9},{9,8},{10,11... | collective-permute-start | bytes 392 | tf_op jit(solution)/shard_map/ppermute | solution.py:359
  29.8 1.2 %collective-permute-start.5 = (f32[16,128]{1,0:T(8,128)S(1)}, f32[16,128]{1,0:T(8,128)S(1)}, u32[]{:S(2)}, u32[]{:S(2)}) collective-permute-start(f32[16,128]{1,0:T(8,128)S(1)} %reduce_sum.18.mine_ref), channel_id=1, source_target_pairs={{0,1},{1,0},{2,3},{3,2},{4,5},{5,4},{6,7},{7,6},{8,9},{9,8},{10,11... | collective-permute-start | bytes 24584 | tf_op jit(solution)/shard_map/ppermute | solution.py:359
  31.1 1.6 %copy-start.1 = (f32[8,4,128,128]{3,2,1,0:T(8,128)S(1)}, f32[8,4,128,128]{3,2,1,0:T(8,128)}, u32[]{:S(2)}) copy-start(f32[8,4,128,128]{3,2,1,0:T(8,128)} %copy-done) | copy-start | bytes 6291460
  33.8 3.6 %collective-permute-start.7 = (f32[2,128]{1,0:T(2,128)S(1)}, f32[2,128]{1,0:T(2,128)S(1)}, u32[]{:S(2)}, u32[]{:S(2)}) collective-permute-start(f32[2,128]{1,0:T(2,128)S(1)} %get-tuple-element.64), channel_id=1, source_target_pairs={{2,0},{4,2},{6,4},{8,6},{10,8},{12,10},{14,12},{0,14},{3,1},{5,3},... | collective-permute-start | bytes 3080 | tf_op jit(solution)/shard_map/ppermute | solution.py:356
  34.7 6.3 %collective-permute-start.6 = (f32[2,128]{1,0:T(2,128)S(1)}, f32[2,128]{1,0:T(2,128)S(1)}, u32[]{:S(2)}, u32[]{:S(2)}) collective-permute-start(f32[2,128]{1,0:T(2,128)S(1)} %get-tuple-element.65), channel_id=1, source_target_pairs={{14,0},{0,2},{2,4},{4,6},{6,8},{8,10},{10,12},{12,14},{15,1},{1,3}... | collective-permute-start | bytes 3080 | tf_op jit(solution)/shard_map/ppermute | solution.py:356
  42.1 4.9 %collective-permute-start.10 = (f32[8,128]{1,0:T(8,128)S(1)}, f32[8,128]{1,0:T(8,128)S(1)}, u32[]{:S(2)}, u32[]{:S(2)}) collective-permute-start(f32[8,128]{1,0:T(8,128)S(1)} %shard_map.97.e0), channel_id=1, source_target_pairs={{8,0},{10,2},{12,4},{14,6},{0,8},{2,10},{4,12},{6,14},{9,1},{11,3}... | collective-permute-start | bytes 12296 | tf_op jit(solution)/shard_map/ppermute | solution.py:356
  42.1 6.4 %collective-permute-start.9 = (f32[8,128]{1,0:T(8,128)S(1)}, f32[8,128]{1,0:T(8,128)S(1)}, u32[]{:S(2)}, u32[]{:S(2)}) collective-permute-start(f32[8,128]{1,0:T(8,128)S(1)} %shard_map.97.e0), channel_id=1, source_target_pairs={{14,0},{0,2},{2,4},{4,6},{6,8},{8,10},{10,12},{12,14},{15,1},{1,3}... | collective-permute-start | bytes 12296 | tf_op jit(solution)/shard_map/ppermute | solution.py:356
  42.2 6.3 %collective-permute-start.8 = (f32[8,128]{1,0:T(8,128)S(1)}, f32[8,128]{1,0:T(8,128)S(1)}, u32[]{:S(2)}, u32[]{:S(2)}) collective-permute-start(f32[8,128]{1,0:T(8,128)S(1)} %shard_map.97.e0), channel_id=1, source_target_pairs={{2,0},{4,2},{6,4},{8,6},{10,8},{12,10},{14,12},{0,14},{3,1},{5,3},... | collective-permute-start | bytes 12296 | tf_op jit(solution)/shard_map/ppermute | solution.py:356
  62.2 1.2 %collective-permute-start.11 = (f32[16,128]{1,0:T(8,128)S(1)}, f32[16,128]{1,0:T(8,128)S(1)}, u32[]{:S(2)}, u32[]{:S(2)}) collective-permute-start(f32[16,128]{1,0:T(8,128)S(1)} %reduce_sum.19.mine_ref), channel_id=1, source_target_pairs={{0,1},{1,0},{2,3},{3,2},{4,5},{5,4},{6,7},{7,6},{8,9},{9,8},{10,11... | collective-permute-start | bytes 24584 | tf_op jit(solution)/shard_map/ppermute | solution.py:359
  63.5 1.6 %copy-start.2 = (f32[8,4,128,128]{3,2,1,0:T(8,128)S(1)}, f32[8,4,128,128]{3,2,1,0:T(8,128)}, u32[]{:S(2)}) copy-start(f32[8,4,128,128]{3,2,1,0:T(8,128)} %copy-done) | copy-start | bytes 6291460
  66.2 3.6 %collective-permute-start.13 = (f32[2,128]{1,0:T(2,128)S(1)}, f32[2,128]{1,0:T(2,128)S(1)}, u32[]{:S(2)}, u32[]{:S(2)}) collective-permute-start(f32[2,128]{1,0:T(2,128)S(1)} %get-tuple-element.62), channel_id=1, source_target_pairs={{2,0},{4,2},{6,4},{8,6},{10,8},{12,10},{14,12},{0,14},{3,1},{5,3},... | collective-permute-start | bytes 3080 | tf_op jit(solution)/shard_map/ppermute | solution.py:356
  67.1 6.3 %collective-permute-start.12 = (f32[2,128]{1,0:T(2,128)S(1)}, f32[2,128]{1,0:T(2,128)S(1)}, u32[]{:S(2)}, u32[]{:S(2)}) collective-permute-start(f32[2,128]{1,0:T(2,128)S(1)} %get-tuple-element.63), channel_id=1, source_target_pairs={{14,0},{0,2},{2,4},{4,6},{6,8},{8,10},{10,12},{12,14},{15,1},{1,3}... | collective-permute-start | bytes 3080 | tf_op jit(solution)/shard_map/ppermute | solution.py:356
  75.1 3.7 %collective-permute-start.14 = (f32[10,128]{1,0:T(8,128)S(1)}, f32[10,128]{1,0:T(8,128)S(1)}, u32[]{:S(2)}, u32[]{:S(2)}) collective-permute-start(f32[10,128]{1,0:T(8,128)S(1)} %get-tuple-element.54), channel_id=1, source_target_pairs={{2,0},{4,2},{6,4},{8,6},{10,8},{12,10},{14,12},{0,14},{3,1},{5,3},... | collective-permute-start | bytes 15368 | tf_op jit(solution)/shard_map/ppermute | solution.py:356
  75.1 6.3 %collective-permute-start.15 = (f32[10,128]{1,0:T(8,128)S(1)}, f32[10,128]{1,0:T(8,128)S(1)}, u32[]{:S(2)}, u32[]{:S(2)}) collective-permute-start(f32[10,128]{1,0:T(8,128)S(1)} %get-tuple-element.55), channel_id=1, source_target_pairs={{14,0},{0,2},{2,4},{4,6},{6,8},{8,10},{10,12},{12,14},{15,1},{1,3}... | collective-permute-start | bytes 15368 | tf_op jit(solution)/shard_map/ppermute | solution.py:356
  77.1 6.1 %collective-permute-start.16 = (f32[8,128]{1,0:T(8,128)S(1)}, f32[8,128]{1,0:T(8,128)S(1)}, u32[]{:S(2)}, u32[]{:S(2)}) collective-permute-start(f32[8,128]{1,0:T(8,128)S(1)} %get-tuple-element.53.e0), channel_id=1, source_target_pairs={{8,0},{10,2},{12,4},{14,6},{0,8},{2,10},{4,12},{6,14},{9,1},{11,3}... | collective-permute-start | bytes 12296 | tf_op jit(solution)/shard_map/ppermute | solution.py:356
  (3 other events, 2.0 us)

commit v4 on v3

v4 whole, which is shorter than its diff:
```python
import functools

import jax
import jax.numpy as jnp
from jax import lax
from jax.experimental import pallas as pl
from jax.experimental.pallas import tpu as pltpu
from jax.sharding import PartitionSpec as P

HALO = 2
SWEEPS = 3
LANES = 128

TIME_STEP = 0.02
NERNST_SCALE = 0.267
SODIUM_OUT = 1.4
POTASSIUM_OUT = 0.054
CALCIUM_OUT = 2000.0
COND_SODIUM = 8.0
COND_CALCIUM = 1.0
COND_TRANSIENT = 0.3
COND_RAPID = 0.2
COND_SLOW = 0.3
COND_INWARD = 2.0
COND_RELEASE = 3.0
MEMBRANE_RATE = 2.0
TORSO_COUPLING = 0.5
FEEDBACK_RATE = 5.0
CHEB_THETA = 1.0
CHEB_DELTA = 0.5
GATE_MIDPOINT = [-0.56, -0.7, -0.7, -0.08, -0.2, -0.3, 0.2, -0.28, -0.26, -0.88, 0.05, -0.8, -0.5]
GATE_STEEPNESS = [0.09, -0.07, -0.07, 0.07, -0.07, -0.09, 0.06, -0.05, 0.07, -0.24, 0.14, -0.1, 0.08]
TIME_BASE = [0.02, 0.3, 1.0, 0.1, 2.0, 0.5, 0.1, 1.0, 1.0, 0.5, 1.0, 0.05, 0.2]
TIME_PEAK = [0.1, 1.0, 3.0, 0.5, 5.0, 2.0, 0.3, 5.0, 3.0, 2.0, 4.0, 0.1, 1.0]

SIGMA = CHEB_THETA / CHEB_DELTA
KEEP, PULL = [], []
_ratio = 1.0 / SIGMA
for _ in range(SWEEPS - 1):
    _next = 1.0 / (2.0 * SIGMA - _ratio)
    KEEP.append(_next * _ratio)
    PULL.append(2.0 * _next / CHEB_DELTA)
    _ratio = _next

VMEM = pl.BlockSpec(memory_space=pltpu.VMEM)
SMEM = pl.BlockSpec(memory_space=pltpu.SMEM)
F32 = jnp.float32


def call(kernel, outs, scratch=(), limit=16, cost=4_000_000):
    return functools.partial(
        pl.pallas_call,
        kernel,
        out_shape=outs,
        out_specs=jax.tree.map(lambda _: VMEM, outs),
        scratch_shapes=list(scratch),
        compiler_params=pltpu.CompilerParams(vmem_limit_bytes=limit << 20),
        cost_estimate=pl.CostEstimate(flops=cost, bytes_accessed=1 << 18, transcendentals=0),
    )


def ionic_rows(rows):
    voltage, gating = rows[0], rows[1:14]
    sodium, potassium, calcium, reticulum, subspace = rows[14:19]
    moved = []
    for i, gate in enumerate(gating):
        shifted = voltage - GATE_MIDPOINT[i]
        steady = jax.nn.sigmoid(shifted / GATE_STEEPNESS[i])
        time_const = TIME_BASE[i] + TIME_PEAK[i] * jnp.exp(-jnp.square(shifted / 0.3))
        moved.append(steady + (gate - steady) * jnp.exp(-TIME_STEP / time_const))
    g = moved
    sodium_rev = NERNST_SCALE * jnp.log(SODIUM_OUT / sodium)
    potassium_rev = NERNST_SCALE * jnp.log(POTASSIUM_OUT / potassium)
    calcium_rev = 0.5 * NERNST_SCALE * jnp.log(CALCIUM_OUT / subspace)
    sodium_flow = COND_SODIUM * (g[0] * g[0] * g[0]) * g[1] * g[2] * (voltage - sodium_rev)
    calcium_flow = COND_CALCIUM * g[3] * g[4] * g[5] * (voltage - calcium_rev)
    potassium_cond = (
        COND_TRANSIENT * g[6] * g[7]
        + COND_RAPID * g[8] * g[9]
        + COND_SLOW * (g[10] * g[10])
        + COND_INWARD * g[11]
    )
    potassium_flow = potassium_cond * (voltage - potassium_rev)
    current = sodium_flow + calcium_flow + potassium_flow
    release = COND_RELEASE * g[12] * (reticulum - subspace) / (reticulum + subspace)
    sodium = sodium * jnp.exp(-0.5 * TIME_STEP * sodium_flow)
    potassium = potassium * jnp.exp(-0.5 * TIME_STEP * potassium_flow)
    calcium = calcium * jnp.exp(-0.5 * TIME_STEP * calcium_flow)
    subspace = subspace * jnp.exp(TIME_STEP * (release - 0.5 * calcium_flow))
    reticulum = reticulum * jnp.exp(-TIME_STEP * release)
    voltage = voltage - TIME_STEP * MEMBRANE_RATE * current
    return [voltage, *moved, sodium, potassium, calcium, reticulum, subspace], current


def pairs_of(index):
    chunks = [index[:, k : k + LANES] for k in range(0, index.shape[1], LANES)]
    return [jnp.concatenate(chunks[k : k + 2], axis=0) for k in range(0, len(chunks), 2)]


def gather(source, rows, index):
    peers = index.shape[0]
    out = []
    for pair in pairs_of(index):
        high, low = pair >> 7, pair & (LANES - 1)
        total = jnp.zeros(pair.shape, F32)
        for h in range(rows):
            picked = jnp.take_along_axis(source(h), low, axis=1)
            total = jnp.where(high == h, picked, total)
        out += [total[:peers], total[peers:]]
    return jnp.concatenate(out, axis=1)


def scatter(values, index, rows):
    slots = values.shape[1]
    high, low = index >> 7, index & (LANES - 1)
    first = values.astype(jnp.bfloat16).astype(F32)
    rest = values - first
    second = rest.astype(jnp.bfloat16).astype(F32)
    third = rest - second
    mine = lax.broadcasted_iota(jnp.int32, (rows, slots), 0) == high
    left = jnp.concatenate([jnp.where(mine, part, 0.0) for part in (first, second, third)], axis=0)
    spread = lax.broadcasted_iota(jnp.int32, (LANES, slots), 0) == low
    right = jnp.where(spread, 1.0, 0.0).astype(jnp.bfloat16)
    sums = lax.dot_general(
        left.astype(jnp.bfloat16), right, (((1,), (1,)), ((), ())), preferred_element_type=F32
    )
    return sums[:rows] + sums[rows : 2 * rows] + sums[2 * rows :]


def pick_current(current, nodes):
    rows, peers = current.shape[0], nodes.shape[0]
    return gather(
        lambda h: jnp.broadcast_to(current[h : h + 1], (2 * peers, LANES)), rows, nodes
    )


def is_even():
    return lax.rem(lax.axis_index("dom"), 2) == 0


def by_side(first, second):
    even = is_even()
    return jnp.where(even, first, second), jnp.where(even, second, first)


def spread_current(outgoing, maps, own_ref, first_ref, second_ref, far_ref):
    torso = own_ref.shape[0]
    own, after, before, far = (
        scatter(outgoing[o : o + 1], maps[o : o + 1], torso) for o in range(maps.shape[0])
    )
    even = is_even()
    own_ref[...] = own
    first_ref[...] = jnp.where(even, after, before)
    second_ref[...] = jnp.where(even, before, after)
    far_ref[...] = far


def feedback_of(estimates, nodes, maps, heart):
    peers = nodes.shape[0]
    torso = estimates[0].shape[0]

    def source(h):
        rows = [estimate[h : h + 1] for estimate in estimates]
        return jnp.concatenate(rows * 2, axis=0)

    returned = gather(source, torso, maps)
    total = jnp.zeros((heart, LANES), F32)
    for o in range(peers):
        total = total + scatter(returned[o : o + 1], nodes[o : o + 1], heart)
    return total


def product(own_ref, other_ref, own_cols, other_cols, window_ref, out_ref):
    tiles, slots = own_ref.shape[0], own_ref.shape[1]
    eye = lax.broadcasted_iota(jnp.int32, (LANES, LANES), 0) == lax.broadcasted_iota(
        jnp.int32, (LANES, LANES), 1
    )
    for t in range(tiles):
        total = None
        for ref, cols in ((own_ref, own_cols), (other_ref, other_cols)):
            for k in range(slots):
                term = ref[t, k] * window_ref[pl.ds(cols[k, t], 1), :]
                total = term if total is None else total + term
        column = jnp.sum(total, axis=1, keepdims=True)
        out_ref[t : t + 1, :] = jnp.sum(jnp.where(eye, column, 0.0), axis=0, keepdims=True)


def fetch(pairs, sems):
    copies = [pltpu.make_async_copy(a, b, sems.at[i]) for i, (a, b) in enumerate(pairs)]
    for copy in copies:
        copy.start()
    return copies


def begin(states_ref, nodes_ref, rows_ref, out_ref, outgoing_ref, own_rows):
    own_rows[...] = rows_ref[0, 0:1]
    for k in range(out_ref.shape[1]):
        out_ref[:, k, :] = states_ref[:, k * LANES : (k + 1) * LANES]
    rows, current = ionic_rows([out_ref[i] for i in range(out_ref.shape[0])])
    for i, row in enumerate(rows):
        out_ref[i] = row
    outgoing_ref[...] = pick_current(current, nodes_ref[...])


def bring(tiles_ref, cols_ref, diag_ref, own_ref, cols_out, diag_out, own_out):
    cols_out[...] = cols_ref[...]
    diag_out[...] = diag_ref[...]
    own_out[...] = own_ref[...]
    del tiles_ref


def first_shares(
    outgoing_ref, nodes_ref, own_rows, first_rows, second_rows, far_rows,
    maps_ref, own_ref, first_ref, second_ref, far_ref,
):
    after, before = by_side(first_rows[0], second_rows[0])
    rows = jnp.concatenate([own_rows[...], after[1:2], before[2:3], far_rows[0, 3:4]], axis=0)
    maps = jnp.where(nodes_ref[...] < 0, -1, rows)
    maps_ref[...] = maps
    spread_current(outgoing_ref[...], maps, own_ref, first_ref, second_ref, far_ref)


def next_shares(
    states_ref, own_estimate, first_estimate, second_estimate, far_estimate, nodes_ref, maps_ref,
    out_ref, own_ref, first_ref, second_ref, far_ref,
):
    nodes, maps = nodes_ref[...], maps_ref[...]
    after, before = by_side(first_estimate[...], second_estimate[...])
    estimates = [own_estimate[...], after, before, far_estimate[...]]
    feedback = feedback_of(estimates, nodes, maps, states_ref.shape[1])
    rows = [states_ref[i] for i in range(states_ref.shape[0])]
    rows[0] = rows[0] + TIME_STEP * FEEDBACK_RATE * feedback
    rows, current = ionic_rows(rows)
    for i, row in enumerate(rows):
        out_ref[i] = row
    outgoing = pick_current(current, nodes)
    spread_current(outgoing, maps, own_ref, first_ref, second_ref, far_ref)


def last_feedback(
    states_ref, own_estimate, first_estimate, second_estimate, far_estimate, nodes_ref, maps_ref,
    out_ref, dense_ref,
):
    nodes, maps = nodes_ref[...], maps_ref[...]
    torso = own_estimate.shape[0]
    after, before = by_side(first_estimate[0:torso], second_estimate[0:torso])
    estimates = [own_estimate[...], after, before, far_estimate[...]]
    feedback = feedback_of(estimates, nodes, maps, states_ref.shape[1])
    dense_ref[...] = states_ref[...]
    dense_ref[0] = states_ref[0] + TIME_STEP * FEEDBACK_RATE * feedback
    for k in range(states_ref.shape[1]):
        out_ref[:, k * LANES : (k + 1) * LANES] = dense_ref[:, k, :]


def fill_window(chain, direction, first, second, window_ref):
    torso = direction.shape[0]
    here = lax.axis_index("dom")
    after, before = by_side(first, second)
    window_ref[0:HALO] = jnp.where(here > 0, before[torso - HALO :], 0.0)
    window_ref[HALO : HALO + torso] = direction
    window_ref[HALO + torso : 2 * HALO + torso] = jnp.where(here < chain - 1, after[0:HALO], 0.0)


def sweep_one(
    chain, own_cols, other_cols, own_ref, other_ref, mine_ref, yours_ref, diag_ref,
    residual_ref, direction_ref, estimate_ref, window_ref, product_ref,
):
    torso = residual_ref.shape[0]
    total = mine_ref[...] + yours_ref[...]
    diag = diag_ref[...]
    residual = total[0:torso]
    direction = residual / (CHEB_THETA * diag)
    fill_window(chain, direction, total[torso : 2 * torso], total[2 * torso :], window_ref)
    product(own_ref, other_ref, own_cols, other_cols, window_ref, product_ref)
    residual = residual - (diag * direction + product_ref[...])
    estimate = direction
    direction = KEEP[0] * direction + PULL[0] * (residual / diag)
    residual_ref[...] = residual
    direction_ref[...] = direction
    estimate_ref[...] = estimate + direction


def sweep_two(
    chain, last, own_cols, other_cols, own_ref, other_ref, first_ref, second_ref, direction_in,
    residual_in, estimate_in, diag_ref, *refs,
):
    estimate_ref, window_ref, product_ref = refs[0], refs[-2], refs[-1]
    torso = estimate_ref.shape[0]
    diag = diag_ref[...]
    direction = direction_in[...]
    fill_window(chain, direction, first_ref[...], second_ref[...], window_ref)
    product(own_ref, other_ref, own_cols, other_cols, window_ref, product_ref)
    residual = residual_in[...] - (diag * direction + product_ref[...])
    direction = KEEP[1] * direction + PULL[1] * (residual / diag)
    estimate = estimate_in[...] + direction
    estimate_ref[...] = estimate
    if last:
        final_ref, residual_ref, packed_ref = refs[1:-2]
        final_ref[...] = estimate
        residual_ref[...] = residual
        packed_ref[0:torso] = estimate
        packed_ref[torso : 2 * torso] = direction


def last_residual(
    chain, own_cols, other_cols, own_ref, other_ref, first_ref, second_ref, packed_ref,
    residual_in, diag_ref, residual_ref, window_ref, product_ref,
):
    torso = residual_ref.shape[0]
    tail = slice(torso, 2 * torso)
    direction = packed_ref[tail]
    fill_window(chain, direction, first_ref[tail], second_ref[tail], window_ref)
    product(own_ref, other_ref, own_cols, other_cols, window_ref, product_ref)
    residual_ref[...] = residual_in[...] - (diag_ref[...] * direction + product_ref[...])


def on_device(states, send_node, send_count, recv_row, columns, tile_values, diagonal):
    chain = lax.axis_size("dom")
    peers, slots = send_node.shape[1:]
    node_count = states.shape[1]
    heart = node_count // LANES
    torso = diagonal.shape[0] // LANES

    def swap(value, partner):
        return lax.ppermute(value, "dom", [(i, partner(i) % chain) for i in range(chain)])

    def with_first(value):
        return swap(value, lambda i: i ^ 1)

    def with_second(value):
        return swap(value, lambda i: ((i + 1) ^ 1) - 1)

    def with_far(value):
        return swap(value, lambda i: i + chain // 2)

    def from_sibling(value):
        return lax.ppermute(value, "sub", [(0, 1), (1, 0)])

    def shape(*dims, dtype=F32):
        return jax.ShapeDtypeStruct(dims, dtype)

    dense = shape(states.shape[0], heart, LANES)
    field = shape(torso, LANES)
    packed = shape(2 * torso, LANES)
    table = shape(peers, slots, dtype=jnp.int32)
    work = (pltpu.VMEM((torso + 2 * HALO, LANES), F32), pltpu.VMEM((torso, LANES), F32))

    rows = [with_first(recv_row), with_second(recv_row), with_far(recv_row)]
    other_tiles = from_sibling(tile_values)
    live = jnp.arange(slots, dtype=jnp.int32)[None, :] < send_count[0][:, None]
    nodes = jnp.where(live, send_node[0], -1)
    row = shape(1, slots, dtype=jnp.int32)
    states, outgoing, own_rows = call(begin, (dense, shape(peers, slots), row))(
        in_specs=[VMEM] * 3
    )(states, nodes, recv_row)
    maps, own, *shares = call(first_shares, (table,) + (field,) * 4)(in_specs=[VMEM] * 6)(
        outgoing, nodes, own_rows, *rows
    )
    columns, diag, own = call(bring, (shape(*columns.shape[::-1], dtype=jnp.int32), field, field))(
        in_specs=[VMEM] * 4
    )(tile_values, columns.T, diagonal.reshape(torso, LANES), own)
    stored = (columns, from_sibling(columns), tile_values, other_tiles)
    for time_step in range(2):
        last = time_step == 1
        first, second, far = shares
        forcing = TORSO_COUPLING * (own + with_first(first) + with_second(second) + with_far(far))
        direction = forcing / (CHEB_THETA * diag)
        mine = jnp.concatenate([forcing, with_first(direction), with_second(direction)])
        residual, direction, estimate = call(
            functools.partial(sweep_one, chain), (field,) * 3, work
        )(in_specs=[SMEM] * 2 + [VMEM] * 5)(*stored, mine, from_sibling(mine), diag)
        estimate, *rest = call(
            functools.partial(sweep_two, chain, last),
            (field,) * 3 + (packed,) if last else (field,),
            work,
        )(in_specs=[SMEM] * 2 + [VMEM] * 8)(
            *stored, with_first(direction), with_second(direction), direction, residual, estimate,
            diag,
        )
        if not last:
            states, own, *shares = call(next_shares, (dense,) + (field,) * 4)(
                in_specs=[VMEM] * 7
            )(
                states, estimate, with_first(estimate), with_second(estimate), with_far(estimate),
                nodes, maps,
            )
    potential, residual, both = rest
    first, second = with_first(both), with_second(both)
    residual = call(functools.partial(last_residual, chain), field, work)(
        in_specs=[SMEM] * 2 + [VMEM] * 7
    )(*stored, first, second, both, residual, diag)
    new_states = call(
        last_feedback, shape(*dense.shape[:1], node_count), (pltpu.VMEM(dense.shape, F32),)
    )(in_specs=[VMEM] * 7)(states, estimate, first, second, with_far(estimate), nodes, maps)
    return new_states, potential.reshape(-1), residual.reshape(-1)


def solution(mesh):
    placed = (
        P(None, ("case", "dom", "sub")),
        P(("case", "dom", "sub"), None, None),
        P(("case", "dom", "sub"), None),
        P(("case", "dom", "sub"), None, None),
        P(("case", "dom"), "sub"),
        P(("case", "dom"), "sub", None, None),
        P(("case", "dom")),
    )
    return jax.shard_map(
        on_device,
        mesh=mesh,
        in_specs=placed,
        out_specs=(P(None, ("case", "dom", "sub")), P(("case", "dom")), P(("case", "dom"))),
        check_vma=False,
    )
```

time: 84.7 us -> 76.7 us (0.906)
  blocking collectives: 25.4 us -> 0 us
  waiting for transfers between devices: 19.1 us -> 32.2 us
  starting transfers between devices: 17.6 us -> 29 us
  local copies, waits for them, and re-layouts: 11.3 us -> 4.58 us
  Pallas kernels: 10.1 us -> 8.98 us
    all_to_all x2 -> x0, blocking collectives: 25.4 us -> none  [on_device(): lax.all_to_all(parts, 'dom', split_axis=0, concat_axis=0, tiled=True)]
    ppermute x13 -> x23, waiting for transfers between devices: 16 us -> 30.2 us  [swap(): lax.ppermute(value, 'dom', [(i, partner(i) % chain) for i in range(chain)])]
    ppermute x13 -> x23, starting transfers between devices: 17 us -> 28 us  [swap(): lax.ppermute(value, 'dom', [(i, partner(i) % chain) for i in range(chain)])]
    unnamed x20 -> x12, local copies, waits for them, and re-layouts: 10.5 us -> 4.58 us
    ppermute x4, waiting for transfers between devices: 3.09 us -> 2 us  [from_sibling(): return lax.ppermute(value, 'sub', [(0, 1), (1, 0)])]
    pallas_call x5 -> x6, Pallas kernels: 5.03 us -> 4.15 us  [the longest x2 2.69 us: on_device(): call(functools.partial(sweep_two, chain, last), (field,) * 3 + (packed,)...]
  transfers between devices with their start and end apart: 17 -> 27, of which waited for: 10 -> 15; matrix products, arithmetic and copies ran while one was open for 1% -> 1% of each run, Pallas kernels for 3% -> 3%
where the time goes in v4:
time: 76.7 us; the launch traced here: 76.3 us
  waiting for transfers between devices  32.2 us (42%)
  starting transfers between devices  29 us (38%)
  Pallas kernels  8.98 us (12%)
  local copies, waits for them, and re-layouts  4.58 us (6%)
  other arithmetic  0.79 us (1%)
    ppermute x23, waiting for transfers between devices, swap(): lax.ppermute(value, 'dom', [(i, partner(i) % chain) for i in range(chain)])  30.2 us
    ppermute x23, starting transfers between devices, swap(): lax.ppermute(value, 'dom', [(i, partner(i) % chain) for i in range(chain)])  28 us
    unnamed x12, local copies, waits for them, and re-layouts  4.58 us
    pallas_call x2, Pallas kernels, on_device(): call(functools.partial(sweep_two, chain, last), (field,) * 3 + (packed,)...  2.69 us
    pallas_call x2, Pallas kernels, on_device(): call(functools.partial(sweep_one, chain), (field,) * 3, work)  2.08 us
    ppermute x4, waiting for transfers between devices, from_sibling(): return lax.ppermute(value, 'sub', [(0, 1), (1, 0)])  2 us
    pallas_call x1, Pallas kernels, on_device(): call(functools.partial(last_residual, chain), field, work)  1.65 us
  transfers between devices with their start and end apart: 27, of which 15 were waited for; matrix products, arithmetic and copies ran while one was open for 1% of the time, Pallas kernels for 3%

profile of v4, /device:TPU:0, one launch (start us, length us, event | category | flops | bytes accessed | tf_op | source)
XLA Modules:
  0.0 76.3 jit_solution(9559504410347348180)
XLA Ops:
  1.1 2.6 %collective-permute-start = (s32[1,4,512]{2,1,0:T(4,128)}, s32[1,4,512]{2,1,0:T(4,128)S(1)}, u32[]{:S(2)}, u32[]{:S(2)}) collective-permute-start(s32[1,4,512]{2,1,0:T(4,128)} %rows_ref.1), channel_id=1, source_target_pairs={{0,2},{2,0},{4,6},{6,4},{8,10},{10,8},{12,14},{14,12},{1,3},{3,1},... | collective-permute-start | bytes 24584 | tf_op jit(solution)/shard_map/ppermute | solution.py:325
  3.7 2.6 %collective-permute-start.2 = (s32[1,4,512]{2,1,0:T(4,128)}, s32[1,4,512]{2,1,0:T(4,128)S(1)}, u32[]{:S(2)}, u32[]{:S(2)}) collective-permute-start(s32[1,4,512]{2,1,0:T(4,128)} %rows_ref.1), channel_id=1, source_target_pairs={{0,8},{2,10},{4,12},{6,14},{8,0},{10,2},{12,4},{14,6},{1,9},{3,11}... | collective-permute-start | bytes 24584 | tf_op jit(solution)/shard_map/ppermute | solution.py:325
  6.3 1.3 %collective-permute-start.1 = (s32[1,4,512]{2,1,0:T(4,128)}, s32[1,4,512]{2,1,0:T(4,128)S(1)}, u32[]{:S(2)}, u32[]{:S(2)}) collective-permute-start(s32[1,4,512]{2,1,0:T(4,128)} %rows_ref.1), channel_id=1, source_target_pairs={{0,14},{2,4},{4,2},{6,8},{8,6},{10,12},{12,10},{14,0},{1,15},{3,5}... | collective-permute-start | bytes 24584 | tf_op jit(solution)/shard_map/ppermute | solution.py:325
  10.3 2.5 %collective-permute-done.1.second_rows = s32[1,4,512]{2,1,0:T(4,128)S(1)} collective-permute-done((s32[1,4,512]{2,1,0:T(4,128)}, s32[1,4,512]{2,1,0:T(4,128)S(1)}, u32[]{:S(2)}, u32[]{:S(2)}) %collective-permute-start.1) | collective-permute-done | bytes 8224 | tf_op jit(solution)/shard_map/ppermute | solution.py:325
  13.2 1.4 %collective-permute-start.6 = (f32[8,128]{1,0:T(8,128)S(1)}, f32[8,128]{1,0:T(8,128)S(1)}, u32[]{:S(2)}, u32[]{:S(2)}) collective-permute-start(f32[8,128]{1,0:T(8,128)S(1)} %get-tuple-element.36), channel_id=1, source_target_pairs={{0,14},{2,4},{4,2},{6,8},{8,6},{10,12},{12,10},{14,0},{1,15},{3,5}... | collective-permute-start | bytes 12296 | tf_op jit(solution)/shard_map/ppermute | solution.py:325
  14.6 1.3 %collective-permute-start.7 = (f32[8,128]{1,0:T(8,128)S(1)}, f32[8,128]{1,0:T(8,128)S(1)}, u32[]{:S(2)}, u32[]{:S(2)}) collective-permute-start(f32[8,128]{1,0:T(8,128)S(1)} %get-tuple-element.37), channel_id=1, source_target_pairs={{0,8},{2,10},{4,12},{6,14},{8,0},{10,2},{12,4},{14,6},{1,9},{3,11}... | collective-permute-start | bytes 12296 | tf_op jit(solution)/shard_map/ppermute | solution.py:325
  15.9 1.6 %copy-done = f32[8,4,128,128]{3,2,1,0:T(8,128)S(1)} copy-done((f32[8,4,128,128]{3,2,1,0:T(8,128)S(1)}, f32[8,4,128,128]{3,2,1,0:T(8,128)}, u32[]{:S(2)}) %copy-start) | copy-done | bytes 2097176
  19.6 2.9 %collective-permute-start.9 = (f32[8,128]{1,0:T(8,128)S(1)}, f32[8,128]{1,0:T(8,128)S(1)}, u32[]{:S(2)}, u32[]{:S(2)}) collective-permute-start(f32[8,128]{1,0:T(8,128)S(1)} %get-tuple-element.57), channel_id=1, source_target_pairs={{0,14},{2,4},{4,2},{6,8},{8,6},{10,12},{12,10},{14,0},{1,15},{3,5}... | collective-permute-start | bytes 12296 | tf_op jit(solution)/shard_map/ppermute | solution.py:325
  22.7 3.3 %collective-permute-done.9 = f32[8,128]{1,0:T(8,128)S(1)} collective-permute-done((f32[8,128]{1,0:T(8,128)S(1)}, f32[8,128]{1,0:T(8,128)S(1)}, u32[]{:S(2)}, u32[]{:S(2)}) %collective-permute-start.9) | collective-permute-done | bytes 4128 | tf_op jit(solution)/shard_map/ppermute | solution.py:325
  28.5 2.8 %collective-permute-start.12 = (f32[8,128]{1,0:T(8,128)S(1)}, f32[8,128]{1,0:T(8,128)S(1)}, u32[]{:S(2)}, u32[]{:S(2)}) collective-permute-start(f32[8,128]{1,0:T(8,128)S(1)} %get-tuple-element.39.direction_in), channel_id=1, source_target_pairs={{0,14},{2,4},{4,2},{6,8},{8,6},{10,12},{12,10},{14,0},{1,15},{3,5}... | collective-permute-start | bytes 12296 | tf_op jit(solution)/shard_map/ppermute | solution.py:325
  31.3 3.6 %collective-permute-done.12.second_ref = f32[8,128]{1,0:T(8,128)S(1)} collective-permute-done((f32[8,128]{1,0:T(8,128)S(1)}, f32[8,128]{1,0:T(8,128)S(1)}, u32[]{:S(2)}, u32[]{:S(2)}) %collective-permute-start.12) | collective-permute-done | bytes 4128 | tf_op jit(solution)/shard_map/ppermute | solution.py:325
  36.0 2.7 %collective-permute-start.14 = (f32[8,128]{1,0:T(8,128)S(1)}, f32[8,128]{1,0:T(8,128)S(1)}, u32[]{:S(2)}, u32[]{:S(2)}) collective-permute-start(f32[8,128]{1,0:T(8,128)S(1)} %shard_map.98.own_estimate), channel_id=1, source_target_pairs={{0,14},{2,4},{4,2},{6,8},{8,6},{10,12},{12,10},{14,0},{1,15},{3,5}... | collective-permute-start | bytes 12296 | tf_op jit(solution)/shard_map/ppermute | solution.py:325
  38.8 1.8 %collective-permute-done.15.far_estimate = f32[8,128]{1,0:T(8,128)S(1)} collective-permute-done((f32[8,128]{1,0:T(8,128)S(1)}, f32[8,128]{1,0:T(8,128)S(1)}, u32[]{:S(2)}, u32[]{:S(2)}) %collective-permute-start.15) | collective-permute-done | bytes 4128 | tf_op jit(solution)/shard_map/ppermute | solution.py:325
  40.5 1.9 %collective-permute-done.14.second_estimate = f32[8,128]{1,0:T(8,128)S(1)} collective-permute-done((f32[8,128]{1,0:T(8,128)S(1)}, f32[8,128]{1,0:T(8,128)S(1)}, u32[]{:S(2)}, u32[]{:S(2)}) %collective-permute-start.14) | collective-permute-done | bytes 4128 | tf_op jit(solution)/shard_map/ppermute | solution.py:325
  43.4 2.7 %collective-permute-start.17 = (f32[8,128]{1,0:T(8,128)S(1)}, f32[8,128]{1,0:T(8,128)S(1)}, u32[]{:S(2)}, u32[]{:S(2)}) collective-permute-start(f32[8,128]{1,0:T(8,128)S(1)} %get-tuple-element.46), channel_id=1, source_target_pairs={{0,14},{2,4},{4,2},{6,8},{8,6},{10,12},{12,10},{14,0},{1,15},{3,5}... | collective-permute-start | bytes 12296 | tf_op jit(solution)/shard_map/ppermute | solution.py:325
  47.0 2.8 %collective-permute-done.17 = f32[8,128]{1,0:T(8,128)S(1)} collective-permute-done((f32[8,128]{1,0:T(8,128)S(1)}, f32[8,128]{1,0:T(8,128)S(1)}, u32[]{:S(2)}, u32[]{:S(2)}) %collective-permute-start.17) | collective-permute-done | bytes 4128 | tf_op jit(solution)/shard_map/ppermute | solution.py:325
  50.7 2.1 %collective-permute-start.20 = (f32[8,128]{1,0:T(8,128)S(1)}, f32[8,128]{1,0:T(8,128)S(1)}, u32[]{:S(2)}, u32[]{:S(2)}) collective-permute-start(f32[8,128]{1,0:T(8,128)S(1)} %get-tuple-element.55), channel_id=1, source_target_pairs={{0,14},{2,4},{4,2},{6,8},{8,6},{10,12},{12,10},{14,0},{1,15},{3,5}... | collective-permute-start | bytes 12296 | tf_op jit(solution)/shard_map/ppermute | solution.py:325
  52.9 4.1 %collective-permute-done.20 = f32[8,128]{1,0:T(8,128)S(1)} collective-permute-done((f32[8,128]{1,0:T(8,128)S(1)}, f32[8,128]{1,0:T(8,128)S(1)}, u32[]{:S(2)}, u32[]{:S(2)}) %collective-permute-start.20) | collective-permute-done | bytes 4128 | tf_op jit(solution)/shard_map/ppermute | solution.py:325
  59.2 2.1 %collective-permute-start.23 = (f32[8,128]{1,0:T(8,128)S(1)}, f32[8,128]{1,0:T(8,128)S(1)}, u32[]{:S(2)}, u32[]{:S(2)}) collective-permute-start(f32[8,128]{1,0:T(8,128)S(1)} %get-tuple-element.48.direction_in), channel_id=1, source_target_pairs={{0,14},{2,4},{4,2},{6,8},{8,6},{10,12},{12,10},{14,0},{1,15},{3,5}... | collective-permute-start | bytes 12296 | tf_op jit(solution)/shard_map/ppermute | solution.py:325
  61.3 4.2 %collective-permute-done.23.second_ref = f32[8,128]{1,0:T(8,128)S(1)} collective-permute-done((f32[8,128]{1,0:T(8,128)S(1)}, f32[8,128]{1,0:T(8,128)S(1)}, u32[]{:S(2)}, u32[]{:S(2)}) %collective-permute-start.23) | collective-permute-done | bytes 4128 | tf_op jit(solution)/shard_map/ppermute | solution.py:325
  65.6 1.7 %shard_map.101 = (f32[8,128]{1,0:T(8,128)S(1)}, f32[8,128]{1,0:T(8,128)}, f32[8,128]{1,0:T(8,128)S(1)}, f32[16,128]{1,0:T(8,128)S(1)}) custom-call(s32[4,8]{1,0:T(4,128)S(1)} %get-tuple-element.33.own_cols, s32[4,8]{1,0:T(4,128)S(1)} %collective-permute-done.3.other_cols, f32[8,4,128,128]{3,2,1,0:T(8,128)S(1)} %copy-done.1, ...), custom_call_target="tpu_custom_call" | custom-call | flops 4000000 | bytes 262144 | tf_op jit(solution)/shard_map/pallas_call | solution.py:372
  67.2 2.1 %collective-permute-start.25 = (f32[16,128]{1,0:T(8,128)S(1)}, f32[16,128]{1,0:T(8,128)S(1)}, u32[]{:S(2)}, u32[]{:S(2)}) collective-permute-start(f32[16,128]{1,0:T(8,128)S(1)} %get-tuple-element.52.packed_ref), channel_id=1, source_target_pairs={{0,14},{2,4},{4,2},{6,8},{8,6},{10,12},{12,10},{14,0},{1,15},{3,5}... | collective-permute-start | bytes 24584 | tf_op jit(solution)/shard_map/ppermute | solution.py:325
  69.8 3.8 %collective-permute-done.25.second_estimate.second_ref = f32[16,128]{1,0:T(8,128)S(1)} collective-permute-done((f32[16,128]{1,0:T(8,128)S(1)}, f32[16,128]{1,0:T(8,128)S(1)}, u32[]{:S(2)}, u32[]{:S(2)}) %collective-permute-start.25) | collective-permute-done | bytes 8224 | tf_op jit(solution)/shard_map/ppermute | solution.py:325
  73.6 1.6 %shard_map.103 = f32[8,128]{1,0:T(8,128)} custom-call(s32[4,8]{1,0:T(4,128)S(1)} %get-tuple-element.33.own_cols, s32[4,8]{1,0:T(4,128)S(1)} %collective-permute-done.3.other_cols, f32[8,4,128,128]{3,2,1,0:T(8,128)S(1)} %copy-done.1, f32[8,4,128,128]{3,2,1,0:T(8,128)S(1)} %collective-permute-done.4.other_ref, ...), custom_call_target="tpu_custom_call" | custom-call | flops 4000000 | bytes 262144 | tf_op jit(solution)/shard_map/pallas_call | solution.py:389
  (57 shorter events, 16.2 us)
Async XLA Ops:
  0.6 26.8 %collective-permute-start.4 = (f32[8,4,128,128]{3,2,1,0:T(8,128)}, f32[8,4,128,128]{3,2,1,0:T(8,128)S(1)}, u32[]{:S(2)}, u32[]{:S(2)}) collective-permute-start(f32[8,4,128,128]{3,2,1,0:T(8,128)} %own_ref.9), channel_id=1, source_target_pairs={{0,1},{1,0},{2,3},{3,2},{4,5},{5,4},{6,7},{7,6},{8,9},{9,8},{10,11... | collective-permute-start | bytes 6291464 | tf_op jit(solution)/shard_map/ppermute | solution.py:337
  1.1 9.2 %collective-permute-start = (s32[1,4,512]{2,1,0:T(4,128)}, s32[1,4,512]{2,1,0:T(4,128)S(1)}, u32[]{:S(2)}, u32[]{:S(2)}) collective-permute-start(s32[1,4,512]{2,1,0:T(4,128)} %rows_ref.1), channel_id=1, source_target_pairs={{0,2},{2,0},{4,6},{6,4},{8,10},{10,8},{12,14},{14,12},{1,3},{3,1},... | collective-permute-start | bytes 24584 | tf_op jit(solution)/shard_map/ppermute | solution.py:325
  3.7 6.6 %collective-permute-start.2 = (s32[1,4,512]{2,1,0:T(4,128)}, s32[1,4,512]{2,1,0:T(4,128)S(1)}, u32[]{:S(2)}, u32[]{:S(2)}) collective-permute-start(s32[1,4,512]{2,1,0:T(4,128)} %rows_ref.1), channel_id=1, source_target_pairs={{0,8},{2,10},{4,12},{6,14},{8,0},{10,2},{12,4},{14,6},{1,9},{3,11}... | collective-permute-start | bytes 24584 | tf_op jit(solution)/shard_map/ppermute | solution.py:325
  6.3 6.6 %collective-permute-start.1 = (s32[1,4,512]{2,1,0:T(4,128)}, s32[1,4,512]{2,1,0:T(4,128)S(1)}, u32[]{:S(2)}, u32[]{:S(2)}) collective-permute-start(s32[1,4,512]{2,1,0:T(4,128)} %rows_ref.1), channel_id=1, source_target_pairs={{0,14},{2,4},{4,2},{6,8},{8,6},{10,12},{12,10},{14,0},{1,15},{3,5}... | collective-permute-start | bytes 24584 | tf_op jit(solution)/shard_map/ppermute | solution.py:325
  13.1 5.7 %collective-permute-start.5 = (f32[8,128]{1,0:T(8,128)S(1)}, f32[8,128]{1,0:T(8,128)S(1)}, u32[]{:S(2)}, u32[]{:S(2)}) collective-permute-start(f32[8,128]{1,0:T(8,128)S(1)} %get-tuple-element.35), channel_id=1, source_target_pairs={{0,2},{2,0},{4,6},{6,4},{8,10},{10,8},{12,14},{14,12},{1,3},{3,1},... | collective-permute-start | bytes 12296 | tf_op jit(solution)/shard_map/ppermute | solution.py:325
  13.2 6.4 %collective-permute-start.6 = (f32[8,128]{1,0:T(8,128)S(1)}, f32[8,128]{1,0:T(8,128)S(1)}, u32[]{:S(2)}, u32[]{:S(2)}) collective-permute-start(f32[8,128]{1,0:T(8,128)S(1)} %get-tuple-element.36), channel_id=1, source_target_pairs={{0,14},{2,4},{4,2},{6,8},{8,6},{10,12},{12,10},{14,0},{1,15},{3,5}... | collective-permute-start | bytes 12296 | tf_op jit(solution)/shard_map/ppermute | solution.py:325
  14.6 5.0 %collective-permute-start.7 = (f32[8,128]{1,0:T(8,128)S(1)}, f32[8,128]{1,0:T(8,128)S(1)}, u32[]{:S(2)}, u32[]{:S(2)}) collective-permute-start(f32[8,128]{1,0:T(8,128)S(1)} %get-tuple-element.37), channel_id=1, source_target_pairs={{0,8},{2,10},{4,12},{6,14},{8,0},{10,2},{12,4},{14,6},{1,9},{3,11}... | collective-permute-start | bytes 12296 | tf_op jit(solution)/shard_map/ppermute | solution.py:325
  19.6 6.4 %collective-permute-start.9 = (f32[8,128]{1,0:T(8,128)S(1)}, f32[8,128]{1,0:T(8,128)S(1)}, u32[]{:S(2)}, u32[]{:S(2)}) collective-permute-start(f32[8,128]{1,0:T(8,128)S(1)} %get-tuple-element.57), channel_id=1, source_target_pairs={{0,14},{2,4},{4,2},{6,8},{8,6},{10,12},{12,10},{14,0},{1,15},{3,5}... | collective-permute-start | bytes 12296 | tf_op jit(solution)/shard_map/ppermute | solution.py:325
  22.5 3.6 %collective-permute-start.8 = (f32[8,128]{1,0:T(8,128)S(1)}, f32[8,128]{1,0:T(8,128)S(1)}, u32[]{:S(2)}, u32[]{:S(2)}) collective-permute-start(f32[8,128]{1,0:T(8,128)S(1)} %get-tuple-element.57), channel_id=1, source_target_pairs={{0,2},{2,0},{4,6},{6,4},{8,10},{10,8},{12,14},{14,12},{1,3},{3,1},... | collective-permute-start | bytes 12296 | tf_op jit(solution)/shard_map/ppermute | solution.py:325
  28.5 6.4 %collective-permute-start.12 = (f32[8,128]{1,0:T(8,128)S(1)}, f32[8,128]{1,0:T(8,128)S(1)}, u32[]{:S(2)}, u32[]{:S(2)}) collective-permute-start(f32[8,128]{1,0:T(8,128)S(1)} %get-tuple-element.39.direction_in), channel_id=1, source_target_pairs={{0,14},{2,4},{4,2},{6,8},{8,6},{10,12},{12,10},{14,0},{1,15},{3,5}... | collective-permute-start | bytes 12296 | tf_op jit(solution)/shard_map/ppermute | solution.py:325
  31.3 3.7 %collective-permute-start.11 = (f32[8,128]{1,0:T(8,128)S(1)}, f32[8,128]{1,0:T(8,128)S(1)}, u32[]{:S(2)}, u32[]{:S(2)}) collective-permute-start(f32[8,128]{1,0:T(8,128)S(1)} %get-tuple-element.39.direction_in), channel_id=1, source_target_pairs={{0,2},{2,0},{4,6},{6,4},{8,10},{10,8},{12,14},{14,12},{1,3},{3,1},... | collective-permute-start | bytes 12296 | tf_op jit(solution)/shard_map/ppermute | solution.py:325
  36.0 4.6 %collective-permute-start.15 = (f32[8,128]{1,0:T(8,128)S(1)}, f32[8,128]{1,0:T(8,128)S(1)}, u32[]{:S(2)}, u32[]{:S(2)}) collective-permute-start(f32[8,128]{1,0:T(8,128)S(1)} %shard_map.98.own_estimate), channel_id=1, source_target_pairs={{0,8},{2,10},{4,12},{6,14},{8,0},{10,2},{12,4},{14,6},{1,9},{3,11}... | collective-permute-start | bytes 12296 | tf_op jit(solution)/shard_map/ppermute | solution.py:325
  36.0 6.4 %collective-permute-start.14 = (f32[8,128]{1,0:T(8,128)S(1)}, f32[8,128]{1,0:T(8,128)S(1)}, u32[]{:S(2)}, u32[]{:S(2)}) collective-permute-start(f32[8,128]{1,0:T(8,128)S(1)} %shard_map.98.own_estimate), channel_id=1, source_target_pairs={{0,14},{2,4},{4,2},{6,8},{8,6},{10,12},{12,10},{14,0},{1,15},{3,5}... | collective-permute-start | bytes 12296 | tf_op jit(solution)/shard_map/ppermute | solution.py:325
  38.7 3.7 %collective-permute-start.13 = (f32[8,128]{1,0:T(8,128)S(1)}, f32[8,128]{1,0:T(8,128)S(1)}, u32[]{:S(2)}, u32[]{:S(2)}) collective-permute-start(f32[8,128]{1,0:T(8,128)S(1)} %shard_map.98.own_estimate), channel_id=1, source_target_pairs={{0,2},{2,0},{4,6},{6,4},{8,10},{10,8},{12,14},{14,12},{1,3},{3,1},... | collective-permute-start | bytes 12296 | tf_op jit(solution)/shard_map/ppermute | solution.py:325
  43.3 3.7 %collective-permute-start.16 = (f32[8,128]{1,0:T(8,128)S(1)}, f32[8,128]{1,0:T(8,128)S(1)}, u32[]{:S(2)}, u32[]{:S(2)}) collective-permute-start(f32[8,128]{1,0:T(8,128)S(1)} %get-tuple-element.45), channel_id=1, source_target_pairs={{0,2},{2,0},{4,6},{6,4},{8,10},{10,8},{12,14},{14,12},{1,3},{3,1},... | collective-permute-start | bytes 12296 | tf_op jit(solution)/shard_map/ppermute | solution.py:325
  43.4 6.4 %collective-permute-start.17 = (f32[8,128]{1,0:T(8,128)S(1)}, f32[8,128]{1,0:T(8,128)S(1)}, u32[]{:S(2)}, u32[]{:S(2)}) collective-permute-start(f32[8,128]{1,0:T(8,128)S(1)} %get-tuple-element.46), channel_id=1, source_target_pairs={{0,14},{2,4},{4,2},{6,8},{8,6},{10,12},{12,10},{14,0},{1,15},{3,5}... | collective-permute-start | bytes 12296 | tf_op jit(solution)/shard_map/ppermute | solution.py:325
  46.1 4.5 %collective-permute-start.18 = (f32[8,128]{1,0:T(8,128)S(1)}, f32[8,128]{1,0:T(8,128)S(1)}, u32[]{:S(2)}, u32[]{:S(2)}) collective-permute-start(f32[8,128]{1,0:T(8,128)S(1)} %get-tuple-element.47), channel_id=1, source_target_pairs={{0,8},{2,10},{4,12},{6,14},{8,0},{10,2},{12,4},{14,6},{1,9},{3,11}... | collective-permute-start | bytes 12296 | tf_op jit(solution)/shard_map/ppermute | solution.py:325
  50.7 6.3 %collective-permute-start.20 = (f32[8,128]{1,0:T(8,128)S(1)}, f32[8,128]{1,0:T(8,128)S(1)}, u32[]{:S(2)}, u32[]{:S(2)}) collective-permute-start(f32[8,128]{1,0:T(8,128)S(1)} %get-tuple-element.55), channel_id=1, source_target_pairs={{0,14},{2,4},{4,2},{6,8},{8,6},{10,12},{12,10},{14,0},{1,15},{3,5}... | collective-permute-start | bytes 12296 | tf_op jit(solution)/shard_map/ppermute | solution.py:325
  52.7 4.2 %collective-permute-start.19 = (f32[8,128]{1,0:T(8,128)S(1)}, f32[8,128]{1,0:T(8,128)S(1)}, u32[]{:S(2)}, u32[]{:S(2)}) collective-permute-start(f32[8,128]{1,0:T(8,128)S(1)} %get-tuple-element.55), channel_id=1, source_target_pairs={{0,2},{2,0},{4,6},{6,4},{8,10},{10,8},{12,14},{14,12},{1,3},{3,1},... | collective-permute-start | bytes 12296 | tf_op jit(solution)/shard_map/ppermute | solution.py:325
  59.2 6.4 %collective-permute-start.23 = (f32[8,128]{1,0:T(8,128)S(1)}, f32[8,128]{1,0:T(8,128)S(1)}, u32[]{:S(2)}, u32[]{:S(2)}) collective-permute-start(f32[8,128]{1,0:T(8,128)S(1)} %get-tuple-element.48.direction_in), channel_id=1, source_target_pairs={{0,14},{2,4},{4,2},{6,8},{8,6},{10,12},{12,10},{14,0},{1,15},{3,5}... | collective-permute-start | bytes 12296 | tf_op jit(solution)/shard_map/ppermute | solution.py:325
  61.3 4.2 %collective-permute-start.22 = (f32[8,128]{1,0:T(8,128)S(1)}, f32[8,128]{1,0:T(8,128)S(1)}, u32[]{:S(2)}, u32[]{:S(2)}) collective-permute-start(f32[8,128]{1,0:T(8,128)S(1)} %get-tuple-element.48.direction_in), channel_id=1, source_target_pairs={{0,2},{2,0},{4,6},{6,4},{8,10},{10,8},{12,14},{14,12},{1,3},{3,1},... | collective-permute-start | bytes 12296 | tf_op jit(solution)/shard_map/ppermute | solution.py:325
  67.2 6.3 %collective-permute-start.25 = (f32[16,128]{1,0:T(8,128)S(1)}, f32[16,128]{1,0:T(8,128)S(1)}, u32[]{:S(2)}, u32[]{:S(2)}) collective-permute-start(f32[16,128]{1,0:T(8,128)S(1)} %get-tuple-element.52.packed_ref), channel_id=1, source_target_pairs={{0,14},{2,4},{4,2},{6,8},{8,6},{10,12},{12,10},{14,0},{1,15},{3,5}... | collective-permute-start | bytes 24584 | tf_op jit(solution)/shard_map/ppermute | solution.py:325
  69.3 4.3 %collective-permute-start.24 = (f32[16,128]{1,0:T(8,128)S(1)}, f32[16,128]{1,0:T(8,128)S(1)}, u32[]{:S(2)}, u32[]{:S(2)}) collective-permute-start(f32[16,128]{1,0:T(8,128)S(1)} %get-tuple-element.52.packed_ref), channel_id=1, source_target_pairs={{0,2},{2,0},{4,6},{6,4},{8,10},{10,8},{12,14},{14,12},{1,3},{3,1},... | collective-permute-start | bytes 24584 | tf_op jit(solution)/shard_map/ppermute | solution.py:325
  69.3 5.9 %collective-permute-start.26 = (f32[8,128]{1,0:T(8,128)S(1)}, f32[8,128]{1,0:T(8,128)S(1)}, u32[]{:S(2)}, u32[]{:S(2)}) collective-permute-start(f32[8,128]{1,0:T(8,128)S(1)} %get-tuple-element.51.own_estimate), channel_id=1, source_target_pairs={{0,8},{2,10},{4,12},{6,14},{8,0},{10,2},{12,4},{14,6},{1,9},{3,11}... | collective-permute-start | bytes 12296 | tf_op jit(solution)/shard_map/ppermute | solution.py:325
  (9 other events, 17.0 us)

commit v5 on v4

--- a/solution.py
+++ b/solution.py
@@ -192,39 +192,49 @@
     return copies
 
 
-def begin(states_ref, nodes_ref, rows_ref, out_ref, outgoing_ref, own_rows):
-    own_rows[...] = rows_ref[0, 0:1]
+def begin(states_ref, table_ref, out_ref, payload_ref):
+    peers = table_ref.shape[0] // 2
     for k in range(out_ref.shape[1]):
         out_ref[:, k, :] = states_ref[:, k * LANES : (k + 1) * LANES]
     rows, current = ionic_rows([out_ref[i] for i in range(out_ref.shape[0])])
     for i, row in enumerate(rows):
         out_ref[i] = row
-    outgoing_ref[...] = pick_current(current, nodes_ref[...])
-
-
-def bring(tiles_ref, cols_ref, diag_ref, own_ref, cols_out, diag_out, own_out):
+    payload_ref[0:peers] = pick_current(current, table_ref[0:peers])
+    payload_ref[peers:] = table_ref[peers:].astype(F32)
+
+
+def bring(tiles_ref, cols_ref, diag_ref, payload_ref, cols_out, diag_out, payload_out):
     cols_out[...] = cols_ref[...]
     diag_out[...] = diag_ref[...]
-    own_out[...] = own_ref[...]
+    payload_out[...] = payload_ref[...]
     del tiles_ref
 
 
-def first_shares(
-    outgoing_ref, nodes_ref, own_rows, first_rows, second_rows, far_rows,
-    maps_ref, own_ref, first_ref, second_ref, far_ref,
+def first_forcing(
+    table_ref, own_ref, first_ref, second_ref, far_ref, diag_ref,
+    maps_ref, forcing_ref, direction_ref,
 ):
-    after, before = by_side(first_rows[0], second_rows[0])
-    rows = jnp.concatenate([own_rows[...], after[1:2], before[2:3], far_rows[0, 3:4]], axis=0)
-    maps = jnp.where(nodes_ref[...] < 0, -1, rows)
-    maps_ref[...] = maps
-    spread_current(outgoing_ref[...], maps, own_ref, first_ref, second_ref, far_ref)
+    peers = table_ref.shape[0] // 2
+    after, before = by_side(first_ref[...], second_ref[...])
+    come = [own_ref[0:1], before[1:2], after[2:3], far_ref[3:4]]
+    rows = [own_ref[peers : peers + 1], after[peers + 1 : peers + 2]]
+    rows += [before[peers + 2 : peers + 3], far_ref[peers + 3 : peers + 4]]
+    nodes = table_ref[0:peers]
+    maps_ref[...] = jnp.where(nodes < 0, -1, jnp.concatenate(rows, axis=0).astype(jnp.int32))
+    total = None
+    for o in range(peers):
+        part = scatter(come[o], table_ref[peers + o : peers + o + 1], forcing_ref.shape[0])
+        total = part if total is None else total + part
+    forcing = TORSO_COUPLING * total
+    forcing_ref[...] = forcing
+    direction_ref[...] = forcing / (CHEB_THETA * diag_ref[...])
 
 
 def next_shares(
-    states_ref, own_estimate, first_estimate, second_estimate, far_estimate, nodes_ref, maps_ref,
+    states_ref, own_estimate, first_estimate, second_estimate, far_estimate, table_ref, maps_ref,
     out_ref, own_ref, first_ref, second_ref, far_ref,
 ):
-    nodes, maps = nodes_ref[...], maps_ref[...]
+    nodes, maps = table_ref[0 : table_ref.shape[0] // 2], maps_ref[...]
     after, before = by_side(first_estimate[...], second_estimate[...])
     estimates = [own_estimate[...], after, before, far_estimate[...]]
     feedback = feedback_of(estimates, nodes, maps, states_ref.shape[1])
@@ -235,21 +245,6 @@
         out_ref[i] = row
     outgoing = pick_current(current, nodes)
     spread_current(outgoing, maps, own_ref, first_ref, second_ref, far_ref)
-
-
-def last_feedback(
-    states_ref, own_estimate, first_estimate, second_estimate, far_estimate, nodes_ref, maps_ref,
-    out_ref, dense_ref,
-):
-    nodes, maps = nodes_ref[...], maps_ref[...]
-    torso = own_estimate.shape[0]
-    after, before = by_side(first_estimate[0:torso], second_estimate[0:torso])
-    estimates = [own_estimate[...], after, before, far_estimate[...]]
-    feedback = feedback_of(estimates, nodes, maps, states_ref.shape[1])
-    dense_ref[...] = states_ref[...]
-    dense_ref[0] = states_ref[0] + TIME_STEP * FEEDBACK_RATE * feedback
-    for k in range(states_ref.shape[1]):
-        out_ref[:, k * LANES : (k + 1) * LANES] = dense_ref[:, k, :]
 
 
 def fill_window(chain, direction, first, second, window_ref):
@@ -295,20 +290,31 @@
     estimate = estimate_in[...] + direction
     estimate_ref[...] = estimate
     if last:
-        final_ref, residual_ref, packed_ref = refs[1:-2]
-        final_ref[...] = estimate
+        residual_ref, packed_ref = refs[1:-2]
         residual_ref[...] = residual
         packed_ref[0:torso] = estimate
         packed_ref[torso : 2 * torso] = direction
 
 
-def last_residual(
-    chain, own_cols, other_cols, own_ref, other_ref, first_ref, second_ref, packed_ref,
-    residual_in, diag_ref, residual_ref, window_ref, product_ref,
+def finish(
+    chain, own_cols, other_cols, own_ref, other_ref, first_ref, second_ref, packed_ref, far_ref,
+    residual_in, diag_ref, states_ref, table_ref, maps_ref,
+    out_ref, potential_ref, residual_ref, window_ref, product_ref, dense_ref,
 ):
     torso = residual_ref.shape[0]
-    tail = slice(torso, 2 * torso)
-    direction = packed_ref[tail]
+    peers = maps_ref.shape[0]
+    head, tail = slice(0, torso), slice(torso, 2 * torso)
+    estimate, direction = packed_ref[head], packed_ref[tail]
+    potential_ref[...] = estimate
+    after, before = by_side(first_ref[head], second_ref[head])
+    feedback = feedback_of(
+        [estimate, after, before, far_ref[...]], table_ref[0:peers], maps_ref[...],
+        states_ref.shape[1],
+    )
+    dense_ref[...] = states_ref[...]
+    dense_ref[0] = states_ref[0] + TIME_STEP * FEEDBACK_RATE * feedback
+    for k in range(states_ref.shape[1]):
+        out_ref[:, k * LANES : (k + 1) * LANES] = dense_ref[:, k, :]
     fill_window(chain, direction, first_ref[tail], second_ref[tail], window_ref)
     product(own_ref, other_ref, own_cols, other_cols, window_ref, product_ref)
     residual_ref[...] = residual_in[...] - (diag_ref[...] * direction + product_ref[...])
@@ -330,6 +336,10 @@
     def with_second(value):
         return swap(value, lambda i: ((i + 1) ^ 1) - 1)
 
+    def with_inner(value):
+        ends = (0, chain - 1)
+        return swap(value, lambda i: i if i in ends else ((i + 1) ^ 1) - 1)
+
     def with_far(value):
         return swap(value, lambda i: i + chain // 2)
 
@@ -342,56 +352,56 @@
     dense = shape(states.shape[0], heart, LANES)
     field = shape(torso, LANES)
     packed = shape(2 * torso, LANES)
-    table = shape(peers, slots, dtype=jnp.int32)
     work = (pltpu.VMEM((torso + 2 * HALO, LANES), F32), pltpu.VMEM((torso, LANES), F32))
 
-    rows = [with_first(recv_row), with_second(recv_row), with_far(recv_row)]
     other_tiles = from_sibling(tile_values)
     live = jnp.arange(slots, dtype=jnp.int32)[None, :] < send_count[0][:, None]
-    nodes = jnp.where(live, send_node[0], -1)
-    row = shape(1, slots, dtype=jnp.int32)
-    states, outgoing, own_rows = call(begin, (dense, shape(peers, slots), row))(
-        in_specs=[VMEM] * 3
-    )(states, nodes, recv_row)
-    maps, own, *shares = call(first_shares, (table,) + (field,) * 4)(in_specs=[VMEM] * 6)(
-        outgoing, nodes, own_rows, *rows
-    )
-    columns, diag, own = call(bring, (shape(*columns.shape[::-1], dtype=jnp.int32), field, field))(
-        in_specs=[VMEM] * 4
-    )(tile_values, columns.T, diagonal.reshape(torso, LANES), own)
+    table = jnp.concatenate([jnp.where(live, send_node[0], -1), recv_row[0]])
+    states, payload = call(begin, (dense, shape(2 * peers, slots)))(in_specs=[VMEM] * 2)(
+        states, table
+    )
+    columns, diag, own = call(
+        bring, (shape(*columns.shape[::-1], dtype=jnp.int32), field, shape(2 * peers, slots))
+    )(in_specs=[VMEM] * 4)(tile_values, columns.T, diagonal.reshape(torso, LANES), payload)
     stored = (columns, from_sibling(columns), tile_values, other_tiles)
+    maps, forcing, direction = call(
+        first_forcing, (shape(peers, slots, dtype=jnp.int32), field, field)
+    )(in_specs=[VMEM] * 6)(
+        table, own, with_first(payload), with_second(payload), with_far(payload), diag
+    )
     for time_step in range(2):
         last = time_step == 1
-        first, second, far = shares
-        forcing = TORSO_COUPLING * (own + with_first(first) + with_second(second) + with_far(far))
-        direction = forcing / (CHEB_THETA * diag)
-        mine = jnp.concatenate([forcing, with_first(direction), with_second(direction)])
+        mine = jnp.concatenate([forcing, with_first(direction), with_inner(direction)])
         residual, direction, estimate = call(
             functools.partial(sweep_one, chain), (field,) * 3, work
         )(in_specs=[SMEM] * 2 + [VMEM] * 5)(*stored, mine, from_sibling(mine), diag)
         estimate, *rest = call(
             functools.partial(sweep_two, chain, last),
-            (field,) * 3 + (packed,) if last else (field,),
+            (field,) * 2 + (packed,) if last else (field,),
             work,
         )(in_specs=[SMEM] * 2 + [VMEM] * 8)(
-            *stored, with_first(direction), with_second(direction), direction, residual, estimate,
+            *stored, with_first(direction), with_inner(direction), direction, residual, estimate,
             diag,
         )
         if not last:
-            states, own, *shares = call(next_shares, (dense,) + (field,) * 4)(
+            states, own, first, second, far = call(next_shares, (dense,) + (field,) * 4)(
                 in_specs=[VMEM] * 7
             )(
                 states, estimate, with_first(estimate), with_second(estimate), with_far(estimate),
-                nodes, maps,
+                table, maps,
             )
-    potential, residual, both = rest
-    first, second = with_first(both), with_second(both)
-    residual = call(functools.partial(last_residual, chain), field, work)(
-        in_specs=[SMEM] * 2 + [VMEM] * 7
-    )(*stored, first, second, both, residual, diag)
-    new_states = call(
-        last_feedback, shape(*dense.shape[:1], node_count), (pltpu.VMEM(dense.shape, F32),)
-    )(in_specs=[VMEM] * 7)(states, estimate, first, second, with_far(estimate), nodes, maps)
+            forcing = own + with_first(first) + with_second(second) + with_far(far)
+            forcing = TORSO_COUPLING * forcing
+            direction = forcing / (CHEB_THETA * diag)
+    residual, both = rest
+    new_states, potential, residual = call(
+        functools.partial(finish, chain),
+        (shape(*dense.shape[:1], node_count), field, field),
+        work + (pltpu.VMEM(dense.shape, F32),),
+    )(in_specs=[SMEM] * 2 + [VMEM] * 11)(
+        *stored, with_first(both), with_second(both), both, with_far(estimate), residual, diag,
+        states, table, maps,
+    )
     return new_states, potential.reshape(-1), residual.reshape(-1)
 
 

time: 76.7 us -> 74.3 us (0.969)
  waiting for transfers between devices: 32.2 us -> 19.9 us
  starting transfers between devices: 29 us -> 40.2 us
  Pallas kernels: 8.98 us -> 7.76 us
    ppermute x23 -> x20, waiting for transfers between devices: 30.2 us -> 17.9 us  [swap(): lax.ppermute(value, 'dom', [(i, partner(i) % chain) for i in range(chain)])]
    ppermute x23 -> x20, starting transfers between devices: 28 us -> 39.1 us  [swap(): lax.ppermute(value, 'dom', [(i, partner(i) % chain) for i in range(chain)])]
    pallas_call x7 -> x6, Pallas kernels: 5.96 us -> 4.68 us  [the longest x2 2.14 us: on_device(): call(functools.partial(sweep_two, chain, last), (field,) * 2 + (packed,)...]
  transfers between devices with their start and end apart: 27 -> 24, of which waited for: 15 -> 12; matrix products, arithmetic and copies ran while one was open for 1% -> 2% of each run, Pallas kernels for 3% -> 1%
where the time goes in v5:
time: 74.3 us; the launch traced here: 73.9 us
  starting transfers between devices  40.2 us (54%)
  waiting for transfers between devices  19.9 us (27%)
  Pallas kernels  7.76 us (10%)
  local copies, waits for them, and re-layouts  3.89 us (5%)
  other arithmetic  1.48 us (2%)
    ppermute x20, starting transfers between devices, swap(): lax.ppermute(value, 'dom', [(i, partner(i) % chain) for i in range(chain)])  39.1 us
    ppermute x20, waiting for transfers between devices, swap(): lax.ppermute(value, 'dom', [(i, partner(i) % chain) for i in range(chain)])  17.9 us
    unnamed x12, local copies, waits for them, and re-layouts  3.89 us
    pallas_call x2, Pallas kernels, on_device(): call(functools.partial(sweep_one, chain), (field,) * 3, work)  2.14 us
    pallas_call x2, Pallas kernels, on_device(): call(functools.partial(sweep_two, chain, last), (field,) * 2 + (packed,)...  2.14 us
    ppermute x4, waiting for transfers between devices, from_sibling(): return lax.ppermute(value, 'sub', [(0, 1), (1, 0)])  2 us
    pallas_call x1, Pallas kernels, on_device(): call(functools.partial(finish, chain), (shape(*dense.shape[:1], node_coun...  1.97 us
  transfers between devices with their start and end apart: 24, of which 12 were waited for; matrix products, arithmetic and copies ran while one was open for 2% of the time, Pallas kernels for 1%

profile of v5, /device:TPU:0, one launch (start us, length us, event | category | flops | bytes accessed | tf_op | source)
XLA Modules:
  0.0 73.9 jit_solution(16124927063422026253)
XLA Ops:
  3.8 3.7 %collective-permute-start.4 = (f32[8,512]{1,0:T(8,128)S(1)}, f32[8,512]{1,0:T(8,128)S(1)}, u32[]{:S(2)}, u32[]{:S(2)}) collective-permute-start(f32[8,512]{1,0:T(8,128)S(1)} %get-tuple-element.28.payload_ref), channel_id=1, source_target_pairs={{0,8},{2,10},{4,12},{6,14},{8,0},{10,2},{12,4},{14,6},{1,9},{3,11}... | collective-permute-start | bytes 49160 | tf_op jit(solution)/shard_map/ppermute | solution.py:331
  7.5 2.3 %collective-permute-start.3 = (f32[8,512]{1,0:T(8,128)S(1)}, f32[8,512]{1,0:T(8,128)S(1)}, u32[]{:S(2)}, u32[]{:S(2)}) collective-permute-start(f32[8,512]{1,0:T(8,128)S(1)} %get-tuple-element.28.payload_ref), channel_id=1, source_target_pairs={{0,14},{2,4},{4,2},{6,8},{8,6},{10,12},{12,10},{14,0},{1,15},{3,5}... | collective-permute-start | bytes 49160 | tf_op jit(solution)/shard_map/ppermute | solution.py:331
  10.5 1.6 %copy-done = f32[8,4,128,128]{3,2,1,0:T(8,128)S(1)} copy-done((f32[8,4,128,128]{3,2,1,0:T(8,128)S(1)}, f32[8,4,128,128]{3,2,1,0:T(8,128)}, u32[]{:S(2)}) %copy-start) | copy-done | bytes 2097176
  14.9 3.0 %collective-permute-start.5 = (f32[8,128]{1,0:T(8,128)S(1)}, f32[8,128]{1,0:T(8,128)S(1)}, u32[]{:S(2)}, u32[]{:S(2)}) collective-permute-start(f32[8,128]{1,0:T(8,128)S(1)} %get-tuple-element.34), channel_id=1, source_target_pairs={{0,2},{2,0},{4,6},{6,4},{8,10},{10,8},{12,14},{14,12},{1,3},{3,1},... | collective-permute-start | bytes 12296 | tf_op jit(solution)/shard_map/ppermute | solution.py:331
  17.9 1.6 %collective-permute-done.5 = f32[8,128]{1,0:T(8,128)S(1)} collective-permute-done((f32[8,128]{1,0:T(8,128)S(1)}, f32[8,128]{1,0:T(8,128)S(1)}, u32[]{:S(2)}, u32[]{:S(2)}) %collective-permute-start.5) | collective-permute-done | bytes 4128 | tf_op jit(solution)/shard_map/ppermute | solution.py:331
  20.9 1.1 %shard_map.97 = (f32[8,128]{1,0:T(8,128)S(1)}, f32[8,128]{1,0:T(8,128)S(1)}, f32[8,128]{1,0:T(8,128)S(1)}) custom-call(s32[4,8]{1,0:T(4,128)S(1)} %get-tuple-element.29.own_cols, s32[4,8]{1,0:T(4,128)S(1)} %collective-permute-done.other_cols, f32[8,4,128,128]{3,2,1,0:T(8,128)S(1)} %copy-done.1, f32[8,4,128,128]{3,2,1,0:T(8,128)S(1)} %collective-permute-done.1.other_ref, ...), custom_call_target="tpu_custom_call" | custom-call | flops 4000000 | bytes 262144 | tf_op jit(solution)/shard_map/pallas_call | solution.py:375
  22.7 5.5 %collective-permute-start.8 = (f32[8,128]{1,0:T(8,128)S(1)}, f32[8,128]{1,0:T(8,128)S(1)}, u32[]{:S(2)}, u32[]{:S(2)}) collective-permute-start(f32[8,128]{1,0:T(8,128)S(1)} %get-tuple-element.35.direction_in), channel_id=1, source_target_pairs={{0,2},{2,0},{4,6},{6,4},{8,10},{10,8},{12,14},{14,12},{1,3},{3,1},... | collective-permute-start | bytes 12296 | tf_op jit(solution)/shard_map/ppermute | solution.py:331
  28.2 1.6 %collective-permute-done.8.first_ref = f32[8,128]{1,0:T(8,128)S(1)} collective-permute-done((f32[8,128]{1,0:T(8,128)S(1)}, f32[8,128]{1,0:T(8,128)S(1)}, u32[]{:S(2)}, u32[]{:S(2)}) %collective-permute-start.8) | collective-permute-done | bytes 4128 | tf_op jit(solution)/shard_map/ppermute | solution.py:331
  29.8 1.1 %shard_map.98.own_estimate = f32[8,128]{1,0:T(8,128)S(1)} custom-call(s32[4,8]{1,0:T(4,128)S(1)} %get-tuple-element.29.own_cols, s32[4,8]{1,0:T(4,128)S(1)} %collective-permute-done.other_cols, f32[8,4,128,128]{3,2,1,0:T(8,128)S(1)} %copy-done.1, f32[8,4,128,128]{3,2,1,0:T(8,128)S(1)} %collective-permute-done.1.other_ref, ...), custom_call_target="tpu_custom_call" | custom-call | flops 4000000 | bytes 262144 | tf_op jit(solution)/shard_map/pallas_call | solution.py:378
  30.9 2.4 %collective-permute-start.12 = (f32[8,128]{1,0:T(8,128)S(1)}, f32[8,128]{1,0:T(8,128)S(1)}, u32[]{:S(2)}, u32[]{:S(2)}) collective-permute-start(f32[8,128]{1,0:T(8,128)S(1)} %shard_map.98.own_estimate), channel_id=1, source_target_pairs={{0,8},{2,10},{4,12},{6,14},{8,0},{10,2},{12,4},{14,6},{1,9},{3,11}... | collective-permute-start | bytes 12296 | tf_op jit(solution)/shard_map/ppermute | solution.py:331
  33.2 2.2 %collective-permute-start.11 = (f32[8,128]{1,0:T(8,128)S(1)}, f32[8,128]{1,0:T(8,128)S(1)}, u32[]{:S(2)}, u32[]{:S(2)}) collective-permute-start(f32[8,128]{1,0:T(8,128)S(1)} %shard_map.98.own_estimate), channel_id=1, source_target_pairs={{0,14},{2,4},{4,2},{6,8},{8,6},{10,12},{12,10},{14,0},{1,15},{3,5}... | collective-permute-start | bytes 12296 | tf_op jit(solution)/shard_map/ppermute | solution.py:331
  36.0 3.6 %collective-permute-done.11.second_estimate = f32[8,128]{1,0:T(8,128)S(1)} collective-permute-done((f32[8,128]{1,0:T(8,128)S(1)}, f32[8,128]{1,0:T(8,128)S(1)}, u32[]{:S(2)}, u32[]{:S(2)}) %collective-permute-start.11) | collective-permute-done | bytes 4128 | tf_op jit(solution)/shard_map/ppermute | solution.py:331
  40.6 2.3 %collective-permute-start.14 = (f32[8,128]{1,0:T(8,128)S(1)}, f32[8,128]{1,0:T(8,128)S(1)}, u32[]{:S(2)}, u32[]{:S(2)}) collective-permute-start(f32[8,128]{1,0:T(8,128)S(1)} %get-tuple-element.41), channel_id=1, source_target_pairs={{0,14},{2,4},{4,2},{6,8},{8,6},{10,12},{12,10},{14,0},{1,15},{3,5}... | collective-permute-start | bytes 12296 | tf_op jit(solution)/shard_map/ppermute | solution.py:331
  44.1 2.8 %collective-permute-done.14 = f32[8,128]{1,0:T(8,128)S(1)} collective-permute-done((f32[8,128]{1,0:T(8,128)S(1)}, f32[8,128]{1,0:T(8,128)S(1)}, u32[]{:S(2)}, u32[]{:S(2)}) %collective-permute-start.14) | collective-permute-done | bytes 4128 | tf_op jit(solution)/shard_map/ppermute | solution.py:331
  48.0 3.9 %collective-permute-start.16 = (f32[8,128]{1,0:T(8,128)S(1)}, f32[8,128]{1,0:T(8,128)S(1)}, u32[]{:S(2)}, u32[]{:S(2)}) collective-permute-start(f32[8,128]{1,0:T(8,128)S(1)} %get-tuple-element.53), channel_id=1, source_target_pairs={{0,2},{2,0},{4,6},{6,4},{8,10},{10,8},{12,14},{14,12},{1,3},{3,1},... | collective-permute-start | bytes 12296 | tf_op jit(solution)/shard_map/ppermute | solution.py:331
  52.0 1.6 %collective-permute-done.16 = f32[8,128]{1,0:T(8,128)S(1)} collective-permute-done((f32[8,128]{1,0:T(8,128)S(1)}, f32[8,128]{1,0:T(8,128)S(1)}, u32[]{:S(2)}, u32[]{:S(2)}) %collective-permute-start.16) | collective-permute-done | bytes 4128 | tf_op jit(solution)/shard_map/ppermute | solution.py:331
  53.6 1.2 %collective-permute-done.18.yours_ref = f32[24,128]{1,0:T(8,128)S(1)} collective-permute-done((f32[24,128]{1,0:T(8,128)S(1)}, f32[24,128]{1,0:T(8,128)S(1)}, u32[]{:S(2)}, u32[]{:S(2)}) %collective-permute-start.18) | collective-permute-done | bytes 12320 | tf_op jit(solution)/shard_map/ppermute | solution.py:347
  54.7 1.1 %shard_map.100 = (f32[8,128]{1,0:T(8,128)S(1)}, f32[8,128]{1,0:T(8,128)S(1)}, f32[8,128]{1,0:T(8,128)S(1)}) custom-call(s32[4,8]{1,0:T(4,128)S(1)} %get-tuple-element.29.own_cols, s32[4,8]{1,0:T(4,128)S(1)} %collective-permute-done.other_cols, f32[8,4,128,128]{3,2,1,0:T(8,128)S(1)} %copy-done.1, f32[8,4,128,128]{3,2,1,0:T(8,128)S(1)} %collective-permute-done.1.other_ref, ...), custom_call_target="tpu_custom_call" | custom-call | flops 4000000 | bytes 262144 | tf_op jit(solution)/shard_map/pallas_call | solution.py:375
  56.5 4.1 %collective-permute-start.19 = (f32[8,128]{1,0:T(8,128)S(1)}, f32[8,128]{1,0:T(8,128)S(1)}, u32[]{:S(2)}, u32[]{:S(2)}) collective-permute-start(f32[8,128]{1,0:T(8,128)S(1)} %get-tuple-element.43.direction_in), channel_id=1, source_target_pairs={{0,2},{2,0},{4,6},{6,4},{8,10},{10,8},{12,14},{14,12},{1,3},{3,1},... | collective-permute-start | bytes 12296 | tf_op jit(solution)/shard_map/ppermute | solution.py:331
  60.6 1.6 %collective-permute-done.19.first_ref = f32[8,128]{1,0:T(8,128)S(1)} collective-permute-done((f32[8,128]{1,0:T(8,128)S(1)}, f32[8,128]{1,0:T(8,128)S(1)}, u32[]{:S(2)}, u32[]{:S(2)}) %collective-permute-start.19) | collective-permute-done | bytes 4128 | tf_op jit(solution)/shard_map/ppermute | solution.py:331
  63.3 2.3 %collective-permute-start.22 = (f32[16,128]{1,0:T(8,128)S(1)}, f32[16,128]{1,0:T(8,128)S(1)}, u32[]{:S(2)}, u32[]{:S(2)}) collective-permute-start(f32[16,128]{1,0:T(8,128)S(1)} %get-tuple-element.46.packed_ref), channel_id=1, source_target_pairs={{0,14},{2,4},{4,2},{6,8},{8,6},{10,12},{12,10},{14,0},{1,15},{3,5}... | collective-permute-start | bytes 24584 | tf_op jit(solution)/shard_map/ppermute | solution.py:331
  65.5 1.9 %collective-permute-start.21 = (f32[16,128]{1,0:T(8,128)S(1)}, f32[16,128]{1,0:T(8,128)S(1)}, u32[]{:S(2)}, u32[]{:S(2)}) collective-permute-start(f32[16,128]{1,0:T(8,128)S(1)} %get-tuple-element.46.packed_ref), channel_id=1, source_target_pairs={{0,2},{2,0},{4,6},{6,4},{8,10},{10,8},{12,14},{14,12},{1,3},{3,1},... | collective-permute-start | bytes 24584 | tf_op jit(solution)/shard_map/ppermute | solution.py:331
  68.2 3.8 %collective-permute-done.23.far_ref = f32[8,128]{1,0:T(8,128)S(1)} collective-permute-done((f32[8,128]{1,0:T(8,128)S(1)}, f32[8,128]{1,0:T(8,128)S(1)}, u32[]{:S(2)}, u32[]{:S(2)}) %collective-permute-start.23) | collective-permute-done | bytes 4128 | tf_op jit(solution)/shard_map/ppermute | solution.py:331
  72.0 2.0 %shard_map.102 = (f32[19,2048]{1,0:T(8,128)}, f32[8,128]{1,0:T(8,128)}, f32[8,128]{1,0:T(8,128)}) custom-call(s32[4,8]{1,0:T(4,128)S(1)} %get-tuple-element.29.own_cols, s32[4,8]{1,0:T(4,128)S(1)} %collective-permute-done.other_cols, f32[8,4,128,128]{3,2,1,0:T(8,128)S(1)} %copy-done.1, f32[8,4,128,128]{3,2,1,0:T(8,128)S(1)} %collective-permute-done.1.other_ref, ...), custom_call_target="tpu_custom_call" | custom-call | flops 4000000 | bytes 262144 | tf_op jit(solution)/shard_map/pallas_call | solution.py:397
  (50 shorter events, 15.2 us)
Async XLA Ops:
  0.6 20.3 %collective-permute-start.1 = (f32[8,4,128,128]{3,2,1,0:T(8,128)}, f32[8,4,128,128]{3,2,1,0:T(8,128)S(1)}, u32[]{:S(2)}, u32[]{:S(2)}) collective-permute-start(f32[8,4,128,128]{3,2,1,0:T(8,128)} %own_ref.9), channel_id=1, source_target_pairs={{0,1},{1,0},{2,3},{3,2},{4,5},{5,4},{6,7},{7,6},{8,9},{9,8},{10,11... | collective-permute-start | bytes 6291464 | tf_op jit(solution)/shard_map/ppermute | solution.py:347
  3.8 9.7 %collective-permute-start.4 = (f32[8,512]{1,0:T(8,128)S(1)}, f32[8,512]{1,0:T(8,128)S(1)}, u32[]{:S(2)}, u32[]{:S(2)}) collective-permute-start(f32[8,512]{1,0:T(8,128)S(1)} %get-tuple-element.28.payload_ref), channel_id=1, source_target_pairs={{0,8},{2,10},{4,12},{6,14},{8,0},{10,2},{12,4},{14,6},{1,9},{3,11}... | collective-permute-start | bytes 49160 | tf_op jit(solution)/shard_map/ppermute | solution.py:331
  7.5 6.4 %collective-permute-start.3 = (f32[8,512]{1,0:T(8,128)S(1)}, f32[8,512]{1,0:T(8,128)S(1)}, u32[]{:S(2)}, u32[]{:S(2)}) collective-permute-start(f32[8,512]{1,0:T(8,128)S(1)} %get-tuple-element.28.payload_ref), channel_id=1, source_target_pairs={{0,14},{2,4},{4,2},{6,8},{8,6},{10,12},{12,10},{14,0},{1,15},{3,5}... | collective-permute-start | bytes 49160 | tf_op jit(solution)/shard_map/ppermute | solution.py:331
  9.8 4.2 %collective-permute-start.2 = (f32[8,512]{1,0:T(8,128)S(1)}, f32[8,512]{1,0:T(8,128)S(1)}, u32[]{:S(2)}, u32[]{:S(2)}) collective-permute-start(f32[8,512]{1,0:T(8,128)S(1)} %get-tuple-element.28.payload_ref), channel_id=1, source_target_pairs={{0,2},{2,0},{4,6},{6,4},{8,10},{10,8},{12,14},{14,12},{1,3},{3,1},... | collective-permute-start | bytes 49160 | tf_op jit(solution)/shard_map/ppermute | solution.py:331
  14.2 5.3 %collective-permute-start.6 = (f32[8,128]{1,0:T(8,128)S(1)}, f32[8,128]{1,0:T(8,128)S(1)}, u32[]{:S(2)}, u32[]{:S(2)}) collective-permute-start(f32[8,128]{1,0:T(8,128)S(1)} %get-tuple-element.34), channel_id=1, source_target_pairs={{0,0},{2,4},{4,2},{6,8},{8,6},{10,12},{12,10},{14,14},{1,1},{3,5},... | collective-permute-start | bytes 12296 | tf_op jit(solution)/shard_map/ppermute | solution.py:331
  14.9 4.6 %collective-permute-start.5 = (f32[8,128]{1,0:T(8,128)S(1)}, f32[8,128]{1,0:T(8,128)S(1)}, u32[]{:S(2)}, u32[]{:S(2)}) collective-permute-start(f32[8,128]{1,0:T(8,128)S(1)} %get-tuple-element.34), channel_id=1, source_target_pairs={{0,2},{2,0},{4,6},{6,4},{8,10},{10,8},{12,14},{14,12},{1,3},{3,1},... | collective-permute-start | bytes 12296 | tf_op jit(solution)/shard_map/ppermute | solution.py:331
  19.5 1.4 %collective-permute-start.7 = (f32[24,128]{1,0:T(8,128)S(1)}, f32[24,128]{1,0:T(8,128)S(1)}, u32[]{:S(2)}, u32[]{:S(2)}) collective-permute-start(f32[24,128]{1,0:T(8,128)S(1)} %constant_dynamic-update-slice_fusion.mine_ref), channel_id=1, source_target_pairs={{0,1},{1,0},{2,3},{3,2},{4,5},{5,4},{6,7},{7,6},{8,9},{9,8},{10,11... | collective-permute-start | bytes 36872 | tf_op jit(solution)/shard_map/ppermute | solution.py:347
  19.6 1.3 %collective-permute-start = (s32[4,8]{1,0:T(4,128)S(1)}, s32[4,8]{1,0:T(4,128)S(1)}, u32[]{:S(2)}, u32[]{:S(2)}) collective-permute-start(s32[4,8]{1,0:T(4,128)S(1)} %get-tuple-element.29.own_cols), channel_id=1, source_target_pairs={{0,1},{1,0},{2,3},{3,2},{4,5},{5,4},{6,7},{7,6},{8,9},{9,8},{10,11... | collective-permute-start | bytes 392 | tf_op jit(solution)/shard_map/ppermute | solution.py:347
  22.0 6.2 %collective-permute-start.9 = (f32[8,128]{1,0:T(8,128)S(1)}, f32[8,128]{1,0:T(8,128)S(1)}, u32[]{:S(2)}, u32[]{:S(2)}) collective-permute-start(f32[8,128]{1,0:T(8,128)S(1)} %get-tuple-element.35.direction_in), channel_id=1, source_target_pairs={{0,0},{2,4},{4,2},{6,8},{8,6},{10,12},{12,10},{14,14},{1,1},{3,5},... | collective-permute-start | bytes 12296 | tf_op jit(solution)/shard_map/ppermute | solution.py:331
  22.7 7.1 %collective-permute-start.8 = (f32[8,128]{1,0:T(8,128)S(1)}, f32[8,128]{1,0:T(8,128)S(1)}, u32[]{:S(2)}, u32[]{:S(2)}) collective-permute-start(f32[8,128]{1,0:T(8,128)S(1)} %get-tuple-element.35.direction_in), channel_id=1, source_target_pairs={{0,2},{2,0},{4,6},{6,4},{8,10},{10,8},{12,14},{14,12},{1,3},{3,1},... | collective-permute-start | bytes 12296 | tf_op jit(solution)/shard_map/ppermute | solution.py:331
  30.9 5.1 %collective-permute-start.12 = (f32[8,128]{1,0:T(8,128)S(1)}, f32[8,128]{1,0:T(8,128)S(1)}, u32[]{:S(2)}, u32[]{:S(2)}) collective-permute-start(f32[8,128]{1,0:T(8,128)S(1)} %shard_map.98.own_estimate), channel_id=1, source_target_pairs={{0,8},{2,10},{4,12},{6,14},{8,0},{10,2},{12,4},{14,6},{1,9},{3,11}... | collective-permute-start | bytes 12296 | tf_op jit(solution)/shard_map/ppermute | solution.py:331
  33.2 6.3 %collective-permute-start.11 = (f32[8,128]{1,0:T(8,128)S(1)}, f32[8,128]{1,0:T(8,128)S(1)}, u32[]{:S(2)}, u32[]{:S(2)}) collective-permute-start(f32[8,128]{1,0:T(8,128)S(1)} %shard_map.98.own_estimate), channel_id=1, source_target_pairs={{0,14},{2,4},{4,2},{6,8},{8,6},{10,12},{12,10},{14,0},{1,15},{3,5}... | collective-permute-start | bytes 12296 | tf_op jit(solution)/shard_map/ppermute | solution.py:331
  35.4 4.1 %collective-permute-start.10 = (f32[8,128]{1,0:T(8,128)S(1)}, f32[8,128]{1,0:T(8,128)S(1)}, u32[]{:S(2)}, u32[]{:S(2)}) collective-permute-start(f32[8,128]{1,0:T(8,128)S(1)} %shard_map.98.own_estimate), channel_id=1, source_target_pairs={{0,2},{2,0},{4,6},{6,4},{8,10},{10,8},{12,14},{14,12},{1,3},{3,1},... | collective-permute-start | bytes 12296 | tf_op jit(solution)/shard_map/ppermute | solution.py:331
  40.5 3.7 %collective-permute-start.13 = (f32[8,128]{1,0:T(8,128)S(1)}, f32[8,128]{1,0:T(8,128)S(1)}, u32[]{:S(2)}, u32[]{:S(2)}) collective-permute-start(f32[8,128]{1,0:T(8,128)S(1)} %get-tuple-element.40), channel_id=1, source_target_pairs={{0,2},{2,0},{4,6},{6,4},{8,10},{10,8},{12,14},{14,12},{1,3},{3,1},... | collective-permute-start | bytes 12296 | tf_op jit(solution)/shard_map/ppermute | solution.py:331
  40.6 6.3 %collective-permute-start.14 = (f32[8,128]{1,0:T(8,128)S(1)}, f32[8,128]{1,0:T(8,128)S(1)}, u32[]{:S(2)}, u32[]{:S(2)}) collective-permute-start(f32[8,128]{1,0:T(8,128)S(1)} %get-tuple-element.41), channel_id=1, source_target_pairs={{0,14},{2,4},{4,2},{6,8},{8,6},{10,12},{12,10},{14,0},{1,15},{3,5}... | collective-permute-start | bytes 12296 | tf_op jit(solution)/shard_map/ppermute | solution.py:331
  42.8 4.5 %collective-permute-start.15 = (f32[8,128]{1,0:T(8,128)S(1)}, f32[8,128]{1,0:T(8,128)S(1)}, u32[]{:S(2)}, u32[]{:S(2)}) collective-permute-start(f32[8,128]{1,0:T(8,128)S(1)} %get-tuple-element.42), channel_id=1, source_target_pairs={{0,8},{2,10},{4,12},{6,14},{8,0},{10,2},{12,4},{14,6},{1,9},{3,11}... | collective-permute-start | bytes 12296 | tf_op jit(solution)/shard_map/ppermute | solution.py:331
  47.4 4.6 %collective-permute-start.17 = (f32[8,128]{1,0:T(8,128)S(1)}, f32[8,128]{1,0:T(8,128)S(1)}, u32[]{:S(2)}, u32[]{:S(2)}) collective-permute-start(f32[8,128]{1,0:T(8,128)S(1)} %get-tuple-element.53), channel_id=1, source_target_pairs={{0,0},{2,4},{4,2},{6,8},{8,6},{10,12},{12,10},{14,14},{1,1},{3,5},... | collective-permute-start | bytes 12296 | tf_op jit(solution)/shard_map/ppermute | solution.py:331
  48.0 5.5 %collective-permute-start.16 = (f32[8,128]{1,0:T(8,128)S(1)}, f32[8,128]{1,0:T(8,128)S(1)}, u32[]{:S(2)}, u32[]{:S(2)}) collective-permute-start(f32[8,128]{1,0:T(8,128)S(1)} %get-tuple-element.53), channel_id=1, source_target_pairs={{0,2},{2,0},{4,6},{6,4},{8,10},{10,8},{12,14},{14,12},{1,3},{3,1},... | collective-permute-start | bytes 12296 | tf_op jit(solution)/shard_map/ppermute | solution.py:331
  53.6 1.2 %collective-permute-start.18 = (f32[24,128]{1,0:T(8,128)S(1)}, f32[24,128]{1,0:T(8,128)S(1)}, u32[]{:S(2)}, u32[]{:S(2)}) collective-permute-start(f32[24,128]{1,0:T(8,128)S(1)} %pad_maximum_fusion.mine_ref), channel_id=1, source_target_pairs={{0,1},{1,0},{2,3},{3,2},{4,5},{5,4},{6,7},{7,6},{8,9},{9,8},{10,11... | collective-permute-start | bytes 36872 | tf_op jit(solution)/shard_map/ppermute | solution.py:347
  55.8 4.8 %collective-permute-start.20 = (f32[8,128]{1,0:T(8,128)S(1)}, f32[8,128]{1,0:T(8,128)S(1)}, u32[]{:S(2)}, u32[]{:S(2)}) collective-permute-start(f32[8,128]{1,0:T(8,128)S(1)} %get-tuple-element.43.direction_in), channel_id=1, source_target_pairs={{0,0},{2,4},{4,2},{6,8},{8,6},{10,12},{12,10},{14,14},{1,1},{3,5},... | collective-permute-start | bytes 12296 | tf_op jit(solution)/shard_map/ppermute | solution.py:331
  56.5 5.7 %collective-permute-start.19 = (f32[8,128]{1,0:T(8,128)S(1)}, f32[8,128]{1,0:T(8,128)S(1)}, u32[]{:S(2)}, u32[]{:S(2)}) collective-permute-start(f32[8,128]{1,0:T(8,128)S(1)} %get-tuple-element.43.direction_in), channel_id=1, source_target_pairs={{0,2},{2,0},{4,6},{6,4},{8,10},{10,8},{12,14},{14,12},{1,3},{3,1},... | collective-permute-start | bytes 12296 | tf_op jit(solution)/shard_map/ppermute | solution.py:331
  63.3 8.7 %collective-permute-start.22 = (f32[16,128]{1,0:T(8,128)S(1)}, f32[16,128]{1,0:T(8,128)S(1)}, u32[]{:S(2)}, u32[]{:S(2)}) collective-permute-start(f32[16,128]{1,0:T(8,128)S(1)} %get-tuple-element.46.packed_ref), channel_id=1, source_target_pairs={{0,14},{2,4},{4,2},{6,8},{8,6},{10,12},{12,10},{14,0},{1,15},{3,5}... | collective-permute-start | bytes 24584 | tf_op jit(solution)/shard_map/ppermute | solution.py:331
  65.5 6.4 %collective-permute-start.21 = (f32[16,128]{1,0:T(8,128)S(1)}, f32[16,128]{1,0:T(8,128)S(1)}, u32[]{:S(2)}, u32[]{:S(2)}) collective-permute-start(f32[16,128]{1,0:T(8,128)S(1)} %get-tuple-element.46.packed_ref), channel_id=1, source_target_pairs={{0,2},{2,0},{4,6},{6,4},{8,10},{10,8},{12,14},{14,12},{1,3},{3,1},... | collective-permute-start | bytes 24584 | tf_op jit(solution)/shard_map/ppermute | solution.py:331
  67.5 4.5 %collective-permute-start.23 = (f32[8,128]{1,0:T(8,128)S(1)}, f32[8,128]{1,0:T(8,128)S(1)}, u32[]{:S(2)}, u32[]{:S(2)}) collective-permute-start(f32[8,128]{1,0:T(8,128)S(1)} %get-tuple-element.47), channel_id=1, source_target_pairs={{0,8},{2,10},{4,12},{6,14},{8,0},{10,2},{12,4},{14,6},{1,9},{3,11}... | collective-permute-start | bytes 12296 | tf_op jit(solution)/shard_map/ppermute | solution.py:331
  (5 other events, 11.3 us)

commit v6 on v5

--- a/solution.py
+++ b/solution.py
@@ -138,6 +138,11 @@
     return lax.rem(lax.axis_index("dom"), 2) == 0
 
 
+def by_partner(mine, yours):
+    zero = lax.axis_index("sub") == 0
+    return jnp.where(zero, mine, yours), jnp.where(zero, yours, mine)
+
+
 def by_side(first, second):
     even = is_even()
     return jnp.where(even, first, second), jnp.where(even, second, first)
@@ -192,49 +197,53 @@
     return copies
 
 
-def begin(states_ref, table_ref, out_ref, payload_ref):
-    peers = table_ref.shape[0] // 2
+def begin(states_ref, table_ref, out_ref, payload_ref, nodes_ref):
+    peers, slots = nodes_ref.shape
     for k in range(out_ref.shape[1]):
         out_ref[:, k, :] = states_ref[:, k * LANES : (k + 1) * LANES]
+    slot = lax.broadcasted_iota(jnp.int32, (peers, slots), 1)
+    nodes = jnp.where(slot < table_ref[2 * peers :], table_ref[0:peers], -1)
+    nodes_ref[...] = nodes
     rows, current = ionic_rows([out_ref[i] for i in range(out_ref.shape[0])])
     for i, row in enumerate(rows):
         out_ref[i] = row
-    payload_ref[0:peers] = pick_current(current, table_ref[0:peers])
-    payload_ref[peers:] = table_ref[peers:].astype(F32)
-
-
-def bring(tiles_ref, cols_ref, diag_ref, payload_ref, cols_out, diag_out, payload_out):
+    payload_ref[0:peers] = pick_current(current, nodes)
+    payload_ref[peers:] = table_ref[peers : 2 * peers].astype(F32)
+
+
+def bring(cols_ref, diag_ref, payload_ref, cols_out, diag_out, payload_out):
     cols_out[...] = cols_ref[...]
     diag_out[...] = diag_ref[...]
     payload_out[...] = payload_ref[...]
+
+
+def bring_tiles(tiles_ref, direction_ref, direction_out):
+    direction_out[...] = direction_ref[...]
     del tiles_ref
 
 
 def first_forcing(
-    table_ref, own_ref, first_ref, second_ref, far_ref, diag_ref,
-    maps_ref, forcing_ref, direction_ref,
+    nodes_ref, table_ref, own_ref, first_ref, second_ref, far_ref,
+    maps_ref, forcing_ref,
 ):
-    peers = table_ref.shape[0] // 2
+    peers = nodes_ref.shape[0]
     after, before = by_side(first_ref[...], second_ref[...])
     come = [own_ref[0:1], before[1:2], after[2:3], far_ref[3:4]]
     rows = [own_ref[peers : peers + 1], after[peers + 1 : peers + 2]]
     rows += [before[peers + 2 : peers + 3], far_ref[peers + 3 : peers + 4]]
-    nodes = table_ref[0:peers]
-    maps_ref[...] = jnp.where(nodes < 0, -1, jnp.concatenate(rows, axis=0).astype(jnp.int32))
+    maps_ref[...] = jnp.where(nodes_ref[...] < 0, -1, jnp.concatenate(rows, axis=0).astype(jnp.int32))
     total = None
     for o in range(peers):
         part = scatter(come[o], table_ref[peers + o : peers + o + 1], forcing_ref.shape[0])
         total = part if total is None else total + part
-    forcing = TORSO_COUPLING * total
-    forcing_ref[...] = forcing
-    direction_ref[...] = forcing / (CHEB_THETA * diag_ref[...])
+    forcing_ref[...] = TORSO_COUPLING * total
 
 
 def next_shares(
-    states_ref, own_estimate, first_estimate, second_estimate, far_estimate, table_ref, maps_ref,
+    states_ref, own_estimate, first_estimate, second_estimate, far_estimate, nodes_ref, maps_ref,
     out_ref, own_ref, first_ref, second_ref, far_ref,
 ):
-    nodes, maps = table_ref[0 : table_ref.shape[0] // 2], maps_ref[...]
+    nodes, maps = nodes_ref[...], maps_ref[...]
     after, before = by_side(first_estimate[...], second_estimate[...])
     estimates = [own_estimate[...], after, before, far_estimate[...]]
     feedback = feedback_of(estimates, nodes, maps, states_ref.shape[1])
@@ -257,17 +266,15 @@
 
 
 def sweep_one(
-    chain, own_cols, other_cols, own_ref, other_ref, mine_ref, yours_ref, diag_ref,
-    residual_ref, direction_ref, estimate_ref, window_ref, product_ref,
+    chain, own_cols, other_cols, own_ref, other_ref, mine_ref, yours_ref, forcing_ref,
+    direction_in, diag_ref, residual_ref, direction_ref, estimate_ref, window_ref, product_ref,
 ):
-    torso = residual_ref.shape[0]
-    total = mine_ref[...] + yours_ref[...]
     diag = diag_ref[...]
-    residual = total[0:torso]
-    direction = residual / (CHEB_THETA * diag)
-    fill_window(chain, direction, total[torso : 2 * torso], total[2 * torso :], window_ref)
+    direction = direction_in[...]
+    first, second = by_partner(mine_ref[...], yours_ref[...])
+    fill_window(chain, direction, first, second, window_ref)
     product(own_ref, other_ref, own_cols, other_cols, window_ref, product_ref)
-    residual = residual - (diag * direction + product_ref[...])
+    residual = forcing_ref[...] - (diag * direction + product_ref[...])
     estimate = direction
     direction = KEEP[0] * direction + PULL[0] * (residual / diag)
     residual_ref[...] = residual
@@ -276,14 +283,15 @@
 
 
 def sweep_two(
-    chain, last, own_cols, other_cols, own_ref, other_ref, first_ref, second_ref, direction_in,
+    chain, last, own_cols, other_cols, own_ref, other_ref, mine_ref, yours_ref, direction_in,
     residual_in, estimate_in, diag_ref, *refs,
 ):
     estimate_ref, window_ref, product_ref = refs[0], refs[-2], refs[-1]
     torso = estimate_ref.shape[0]
     diag = diag_ref[...]
     direction = direction_in[...]
-    fill_window(chain, direction, first_ref[...], second_ref[...], window_ref)
+    first, second = by_partner(mine_ref[...], yours_ref[...])
+    fill_window(chain, direction, first, second, window_ref)
     product(own_ref, other_ref, own_cols, other_cols, window_ref, product_ref)
     residual = residual_in[...] - (diag * direction + product_ref[...])
     direction = KEEP[1] * direction + PULL[1] * (residual / diag)
@@ -298,17 +306,16 @@
 
 def finish(
     chain, own_cols, other_cols, own_ref, other_ref, first_ref, second_ref, packed_ref, far_ref,
-    residual_in, diag_ref, states_ref, table_ref, maps_ref,
+    residual_in, diag_ref, states_ref, nodes_ref, maps_ref,
     out_ref, potential_ref, residual_ref, window_ref, product_ref, dense_ref,
 ):
     torso = residual_ref.shape[0]
-    peers = maps_ref.shape[0]
     head, tail = slice(0, torso), slice(torso, 2 * torso)
     estimate, direction = packed_ref[head], packed_ref[tail]
     potential_ref[...] = estimate
     after, before = by_side(first_ref[head], second_ref[head])
     feedback = feedback_of(
-        [estimate, after, before, far_ref[...]], table_ref[0:peers], maps_ref[...],
+        [estimate, after, before, far_ref[...]], nodes_ref[...], maps_ref[...],
         states_ref.shape[1],
     )
     dense_ref[...] = states_ref[...]
@@ -336,9 +343,10 @@
     def with_second(value):
         return swap(value, lambda i: ((i + 1) ^ 1) - 1)
 
-    def with_inner(value):
-        ends = (0, chain - 1)
-        return swap(value, lambda i: i if i in ends else ((i + 1) ^ 1) - 1)
+    def with_either(value):
+        pairs = [(2 * i, 2 * (i ^ 1)) for i in range(chain)]
+        pairs += [(2 * i + 1, 2 * ((((i + 1) ^ 1) - 1) % chain) + 1) for i in range(chain)]
+        return lax.ppermute(value, ("dom", "sub"), pairs)
 
     def with_far(value):
         return swap(value, lambda i: i + chain // 2)
@@ -355,44 +363,50 @@
     work = (pltpu.VMEM((torso + 2 * HALO, LANES), F32), pltpu.VMEM((torso, LANES), F32))
 
     other_tiles = from_sibling(tile_values)
-    live = jnp.arange(slots, dtype=jnp.int32)[None, :] < send_count[0][:, None]
-    table = jnp.concatenate([jnp.where(live, send_node[0], -1), recv_row[0]])
-    states, payload = call(begin, (dense, shape(2 * peers, slots)))(in_specs=[VMEM] * 2)(
+    counts = jnp.broadcast_to(send_count[0][:, None], (peers, slots))
+    table = jnp.concatenate([send_node[0], recv_row[0], counts])
+    index = shape(peers, slots, dtype=jnp.int32)
+    payload = shape(2 * peers, slots)
+    states, payload, nodes = call(begin, (dense, payload, index))(in_specs=[VMEM] * 2)(
         states, table
     )
     columns, diag, own = call(
-        bring, (shape(*columns.shape[::-1], dtype=jnp.int32), field, shape(2 * peers, slots))
-    )(in_specs=[VMEM] * 4)(tile_values, columns.T, diagonal.reshape(torso, LANES), payload)
+        bring, (shape(*columns.shape[::-1], dtype=jnp.int32), field, payload)
+    )(in_specs=[VMEM] * 3)(columns.T, diagonal.reshape(torso, LANES), payload)
     stored = (columns, from_sibling(columns), tile_values, other_tiles)
-    maps, forcing, direction = call(
-        first_forcing, (shape(peers, slots, dtype=jnp.int32), field, field)
-    )(in_specs=[VMEM] * 6)(
-        table, own, with_first(payload), with_second(payload), with_far(payload), diag
+    maps, forcing = call(first_forcing, (index, field))(in_specs=[VMEM] * 6)(
+        nodes, table, own, with_first(payload), with_second(payload), with_far(payload)
     )
     for time_step in range(2):
         last = time_step == 1
-        mine = jnp.concatenate([forcing, with_first(direction), with_inner(direction)])
+        forcing = forcing + from_sibling(forcing)
+        direction = forcing / (CHEB_THETA * diag)
+        halo = with_either(direction)
+        if not last:
+            direction = call(bring_tiles, field)(in_specs=[VMEM] * 2)(tile_values, direction)
+            halo, direction = lax.optimization_barrier((halo, direction))
         residual, direction, estimate = call(
             functools.partial(sweep_one, chain), (field,) * 3, work
-        )(in_specs=[SMEM] * 2 + [VMEM] * 5)(*stored, mine, from_sibling(mine), diag)
+        )(in_specs=[SMEM] * 2 + [VMEM] * 7)(
+            *stored, halo, from_sibling(halo), forcing, direction, diag
+        )
+        halo = with_either(direction)
         estimate, *rest = call(
             functools.partial(sweep_two, chain, last),
             (field,) * 2 + (packed,) if last else (field,),
             work,
         )(in_specs=[SMEM] * 2 + [VMEM] * 8)(
-            *stored, with_first(direction), with_inner(direction), direction, residual, estimate,
-            diag,
+            *stored, halo, from_sibling(halo), direction, residual, estimate, diag
         )
         if not last:
             states, own, first, second, far = call(next_shares, (dense,) + (field,) * 4)(
                 in_specs=[VMEM] * 7
             )(
                 states, estimate, with_first(estimate), with_second(estimate), with_far(estimate),
-                table, maps,
+                nodes, maps,
             )
             forcing = own + with_first(first) + with_second(second) + with_far(far)
             forcing = TORSO_COUPLING * forcing
-            direction = forcing / (CHEB_THETA * diag)
     residual, both = rest
     new_states, potential, residual = call(
         functools.partial(finish, chain),
@@ -400,7 +414,7 @@
         work + (pltpu.VMEM(dense.shape, F32),),
     )(in_specs=[SMEM] * 2 + [VMEM] * 11)(
         *stored, with_first(both), with_second(both), both, with_far(estimate), residual, diag,
-        states, table, maps,
+        states, nodes, maps,
     )
     return new_states, potential.reshape(-1), residual.reshape(-1)
 

time: 74.3 us -> 69.7 us (0.938)
  starting transfers between devices: 40.2 us -> 24.2 us
  waiting for transfers between devices: 19.9 us -> 31.4 us
    ppermute x20 -> x12, starting transfers between devices: 39.1 us -> 14.8 us  [swap(): lax.ppermute(value, 'dom', [(i, partner(i) % chain) for i in range(chain)])]
    ppermute x0 -> x4, waiting for transfers between devices: none -> 11.2 us  [with_either(): return lax.ppermute(value, ('dom', 'sub'), pairs)]
    ppermute x4 -> x8, starting transfers between devices: 1.08 us -> 7.59 us  [from_sibling(): return lax.ppermute(value, 'sub', [(0, 1), (1, 0)])]
    ppermute x4 -> x8, waiting for transfers between devices: 2 us -> 5.95 us  [from_sibling(): return lax.ppermute(value, 'sub', [(0, 1), (1, 0)])]
    ppermute x20 -> x12, waiting for transfers between devices: 17.9 us -> 14.3 us  [swap(): lax.ppermute(value, 'dom', [(i, partner(i) % chain) for i in range(chain)])]
    ppermute x0 -> x4, starting transfers between devices: none -> 1.76 us  [with_either(): return lax.ppermute(value, ('dom', 'sub'), pairs)]
    select_n x1 -> x0, other arithmetic: 0.77 us -> none  [on_device(): table = jnp.concatenate([jnp.where(live, send_node[0], -1), recv_row[0]])]
    unnamed x12 -> x10, local copies, waits for them, and re-layouts: 3.89 us -> 3.89 us
  transfers between devices with their start and end apart: 24 -> 24, of which waited for: 12 -> 17; matrix products, arithmetic and copies ran while one was open for 2% -> 2% of each run, Pallas kernels for 1% -> 1%
where the time goes in v6:
time: 69.7 us; the launch traced here: 69.4 us
  waiting for transfers between devices  31.4 us (45%)
  starting transfers between devices  24.2 us (35%)
  Pallas kernels  7.65 us (11%)
  local copies, waits for them, and re-layouts  4.62 us (7%)
  other arithmetic  0.8 us (1%)
  between operations  0.72 us (1%)
    ppermute x12, starting transfers between devices, swap(): lax.ppermute(value, 'dom', [(i, partner(i) % chain) for i in range(chain)])  14.8 us
    ppermute x12, waiting for transfers between devices, swap(): lax.ppermute(value, 'dom', [(i, partner(i) % chain) for i in range(chain)])  14.3 us
    ppermute x4, waiting for transfers between devices, with_either(): return lax.ppermute(value, ('dom', 'sub'), pairs)  11.2 us
    ppermute x8, starting transfers between devices, from_sibling(): return lax.ppermute(value, 'sub', [(0, 1), (1, 0)])  7.59 us
    ppermute x8, waiting for transfers between devices, from_sibling(): return lax.ppermute(value, 'sub', [(0, 1), (1, 0)])  5.95 us
    unnamed x10, local copies, waits for them, and re-layouts  3.89 us
    pallas_call x2, Pallas kernels, on_device(): call(functools.partial(sweep_one, chain), (field,) * 3, work)  2.11 us
    pallas_call x2, Pallas kernels, on_device(): call(functools.partial(sweep_two, chain, last), (field,) * 2 + (packed,)...  2.1 us
  transfers between devices with their start and end apart: 24, of which 17 were waited for; matrix products, arithmetic and copies ran while one was open for 2% of the time, Pallas kernels for 1%

profile of v6, /device:TPU:0, one launch (start us, length us, event | category | flops | bytes accessed | tf_op | source)
XLA Modules:
  0.0 69.4 jit_solution(7763680806730689721)
XLA Ops:
  3.9 3.7 %collective-permute-start.4 = (f32[8,512]{1,0:T(8,128)S(1)}, f32[8,512]{1,0:T(8,128)S(1)}, u32[]{:S(2)}, u32[]{:S(2)}) collective-permute-start(f32[8,512]{1,0:T(8,128)S(1)} %get-tuple-element.30.payload_ref), channel_id=1, source_target_pairs={{0,8},{2,10},{4,12},{6,14},{8,0},{10,2},{12,4},{14,6},{1,9},{3,11}... | collective-permute-start | bytes 49160 | tf_op jit(solution)/shard_map/ppermute | solution.py:338
  7.5 2.3 %collective-permute-start.3 = (f32[8,512]{1,0:T(8,128)S(1)}, f32[8,512]{1,0:T(8,128)S(1)}, u32[]{:S(2)}, u32[]{:S(2)}) collective-permute-start(f32[8,512]{1,0:T(8,128)S(1)} %get-tuple-element.30.payload_ref), channel_id=1, source_target_pairs={{0,14},{2,4},{4,2},{6,8},{8,6},{10,12},{12,10},{14,0},{1,15},{3,5}... | collective-permute-start | bytes 49160 | tf_op jit(solution)/shard_map/ppermute | solution.py:338
  12.0 2.0 %collective-permute-done.3.second_ref = f32[8,512]{1,0:T(8,128)S(1)} collective-permute-done((f32[8,512]{1,0:T(8,128)S(1)}, f32[8,512]{1,0:T(8,128)S(1)}, u32[]{:S(2)}, u32[]{:S(2)}) %collective-permute-start.3) | collective-permute-done | bytes 16416 | tf_op jit(solution)/shard_map/ppermute | solution.py:338
  14.3 1.2 %collective-permute-done.5 = f32[8,128]{1,0:T(8,128)S(1)} collective-permute-done((f32[8,128]{1,0:T(8,128)S(1)}, f32[8,128]{1,0:T(8,128)S(1)}, u32[]{:S(2)}, u32[]{:S(2)}) %collective-permute-start.5) | collective-permute-done | bytes 4128 | tf_op jit(solution)/shard_map/ppermute | solution.py:355
  15.8 1.6 %copy-done = f32[8,4,128,128]{3,2,1,0:T(8,128)S(1)} copy-done((f32[8,4,128,128]{3,2,1,0:T(8,128)S(1)}, f32[8,4,128,128]{3,2,1,0:T(8,128)}, u32[]{:S(2)}) %copy-start) | copy-done | bytes 2097176
  17.4 1.7 %collective-permute-done.6.mine_ref = f32[8,128]{1,0:T(8,128)S(1)} collective-permute-done((f32[8,128]{1,0:T(8,128)S(1)}, f32[8,128]{1,0:T(8,128)S(1)}, u32[]{:S(2)}, u32[]{:S(2)}) %collective-permute-start.6) | collective-permute-done | bytes 4128 | tf_op jit(solution)/shard_map/ppermute | solution.py:349
  19.1 1.7 %collective-permute-start.7 = (f32[8,128]{1,0:T(8,128)S(1)}, f32[8,128]{1,0:T(8,128)S(1)}, u32[]{:S(2)}, u32[]{:S(2)}) collective-permute-start(f32[8,128]{1,0:T(8,128)S(1)} %collective-permute-done.6.mine_ref), channel_id=1, source_target_pairs={{0,1},{1,0},{2,3},{3,2},{4,5},{5,4},{6,7},{7,6},{8,9},{9,8},{10,11... | collective-permute-start | bytes 12296 | tf_op jit(solution)/shard_map/ppermute | solution.py:355
  20.8 1.2 %collective-permute-done.other_cols = s32[4,8]{1,0:T(4,128)S(1)} collective-permute-done((s32[4,8]{1,0:T(4,128)S(1)}, s32[4,8]{1,0:T(4,128)S(1)}, u32[]{:S(2)}, u32[]{:S(2)}) %collective-permute-start) | collective-permute-done | bytes 160 | tf_op jit(solution)/shard_map/ppermute | solution.py:355
  23.1 3.6 %collective-permute-done.8.mine_ref = f32[8,128]{1,0:T(8,128)S(1)} collective-permute-done((f32[8,128]{1,0:T(8,128)S(1)}, f32[8,128]{1,0:T(8,128)S(1)}, u32[]{:S(2)}, u32[]{:S(2)}) %collective-permute-start.8) | collective-permute-done | bytes 4128 | tf_op jit(solution)/shard_map/ppermute | solution.py:349
  26.7 1.7 %collective-permute-start.9 = (f32[8,128]{1,0:T(8,128)S(1)}, f32[8,128]{1,0:T(8,128)S(1)}, u32[]{:S(2)}, u32[]{:S(2)}) collective-permute-start(f32[8,128]{1,0:T(8,128)S(1)} %collective-permute-done.8.mine_ref), channel_id=1, source_target_pairs={{0,1},{1,0},{2,3},{3,2},{4,5},{5,4},{6,7},{7,6},{8,9},{9,8},{10,11... | collective-permute-start | bytes 12296 | tf_op jit(solution)/shard_map/ppermute | solution.py:355
  30.3 2.3 %collective-permute-start.11 = (f32[8,128]{1,0:T(8,128)S(1)}, f32[8,128]{1,0:T(8,128)S(1)}, u32[]{:S(2)}, u32[]{:S(2)}) collective-permute-start(f32[8,128]{1,0:T(8,128)S(1)} %shard_map.99.own_estimate), channel_id=1, source_target_pairs={{0,14},{2,4},{4,2},{6,8},{8,6},{10,12},{12,10},{14,0},{1,15},{3,5}... | collective-permute-start | bytes 12296 | tf_op jit(solution)/shard_map/ppermute | solution.py:338
  32.7 2.2 %collective-permute-done.12.far_estimate = f32[8,128]{1,0:T(8,128)S(1)} collective-permute-done((f32[8,128]{1,0:T(8,128)S(1)}, f32[8,128]{1,0:T(8,128)S(1)}, u32[]{:S(2)}, u32[]{:S(2)}) %collective-permute-start.12) | collective-permute-done | bytes 4128 | tf_op jit(solution)/shard_map/ppermute | solution.py:338
  34.8 1.9 %collective-permute-done.11.second_estimate = f32[8,128]{1,0:T(8,128)S(1)} collective-permute-done((f32[8,128]{1,0:T(8,128)S(1)}, f32[8,128]{1,0:T(8,128)S(1)}, u32[]{:S(2)}, u32[]{:S(2)}) %collective-permute-start.11) | collective-permute-done | bytes 4128 | tf_op jit(solution)/shard_map/ppermute | solution.py:338
  37.7 2.3 %collective-permute-start.14 = (f32[8,128]{1,0:T(8,128)S(1)}, f32[8,128]{1,0:T(8,128)S(1)}, u32[]{:S(2)}, u32[]{:S(2)}) collective-permute-start(f32[8,128]{1,0:T(8,128)S(1)} %get-tuple-element.45), channel_id=1, source_target_pairs={{0,14},{2,4},{4,2},{6,8},{8,6},{10,12},{12,10},{14,0},{1,15},{3,5}... | collective-permute-start | bytes 12296 | tf_op jit(solution)/shard_map/ppermute | solution.py:338
  41.3 2.8 %collective-permute-done.14 = f32[8,128]{1,0:T(8,128)S(1)} collective-permute-done((f32[8,128]{1,0:T(8,128)S(1)}, f32[8,128]{1,0:T(8,128)S(1)}, u32[]{:S(2)}, u32[]{:S(2)}) %collective-permute-start.14) | collective-permute-done | bytes 4128 | tf_op jit(solution)/shard_map/ppermute | solution.py:338
  44.6 1.2 %collective-permute-done.16 = f32[8,128]{1,0:T(8,128)S(1)} collective-permute-done((f32[8,128]{1,0:T(8,128)S(1)}, f32[8,128]{1,0:T(8,128)S(1)}, u32[]{:S(2)}, u32[]{:S(2)}) %collective-permute-start.16) | collective-permute-done | bytes 4128 | tf_op jit(solution)/shard_map/ppermute | solution.py:355
  45.8 1.3 %collective-permute-start.17 = (f32[8,128]{1,0:T(8,128)S(1)}, f32[8,128]{1,0:T(8,128)S(1)}, u32[]{:S(2)}, u32[]{:S(2)}) collective-permute-start(f32[8,128]{1,0:T(8,128)S(1)} %get-tuple-element.57.direction_in), channel_id=1, source_target_pairs={{0,2},{2,0},{4,6},{6,4},{8,10},{10,8},{12,14},{14,12},{1,15},{3,5}... | collective-permute-start | bytes 12296 | tf_op jit(solution)/shard_map/ppermute | solution.py:349
  47.0 2.3 %collective-permute-done.17.mine_ref = f32[8,128]{1,0:T(8,128)S(1)} collective-permute-done((f32[8,128]{1,0:T(8,128)S(1)}, f32[8,128]{1,0:T(8,128)S(1)}, u32[]{:S(2)}, u32[]{:S(2)}) %collective-permute-start.17) | collective-permute-done | bytes 4128 | tf_op jit(solution)/shard_map/ppermute | solution.py:349
  49.4 1.7 %collective-permute-start.18 = (f32[8,128]{1,0:T(8,128)S(1)}, f32[8,128]{1,0:T(8,128)S(1)}, u32[]{:S(2)}, u32[]{:S(2)}) collective-permute-start(f32[8,128]{1,0:T(8,128)S(1)} %collective-permute-done.17.mine_ref), channel_id=1, source_target_pairs={{0,1},{1,0},{2,3},{3,2},{4,5},{5,4},{6,7},{7,6},{8,9},{9,8},{10,11... | collective-permute-start | bytes 12296 | tf_op jit(solution)/shard_map/ppermute | solution.py:355
  53.0 3.6 %collective-permute-done.19.mine_ref = f32[8,128]{1,0:T(8,128)S(1)} collective-permute-done((f32[8,128]{1,0:T(8,128)S(1)}, f32[8,128]{1,0:T(8,128)S(1)}, u32[]{:S(2)}, u32[]{:S(2)}) %collective-permute-start.19) | collective-permute-done | bytes 4128 | tf_op jit(solution)/shard_map/ppermute | solution.py:349
  56.6 1.9 %collective-permute-start.20 = (f32[8,128]{1,0:T(8,128)S(1)}, f32[8,128]{1,0:T(8,128)S(1)}, u32[]{:S(2)}, u32[]{:S(2)}) collective-permute-start(f32[8,128]{1,0:T(8,128)S(1)} %collective-permute-done.19.mine_ref), channel_id=1, source_target_pairs={{0,1},{1,0},{2,3},{3,2},{4,5},{5,4},{6,7},{7,6},{8,9},{9,8},{10,11... | collective-permute-start | bytes 12296 | tf_op jit(solution)/shard_map/ppermute | solution.py:355
  60.4 2.5 %collective-permute-start.22 = (f32[16,128]{1,0:T(8,128)S(1)}, f32[16,128]{1,0:T(8,128)S(1)}, u32[]{:S(2)}, u32[]{:S(2)}) collective-permute-start(f32[16,128]{1,0:T(8,128)S(1)} %get-tuple-element.50.packed_ref), channel_id=1, source_target_pairs={{0,14},{2,4},{4,2},{6,8},{8,6},{10,12},{12,10},{14,0},{1,15},{3,5}... | collective-permute-start | bytes 24584 | tf_op jit(solution)/shard_map/ppermute | solution.py:338
  62.9 4.5 %collective-permute-done.23.far_ref = f32[8,128]{1,0:T(8,128)S(1)} collective-permute-done((f32[8,128]{1,0:T(8,128)S(1)}, f32[8,128]{1,0:T(8,128)S(1)}, u32[]{:S(2)}, u32[]{:S(2)}) %collective-permute-start.23) | collective-permute-done | bytes 4128 | tf_op jit(solution)/shard_map/ppermute | solution.py:338
  67.4 1.9 %shard_map.103 = (f32[19,2048]{1,0:T(8,128)}, f32[8,128]{1,0:T(8,128)}, f32[8,128]{1,0:T(8,128)}) custom-call(s32[4,8]{1,0:T(4,128)S(1)} %get-tuple-element.31.own_cols, s32[4,8]{1,0:T(4,128)S(1)} %collective-permute-done.other_cols, f32[8,4,128,128]{3,2,1,0:T(8,128)S(1)} %copy-done.1, f32[8,4,128,128]{3,2,1,0:T(8,128)S(1)} %collective-permute-done.1.other_ref, ...), custom_call_target="tpu_custom_call" | custom-call | flops 4000000 | bytes 262144 | tf_op jit(solution)/shard_map/pallas_call | solution.py:411
  (49 shorter events, 15.7 us)
Async XLA Ops:
  0.6 21.3 %collective-permute-start.1 = (f32[8,4,128,128]{3,2,1,0:T(8,128)}, f32[8,4,128,128]{3,2,1,0:T(8,128)S(1)}, u32[]{:S(2)}, u32[]{:S(2)}) collective-permute-start(f32[8,4,128,128]{3,2,1,0:T(8,128)} %own_ref.9), channel_id=1, source_target_pairs={{0,1},{1,0},{2,3},{3,2},{4,5},{5,4},{6,7},{7,6},{8,9},{9,8},{10,11... | collective-permute-start | bytes 6291464 | tf_op jit(solution)/shard_map/ppermute | solution.py:355
  3.9 8.1 %collective-permute-start.4 = (f32[8,512]{1,0:T(8,128)S(1)}, f32[8,512]{1,0:T(8,128)S(1)}, u32[]{:S(2)}, u32[]{:S(2)}) collective-permute-start(f32[8,512]{1,0:T(8,128)S(1)} %get-tuple-element.30.payload_ref), channel_id=1, source_target_pairs={{0,8},{2,10},{4,12},{6,14},{8,0},{10,2},{12,4},{14,6},{1,9},{3,11}... | collective-permute-start | bytes 49160 | tf_op jit(solution)/shard_map/ppermute | solution.py:338
  7.5 6.4 %collective-permute-start.3 = (f32[8,512]{1,0:T(8,128)S(1)}, f32[8,512]{1,0:T(8,128)S(1)}, u32[]{:S(2)}, u32[]{:S(2)}) collective-permute-start(f32[8,512]{1,0:T(8,128)S(1)} %get-tuple-element.30.payload_ref), channel_id=1, source_target_pairs={{0,14},{2,4},{4,2},{6,8},{8,6},{10,12},{12,10},{14,0},{1,15},{3,5}... | collective-permute-start | bytes 49160 | tf_op jit(solution)/shard_map/ppermute | solution.py:338
  9.8 4.2 %collective-permute-start.2 = (f32[8,512]{1,0:T(8,128)S(1)}, f32[8,512]{1,0:T(8,128)S(1)}, u32[]{:S(2)}, u32[]{:S(2)}) collective-permute-start(f32[8,512]{1,0:T(8,128)S(1)} %get-tuple-element.30.payload_ref), channel_id=1, source_target_pairs={{0,2},{2,0},{4,6},{6,4},{8,10},{10,8},{12,14},{14,12},{1,3},{3,1},... | collective-permute-start | bytes 49160 | tf_op jit(solution)/shard_map/ppermute | solution.py:338
  14.3 1.2 %collective-permute-start.5 = (f32[8,128]{1,0:T(8,128)S(1)}, f32[8,128]{1,0:T(8,128)S(1)}, u32[]{:S(2)}, u32[]{:S(2)}) collective-permute-start(f32[8,128]{1,0:T(8,128)S(1)} %get-tuple-element.35), channel_id=1, source_target_pairs={{0,1},{1,0},{2,3},{3,2},{4,5},{5,4},{6,7},{7,6},{8,9},{9,8},{10,11... | collective-permute-start | bytes 12296 | tf_op jit(solution)/shard_map/ppermute | solution.py:355
  15.5 3.6 %collective-permute-start.6 = (f32[8,128]{1,0:T(8,128)S(1)}, f32[8,128]{1,0:T(8,128)S(1)}, u32[]{:S(2)}, u32[]{:S(2)}) collective-permute-start(f32[8,128]{1,0:T(8,128)S(1)} %get-tuple-element.59.direction_ref), channel_id=1, source_target_pairs={{0,2},{2,0},{4,6},{6,4},{8,10},{10,8},{12,14},{14,12},{1,15},{3,5}... | collective-permute-start | bytes 12296 | tf_op jit(solution)/shard_map/ppermute | solution.py:349
  19.1 2.9 %collective-permute-start.7 = (f32[8,128]{1,0:T(8,128)S(1)}, f32[8,128]{1,0:T(8,128)S(1)}, u32[]{:S(2)}, u32[]{:S(2)}) collective-permute-start(f32[8,128]{1,0:T(8,128)S(1)} %collective-permute-done.6.mine_ref), channel_id=1, source_target_pairs={{0,1},{1,0},{2,3},{3,2},{4,5},{5,4},{6,7},{7,6},{8,9},{9,8},{10,11... | collective-permute-start | bytes 12296 | tf_op jit(solution)/shard_map/ppermute | solution.py:355
  20.8 1.2 %collective-permute-start = (s32[4,8]{1,0:T(4,128)S(1)}, s32[4,8]{1,0:T(4,128)S(1)}, u32[]{:S(2)}, u32[]{:S(2)}) collective-permute-start(s32[4,8]{1,0:T(4,128)S(1)} %get-tuple-element.31.own_cols), channel_id=1, source_target_pairs={{0,1},{1,0},{2,3},{3,2},{4,5},{5,4},{6,7},{7,6},{8,9},{9,8},{10,11... | collective-permute-start | bytes 392 | tf_op jit(solution)/shard_map/ppermute | solution.py:355
  23.0 3.7 %collective-permute-start.8 = (f32[8,128]{1,0:T(8,128)S(1)}, f32[8,128]{1,0:T(8,128)S(1)}, u32[]{:S(2)}, u32[]{:S(2)}) collective-permute-start(f32[8,128]{1,0:T(8,128)S(1)} %get-tuple-element.39.direction_in), channel_id=1, source_target_pairs={{0,2},{2,0},{4,6},{6,4},{8,10},{10,8},{12,14},{14,12},{1,15},{3,5}... | collective-permute-start | bytes 12296 | tf_op jit(solution)/shard_map/ppermute | solution.py:349
  26.7 2.5 %collective-permute-start.9 = (f32[8,128]{1,0:T(8,128)S(1)}, f32[8,128]{1,0:T(8,128)S(1)}, u32[]{:S(2)}, u32[]{:S(2)}) collective-permute-start(f32[8,128]{1,0:T(8,128)S(1)} %collective-permute-done.8.mine_ref), channel_id=1, source_target_pairs={{0,1},{1,0},{2,3},{3,2},{4,5},{5,4},{6,7},{7,6},{8,9},{9,8},{10,11... | collective-permute-start | bytes 12296 | tf_op jit(solution)/shard_map/ppermute | solution.py:355
  30.3 4.6 %collective-permute-start.12 = (f32[8,128]{1,0:T(8,128)S(1)}, f32[8,128]{1,0:T(8,128)S(1)}, u32[]{:S(2)}, u32[]{:S(2)}) collective-permute-start(f32[8,128]{1,0:T(8,128)S(1)} %shard_map.99.own_estimate), channel_id=1, source_target_pairs={{0,8},{2,10},{4,12},{6,14},{8,0},{10,2},{12,4},{14,6},{1,9},{3,11}... | collective-permute-start | bytes 12296 | tf_op jit(solution)/shard_map/ppermute | solution.py:338
  30.3 6.4 %collective-permute-start.11 = (f32[8,128]{1,0:T(8,128)S(1)}, f32[8,128]{1,0:T(8,128)S(1)}, u32[]{:S(2)}, u32[]{:S(2)}) collective-permute-start(f32[8,128]{1,0:T(8,128)S(1)} %shard_map.99.own_estimate), channel_id=1, source_target_pairs={{0,14},{2,4},{4,2},{6,8},{8,6},{10,12},{12,10},{14,0},{1,15},{3,5}... | collective-permute-start | bytes 12296 | tf_op jit(solution)/shard_map/ppermute | solution.py:338
  32.7 4.0 %collective-permute-start.10 = (f32[8,128]{1,0:T(8,128)S(1)}, f32[8,128]{1,0:T(8,128)S(1)}, u32[]{:S(2)}, u32[]{:S(2)}) collective-permute-start(f32[8,128]{1,0:T(8,128)S(1)} %shard_map.99.own_estimate), channel_id=1, source_target_pairs={{0,2},{2,0},{4,6},{6,4},{8,10},{10,8},{12,14},{14,12},{1,3},{3,1},... | collective-permute-start | bytes 12296 | tf_op jit(solution)/shard_map/ppermute | solution.py:338
  37.7 3.7 %collective-permute-start.13 = (f32[8,128]{1,0:T(8,128)S(1)}, f32[8,128]{1,0:T(8,128)S(1)}, u32[]{:S(2)}, u32[]{:S(2)}) collective-permute-start(f32[8,128]{1,0:T(8,128)S(1)} %get-tuple-element.44), channel_id=1, source_target_pairs={{0,2},{2,0},{4,6},{6,4},{8,10},{10,8},{12,14},{14,12},{1,3},{3,1},... | collective-permute-start | bytes 12296 | tf_op jit(solution)/shard_map/ppermute | solution.py:338
  37.7 6.4 %collective-permute-start.14 = (f32[8,128]{1,0:T(8,128)S(1)}, f32[8,128]{1,0:T(8,128)S(1)}, u32[]{:S(2)}, u32[]{:S(2)}) collective-permute-start(f32[8,128]{1,0:T(8,128)S(1)} %get-tuple-element.45), channel_id=1, source_target_pairs={{0,14},{2,4},{4,2},{6,8},{8,6},{10,12},{12,10},{14,0},{1,15},{3,5}... | collective-permute-start | bytes 12296 | tf_op jit(solution)/shard_map/ppermute | solution.py:338
  40.1 4.5 %collective-permute-start.15 = (f32[8,128]{1,0:T(8,128)S(1)}, f32[8,128]{1,0:T(8,128)S(1)}, u32[]{:S(2)}, u32[]{:S(2)}) collective-permute-start(f32[8,128]{1,0:T(8,128)S(1)} %get-tuple-element.46), channel_id=1, source_target_pairs={{0,8},{2,10},{4,12},{6,14},{8,0},{10,2},{12,4},{14,6},{1,9},{3,11}... | collective-permute-start | bytes 12296 | tf_op jit(solution)/shard_map/ppermute | solution.py:338
  44.6 1.2 %collective-permute-start.16 = (f32[8,128]{1,0:T(8,128)S(1)}, f32[8,128]{1,0:T(8,128)S(1)}, u32[]{:S(2)}, u32[]{:S(2)}) collective-permute-start(f32[8,128]{1,0:T(8,128)S(1)} %add_multiply_fusion), channel_id=1, source_target_pairs={{0,1},{1,0},{2,3},{3,2},{4,5},{5,4},{6,7},{7,6},{8,9},{9,8},{10,11... | collective-permute-start | bytes 12296 | tf_op jit(solution)/shard_map/ppermute | solution.py:355
  45.8 3.6 %collective-permute-start.17 = (f32[8,128]{1,0:T(8,128)S(1)}, f32[8,128]{1,0:T(8,128)S(1)}, u32[]{:S(2)}, u32[]{:S(2)}) collective-permute-start(f32[8,128]{1,0:T(8,128)S(1)} %get-tuple-element.57.direction_in), channel_id=1, source_target_pairs={{0,2},{2,0},{4,6},{6,4},{8,10},{10,8},{12,14},{14,12},{1,15},{3,5}... | collective-permute-start | bytes 12296 | tf_op jit(solution)/shard_map/ppermute | solution.py:349
  49.4 2.5 %collective-permute-start.18 = (f32[8,128]{1,0:T(8,128)S(1)}, f32[8,128]{1,0:T(8,128)S(1)}, u32[]{:S(2)}, u32[]{:S(2)}) collective-permute-start(f32[8,128]{1,0:T(8,128)S(1)} %collective-permute-done.17.mine_ref), channel_id=1, source_target_pairs={{0,1},{1,0},{2,3},{3,2},{4,5},{5,4},{6,7},{7,6},{8,9},{9,8},{10,11... | collective-permute-start | bytes 12296 | tf_op jit(solution)/shard_map/ppermute | solution.py:355
  53.0 3.7 %collective-permute-start.19 = (f32[8,128]{1,0:T(8,128)S(1)}, f32[8,128]{1,0:T(8,128)S(1)}, u32[]{:S(2)}, u32[]{:S(2)}) collective-permute-start(f32[8,128]{1,0:T(8,128)S(1)} %get-tuple-element.47.direction_in), channel_id=1, source_target_pairs={{0,2},{2,0},{4,6},{6,4},{8,10},{10,8},{12,14},{14,12},{1,15},{3,5}... | collective-permute-start | bytes 12296 | tf_op jit(solution)/shard_map/ppermute | solution.py:349
  56.6 2.7 %collective-permute-start.20 = (f32[8,128]{1,0:T(8,128)S(1)}, f32[8,128]{1,0:T(8,128)S(1)}, u32[]{:S(2)}, u32[]{:S(2)}) collective-permute-start(f32[8,128]{1,0:T(8,128)S(1)} %collective-permute-done.19.mine_ref), channel_id=1, source_target_pairs={{0,1},{1,0},{2,3},{3,2},{4,5},{5,4},{6,7},{7,6},{8,9},{9,8},{10,11... | collective-permute-start | bytes 12296 | tf_op jit(solution)/shard_map/ppermute | solution.py:355
  60.4 7.0 %collective-permute-start.22 = (f32[16,128]{1,0:T(8,128)S(1)}, f32[16,128]{1,0:T(8,128)S(1)}, u32[]{:S(2)}, u32[]{:S(2)}) collective-permute-start(f32[16,128]{1,0:T(8,128)S(1)} %get-tuple-element.50.packed_ref), channel_id=1, source_target_pairs={{0,14},{2,4},{4,2},{6,8},{8,6},{10,12},{12,10},{14,0},{1,15},{3,5}... | collective-permute-start | bytes 24584 | tf_op jit(solution)/shard_map/ppermute | solution.py:338
  62.9 4.5 %collective-permute-start.21 = (f32[16,128]{1,0:T(8,128)S(1)}, f32[16,128]{1,0:T(8,128)S(1)}, u32[]{:S(2)}, u32[]{:S(2)}) collective-permute-start(f32[16,128]{1,0:T(8,128)S(1)} %get-tuple-element.50.packed_ref), channel_id=1, source_target_pairs={{0,2},{2,0},{4,6},{6,4},{8,10},{10,8},{12,14},{14,12},{1,3},{3,1},... | collective-permute-start | bytes 24584 | tf_op jit(solution)/shard_map/ppermute | solution.py:338
  62.9 4.5 %collective-permute-start.23 = (f32[8,128]{1,0:T(8,128)S(1)}, f32[8,128]{1,0:T(8,128)S(1)}, u32[]{:S(2)}, u32[]{:S(2)}) collective-permute-start(f32[8,128]{1,0:T(8,128)S(1)} %get-tuple-element.51), channel_id=1, source_target_pairs={{0,8},{2,10},{4,12},{6,14},{8,0},{10,2},{12,4},{14,6},{1,9},{3,11}... | collective-permute-start | bytes 12296 | tf_op jit(solution)/shard_map/ppermute | solution.py:338
  (5 other events, 8.4 us)

commit v7 on v6

--- a/solution.py
+++ b/solution.py
@@ -201,14 +201,13 @@
     peers, slots = nodes_ref.shape
     for k in range(out_ref.shape[1]):
         out_ref[:, k, :] = states_ref[:, k * LANES : (k + 1) * LANES]
-    slot = lax.broadcasted_iota(jnp.int32, (peers, slots), 1)
-    nodes = jnp.where(slot < table_ref[2 * peers :], table_ref[0:peers], -1)
+    nodes = table_ref[0:peers]
     nodes_ref[...] = nodes
     rows, current = ionic_rows([out_ref[i] for i in range(out_ref.shape[0])])
     for i, row in enumerate(rows):
         out_ref[i] = row
     payload_ref[0:peers] = pick_current(current, nodes)
-    payload_ref[peers:] = table_ref[peers : 2 * peers].astype(F32)
+    payload_ref[peers:] = table_ref[peers:].astype(F32)
 
 
 def bring(cols_ref, diag_ref, payload_ref, cols_out, diag_out, payload_out):
@@ -344,9 +343,19 @@
         return swap(value, lambda i: ((i + 1) ^ 1) - 1)
 
     def with_either(value):
-        pairs = [(2 * i, 2 * (i ^ 1)) for i in range(chain)]
-        pairs += [(2 * i + 1, 2 * ((((i + 1) ^ 1) - 1) % chain) + 1) for i in range(chain)]
-        return lax.ppermute(value, ("dom", "sub"), pairs)
+        cases = lax.axis_size("case")
+        ends = (0, chain - 1) if cases % 2 == 0 else ()
+        pairs = []
+        for case in range(cases):
+            for i in range(chain):
+                me = (case * chain + i) * 2
+                pairs.append((me, (case * chain + (i ^ 1)) * 2))
+                if i in ends:
+                    pairs.append((me + 1, ((case ^ 1) * chain + i) * 2 + 1))
+                else:
+                    second = (((i + 1) ^ 1) - 1) % chain
+                    pairs.append((me + 1, (case * chain + second) * 2 + 1))
+        return lax.ppermute(value, ("case", "dom", "sub"), pairs)
 
     def with_far(value):
         return swap(value, lambda i: i + chain // 2)
@@ -363,8 +372,8 @@
     work = (pltpu.VMEM((torso + 2 * HALO, LANES), F32), pltpu.VMEM((torso, LANES), F32))
 
     other_tiles = from_sibling(tile_values)
-    counts = jnp.broadcast_to(send_count[0][:, None], (peers, slots))
-    table = jnp.concatenate([send_node[0], recv_row[0], counts])
+    live = jnp.arange(slots, dtype=jnp.int32)[None, :] < send_count[0][:, None]
+    table = jnp.concatenate([jnp.where(live, send_node[0], -1), recv_row[0]])
     index = shape(peers, slots, dtype=jnp.int32)
     payload = shape(2 * peers, slots)
     states, payload, nodes = call(begin, (dense, payload, index))(in_specs=[VMEM] * 2)(

time: 69.7 us -> 65.1 us (0.934)
  starting transfers between devices: 24.2 us -> 18.1 us
  waiting for transfers between devices: 31.4 us -> 33 us
  local copies, waits for them, and re-layouts: 4.62 us -> 3.89 us
    ppermute x8, starting transfers between devices: 7.59 us -> 1.06 us  [from_sibling(): return lax.ppermute(value, 'sub', [(0, 1), (1, 0)])]
    ppermute x12, waiting for transfers between devices: 14.3 us -> 15.1 us  [swap(): lax.ppermute(value, 'dom', [(i, partner(i) % chain) for i in range(chain)])]
    select_n x0 -> x1, other arithmetic: none -> 0.77 us  [on_device(): table = jnp.concatenate([jnp.where(live, send_node[0], -1), recv_row[0]])]
    concatenate x1 -> x0, local copies, waits for them, and re-layouts: 0.73 us -> none  [on_device(): table = jnp.concatenate([send_node[0], recv_row[0], counts])]
where the time goes in v7:
time: 65.1 us; the launch traced here: 64.8 us
  waiting for transfers between devices  33 us (51%)
  starting transfers between devices  18.1 us (28%)
  Pallas kernels  7.66 us (12%)
  local copies, waits for them, and re-layouts  3.89 us (6%)
  other arithmetic  1.49 us (2%)
  between operations  0.7 us (1%)
    ppermute x12, starting transfers between devices, swap(): lax.ppermute(value, 'dom', [(i, partner(i) % chain) for i in range(chain)])  15.4 us
    ppermute x12, waiting for transfers between devices, swap(): lax.ppermute(value, 'dom', [(i, partner(i) % chain) for i in range(chain)])  15.1 us
    ppermute x4, waiting for transfers between devices, with_either(): return lax.ppermute(value, ('case', 'dom', 'sub'), pairs)  11.3 us
    ppermute x8, waiting for transfers between devices, from_sibling(): return lax.ppermute(value, 'sub', [(0, 1), (1, 0)])  6.63 us
    unnamed x10, local copies, waits for them, and re-layouts  3.89 us
    pallas_call x2, Pallas kernels, on_device(): call(functools.partial(sweep_one, chain), (field,) * 3, work)  2.11 us
    pallas_call x2, Pallas kernels, on_device(): call(functools.partial(sweep_two, chain, last), (field,) * 2 + (packed,)...  2.1 us
    pallas_call x1, Pallas kernels, on_device(): call(functools.partial(finish, chain), (shape(*dense.shape[:1], node_coun...  1.95 us
  transfers between devices with their start and end apart: 24, of which 17 were waited for; matrix products, arithmetic and copies ran while one was open for 2% of the time, Pallas kernels for 1%

profile of v7, /device:TPU:0, one launch (start us, length us, event | category | flops | bytes accessed | tf_op | source)
XLA Modules:
  0.0 64.8 jit_solution(2560311195694169728)
XLA Ops:
  3.8 3.7 %collective-permute-start.4 = (f32[8,512]{1,0:T(8,128)S(1)}, f32[8,512]{1,0:T(8,128)S(1)}, u32[]{:S(2)}, u32[]{:S(2)}) collective-permute-start(f32[8,512]{1,0:T(8,128)S(1)} %get-tuple-element.30.payload_ref), channel_id=1, source_target_pairs={{0,8},{2,10},{4,12},{6,14},{8,0},{10,2},{12,4},{14,6},{1,9},{3,11}... | collective-permute-start | bytes 49160 | tf_op jit(solution)/shard_map/ppermute | solution.py:337
  7.5 2.3 %collective-permute-start.3 = (f32[8,512]{1,0:T(8,128)S(1)}, f32[8,512]{1,0:T(8,128)S(1)}, u32[]{:S(2)}, u32[]{:S(2)}) collective-permute-start(f32[8,512]{1,0:T(8,128)S(1)} %get-tuple-element.30.payload_ref), channel_id=1, source_target_pairs={{0,14},{2,4},{4,2},{6,8},{8,6},{10,12},{12,10},{14,0},{1,15},{3,5}... | collective-permute-start | bytes 49160 | tf_op jit(solution)/shard_map/ppermute | solution.py:337
  11.9 2.0 %collective-permute-done.3.second_ref = f32[8,512]{1,0:T(8,128)S(1)} collective-permute-done((f32[8,512]{1,0:T(8,128)S(1)}, f32[8,512]{1,0:T(8,128)S(1)}, u32[]{:S(2)}, u32[]{:S(2)}) %collective-permute-start.3) | collective-permute-done | bytes 16416 | tf_op jit(solution)/shard_map/ppermute | solution.py:337
  14.2 1.2 %collective-permute-done.5 = f32[8,128]{1,0:T(8,128)S(1)} collective-permute-done((f32[8,128]{1,0:T(8,128)S(1)}, f32[8,128]{1,0:T(8,128)S(1)}, u32[]{:S(2)}, u32[]{:S(2)}) %collective-permute-start.5) | collective-permute-done | bytes 4128 | tf_op jit(solution)/shard_map/ppermute | solution.py:364
  15.8 1.6 %copy-done = f32[8,4,128,128]{3,2,1,0:T(8,128)S(1)} copy-done((f32[8,4,128,128]{3,2,1,0:T(8,128)S(1)}, f32[8,4,128,128]{3,2,1,0:T(8,128)}, u32[]{:S(2)}) %copy-start) | copy-done | bytes 2097176
  17.4 1.7 %collective-permute-done.6.mine_ref = f32[8,128]{1,0:T(8,128)S(1)} collective-permute-done((f32[8,128]{1,0:T(8,128)S(1)}, f32[8,128]{1,0:T(8,128)S(1)}, u32[]{:S(2)}, u32[]{:S(2)}) %collective-permute-start.6) | collective-permute-done | bytes 4128 | tf_op jit(solution)/shard_map/ppermute | solution.py:358
  20.4 1.1 %shard_map.98 = (f32[8,128]{1,0:T(8,128)S(1)}, f32[8,128]{1,0:T(8,128)S(1)}, f32[8,128]{1,0:T(8,128)S(1)}) custom-call(s32[4,8]{1,0:T(4,128)S(1)} %get-tuple-element.31.own_cols, s32[4,8]{1,0:T(4,128)S(1)} %collective-permute-done.other_cols, f32[8,4,128,128]{3,2,1,0:T(8,128)S(1)} %copy-done.1, f32[8,4,128,128]{3,2,1,0:T(8,128)S(1)} %collective-permute-done.1.other_ref, ...), custom_call_target="tpu_custom_call" | custom-call | flops 4000000 | bytes 262144 | tf_op jit(solution)/shard_map/pallas_call | solution.py:397
  21.8 3.3 %collective-permute-done.8.mine_ref = f32[8,128]{1,0:T(8,128)S(1)} collective-permute-done((f32[8,128]{1,0:T(8,128)S(1)}, f32[8,128]{1,0:T(8,128)S(1)}, u32[]{:S(2)}, u32[]{:S(2)}) %collective-permute-start.8) | collective-permute-done | bytes 4128 | tf_op jit(solution)/shard_map/ppermute | solution.py:358
  25.1 1.2 %collective-permute-done.9.yours_ref = f32[8,128]{1,0:T(8,128)S(1)} collective-permute-done((f32[8,128]{1,0:T(8,128)S(1)}, f32[8,128]{1,0:T(8,128)S(1)}, u32[]{:S(2)}, u32[]{:S(2)}) %collective-permute-start.9) | collective-permute-done | bytes 4128 | tf_op jit(solution)/shard_map/ppermute | solution.py:364
  27.3 1.3 %collective-permute-start.12 = (f32[8,128]{1,0:T(8,128)S(1)}, f32[8,128]{1,0:T(8,128)S(1)}, u32[]{:S(2)}, u32[]{:S(2)}) collective-permute-start(f32[8,128]{1,0:T(8,128)S(1)} %shard_map.99.own_estimate), channel_id=1, source_target_pairs={{0,8},{2,10},{4,12},{6,14},{8,0},{10,2},{12,4},{14,6},{1,9},{3,11}... | collective-permute-start | bytes 12296 | tf_op jit(solution)/shard_map/ppermute | solution.py:337
  28.6 1.8 %collective-permute-start.11 = (f32[8,128]{1,0:T(8,128)S(1)}, f32[8,128]{1,0:T(8,128)S(1)}, u32[]{:S(2)}, u32[]{:S(2)}) collective-permute-start(f32[8,128]{1,0:T(8,128)S(1)} %shard_map.99.own_estimate), channel_id=1, source_target_pairs={{0,14},{2,4},{4,2},{6,8},{8,6},{10,12},{12,10},{14,0},{1,15},{3,5}... | collective-permute-start | bytes 12296 | tf_op jit(solution)/shard_map/ppermute | solution.py:337
  30.5 1.4 %collective-permute-done.12.far_estimate = f32[8,128]{1,0:T(8,128)S(1)} collective-permute-done((f32[8,128]{1,0:T(8,128)S(1)}, f32[8,128]{1,0:T(8,128)S(1)}, u32[]{:S(2)}, u32[]{:S(2)}) %collective-permute-start.12) | collective-permute-done | bytes 4128 | tf_op jit(solution)/shard_map/ppermute | solution.py:337
  31.9 3.1 %collective-permute-done.11.second_estimate = f32[8,128]{1,0:T(8,128)S(1)} collective-permute-done((f32[8,128]{1,0:T(8,128)S(1)}, f32[8,128]{1,0:T(8,128)S(1)}, u32[]{:S(2)}, u32[]{:S(2)}) %collective-permute-start.11) | collective-permute-done | bytes 4128 | tf_op jit(solution)/shard_map/ppermute | solution.py:337
  36.0 2.1 %collective-permute-start.14 = (f32[8,128]{1,0:T(8,128)S(1)}, f32[8,128]{1,0:T(8,128)S(1)}, u32[]{:S(2)}, u32[]{:S(2)}) collective-permute-start(f32[8,128]{1,0:T(8,128)S(1)} %get-tuple-element.45), channel_id=1, source_target_pairs={{0,14},{2,4},{4,2},{6,8},{8,6},{10,12},{12,10},{14,0},{1,15},{3,5}... | collective-permute-start | bytes 12296 | tf_op jit(solution)/shard_map/ppermute | solution.py:337
  38.1 1.5 %collective-permute-done.13 = f32[8,128]{1,0:T(8,128)S(1)} collective-permute-done((f32[8,128]{1,0:T(8,128)S(1)}, f32[8,128]{1,0:T(8,128)S(1)}, u32[]{:S(2)}, u32[]{:S(2)}) %collective-permute-start.13) | collective-permute-done | bytes 4128 | tf_op jit(solution)/shard_map/ppermute | solution.py:337
  39.6 2.8 %collective-permute-done.14 = f32[8,128]{1,0:T(8,128)S(1)} collective-permute-done((f32[8,128]{1,0:T(8,128)S(1)}, f32[8,128]{1,0:T(8,128)S(1)}, u32[]{:S(2)}, u32[]{:S(2)}) %collective-permute-start.14) | collective-permute-done | bytes 4128 | tf_op jit(solution)/shard_map/ppermute | solution.py:337
  42.6 1.2 %collective-permute-done.16 = f32[8,128]{1,0:T(8,128)S(1)} collective-permute-done((f32[8,128]{1,0:T(8,128)S(1)}, f32[8,128]{1,0:T(8,128)S(1)}, u32[]{:S(2)}, u32[]{:S(2)}) %collective-permute-start.16) | collective-permute-done | bytes 4128 | tf_op jit(solution)/shard_map/ppermute | solution.py:364
  44.2 3.2 %collective-permute-done.17.mine_ref = f32[8,128]{1,0:T(8,128)S(1)} collective-permute-done((f32[8,128]{1,0:T(8,128)S(1)}, f32[8,128]{1,0:T(8,128)S(1)}, u32[]{:S(2)}, u32[]{:S(2)}) %collective-permute-start.17) | collective-permute-done | bytes 4128 | tf_op jit(solution)/shard_map/ppermute | solution.py:358
  47.4 1.2 %collective-permute-done.18.yours_ref = f32[8,128]{1,0:T(8,128)S(1)} collective-permute-done((f32[8,128]{1,0:T(8,128)S(1)}, f32[8,128]{1,0:T(8,128)S(1)}, u32[]{:S(2)}, u32[]{:S(2)}) %collective-permute-start.18) | collective-permute-done | bytes 4128 | tf_op jit(solution)/shard_map/ppermute | solution.py:364
  50.0 3.2 %collective-permute-done.19.mine_ref = f32[8,128]{1,0:T(8,128)S(1)} collective-permute-done((f32[8,128]{1,0:T(8,128)S(1)}, f32[8,128]{1,0:T(8,128)S(1)}, u32[]{:S(2)}, u32[]{:S(2)}) %collective-permute-start.19) | collective-permute-done | bytes 4128 | tf_op jit(solution)/shard_map/ppermute | solution.py:358
  53.2 1.2 %collective-permute-done.20.yours_ref = f32[8,128]{1,0:T(8,128)S(1)} collective-permute-done((f32[8,128]{1,0:T(8,128)S(1)}, f32[8,128]{1,0:T(8,128)S(1)}, u32[]{:S(2)}, u32[]{:S(2)}) %collective-permute-start.20) | collective-permute-done | bytes 4128 | tf_op jit(solution)/shard_map/ppermute | solution.py:364
  55.5 2.8 %collective-permute-start.22 = (f32[16,128]{1,0:T(8,128)S(1)}, f32[16,128]{1,0:T(8,128)S(1)}, u32[]{:S(2)}, u32[]{:S(2)}) collective-permute-start(f32[16,128]{1,0:T(8,128)S(1)} %get-tuple-element.50.packed_ref), channel_id=1, source_target_pairs={{0,14},{2,4},{4,2},{6,8},{8,6},{10,12},{12,10},{14,0},{1,15},{3,5}... | collective-permute-start | bytes 24584 | tf_op jit(solution)/shard_map/ppermute | solution.py:337
  58.8 4.1 %collective-permute-done.23.far_ref = f32[8,128]{1,0:T(8,128)S(1)} collective-permute-done((f32[8,128]{1,0:T(8,128)S(1)}, f32[8,128]{1,0:T(8,128)S(1)}, u32[]{:S(2)}, u32[]{:S(2)}) %collective-permute-start.23) | collective-permute-done | bytes 4128 | tf_op jit(solution)/shard_map/ppermute | solution.py:337
  62.9 2.0 %shard_map.103 = (f32[19,2048]{1,0:T(8,128)}, f32[8,128]{1,0:T(8,128)}, f32[8,128]{1,0:T(8,128)}) custom-call(s32[4,8]{1,0:T(4,128)S(1)} %get-tuple-element.31.own_cols, s32[4,8]{1,0:T(4,128)S(1)} %collective-permute-done.other_cols, f32[8,4,128,128]{3,2,1,0:T(8,128)S(1)} %copy-done.1, f32[8,4,128,128]{3,2,1,0:T(8,128)S(1)} %collective-permute-done.1.other_ref, ...), custom_call_target="tpu_custom_call" | custom-call | flops 4000000 | bytes 262144 | tf_op jit(solution)/shard_map/pallas_call | solution.py:420
  (49 shorter events, 13.7 us)
Async XLA Ops:
  0.6 19.7 %collective-permute-start.1 = (f32[8,4,128,128]{3,2,1,0:T(8,128)}, f32[8,4,128,128]{3,2,1,0:T(8,128)S(1)}, u32[]{:S(2)}, u32[]{:S(2)}) collective-permute-start(f32[8,4,128,128]{3,2,1,0:T(8,128)} %own_ref.9), channel_id=1, source_target_pairs={{0,1},{1,0},{2,3},{3,2},{4,5},{5,4},{6,7},{7,6},{8,9},{9,8},{10,11... | collective-permute-start | bytes 6291464 | tf_op jit(solution)/shard_map/ppermute | solution.py:364
  3.8 8.1 %collective-permute-start.4 = (f32[8,512]{1,0:T(8,128)S(1)}, f32[8,512]{1,0:T(8,128)S(1)}, u32[]{:S(2)}, u32[]{:S(2)}) collective-permute-start(f32[8,512]{1,0:T(8,128)S(1)} %get-tuple-element.30.payload_ref), channel_id=1, source_target_pairs={{0,8},{2,10},{4,12},{6,14},{8,0},{10,2},{12,4},{14,6},{1,9},{3,11}... | collective-permute-start | bytes 49160 | tf_op jit(solution)/shard_map/ppermute | solution.py:337
  7.5 6.4 %collective-permute-start.3 = (f32[8,512]{1,0:T(8,128)S(1)}, f32[8,512]{1,0:T(8,128)S(1)}, u32[]{:S(2)}, u32[]{:S(2)}) collective-permute-start(f32[8,512]{1,0:T(8,128)S(1)} %get-tuple-element.30.payload_ref), channel_id=1, source_target_pairs={{0,14},{2,4},{4,2},{6,8},{8,6},{10,12},{12,10},{14,0},{1,15},{3,5}... | collective-permute-start | bytes 49160 | tf_op jit(solution)/shard_map/ppermute | solution.py:337
  9.8 4.2 %collective-permute-start.2 = (f32[8,512]{1,0:T(8,128)S(1)}, f32[8,512]{1,0:T(8,128)S(1)}, u32[]{:S(2)}, u32[]{:S(2)}) collective-permute-start(f32[8,512]{1,0:T(8,128)S(1)} %get-tuple-element.30.payload_ref), channel_id=1, source_target_pairs={{0,2},{2,0},{4,6},{6,4},{8,10},{10,8},{12,14},{14,12},{1,3},{3,1},... | collective-permute-start | bytes 49160 | tf_op jit(solution)/shard_map/ppermute | solution.py:337
  14.2 1.2 %collective-permute-start.5 = (f32[8,128]{1,0:T(8,128)S(1)}, f32[8,128]{1,0:T(8,128)S(1)}, u32[]{:S(2)}, u32[]{:S(2)}) collective-permute-start(f32[8,128]{1,0:T(8,128)S(1)} %get-tuple-element.35), channel_id=1, source_target_pairs={{0,1},{1,0},{2,3},{3,2},{4,5},{5,4},{6,7},{7,6},{8,9},{9,8},{10,11... | collective-permute-start | bytes 12296 | tf_op jit(solution)/shard_map/ppermute | solution.py:364
  15.4 3.6 %collective-permute-start.6 = (f32[8,128]{1,0:T(8,128)S(1)}, f32[8,128]{1,0:T(8,128)S(1)}, u32[]{:S(2)}, u32[]{:S(2)}) collective-permute-start(f32[8,128]{1,0:T(8,128)S(1)} %get-tuple-element.59.direction_ref), channel_id=1, source_target_pairs={{0,2},{1,17},{2,0},{3,5},{4,6},{5,3},{6,4},{7,9},{8,10},{9,7},{10,... | collective-permute-start | bytes 12296 | tf_op jit(solution)/shard_map/ppermute | solution.py:358
  19.0 1.3 %collective-permute-start.7 = (f32[8,128]{1,0:T(8,128)S(1)}, f32[8,128]{1,0:T(8,128)S(1)}, u32[]{:S(2)}, u32[]{:S(2)}) collective-permute-start(f32[8,128]{1,0:T(8,128)S(1)} %collective-permute-done.6.mine_ref), channel_id=1, source_target_pairs={{0,1},{1,0},{2,3},{3,2},{4,5},{5,4},{6,7},{7,6},{8,9},{9,8},{10,11... | collective-permute-start | bytes 12296 | tf_op jit(solution)/shard_map/ppermute | solution.py:364
  19.0 1.3 %collective-permute-start = (s32[4,8]{1,0:T(4,128)S(1)}, s32[4,8]{1,0:T(4,128)S(1)}, u32[]{:S(2)}, u32[]{:S(2)}) collective-permute-start(s32[4,8]{1,0:T(4,128)S(1)} %get-tuple-element.31.own_cols), channel_id=1, source_target_pairs={{0,1},{1,0},{2,3},{3,2},{4,5},{5,4},{6,7},{7,6},{8,9},{9,8},{10,11... | collective-permute-start | bytes 392 | tf_op jit(solution)/shard_map/ppermute | solution.py:364
  21.4 3.7 %collective-permute-start.8 = (f32[8,128]{1,0:T(8,128)S(1)}, f32[8,128]{1,0:T(8,128)S(1)}, u32[]{:S(2)}, u32[]{:S(2)}) collective-permute-start(f32[8,128]{1,0:T(8,128)S(1)} %get-tuple-element.39.direction_in), channel_id=1, source_target_pairs={{0,2},{1,17},{2,0},{3,5},{4,6},{5,3},{6,4},{7,9},{8,10},{9,7},{10,... | collective-permute-start | bytes 12296 | tf_op jit(solution)/shard_map/ppermute | solution.py:358
  25.1 1.2 %collective-permute-start.9 = (f32[8,128]{1,0:T(8,128)S(1)}, f32[8,128]{1,0:T(8,128)S(1)}, u32[]{:S(2)}, u32[]{:S(2)}) collective-permute-start(f32[8,128]{1,0:T(8,128)S(1)} %collective-permute-done.8.mine_ref), channel_id=1, source_target_pairs={{0,1},{1,0},{2,3},{3,2},{4,5},{5,4},{6,7},{7,6},{8,9},{9,8},{10,11... | collective-permute-start | bytes 12296 | tf_op jit(solution)/shard_map/ppermute | solution.py:364
  27.3 4.6 %collective-permute-start.12 = (f32[8,128]{1,0:T(8,128)S(1)}, f32[8,128]{1,0:T(8,128)S(1)}, u32[]{:S(2)}, u32[]{:S(2)}) collective-permute-start(f32[8,128]{1,0:T(8,128)S(1)} %shard_map.99.own_estimate), channel_id=1, source_target_pairs={{0,8},{2,10},{4,12},{6,14},{8,0},{10,2},{12,4},{14,6},{1,9},{3,11}... | collective-permute-start | bytes 12296 | tf_op jit(solution)/shard_map/ppermute | solution.py:337
  28.6 6.3 %collective-permute-start.11 = (f32[8,128]{1,0:T(8,128)S(1)}, f32[8,128]{1,0:T(8,128)S(1)}, u32[]{:S(2)}, u32[]{:S(2)}) collective-permute-start(f32[8,128]{1,0:T(8,128)S(1)} %shard_map.99.own_estimate), channel_id=1, source_target_pairs={{0,14},{2,4},{4,2},{6,8},{8,6},{10,12},{12,10},{14,0},{1,15},{3,5}... | collective-permute-start | bytes 12296 | tf_op jit(solution)/shard_map/ppermute | solution.py:337
  30.4 4.5 %collective-permute-start.10 = (f32[8,128]{1,0:T(8,128)S(1)}, f32[8,128]{1,0:T(8,128)S(1)}, u32[]{:S(2)}, u32[]{:S(2)}) collective-permute-start(f32[8,128]{1,0:T(8,128)S(1)} %shard_map.99.own_estimate), channel_id=1, source_target_pairs={{0,2},{2,0},{4,6},{6,4},{8,10},{10,8},{12,14},{14,12},{1,3},{3,1},... | collective-permute-start | bytes 12296 | tf_op jit(solution)/shard_map/ppermute | solution.py:337
  35.9 3.7 %collective-permute-start.13 = (f32[8,128]{1,0:T(8,128)S(1)}, f32[8,128]{1,0:T(8,128)S(1)}, u32[]{:S(2)}, u32[]{:S(2)}) collective-permute-start(f32[8,128]{1,0:T(8,128)S(1)} %get-tuple-element.44), channel_id=1, source_target_pairs={{0,2},{2,0},{4,6},{6,4},{8,10},{10,8},{12,14},{14,12},{1,3},{3,1},... | collective-permute-start | bytes 12296 | tf_op jit(solution)/shard_map/ppermute | solution.py:337
  36.0 6.4 %collective-permute-start.14 = (f32[8,128]{1,0:T(8,128)S(1)}, f32[8,128]{1,0:T(8,128)S(1)}, u32[]{:S(2)}, u32[]{:S(2)}) collective-permute-start(f32[8,128]{1,0:T(8,128)S(1)} %get-tuple-element.45), channel_id=1, source_target_pairs={{0,14},{2,4},{4,2},{6,8},{8,6},{10,12},{12,10},{14,0},{1,15},{3,5}... | collective-permute-start | bytes 12296 | tf_op jit(solution)/shard_map/ppermute | solution.py:337
  38.0 4.5 %collective-permute-start.15 = (f32[8,128]{1,0:T(8,128)S(1)}, f32[8,128]{1,0:T(8,128)S(1)}, u32[]{:S(2)}, u32[]{:S(2)}) collective-permute-start(f32[8,128]{1,0:T(8,128)S(1)} %get-tuple-element.46), channel_id=1, source_target_pairs={{0,8},{2,10},{4,12},{6,14},{8,0},{10,2},{12,4},{14,6},{1,9},{3,11}... | collective-permute-start | bytes 12296 | tf_op jit(solution)/shard_map/ppermute | solution.py:337
  42.6 1.2 %collective-permute-start.16 = (f32[8,128]{1,0:T(8,128)S(1)}, f32[8,128]{1,0:T(8,128)S(1)}, u32[]{:S(2)}, u32[]{:S(2)}) collective-permute-start(f32[8,128]{1,0:T(8,128)S(1)} %add_multiply_fusion), channel_id=1, source_target_pairs={{0,1},{1,0},{2,3},{3,2},{4,5},{5,4},{6,7},{7,6},{8,9},{9,8},{10,11... | collective-permute-start | bytes 12296 | tf_op jit(solution)/shard_map/ppermute | solution.py:364
  43.7 3.6 %collective-permute-start.17 = (f32[8,128]{1,0:T(8,128)S(1)}, f32[8,128]{1,0:T(8,128)S(1)}, u32[]{:S(2)}, u32[]{:S(2)}) collective-permute-start(f32[8,128]{1,0:T(8,128)S(1)} %get-tuple-element.57.direction_in), channel_id=1, source_target_pairs={{0,2},{1,17},{2,0},{3,5},{4,6},{5,3},{6,4},{7,9},{8,10},{9,7},{10,... | collective-permute-start | bytes 12296 | tf_op jit(solution)/shard_map/ppermute | solution.py:358
  47.3 1.2 %collective-permute-start.18 = (f32[8,128]{1,0:T(8,128)S(1)}, f32[8,128]{1,0:T(8,128)S(1)}, u32[]{:S(2)}, u32[]{:S(2)}) collective-permute-start(f32[8,128]{1,0:T(8,128)S(1)} %collective-permute-done.17.mine_ref), channel_id=1, source_target_pairs={{0,1},{1,0},{2,3},{3,2},{4,5},{5,4},{6,7},{7,6},{8,9},{9,8},{10,11... | collective-permute-start | bytes 12296 | tf_op jit(solution)/shard_map/ppermute | solution.py:364
  49.6 3.7 %collective-permute-start.19 = (f32[8,128]{1,0:T(8,128)S(1)}, f32[8,128]{1,0:T(8,128)S(1)}, u32[]{:S(2)}, u32[]{:S(2)}) collective-permute-start(f32[8,128]{1,0:T(8,128)S(1)} %get-tuple-element.47.direction_in), channel_id=1, source_target_pairs={{0,2},{1,17},{2,0},{3,5},{4,6},{5,3},{6,4},{7,9},{8,10},{9,7},{10,... | collective-permute-start | bytes 12296 | tf_op jit(solution)/shard_map/ppermute | solution.py:358
  53.2 1.2 %collective-permute-start.20 = (f32[8,128]{1,0:T(8,128)S(1)}, f32[8,128]{1,0:T(8,128)S(1)}, u32[]{:S(2)}, u32[]{:S(2)}) collective-permute-start(f32[8,128]{1,0:T(8,128)S(1)} %collective-permute-done.19.mine_ref), channel_id=1, source_target_pairs={{0,1},{1,0},{2,3},{3,2},{4,5},{5,4},{6,7},{7,6},{8,9},{9,8},{10,11... | collective-permute-start | bytes 12296 | tf_op jit(solution)/shard_map/ppermute | solution.py:364
  55.5 7.4 %collective-permute-start.22 = (f32[16,128]{1,0:T(8,128)S(1)}, f32[16,128]{1,0:T(8,128)S(1)}, u32[]{:S(2)}, u32[]{:S(2)}) collective-permute-start(f32[16,128]{1,0:T(8,128)S(1)} %get-tuple-element.50.packed_ref), channel_id=1, source_target_pairs={{0,14},{2,4},{4,2},{6,8},{8,6},{10,12},{12,10},{14,0},{1,15},{3,5}... | collective-permute-start | bytes 24584 | tf_op jit(solution)/shard_map/ppermute | solution.py:337
  58.2 4.7 %collective-permute-start.21 = (f32[16,128]{1,0:T(8,128)S(1)}, f32[16,128]{1,0:T(8,128)S(1)}, u32[]{:S(2)}, u32[]{:S(2)}) collective-permute-start(f32[16,128]{1,0:T(8,128)S(1)} %get-tuple-element.50.packed_ref), channel_id=1, source_target_pairs={{0,2},{2,0},{4,6},{6,4},{8,10},{10,8},{12,14},{14,12},{1,3},{3,1},... | collective-permute-start | bytes 24584 | tf_op jit(solution)/shard_map/ppermute | solution.py:337
  58.4 4.5 %collective-permute-start.23 = (f32[8,128]{1,0:T(8,128)S(1)}, f32[8,128]{1,0:T(8,128)S(1)}, u32[]{:S(2)}, u32[]{:S(2)}) collective-permute-start(f32[8,128]{1,0:T(8,128)S(1)} %get-tuple-element.51), channel_id=1, source_target_pairs={{0,8},{2,10},{4,12},{6,14},{8,0},{10,2},{12,4},{14,6},{1,9},{3,11}... | collective-permute-start | bytes 12296 | tf_op jit(solution)/shard_map/ppermute | solution.py:337
  (5 other events, 6.9 us)

commit v8 on v7

--- a/solution.py
+++ b/solution.py
@@ -43,7 +43,6 @@
     _ratio = _next
 
 VMEM = pl.BlockSpec(memory_space=pltpu.VMEM)
-SMEM = pl.BlockSpec(memory_space=pltpu.SMEM)
 F32 = jnp.float32
 
 
@@ -110,15 +109,18 @@
     return jnp.concatenate(out, axis=1)
 
 
+def three_parts(value):
+    first = value.astype(jnp.bfloat16).astype(F32)
+    rest = value - first
+    second = rest.astype(jnp.bfloat16).astype(F32)
+    return first, second, rest - second
+
+
 def scatter(values, index, rows):
     slots = values.shape[1]
     high, low = index >> 7, index & (LANES - 1)
-    first = values.astype(jnp.bfloat16).astype(F32)
-    rest = values - first
-    second = rest.astype(jnp.bfloat16).astype(F32)
-    third = rest - second
     mine = lax.broadcasted_iota(jnp.int32, (rows, slots), 0) == high
-    left = jnp.concatenate([jnp.where(mine, part, 0.0) for part in (first, second, third)], axis=0)
+    left = jnp.concatenate([jnp.where(mine, part, 0.0) for part in three_parts(values)], axis=0)
     spread = lax.broadcasted_iota(jnp.int32, (LANES, slots), 0) == low
     right = jnp.where(spread, 1.0, 0.0).astype(jnp.bfloat16)
     sums = lax.dot_general(
@@ -175,19 +177,24 @@
     return total
 
 
-def product(own_ref, other_ref, own_cols, other_cols, window_ref, out_ref):
+def product(own_ref, other_ref, pick_ref, window):
     tiles, slots = own_ref.shape[0], own_ref.shape[1]
+    parts = jnp.concatenate(three_parts(window), axis=1).astype(jnp.bfloat16)
+    picked = jnp.dot(pick_ref[...].astype(jnp.bfloat16), parts, preferred_element_type=F32)
+    picked = picked[:, :LANES] + picked[:, LANES : 2 * LANES] + picked[:, 2 * LANES :]
     eye = lax.broadcasted_iota(jnp.int32, (LANES, LANES), 0) == lax.broadcasted_iota(
         jnp.int32, (LANES, LANES), 1
     )
+    rows = []
     for t in range(tiles):
         total = None
-        for ref, cols in ((own_ref, own_cols), (other_ref, other_cols)):
-            for k in range(slots):
-                term = ref[t, k] * window_ref[pl.ds(cols[k, t], 1), :]
-                total = term if total is None else total + term
+        for k in range(2 * slots):
+            tile = own_ref[t, k] if k < slots else other_ref[t, k - slots]
+            term = tile * picked[k * tiles + t : k * tiles + t + 1]
+            total = term if total is None else total + term
         column = jnp.sum(total, axis=1, keepdims=True)
-        out_ref[t : t + 1, :] = jnp.sum(jnp.where(eye, column, 0.0), axis=0, keepdims=True)
+        rows.append(jnp.sum(jnp.where(eye, column, 0.0), axis=0, keepdims=True))
+    return jnp.concatenate(rows, axis=0)
 
 
 def fetch(pairs, sems):
@@ -201,13 +208,15 @@
     peers, slots = nodes_ref.shape
     for k in range(out_ref.shape[1]):
         out_ref[:, k, :] = states_ref[:, k * LANES : (k + 1) * LANES]
-    nodes = table_ref[0:peers]
-    nodes_ref[...] = nodes
+    slot = lax.broadcasted_iota(jnp.int32, (1, slots), 1)
+    for o in range(peers):
+        live = slot < table_ref[2 * peers : 2 * peers + 1, o : o + 1]
+        nodes_ref[o : o + 1] = jnp.where(live, table_ref[o : o + 1], -1)
     rows, current = ionic_rows([out_ref[i] for i in range(out_ref.shape[0])])
     for i, row in enumerate(rows):
         out_ref[i] = row
-    payload_ref[0:peers] = pick_current(current, nodes)
-    payload_ref[peers:] = table_ref[peers:].astype(F32)
+    payload_ref[0:peers] = pick_current(current, nodes_ref[...])
+    payload_ref[peers:] = table_ref[peers : 2 * peers].astype(F32)
 
 
 def bring(cols_ref, diag_ref, payload_ref, cols_out, diag_out, payload_out):
@@ -216,13 +225,22 @@
     payload_out[...] = payload_ref[...]
 
 
-def bring_tiles(tiles_ref, direction_ref, direction_out):
+def bring_tiles(tiles_ref, own_cols, other_cols, direction_ref, direction_out, pick_ref):
     direction_out[...] = direction_ref[...]
+    slots, tiles = own_cols.shape
+    eye = lax.broadcasted_iota(jnp.int32, (tiles, tiles), 0) == lax.broadcasted_iota(
+        jnp.int32, (tiles, tiles), 1
+    )
+    place = lax.broadcasted_iota(jnp.int32, (tiles, pick_ref.shape[1]), 1)
+    for k in range(2 * slots):
+        row = own_cols[k : k + 1] if k < slots else other_cols[k - slots : k - slots + 1]
+        column = jnp.sum(jnp.where(eye, row.astype(F32), 0.0), axis=1, keepdims=True)
+        pick_ref[k * tiles : (k + 1) * tiles] = jnp.where(place == column.astype(jnp.int32), 1.0, 0.0)
     del tiles_ref
 
 
 def first_forcing(
-    nodes_ref, table_ref, own_ref, first_ref, second_ref, far_ref,
+    nodes_ref, table_ref, own_ref, first_ref, far_ref, second_ref,
     maps_ref, forcing_ref,
 ):
     peers = nodes_ref.shape[0]
@@ -239,7 +257,7 @@
 
 
 def next_shares(
-    states_ref, own_estimate, first_estimate, second_estimate, far_estimate, nodes_ref, maps_ref,
+    states_ref, own_estimate, first_estimate, far_estimate, second_estimate, nodes_ref, maps_ref,
     out_ref, own_ref, first_ref, second_ref, far_ref,
 ):
     nodes, maps = nodes_ref[...], maps_ref[...]
@@ -255,25 +273,25 @@
     spread_current(outgoing, maps, own_ref, first_ref, second_ref, far_ref)
 
 
-def fill_window(chain, direction, first, second, window_ref):
+def window_of(chain, direction, first, second):
     torso = direction.shape[0]
     here = lax.axis_index("dom")
     after, before = by_side(first, second)
-    window_ref[0:HALO] = jnp.where(here > 0, before[torso - HALO :], 0.0)
-    window_ref[HALO : HALO + torso] = direction
-    window_ref[HALO + torso : 2 * HALO + torso] = jnp.where(here < chain - 1, after[0:HALO], 0.0)
+    before = jnp.where(here > 0, before[torso - HALO :], 0.0)
+    after = jnp.where(here < chain - 1, after[0:HALO], 0.0)
+    filler = jnp.zeros((torso - 2 * HALO, LANES), F32)
+    return jnp.concatenate([before, direction, after, filler], axis=0)
 
 
 def sweep_one(
-    chain, own_cols, other_cols, own_ref, other_ref, mine_ref, yours_ref, forcing_ref,
-    direction_in, diag_ref, residual_ref, direction_ref, estimate_ref, window_ref, product_ref,
+    chain, own_ref, other_ref, pick_ref, mine_ref, yours_ref, forcing_ref, direction_in, diag_ref,
+    residual_ref, direction_ref, estimate_ref,
 ):
     diag = diag_ref[...]
     direction = direction_in[...]
-    first, second = by_partner(mine_ref[...], yours_ref[...])
-    fill_window(chain, direction, first, second, window_ref)
-    product(own_ref, other_ref, own_cols, other_cols, window_ref, product_ref)
-    residual = forcing_ref[...] - (diag * direction + product_ref[...])
+    window = window_of(chain, direction, *by_partner(mine_ref[...], yours_ref[...]))
+    moved = product(own_ref, other_ref, pick_ref, window)
+    residual = forcing_ref[...] - (diag * direction + moved)
     estimate = direction
     direction = KEEP[0] * direction + PULL[0] * (residual / diag)
     residual_ref[...] = residual
@@ -282,31 +300,29 @@
 
 
 def sweep_two(
-    chain, last, own_cols, other_cols, own_ref, other_ref, mine_ref, yours_ref, direction_in,
-    residual_in, estimate_in, diag_ref, *refs,
+    chain, last, own_ref, other_ref, pick_ref, mine_ref, yours_ref, direction_in, residual_in,
+    estimate_in, diag_ref, estimate_ref, *refs,
 ):
-    estimate_ref, window_ref, product_ref = refs[0], refs[-2], refs[-1]
     torso = estimate_ref.shape[0]
     diag = diag_ref[...]
     direction = direction_in[...]
-    first, second = by_partner(mine_ref[...], yours_ref[...])
-    fill_window(chain, direction, first, second, window_ref)
-    product(own_ref, other_ref, own_cols, other_cols, window_ref, product_ref)
-    residual = residual_in[...] - (diag * direction + product_ref[...])
+    window = window_of(chain, direction, *by_partner(mine_ref[...], yours_ref[...]))
+    moved = product(own_ref, other_ref, pick_ref, window)
+    residual = residual_in[...] - (diag * direction + moved)
     direction = KEEP[1] * direction + PULL[1] * (residual / diag)
     estimate = estimate_in[...] + direction
-    estimate_ref[...] = estimate
     if last:
-        residual_ref, packed_ref = refs[1:-2]
+        residual_ref, = refs
         residual_ref[...] = residual
-        packed_ref[0:torso] = estimate
-        packed_ref[torso : 2 * torso] = direction
+        estimate_ref[0 : torso // 2] = estimate
+        estimate_ref[torso // 2 :] = direction
+    else:
+        estimate_ref[...] = estimate
 
 
 def finish(
-    chain, own_cols, other_cols, own_ref, other_ref, first_ref, second_ref, packed_ref, far_ref,
-    residual_in, diag_ref, states_ref, nodes_ref, maps_ref,
-    out_ref, potential_ref, residual_ref, window_ref, product_ref, dense_ref,
+    chain, own_ref, other_ref, pick_ref, packed_ref, first_ref, far_ref, second_ref, residual_in,
+    diag_ref, states_ref, nodes_ref, maps_ref, out_ref, potential_ref, residual_ref, dense_ref,
 ):
     torso = residual_ref.shape[0]
     head, tail = slice(0, torso), slice(torso, 2 * torso)
@@ -314,16 +330,16 @@
     potential_ref[...] = estimate
     after, before = by_side(first_ref[head], second_ref[head])
     feedback = feedback_of(
-        [estimate, after, before, far_ref[...]], nodes_ref[...], maps_ref[...],
+        [estimate, after, before, far_ref[head]], nodes_ref[...], maps_ref[...],
         states_ref.shape[1],
     )
     dense_ref[...] = states_ref[...]
     dense_ref[0] = states_ref[0] + TIME_STEP * FEEDBACK_RATE * feedback
     for k in range(states_ref.shape[1]):
         out_ref[:, k * LANES : (k + 1) * LANES] = dense_ref[:, k, :]
-    fill_window(chain, direction, first_ref[tail], second_ref[tail], window_ref)
-    product(own_ref, other_ref, own_cols, other_cols, window_ref, product_ref)
-    residual_ref[...] = residual_in[...] - (diag_ref[...] * direction + product_ref[...])
+    window = window_of(chain, direction, first_ref[tail], second_ref[tail])
+    moved = product(own_ref, other_ref, pick_ref, window)
+    residual_ref[...] = residual_in[...] - (diag_ref[...] * direction + moved)
 
 
 def on_device(states, send_node, send_count, recv_row, columns, tile_values, diagonal):
@@ -369,11 +385,9 @@
     dense = shape(states.shape[0], heart, LANES)
     field = shape(torso, LANES)
     packed = shape(2 * torso, LANES)
-    work = (pltpu.VMEM((torso + 2 * HALO, LANES), F32), pltpu.VMEM((torso, LANES), F32))
-
     other_tiles = from_sibling(tile_values)
-    live = jnp.arange(slots, dtype=jnp.int32)[None, :] < send_count[0][:, None]
-    table = jnp.concatenate([jnp.where(live, send_node[0], -1), recv_row[0]])
+    counts = jnp.pad(send_count, ((0, 0), (0, slots - peers)))
+    table = jnp.concatenate([send_node[0], recv_row[0], counts])
     index = shape(peers, slots, dtype=jnp.int32)
     payload = shape(2 * peers, slots)
     states, payload, nodes = call(begin, (dense, payload, index))(in_specs=[VMEM] * 2)(
@@ -382,9 +396,9 @@
     columns, diag, own = call(
         bring, (shape(*columns.shape[::-1], dtype=jnp.int32), field, payload)
     )(in_specs=[VMEM] * 3)(columns.T, diagonal.reshape(torso, LANES), payload)
-    stored = (columns, from_sibling(columns), tile_values, other_tiles)
+    first, far, second = with_first(payload), with_far(payload), with_second(payload)
     maps, forcing = call(first_forcing, (index, field))(in_specs=[VMEM] * 6)(
-        nodes, table, own, with_first(payload), with_second(payload), with_far(payload)
+        nodes, table, own, first, far, second
     )
     for time_step in range(2):
         last = time_step == 1
@@ -392,38 +406,35 @@
         direction = forcing / (CHEB_THETA * diag)
         halo = with_either(direction)
         if not last:
-            direction = call(bring_tiles, field)(in_specs=[VMEM] * 2)(tile_values, direction)
+            choices = 2 * columns.shape[0] * torso
+            direction, pick = call(bring_tiles, (field, shape(choices, 2 * torso)))(
+                in_specs=[VMEM] * 4
+            )(tile_values, columns, from_sibling(columns), direction)
             halo, direction = lax.optimization_barrier((halo, direction))
+            stored = (tile_values, other_tiles, pick)
         residual, direction, estimate = call(
-            functools.partial(sweep_one, chain), (field,) * 3, work
-        )(in_specs=[SMEM] * 2 + [VMEM] * 7)(
-            *stored, halo, from_sibling(halo), forcing, direction, diag
-        )
+            functools.partial(sweep_one, chain), (field,) * 3
+        )(in_specs=[VMEM] * 8)(*stored, halo, from_sibling(halo), forcing, direction, diag)
         halo = with_either(direction)
-        estimate, *rest = call(
-            functools.partial(sweep_two, chain, last),
-            (field,) * 2 + (packed,) if last else (field,),
-            work,
-        )(in_specs=[SMEM] * 2 + [VMEM] * 8)(
+        swept = call(
+            functools.partial(sweep_two, chain, last), (packed, field) if last else field
+        )(in_specs=[VMEM] * 9)(
             *stored, halo, from_sibling(halo), direction, residual, estimate, diag
         )
+        estimate, residual = swept if last else (swept, None)
+        first, far, second = with_first(estimate), with_far(estimate), with_second(estimate)
         if not last:
-            states, own, first, second, far = call(next_shares, (dense,) + (field,) * 4)(
+            states, own, *shares = call(next_shares, (dense,) + (field,) * 4)(
                 in_specs=[VMEM] * 7
-            )(
-                states, estimate, with_first(estimate), with_second(estimate), with_far(estimate),
-                nodes, maps,
-            )
-            forcing = own + with_first(first) + with_second(second) + with_far(far)
+            )(states, estimate, first, far, second, nodes, maps)
+            forcing = own + with_second(shares[1]) + with_far(shares[2]) + with_first(shares[0])
             forcing = TORSO_COUPLING * forcing
-    residual, both = rest
     new_states, potential, residual = call(
         functools.partial(finish, chain),
         (shape(*dense.shape[:1], node_count), field, field),
-        work + (pltpu.VMEM(dense.shape, F32),),
-    )(in_specs=[SMEM] * 2 + [VMEM] * 11)(
-        *stored, with_first(both), with_second(both), both, with_far(estimate), residual, diag,
-        states, nodes, maps,
+        (pltpu.VMEM(dense.shape, F32),),
+    )(in_specs=[VMEM] * 12)(
+        *stored, estimate, first, far, second, residual, diag, states, nodes, maps
     )
     return new_states, potential.reshape(-1), residual.reshape(-1)
 

time: 65.1 us -> 61.8 us (0.949)
  waiting for transfers between devices: 33 us -> 30 us
  starting transfers between devices: 18.1 us -> 20.9 us
  Pallas kernels: 7.66 us -> 5.24 us
  other arithmetic: 1.49 us -> 0.76 us
    ppermute x12, waiting for transfers between devices: 15.1 us -> 13 us  [swap(): lax.ppermute(value, 'dom', [(i, partner(i) % chain) for i in range(chain)])]
    pallas_call x5, Pallas kernels: 4.22 us -> 2.29 us  [the longest x2 1.1 us: on_device(): call(functools.partial(sweep_one, chain), (field,) * 3)(in_specs=[VMEM] * 8)]
    ppermute x12, starting transfers between devices: 15.4 us -> 17.1 us  [swap(): lax.ppermute(value, 'dom', [(i, partner(i) % chain) for i in range(chain)])]
    ppermute x4, waiting for transfers between devices: 11.3 us -> 9.62 us  [with_either(): return lax.ppermute(value, ('case', 'dom', 'sub'), pairs)]
    ppermute x8, starting transfers between devices: 1.06 us -> 2.18 us  [from_sibling(): return lax.ppermute(value, 'sub', [(0, 1), (1, 0)])]
    ppermute x8, waiting for transfers between devices: 6.63 us -> 7.46 us  [from_sibling(): return lax.ppermute(value, 'sub', [(0, 1), (1, 0)])]
    select_n x1 -> x0, other arithmetic: 0.77 us -> none  [on_device(): table = jnp.concatenate([jnp.where(live, send_node[0], -1), recv_row[0]])]
  transfers between devices with their start and end apart: 24 -> 24, of which waited for: 17 -> 19; matrix products, arithmetic and copies ran while one was open for 2% -> 1% of each run, Pallas kernels for 1% -> 1%
where the time goes in v8:
time: 61.8 us; the launch traced here: 61.5 us
  waiting for transfers between devices  30 us (49%)
  starting transfers between devices  20.9 us (34%)
  Pallas kernels  5.24 us (8%)
  local copies, waits for them, and re-layouts  3.88 us (6%)
  other arithmetic  0.76 us (1%)
  between operations  0.71 us (1%)
    ppermute x12, starting transfers between devices, swap(): lax.ppermute(value, 'dom', [(i, partner(i) % chain) for i in range(chain)])  17.1 us
    ppermute x12, waiting for transfers between devices, swap(): lax.ppermute(value, 'dom', [(i, partner(i) % chain) for i in range(chain)])  13 us
    ppermute x4, waiting for transfers between devices, with_either(): return lax.ppermute(value, ('case', 'dom', 'sub'), pairs)  9.62 us
    ppermute x8, waiting for transfers between devices, from_sibling(): return lax.ppermute(value, 'sub', [(0, 1), (1, 0)])  7.46 us
    unnamed x10, local copies, waits for them, and re-layouts  3.88 us
    ppermute x8, starting transfers between devices, from_sibling(): return lax.ppermute(value, 'sub', [(0, 1), (1, 0)])  2.18 us
    ppermute x4, starting transfers between devices, with_either(): return lax.ppermute(value, ('case', 'dom', 'sub'), pairs)  1.54 us
    pallas_call x1, Pallas kernels, on_device(): call(functools.partial(finish, chain), (shape(*dense.shape[:1], node_coun...  1.45 us
  transfers between devices with their start and end apart: 24, of which 19 were waited for; matrix products, arithmetic and copies ran while one was open for 1% of the time, Pallas kernels for 1%

profile of v8, /device:TPU:0, one launch (start us, length us, event | category | flops | bytes accessed | tf_op | source)
XLA Modules:
  0.0 61.5 jit_solution(13793489379455626049)
XLA Ops:
  3.1 5.6 %collective-permute-start.4 = (f32[8,512]{1,0:T(8,128)S(1)}, f32[8,512]{1,0:T(8,128)S(1)}, u32[]{:S(2)}, u32[]{:S(2)}) collective-permute-start(f32[8,512]{1,0:T(8,128)S(1)} %get-tuple-element.31.payload_ref), channel_id=1, source_target_pairs={{0,14},{2,4},{4,2},{6,8},{8,6},{10,12},{12,10},{14,0},{1,15},{3,5}... | collective-permute-start | bytes 49160 | tf_op jit(solution)/shard_map/ppermute | solution.py:353
  8.7 1.1 %collective-permute-start.2 = (f32[8,512]{1,0:T(8,128)S(1)}, f32[8,512]{1,0:T(8,128)S(1)}, u32[]{:S(2)}, u32[]{:S(2)}) collective-permute-start(f32[8,512]{1,0:T(8,128)S(1)} %get-tuple-element.31.payload_ref), channel_id=1, source_target_pairs={{0,2},{2,0},{4,6},{6,4},{8,10},{10,8},{12,14},{14,12},{1,3},{3,1},... | collective-permute-start | bytes 49160 | tf_op jit(solution)/shard_map/ppermute | solution.py:353
  11.2 2.2 %collective-permute-done.3.far_ref = f32[8,512]{1,0:T(8,128)S(1)} collective-permute-done((f32[8,512]{1,0:T(8,128)S(1)}, f32[8,512]{1,0:T(8,128)S(1)}, u32[]{:S(2)}, u32[]{:S(2)}) %collective-permute-start.3) | collective-permute-done | bytes 16416 | tf_op jit(solution)/shard_map/ppermute | solution.py:353
  13.7 1.2 %collective-permute-done.5 = f32[8,128]{1,0:T(8,128)S(1)} collective-permute-done((f32[8,128]{1,0:T(8,128)S(1)}, f32[8,128]{1,0:T(8,128)S(1)}, u32[]{:S(2)}, u32[]{:S(2)}) %collective-permute-start.5) | collective-permute-done | bytes 4128 | tf_op jit(solution)/shard_map/ppermute | solution.py:380
  15.0 1.2 %collective-permute-start.1 = (s32[4,8]{1,0:T(4,128)S(1)}, s32[4,8]{1,0:T(4,128)S(1)}, u32[]{:S(2)}, u32[]{:S(2)}) collective-permute-start(s32[4,8]{1,0:T(4,128)S(1)} %get-tuple-element.32.own_cols), channel_id=1, source_target_pairs={{0,1},{1,0},{2,3},{3,2},{4,5},{5,4},{6,7},{7,6},{8,9},{9,8},{10,11... | collective-permute-start | bytes 392 | tf_op jit(solution)/shard_map/ppermute | solution.py:380
  17.1 1.6 %copy-done = f32[8,4,128,128]{3,2,1,0:T(8,128)S(1)} copy-done((f32[8,4,128,128]{3,2,1,0:T(8,128)S(1)}, f32[8,4,128,128]{3,2,1,0:T(8,128)}, u32[]{:S(2)}) %copy-start) | copy-done | bytes 2097176
  20.6 1.0 %collective-permute-start.8 = (f32[8,128]{1,0:T(8,128)S(1)}, f32[8,128]{1,0:T(8,128)S(1)}, u32[]{:S(2)}, u32[]{:S(2)}) collective-permute-start(f32[8,128]{1,0:T(8,128)S(1)} %get-tuple-element.42.direction_in), channel_id=1, source_target_pairs={{0,2},{1,17},{2,0},{3,5},{4,6},{5,3},{6,4},{7,9},{8,10},{9,7},{10,... | collective-permute-start | bytes 12296 | tf_op jit(solution)/shard_map/ppermute | solution.py:374
  21.6 2.7 %collective-permute-done.8.mine_ref = f32[8,128]{1,0:T(8,128)S(1)} collective-permute-done((f32[8,128]{1,0:T(8,128)S(1)}, f32[8,128]{1,0:T(8,128)S(1)}, u32[]{:S(2)}, u32[]{:S(2)}) %collective-permute-start.8) | collective-permute-done | bytes 4128 | tf_op jit(solution)/shard_map/ppermute | solution.py:374
  24.3 1.2 %collective-permute-done.9.yours_ref = f32[8,128]{1,0:T(8,128)S(1)} collective-permute-done((f32[8,128]{1,0:T(8,128)S(1)}, f32[8,128]{1,0:T(8,128)S(1)}, u32[]{:S(2)}, u32[]{:S(2)}) %collective-permute-start.9) | collective-permute-done | bytes 4128 | tf_op jit(solution)/shard_map/ppermute | solution.py:380
  26.0 1.9 %collective-permute-start.12 = (f32[8,128]{1,0:T(8,128)S(1)}, f32[8,128]{1,0:T(8,128)S(1)}, u32[]{:S(2)}, u32[]{:S(2)}) collective-permute-start(f32[8,128]{1,0:T(8,128)S(1)} %shard_map.99.own_estimate), channel_id=1, source_target_pairs={{0,14},{2,4},{4,2},{6,8},{8,6},{10,12},{12,10},{14,0},{1,15},{3,5}... | collective-permute-start | bytes 12296 | tf_op jit(solution)/shard_map/ppermute | solution.py:353
  27.9 1.6 %collective-permute-start.11 = (f32[8,128]{1,0:T(8,128)S(1)}, f32[8,128]{1,0:T(8,128)S(1)}, u32[]{:S(2)}, u32[]{:S(2)}) collective-permute-start(f32[8,128]{1,0:T(8,128)S(1)} %shard_map.99.own_estimate), channel_id=1, source_target_pairs={{0,8},{2,10},{4,12},{6,14},{8,0},{10,2},{12,4},{14,6},{1,9},{3,11}... | collective-permute-start | bytes 12296 | tf_op jit(solution)/shard_map/ppermute | solution.py:353
  29.5 2.9 %collective-permute-done.12.second_estimate = f32[8,128]{1,0:T(8,128)S(1)} collective-permute-done((f32[8,128]{1,0:T(8,128)S(1)}, f32[8,128]{1,0:T(8,128)S(1)}, u32[]{:S(2)}, u32[]{:S(2)}) %collective-permute-start.12) | collective-permute-done | bytes 4128 | tf_op jit(solution)/shard_map/ppermute | solution.py:353
  34.1 2.3 %collective-permute-start.13 = (f32[8,128]{1,0:T(8,128)S(1)}, f32[8,128]{1,0:T(8,128)S(1)}, u32[]{:S(2)}, u32[]{:S(2)}) collective-permute-start(f32[8,128]{1,0:T(8,128)S(1)} %get-tuple-element.47), channel_id=1, source_target_pairs={{0,14},{2,4},{4,2},{6,8},{8,6},{10,12},{12,10},{14,0},{1,15},{3,5}... | collective-permute-start | bytes 12296 | tf_op jit(solution)/shard_map/ppermute | solution.py:353
  36.4 1.1 %collective-permute-start.14 = (f32[8,128]{1,0:T(8,128)S(1)}, f32[8,128]{1,0:T(8,128)S(1)}, u32[]{:S(2)}, u32[]{:S(2)}) collective-permute-start(f32[8,128]{1,0:T(8,128)S(1)} %get-tuple-element.48), channel_id=1, source_target_pairs={{0,8},{2,10},{4,12},{6,14},{8,0},{10,2},{12,4},{14,6},{1,9},{3,11}... | collective-permute-start | bytes 12296 | tf_op jit(solution)/shard_map/ppermute | solution.py:353
  37.5 2.9 %collective-permute-done.13 = f32[8,128]{1,0:T(8,128)S(1)} collective-permute-done((f32[8,128]{1,0:T(8,128)S(1)}, f32[8,128]{1,0:T(8,128)S(1)}, u32[]{:S(2)}, u32[]{:S(2)}) %collective-permute-start.13) | collective-permute-done | bytes 4128 | tf_op jit(solution)/shard_map/ppermute | solution.py:353
  41.1 1.2 %collective-permute-done.16 = f32[8,128]{1,0:T(8,128)S(1)} collective-permute-done((f32[8,128]{1,0:T(8,128)S(1)}, f32[8,128]{1,0:T(8,128)S(1)}, u32[]{:S(2)}, u32[]{:S(2)}) %collective-permute-start.16) | collective-permute-done | bytes 4128 | tf_op jit(solution)/shard_map/ppermute | solution.py:380
  42.4 3.5 %collective-permute-done.17.mine_ref = f32[8,128]{1,0:T(8,128)S(1)} collective-permute-done((f32[8,128]{1,0:T(8,128)S(1)}, f32[8,128]{1,0:T(8,128)S(1)}, u32[]{:S(2)}, u32[]{:S(2)}) %collective-permute-start.17) | collective-permute-done | bytes 4128 | tf_op jit(solution)/shard_map/ppermute | solution.py:374
  45.9 1.2 %collective-permute-done.18.yours_ref = f32[8,128]{1,0:T(8,128)S(1)} collective-permute-done((f32[8,128]{1,0:T(8,128)S(1)}, f32[8,128]{1,0:T(8,128)S(1)}, u32[]{:S(2)}, u32[]{:S(2)}) %collective-permute-start.18) | collective-permute-done | bytes 4128 | tf_op jit(solution)/shard_map/ppermute | solution.py:380
  47.7 3.5 %collective-permute-done.19.mine_ref = f32[8,128]{1,0:T(8,128)S(1)} collective-permute-done((f32[8,128]{1,0:T(8,128)S(1)}, f32[8,128]{1,0:T(8,128)S(1)}, u32[]{:S(2)}, u32[]{:S(2)}) %collective-permute-start.19) | collective-permute-done | bytes 4128 | tf_op jit(solution)/shard_map/ppermute | solution.py:374
  51.2 1.2 %collective-permute-done.20.yours_ref = f32[8,128]{1,0:T(8,128)S(1)} collective-permute-done((f32[8,128]{1,0:T(8,128)S(1)}, f32[8,128]{1,0:T(8,128)S(1)}, u32[]{:S(2)}, u32[]{:S(2)}) %collective-permute-start.20) | collective-permute-done | bytes 4128 | tf_op jit(solution)/shard_map/ppermute | solution.py:380
  52.9 2.4 %collective-permute-start.23 = (f32[16,128]{1,0:T(8,128)S(1)}, f32[16,128]{1,0:T(8,128)S(1)}, u32[]{:S(2)}, u32[]{:S(2)}) collective-permute-start(f32[16,128]{1,0:T(8,128)S(1)} %get-tuple-element.53.packed_ref), channel_id=1, source_target_pairs={{0,14},{2,4},{4,2},{6,8},{8,6},{10,12},{12,10},{14,0},{1,15},{3,5}... | collective-permute-start | bytes 24584 | tf_op jit(solution)/shard_map/ppermute | solution.py:353
  55.3 1.1 %collective-permute-start.22 = (f32[16,128]{1,0:T(8,128)S(1)}, f32[16,128]{1,0:T(8,128)S(1)}, u32[]{:S(2)}, u32[]{:S(2)}) collective-permute-start(f32[16,128]{1,0:T(8,128)S(1)} %get-tuple-element.53.packed_ref), channel_id=1, source_target_pairs={{0,8},{2,10},{4,12},{6,14},{8,0},{10,2},{12,4},{14,6},{1,9},{3,11}... | collective-permute-start | bytes 24584 | tf_op jit(solution)/shard_map/ppermute | solution.py:353
  56.4 2.9 %collective-permute-done.23.second_ref = f32[16,128]{1,0:T(8,128)S(1)} collective-permute-done((f32[16,128]{1,0:T(8,128)S(1)}, f32[16,128]{1,0:T(8,128)S(1)}, u32[]{:S(2)}, u32[]{:S(2)}) %collective-permute-start.23) | collective-permute-done | bytes 8224 | tf_op jit(solution)/shard_map/ppermute | solution.py:353
  60.0 1.4 %shard_map.103 = (f32[19,2048]{1,0:T(8,128)}, f32[8,128]{1,0:T(8,128)}, f32[8,128]{1,0:T(8,128)}) custom-call(f32[8,4,128,128]{3,2,1,0:T(8,128)S(1)} %copy-done.1, f32[8,4,128,128]{3,2,1,0:T(8,128)S(1)} %collective-permute-done.other_ref, f32[64,16]{1,0:T(8,128)S(1)} %get-tuple-element.37.pick_ref, f32[16,128]{1,0:T(8,128)S(1)} %get-tuple-element.53.packed_ref, ...), custom_call_target="tpu_custom_call" | custom-call | flops 4000000 | bytes 262144 | tf_op jit(solution)/shard_map/pallas_call | solution.py:432
  (48 shorter events, 12.1 us)
Async XLA Ops:
  0.6 19.4 %collective-permute-start = (f32[8,4,128,128]{3,2,1,0:T(8,128)}, f32[8,4,128,128]{3,2,1,0:T(8,128)S(1)}, u32[]{:S(2)}, u32[]{:S(2)}) collective-permute-start(f32[8,4,128,128]{3,2,1,0:T(8,128)} %own_ref.9), channel_id=1, source_target_pairs={{0,1},{1,0},{2,3},{3,2},{4,5},{5,4},{6,7},{7,6},{8,9},{9,8},{10,11... | collective-permute-start | bytes 6291464 | tf_op jit(solution)/shard_map/ppermute | solution.py:380
  3.1 8.1 %collective-permute-start.4 = (f32[8,512]{1,0:T(8,128)S(1)}, f32[8,512]{1,0:T(8,128)S(1)}, u32[]{:S(2)}, u32[]{:S(2)}) collective-permute-start(f32[8,512]{1,0:T(8,128)S(1)} %get-tuple-element.31.payload_ref), channel_id=1, source_target_pairs={{0,14},{2,4},{4,2},{6,8},{8,6},{10,12},{12,10},{14,0},{1,15},{3,5}... | collective-permute-start | bytes 49160 | tf_op jit(solution)/shard_map/ppermute | solution.py:353
  8.7 4.6 %collective-permute-start.3 = (f32[8,512]{1,0:T(8,128)S(1)}, f32[8,512]{1,0:T(8,128)S(1)}, u32[]{:S(2)}, u32[]{:S(2)}) collective-permute-start(f32[8,512]{1,0:T(8,128)S(1)} %get-tuple-element.31.payload_ref), channel_id=1, source_target_pairs={{0,8},{2,10},{4,12},{6,14},{8,0},{10,2},{12,4},{14,6},{1,9},{3,11}... | collective-permute-start | bytes 49160 | tf_op jit(solution)/shard_map/ppermute | solution.py:353
  8.7 4.6 %collective-permute-start.2 = (f32[8,512]{1,0:T(8,128)S(1)}, f32[8,512]{1,0:T(8,128)S(1)}, u32[]{:S(2)}, u32[]{:S(2)}) collective-permute-start(f32[8,512]{1,0:T(8,128)S(1)} %get-tuple-element.31.payload_ref), channel_id=1, source_target_pairs={{0,2},{2,0},{4,6},{6,4},{8,10},{10,8},{12,14},{14,12},{1,3},{3,1},... | collective-permute-start | bytes 49160 | tf_op jit(solution)/shard_map/ppermute | solution.py:353
  13.6 1.2 %collective-permute-start.5 = (f32[8,128]{1,0:T(8,128)S(1)}, f32[8,128]{1,0:T(8,128)S(1)}, u32[]{:S(2)}, u32[]{:S(2)}) collective-permute-start(f32[8,128]{1,0:T(8,128)S(1)} %get-tuple-element.35), channel_id=1, source_target_pairs={{0,1},{1,0},{2,3},{3,2},{4,5},{5,4},{6,7},{7,6},{8,9},{9,8},{10,11... | collective-permute-start | bytes 12296 | tf_op jit(solution)/shard_map/ppermute | solution.py:380
  14.8 3.9 %collective-permute-start.6 = (f32[8,128]{1,0:T(8,128)S(1)}, f32[8,128]{1,0:T(8,128)S(1)}, u32[]{:S(2)}, u32[]{:S(2)}) collective-permute-start(f32[8,128]{1,0:T(8,128)S(1)} %get-tuple-element.61.direction_ref), channel_id=1, source_target_pairs={{0,2},{1,17},{2,0},{3,5},{4,6},{5,3},{6,4},{7,9},{8,10},{9,7},{10,... | collective-permute-start | bytes 12296 | tf_op jit(solution)/shard_map/ppermute | solution.py:374
  15.0 2.0 %collective-permute-start.1 = (s32[4,8]{1,0:T(4,128)S(1)}, s32[4,8]{1,0:T(4,128)S(1)}, u32[]{:S(2)}, u32[]{:S(2)}) collective-permute-start(s32[4,8]{1,0:T(4,128)S(1)} %get-tuple-element.32.own_cols), channel_id=1, source_target_pairs={{0,1},{1,0},{2,3},{3,2},{4,5},{5,4},{6,7},{7,6},{8,9},{9,8},{10,11... | collective-permute-start | bytes 392 | tf_op jit(solution)/shard_map/ppermute | solution.py:380
  18.8 1.2 %collective-permute-start.7 = (f32[8,128]{1,0:T(8,128)S(1)}, f32[8,128]{1,0:T(8,128)S(1)}, u32[]{:S(2)}, u32[]{:S(2)}) collective-permute-start(f32[8,128]{1,0:T(8,128)S(1)} %collective-permute-done.6.mine_ref), channel_id=1, source_target_pairs={{0,1},{1,0},{2,3},{3,2},{4,5},{5,4},{6,7},{7,6},{8,9},{9,8},{10,11... | collective-permute-start | bytes 12296 | tf_op jit(solution)/shard_map/ppermute | solution.py:380
  20.6 3.7 %collective-permute-start.8 = (f32[8,128]{1,0:T(8,128)S(1)}, f32[8,128]{1,0:T(8,128)S(1)}, u32[]{:S(2)}, u32[]{:S(2)}) collective-permute-start(f32[8,128]{1,0:T(8,128)S(1)} %get-tuple-element.42.direction_in), channel_id=1, source_target_pairs={{0,2},{1,17},{2,0},{3,5},{4,6},{5,3},{6,4},{7,9},{8,10},{9,7},{10,... | collective-permute-start | bytes 12296 | tf_op jit(solution)/shard_map/ppermute | solution.py:374
  24.3 1.2 %collective-permute-start.9 = (f32[8,128]{1,0:T(8,128)S(1)}, f32[8,128]{1,0:T(8,128)S(1)}, u32[]{:S(2)}, u32[]{:S(2)}) collective-permute-start(f32[8,128]{1,0:T(8,128)S(1)} %collective-permute-done.8.mine_ref), channel_id=1, source_target_pairs={{0,1},{1,0},{2,3},{3,2},{4,5},{5,4},{6,7},{7,6},{8,9},{9,8},{10,11... | collective-permute-start | bytes 12296 | tf_op jit(solution)/shard_map/ppermute | solution.py:380
  26.0 6.4 %collective-permute-start.12 = (f32[8,128]{1,0:T(8,128)S(1)}, f32[8,128]{1,0:T(8,128)S(1)}, u32[]{:S(2)}, u32[]{:S(2)}) collective-permute-start(f32[8,128]{1,0:T(8,128)S(1)} %shard_map.99.own_estimate), channel_id=1, source_target_pairs={{0,14},{2,4},{4,2},{6,8},{8,6},{10,12},{12,10},{14,0},{1,15},{3,5}... | collective-permute-start | bytes 12296 | tf_op jit(solution)/shard_map/ppermute | solution.py:353
  27.9 4.5 %collective-permute-start.11 = (f32[8,128]{1,0:T(8,128)S(1)}, f32[8,128]{1,0:T(8,128)S(1)}, u32[]{:S(2)}, u32[]{:S(2)}) collective-permute-start(f32[8,128]{1,0:T(8,128)S(1)} %shard_map.99.own_estimate), channel_id=1, source_target_pairs={{0,8},{2,10},{4,12},{6,14},{8,0},{10,2},{12,4},{14,6},{1,9},{3,11}... | collective-permute-start | bytes 12296 | tf_op jit(solution)/shard_map/ppermute | solution.py:353
  29.5 3.6 %collective-permute-start.10 = (f32[8,128]{1,0:T(8,128)S(1)}, f32[8,128]{1,0:T(8,128)S(1)}, u32[]{:S(2)}, u32[]{:S(2)}) collective-permute-start(f32[8,128]{1,0:T(8,128)S(1)} %shard_map.99.own_estimate), channel_id=1, source_target_pairs={{0,2},{2,0},{4,6},{6,4},{8,10},{10,8},{12,14},{14,12},{1,3},{3,1},... | collective-permute-start | bytes 12296 | tf_op jit(solution)/shard_map/ppermute | solution.py:353
  34.1 6.4 %collective-permute-start.13 = (f32[8,128]{1,0:T(8,128)S(1)}, f32[8,128]{1,0:T(8,128)S(1)}, u32[]{:S(2)}, u32[]{:S(2)}) collective-permute-start(f32[8,128]{1,0:T(8,128)S(1)} %get-tuple-element.47), channel_id=1, source_target_pairs={{0,14},{2,4},{4,2},{6,8},{8,6},{10,12},{12,10},{14,0},{1,15},{3,5}... | collective-permute-start | bytes 12296 | tf_op jit(solution)/shard_map/ppermute | solution.py:353
  36.4 4.5 %collective-permute-start.14 = (f32[8,128]{1,0:T(8,128)S(1)}, f32[8,128]{1,0:T(8,128)S(1)}, u32[]{:S(2)}, u32[]{:S(2)}) collective-permute-start(f32[8,128]{1,0:T(8,128)S(1)} %get-tuple-element.48), channel_id=1, source_target_pairs={{0,8},{2,10},{4,12},{6,14},{8,0},{10,2},{12,4},{14,6},{1,9},{3,11}... | collective-permute-start | bytes 12296 | tf_op jit(solution)/shard_map/ppermute | solution.py:353
  37.5 3.6 %collective-permute-start.15 = (f32[8,128]{1,0:T(8,128)S(1)}, f32[8,128]{1,0:T(8,128)S(1)}, u32[]{:S(2)}, u32[]{:S(2)}) collective-permute-start(f32[8,128]{1,0:T(8,128)S(1)} %get-tuple-element.49), channel_id=1, source_target_pairs={{0,2},{2,0},{4,6},{6,4},{8,10},{10,8},{12,14},{14,12},{1,3},{3,1},... | collective-permute-start | bytes 12296 | tf_op jit(solution)/shard_map/ppermute | solution.py:353
  41.1 1.2 %collective-permute-start.16 = (f32[8,128]{1,0:T(8,128)S(1)}, f32[8,128]{1,0:T(8,128)S(1)}, u32[]{:S(2)}, u32[]{:S(2)}) collective-permute-start(f32[8,128]{1,0:T(8,128)S(1)} %add_multiply_fusion), channel_id=1, source_target_pairs={{0,1},{1,0},{2,3},{3,2},{4,5},{5,4},{6,7},{7,6},{8,9},{9,8},{10,11... | collective-permute-start | bytes 12296 | tf_op jit(solution)/shard_map/ppermute | solution.py:380
  42.3 3.6 %collective-permute-start.17 = (f32[8,128]{1,0:T(8,128)S(1)}, f32[8,128]{1,0:T(8,128)S(1)}, u32[]{:S(2)}, u32[]{:S(2)}) collective-permute-start(f32[8,128]{1,0:T(8,128)S(1)} %get-tuple-element.59.direction_in), channel_id=1, source_target_pairs={{0,2},{1,17},{2,0},{3,5},{4,6},{5,3},{6,4},{7,9},{8,10},{9,7},{10,... | collective-permute-start | bytes 12296 | tf_op jit(solution)/shard_map/ppermute | solution.py:374
  45.9 1.2 %collective-permute-start.18 = (f32[8,128]{1,0:T(8,128)S(1)}, f32[8,128]{1,0:T(8,128)S(1)}, u32[]{:S(2)}, u32[]{:S(2)}) collective-permute-start(f32[8,128]{1,0:T(8,128)S(1)} %collective-permute-done.17.mine_ref), channel_id=1, source_target_pairs={{0,1},{1,0},{2,3},{3,2},{4,5},{5,4},{6,7},{7,6},{8,9},{9,8},{10,11... | collective-permute-start | bytes 12296 | tf_op jit(solution)/shard_map/ppermute | solution.py:380
  47.5 3.7 %collective-permute-start.19 = (f32[8,128]{1,0:T(8,128)S(1)}, f32[8,128]{1,0:T(8,128)S(1)}, u32[]{:S(2)}, u32[]{:S(2)}) collective-permute-start(f32[8,128]{1,0:T(8,128)S(1)} %get-tuple-element.50.direction_in), channel_id=1, source_target_pairs={{0,2},{1,17},{2,0},{3,5},{4,6},{5,3},{6,4},{7,9},{8,10},{9,7},{10,... | collective-permute-start | bytes 12296 | tf_op jit(solution)/shard_map/ppermute | solution.py:374
  51.2 1.2 %collective-permute-start.20 = (f32[8,128]{1,0:T(8,128)S(1)}, f32[8,128]{1,0:T(8,128)S(1)}, u32[]{:S(2)}, u32[]{:S(2)}) collective-permute-start(f32[8,128]{1,0:T(8,128)S(1)} %collective-permute-done.19.mine_ref), channel_id=1, source_target_pairs={{0,1},{1,0},{2,3},{3,2},{4,5},{5,4},{6,7},{7,6},{8,9},{9,8},{10,11... | collective-permute-start | bytes 12296 | tf_op jit(solution)/shard_map/ppermute | solution.py:380
  52.9 6.4 %collective-permute-start.23 = (f32[16,128]{1,0:T(8,128)S(1)}, f32[16,128]{1,0:T(8,128)S(1)}, u32[]{:S(2)}, u32[]{:S(2)}) collective-permute-start(f32[16,128]{1,0:T(8,128)S(1)} %get-tuple-element.53.packed_ref), channel_id=1, source_target_pairs={{0,14},{2,4},{4,2},{6,8},{8,6},{10,12},{12,10},{14,0},{1,15},{3,5}... | collective-permute-start | bytes 24584 | tf_op jit(solution)/shard_map/ppermute | solution.py:353
  55.3 4.5 %collective-permute-start.22 = (f32[16,128]{1,0:T(8,128)S(1)}, f32[16,128]{1,0:T(8,128)S(1)}, u32[]{:S(2)}, u32[]{:S(2)}) collective-permute-start(f32[16,128]{1,0:T(8,128)S(1)} %get-tuple-element.53.packed_ref), channel_id=1, source_target_pairs={{0,8},{2,10},{4,12},{6,14},{8,0},{10,2},{12,4},{14,6},{1,9},{3,11}... | collective-permute-start | bytes 24584 | tf_op jit(solution)/shard_map/ppermute | solution.py:353
  56.4 3.7 %collective-permute-start.21 = (f32[16,128]{1,0:T(8,128)S(1)}, f32[16,128]{1,0:T(8,128)S(1)}, u32[]{:S(2)}, u32[]{:S(2)}) collective-permute-start(f32[16,128]{1,0:T(8,128)S(1)} %get-tuple-element.53.packed_ref), channel_id=1, source_target_pairs={{0,2},{2,0},{4,6},{6,4},{8,10},{10,8},{12,14},{14,12},{1,3},{3,1},... | collective-permute-start | bytes 24584 | tf_op jit(solution)/shard_map/ppermute | solution.py:353
  (5 other events, 25.5 us)

commit v9 on v8

--- a/solution.py
+++ b/solution.py
@@ -140,6 +140,10 @@
     return lax.rem(lax.axis_index("dom"), 2) == 0
 
 
+def meets_next():
+    return is_even() == (lax.axis_index("sub") == 0)
+
+
 def by_partner(mine, yours):
     zero = lax.axis_index("sub") == 0
     return jnp.where(zero, mine, yours), jnp.where(zero, yours, mine)
@@ -150,15 +154,15 @@
     return jnp.where(even, first, second), jnp.where(even, second, first)
 
 
-def spread_current(outgoing, maps, own_ref, first_ref, second_ref, far_ref):
+def spread_current(outgoing, maps, own_ref, keep_ref, give_ref, far_ref):
     torso = own_ref.shape[0]
     own, after, before, far = (
         scatter(outgoing[o : o + 1], maps[o : o + 1], torso) for o in range(maps.shape[0])
     )
-    even = is_even()
+    ahead = meets_next()
     own_ref[...] = own
-    first_ref[...] = jnp.where(even, after, before)
-    second_ref[...] = jnp.where(even, before, after)
+    keep_ref[...] = jnp.where(ahead, after, before)
+    give_ref[...] = jnp.where(ahead, before, after)
     far_ref[...] = far
 
 
@@ -257,11 +261,11 @@
 
 
 def next_shares(
-    states_ref, own_estimate, first_estimate, far_estimate, second_estimate, nodes_ref, maps_ref,
-    out_ref, own_ref, first_ref, second_ref, far_ref,
+    states_ref, own_estimate, far_estimate, mine_ref, yours_ref, nodes_ref, maps_ref,
+    out_ref, own_ref, keep_ref, give_ref, far_ref,
 ):
     nodes, maps = nodes_ref[...], maps_ref[...]
-    after, before = by_side(first_estimate[...], second_estimate[...])
+    after, before = by_side(*by_partner(mine_ref[...], yours_ref[...]))
     estimates = [own_estimate[...], after, before, far_estimate[...]]
     feedback = feedback_of(estimates, nodes, maps, states_ref.shape[1])
     rows = [states_ref[i] for i in range(states_ref.shape[0])]
@@ -270,7 +274,7 @@
     for i, row in enumerate(rows):
         out_ref[i] = row
     outgoing = pick_current(current, nodes)
-    spread_current(outgoing, maps, own_ref, first_ref, second_ref, far_ref)
+    spread_current(outgoing, maps, own_ref, keep_ref, give_ref, far_ref)
 
 
 def window_of(chain, direction, first, second):
@@ -321,14 +325,15 @@
 
 
 def finish(
-    chain, own_ref, other_ref, pick_ref, packed_ref, first_ref, far_ref, second_ref, residual_in,
+    chain, own_ref, other_ref, pick_ref, packed_ref, far_ref, mine_ref, yours_ref, residual_in,
     diag_ref, states_ref, nodes_ref, maps_ref, out_ref, potential_ref, residual_ref, dense_ref,
 ):
     torso = residual_ref.shape[0]
     head, tail = slice(0, torso), slice(torso, 2 * torso)
     estimate, direction = packed_ref[head], packed_ref[tail]
     potential_ref[...] = estimate
-    after, before = by_side(first_ref[head], second_ref[head])
+    first, second = by_partner(mine_ref[...], yours_ref[...])
+    after, before = by_side(first[head], second[head])
     feedback = feedback_of(
         [estimate, after, before, far_ref[head]], nodes_ref[...], maps_ref[...],
         states_ref.shape[1],
@@ -337,7 +342,7 @@
     dense_ref[0] = states_ref[0] + TIME_STEP * FEEDBACK_RATE * feedback
     for k in range(states_ref.shape[1]):
         out_ref[:, k * LANES : (k + 1) * LANES] = dense_ref[:, k, :]
-    window = window_of(chain, direction, first_ref[tail], second_ref[tail])
+    window = window_of(chain, direction, first[tail], second[tail])
     moved = product(own_ref, other_ref, pick_ref, window)
     residual_ref[...] = residual_in[...] - (diag_ref[...] * direction + moved)
 
@@ -358,9 +363,9 @@
     def with_second(value):
         return swap(value, lambda i: ((i + 1) ^ 1) - 1)
 
-    def with_either(value):
+    def with_either(value, closed):
         cases = lax.axis_size("case")
-        ends = (0, chain - 1) if cases % 2 == 0 else ()
+        ends = () if closed or cases % 2 else (0, chain - 1)
         pairs = []
         for case in range(cases):
             for i in range(chain):
@@ -404,7 +409,7 @@
         last = time_step == 1
         forcing = forcing + from_sibling(forcing)
         direction = forcing / (CHEB_THETA * diag)
-        halo = with_either(direction)
+        halo = with_either(direction, False)
         if not last:
             choices = 2 * columns.shape[0] * torso
             direction, pick = call(bring_tiles, (field, shape(choices, 2 * torso)))(
@@ -415,26 +420,28 @@
         residual, direction, estimate = call(
             functools.partial(sweep_one, chain), (field,) * 3
         )(in_specs=[VMEM] * 8)(*stored, halo, from_sibling(halo), forcing, direction, diag)
-        halo = with_either(direction)
+        halo = with_either(direction, False)
         swept = call(
             functools.partial(sweep_two, chain, last), (packed, field) if last else field
         )(in_specs=[VMEM] * 9)(
             *stored, halo, from_sibling(halo), direction, residual, estimate, diag
         )
         estimate, residual = swept if last else (swept, None)
-        first, far, second = with_first(estimate), with_far(estimate), with_second(estimate)
+        far = with_far(estimate)
+        near = with_either(estimate, True)
         if not last:
-            states, own, *shares = call(next_shares, (dense,) + (field,) * 4)(
+            states, own, keep, give, away = call(next_shares, (dense,) + (field,) * 4)(
                 in_specs=[VMEM] * 7
-            )(states, estimate, first, far, second, nodes, maps)
-            forcing = own + with_second(shares[1]) + with_far(shares[2]) + with_first(shares[0])
-            forcing = TORSO_COUPLING * forcing
+            )(states, estimate, far, near, from_sibling(near), nodes, maps)
+            far = with_far(away)
+            near = with_either(keep + from_sibling(give), True)
+            forcing = TORSO_COUPLING * (own + far + near)
     new_states, potential, residual = call(
         functools.partial(finish, chain),
         (shape(*dense.shape[:1], node_count), field, field),
         (pltpu.VMEM(dense.shape, F32),),
     )(in_specs=[VMEM] * 12)(
-        *stored, estimate, first, far, second, residual, diag, states, nodes, maps
+        *stored, estimate, far, near, from_sibling(near), residual, diag, states, nodes, maps
     )
     return new_states, potential.reshape(-1), residual.reshape(-1)
 

time: 61.8 us -> 59.5 us (0.963)
  waiting for transfers between devices: 30 us -> 27.4 us
    ppermute x12 -> x6, waiting for transfers between devices: 13 us -> 5.03 us  [swap(): lax.ppermute(value, 'dom', [(i, partner(i) % chain) for i in range(chain)])]
    ppermute x12 -> x6, starting transfers between devices: 17.1 us -> 10.4 us  [swap(): lax.ppermute(value, 'dom', [(i, partner(i) % chain) for i in range(chain)])]
    ppermute x8 -> x11, starting transfers between devices: 2.18 us -> 7.73 us  [from_sibling(): return lax.ppermute(value, 'sub', [(0, 1), (1, 0)])]
    ppermute x4 -> x7, waiting for transfers between devices: 9.62 us -> 13.7 us  [with_either(): return lax.ppermute(value, ('case', 'dom', 'sub'), pairs)]
    ppermute x4 -> x7, starting transfers between devices: 1.54 us -> 3.08 us  [with_either(): return lax.ppermute(value, ('case', 'dom', 'sub'), pairs)]
    ppermute x8 -> x11, waiting for transfers between devices: 7.46 us -> 8.63 us  [from_sibling(): return lax.ppermute(value, 'sub', [(0, 1), (1, 0)])]
  transfers between devices with their start and end apart: 24 -> 24, of which waited for: 19 -> 18; matrix products, arithmetic and copies ran while one was open for 1% -> 1% of each run, Pallas kernels for 1% -> 1%
where the time goes in v9:
time: 59.5 us; the launch traced here: 59.2 us
  waiting for transfers between devices  27.4 us (46%)
  starting transfers between devices  21.2 us (36%)
  Pallas kernels  5.24 us (9%)
  local copies, waits for them, and re-layouts  3.88 us (7%)
  other arithmetic  0.76 us (1%)
  between operations  0.72 us (1%)
    ppermute x7, waiting for transfers between devices, with_either(): return lax.ppermute(value, ('case', 'dom', 'sub'), pairs)  13.7 us
    ppermute x6, starting transfers between devices, swap(): lax.ppermute(value, 'dom', [(i, partner(i) % chain) for i in range(chain)])  10.4 us
    ppermute x11, waiting for transfers between devices, from_sibling(): return lax.ppermute(value, 'sub', [(0, 1), (1, 0)])  8.63 us
    ppermute x11, starting transfers between devices, from_sibling(): return lax.ppermute(value, 'sub', [(0, 1), (1, 0)])  7.73 us
    ppermute x6, waiting for transfers between devices, swap(): lax.ppermute(value, 'dom', [(i, partner(i) % chain) for i in range(chain)])  5.03 us
    unnamed x10, local copies, waits for them, and re-layouts  3.88 us
    ppermute x7, starting transfers between devices, with_either(): return lax.ppermute(value, ('case', 'dom', 'sub'), pairs)  3.08 us
    pallas_call x1, Pallas kernels, on_device(): call(functools.partial(finish, chain), (shape(*dense.shape[:1], node_coun...  1.45 us
  transfers between devices with their start and end apart: 24, of which 18 were waited for; matrix products, arithmetic and copies ran while one was open for 1% of the time, Pallas kernels for 1%

profile of v9, /device:TPU:0, one launch (start us, length us, event | category | flops | bytes accessed | tf_op | source)
XLA Modules:
  0.0 59.2 jit_solution(17061676427143957076)
XLA Ops:
  1.9 0.9 %copy-done.2 = f32[19,2048]{1,0:T(8,128)S(1)} copy-done((f32[19,2048]{1,0:T(8,128)S(1)}, f32[19,2048]{1,0:T(8,128)}, u32[]{:S(2)}) %copy-start.2) | copy-done | bytes 155672
  3.1 5.6 %collective-permute-start.4 = (f32[8,512]{1,0:T(8,128)S(1)}, f32[8,512]{1,0:T(8,128)S(1)}, u32[]{:S(2)}, u32[]{:S(2)}) collective-permute-start(f32[8,512]{1,0:T(8,128)S(1)} %get-tuple-element.31.payload_ref), channel_id=1, source_target_pairs={{0,14},{2,4},{4,2},{6,8},{8,6},{10,12},{12,10},{14,0},{1,15},{3,5}... | collective-permute-start | bytes 49160 | tf_op jit(solution)/shard_map/ppermute | solution.py:358
  8.7 1.1 %collective-permute-start.2 = (f32[8,512]{1,0:T(8,128)S(1)}, f32[8,512]{1,0:T(8,128)S(1)}, u32[]{:S(2)}, u32[]{:S(2)}) collective-permute-start(f32[8,512]{1,0:T(8,128)S(1)} %get-tuple-element.31.payload_ref), channel_id=1, source_target_pairs={{0,2},{2,0},{4,6},{6,4},{8,10},{10,8},{12,14},{14,12},{1,3},{3,1},... | collective-permute-start | bytes 49160 | tf_op jit(solution)/shard_map/ppermute | solution.py:358
  11.2 2.2 %collective-permute-done.3.far_ref = f32[8,512]{1,0:T(8,128)S(1)} collective-permute-done((f32[8,512]{1,0:T(8,128)S(1)}, f32[8,512]{1,0:T(8,128)S(1)}, u32[]{:S(2)}, u32[]{:S(2)}) %collective-permute-start.3) | collective-permute-done | bytes 16416 | tf_op jit(solution)/shard_map/ppermute | solution.py:358
  13.7 1.2 %collective-permute-done.5 = f32[8,128]{1,0:T(8,128)S(1)} collective-permute-done((f32[8,128]{1,0:T(8,128)S(1)}, f32[8,128]{1,0:T(8,128)S(1)}, u32[]{:S(2)}, u32[]{:S(2)}) %collective-permute-start.5) | collective-permute-done | bytes 4128 | tf_op jit(solution)/shard_map/ppermute | solution.py:385
  15.0 1.2 %collective-permute-start.1 = (s32[4,8]{1,0:T(4,128)S(1)}, s32[4,8]{1,0:T(4,128)S(1)}, u32[]{:S(2)}, u32[]{:S(2)}) collective-permute-start(s32[4,8]{1,0:T(4,128)S(1)} %get-tuple-element.32.own_cols), channel_id=1, source_target_pairs={{0,1},{1,0},{2,3},{3,2},{4,5},{5,4},{6,7},{7,6},{8,9},{9,8},{10,11... | collective-permute-start | bytes 392 | tf_op jit(solution)/shard_map/ppermute | solution.py:385
  17.1 1.6 %copy-done = f32[8,4,128,128]{3,2,1,0:T(8,128)S(1)} copy-done((f32[8,4,128,128]{3,2,1,0:T(8,128)S(1)}, f32[8,4,128,128]{3,2,1,0:T(8,128)}, u32[]{:S(2)}) %copy-start) | copy-done | bytes 2097176
  20.6 1.0 %collective-permute-start.8 = (f32[8,128]{1,0:T(8,128)S(1)}, f32[8,128]{1,0:T(8,128)S(1)}, u32[]{:S(2)}, u32[]{:S(2)}) collective-permute-start(f32[8,128]{1,0:T(8,128)S(1)} %get-tuple-element.42.direction_in), channel_id=1, source_target_pairs={{0,2},{1,17},{2,0},{3,5},{4,6},{5,3},{6,4},{7,9},{8,10},{9,7},{10,... | collective-permute-start | bytes 12296 | tf_op jit(solution)/shard_map/ppermute | solution.py:379
  21.6 2.7 %collective-permute-done.8.mine_ref = f32[8,128]{1,0:T(8,128)S(1)} collective-permute-done((f32[8,128]{1,0:T(8,128)S(1)}, f32[8,128]{1,0:T(8,128)S(1)}, u32[]{:S(2)}, u32[]{:S(2)}) %collective-permute-start.8) | collective-permute-done | bytes 4128 | tf_op jit(solution)/shard_map/ppermute | solution.py:379
  24.3 1.2 %collective-permute-done.9.yours_ref = f32[8,128]{1,0:T(8,128)S(1)} collective-permute-done((f32[8,128]{1,0:T(8,128)S(1)}, f32[8,128]{1,0:T(8,128)S(1)}, u32[]{:S(2)}, u32[]{:S(2)}) %collective-permute-start.9) | collective-permute-done | bytes 4128 | tf_op jit(solution)/shard_map/ppermute | solution.py:385
  26.0 1.0 %collective-permute-start.11 = (f32[8,128]{1,0:T(8,128)S(1)}, f32[8,128]{1,0:T(8,128)S(1)}, u32[]{:S(2)}, u32[]{:S(2)}) collective-permute-start(f32[8,128]{1,0:T(8,128)S(1)} %shard_map.99.own_estimate), channel_id=1, source_target_pairs={{0,2},{1,15},{2,0},{3,5},{4,6},{5,3},{6,4},{7,9},{8,10},{9,7},{10,... | collective-permute-start | bytes 12296 | tf_op jit(solution)/shard_map/ppermute | solution.py:379
  27.1 2.0 %collective-permute-start.10 = (f32[8,128]{1,0:T(8,128)S(1)}, f32[8,128]{1,0:T(8,128)S(1)}, u32[]{:S(2)}, u32[]{:S(2)}) collective-permute-start(f32[8,128]{1,0:T(8,128)S(1)} %shard_map.99.own_estimate), channel_id=1, source_target_pairs={{0,8},{2,10},{4,12},{6,14},{8,0},{10,2},{12,4},{14,6},{1,9},{3,11}... | collective-permute-start | bytes 12296 | tf_op jit(solution)/shard_map/ppermute | solution.py:358
  29.7 1.7 %collective-permute-start.12 = (f32[8,128]{1,0:T(8,128)S(1)}, f32[8,128]{1,0:T(8,128)S(1)}, u32[]{:S(2)}, u32[]{:S(2)}) collective-permute-start(f32[8,128]{1,0:T(8,128)S(1)} %collective-permute-done.11.mine_ref), channel_id=1, source_target_pairs={{0,1},{1,0},{2,3},{3,2},{4,5},{5,4},{6,7},{7,6},{8,9},{9,8},{10,11... | collective-permute-start | bytes 12296 | tf_op jit(solution)/shard_map/ppermute | solution.py:385
  32.3 0.9 %shard_map.100 = (f32[19,16,128]{2,1,0:T(8,128)S(1)}, f32[8,128]{1,0:T(8,128)S(1)}, f32[8,128]{1,0:T(8,128)S(1)}, f32[8,128]{1,0:T(8,128)S(1)}, f32[8,128]{1,0:T(8,128)S(1)}) custom-call(f32[19,16,128]{2,1,0:T(8,128)S(1)} %get-tuple-element.38.states_ref, f32[8,128]{1,0:T(8,128)S(1)} %shard_map.99.own_estimate, ...), custom_call_target="tpu_custom_call" | custom-call | flops 4000000 | bytes 262144 | tf_op jit(solution)/shard_map/pallas_call | solution.py:433
  33.6 1.1 %collective-permute-start.13 = (f32[8,128]{1,0:T(8,128)S(1)}, f32[8,128]{1,0:T(8,128)S(1)}, u32[]{:S(2)}, u32[]{:S(2)}) collective-permute-start(f32[8,128]{1,0:T(8,128)S(1)} %get-tuple-element.47), channel_id=1, source_target_pairs={{0,8},{2,10},{4,12},{6,14},{8,0},{10,2},{12,4},{14,6},{1,9},{3,11}... | collective-permute-start | bytes 12296 | tf_op jit(solution)/shard_map/ppermute | solution.py:358
  35.4 2.7 %collective-permute-done.13 = f32[8,128]{1,0:T(8,128)S(1)} collective-permute-done((f32[8,128]{1,0:T(8,128)S(1)}, f32[8,128]{1,0:T(8,128)S(1)}, u32[]{:S(2)}, u32[]{:S(2)}) %collective-permute-start.13) | collective-permute-done | bytes 4128 | tf_op jit(solution)/shard_map/ppermute | solution.py:358
  38.3 1.7 %collective-permute-start.16 = (f32[8,128]{1,0:T(8,128)S(1)}, f32[8,128]{1,0:T(8,128)S(1)}, u32[]{:S(2)}, u32[]{:S(2)}) collective-permute-start(f32[8,128]{1,0:T(8,128)S(1)} %add_multiply_fusion), channel_id=1, source_target_pairs={{0,1},{1,0},{2,3},{3,2},{4,5},{5,4},{6,7},{7,6},{8,9},{9,8},{10,11... | collective-permute-start | bytes 12296 | tf_op jit(solution)/shard_map/ppermute | solution.py:385
  40.9 3.6 %collective-permute-done.17.mine_ref = f32[8,128]{1,0:T(8,128)S(1)} collective-permute-done((f32[8,128]{1,0:T(8,128)S(1)}, f32[8,128]{1,0:T(8,128)S(1)}, u32[]{:S(2)}, u32[]{:S(2)}) %collective-permute-start.17) | collective-permute-done | bytes 4128 | tf_op jit(solution)/shard_map/ppermute | solution.py:379
  44.5 1.2 %collective-permute-done.18.yours_ref = f32[8,128]{1,0:T(8,128)S(1)} collective-permute-done((f32[8,128]{1,0:T(8,128)S(1)}, f32[8,128]{1,0:T(8,128)S(1)}, u32[]{:S(2)}, u32[]{:S(2)}) %collective-permute-start.18) | collective-permute-done | bytes 4128 | tf_op jit(solution)/shard_map/ppermute | solution.py:385
  46.2 3.6 %collective-permute-done.19.mine_ref = f32[8,128]{1,0:T(8,128)S(1)} collective-permute-done((f32[8,128]{1,0:T(8,128)S(1)}, f32[8,128]{1,0:T(8,128)S(1)}, u32[]{:S(2)}, u32[]{:S(2)}) %collective-permute-start.19) | collective-permute-done | bytes 4128 | tf_op jit(solution)/shard_map/ppermute | solution.py:379
  49.8 1.2 %collective-permute-done.20.yours_ref = f32[8,128]{1,0:T(8,128)S(1)} collective-permute-done((f32[8,128]{1,0:T(8,128)S(1)}, f32[8,128]{1,0:T(8,128)S(1)}, u32[]{:S(2)}, u32[]{:S(2)}) %collective-permute-start.20) | collective-permute-done | bytes 4128 | tf_op jit(solution)/shard_map/ppermute | solution.py:385
  52.2 3.0 %collective-permute-done.22.mine_ref = f32[16,128]{1,0:T(8,128)S(1)} collective-permute-done((f32[16,128]{1,0:T(8,128)S(1)}, f32[16,128]{1,0:T(8,128)S(1)}, u32[]{:S(2)}, u32[]{:S(2)}) %collective-permute-start.22) | collective-permute-done | bytes 8224 | tf_op jit(solution)/shard_map/ppermute | solution.py:379
  55.2 1.7 %collective-permute-start.23 = (f32[16,128]{1,0:T(8,128)S(1)}, f32[16,128]{1,0:T(8,128)S(1)}, u32[]{:S(2)}, u32[]{:S(2)}) collective-permute-start(f32[16,128]{1,0:T(8,128)S(1)} %collective-permute-done.22.mine_ref), channel_id=1, source_target_pairs={{0,1},{1,0},{2,3},{3,2},{4,5},{5,4},{6,7},{7,6},{8,9},{9,8},{10,11... | collective-permute-start | bytes 24584 | tf_op jit(solution)/shard_map/ppermute | solution.py:385
  57.7 1.4 %shard_map.103 = (f32[19,2048]{1,0:T(8,128)}, f32[8,128]{1,0:T(8,128)}, f32[8,128]{1,0:T(8,128)}) custom-call(f32[8,4,128,128]{3,2,1,0:T(8,128)S(1)} %copy-done.1, f32[8,4,128,128]{3,2,1,0:T(8,128)S(1)} %collective-permute-done.other_ref, f32[64,16]{1,0:T(8,128)S(1)} %get-tuple-element.37.pick_ref, f32[16,128]{1,0:T(8,128)S(1)} %get-tuple-element.53.packed_ref, ...), custom_call_target="tpu_custom_call" | custom-call | flops 4000000 | bytes 262144 | tf_op jit(solution)/shard_map/pallas_call | solution.py:439
  (49 shorter events, 13.0 us)
Async XLA Ops:
  0.6 19.4 %collective-permute-start = (f32[8,4,128,128]{3,2,1,0:T(8,128)}, f32[8,4,128,128]{3,2,1,0:T(8,128)S(1)}, u32[]{:S(2)}, u32[]{:S(2)}) collective-permute-start(f32[8,4,128,128]{3,2,1,0:T(8,128)} %own_ref.9), channel_id=1, source_target_pairs={{0,1},{1,0},{2,3},{3,2},{4,5},{5,4},{6,7},{7,6},{8,9},{9,8},{10,11... | collective-permute-start | bytes 6291464 | tf_op jit(solution)/shard_map/ppermute | solution.py:385
  3.1 8.1 %collective-permute-start.4 = (f32[8,512]{1,0:T(8,128)S(1)}, f32[8,512]{1,0:T(8,128)S(1)}, u32[]{:S(2)}, u32[]{:S(2)}) collective-permute-start(f32[8,512]{1,0:T(8,128)S(1)} %get-tuple-element.31.payload_ref), channel_id=1, source_target_pairs={{0,14},{2,4},{4,2},{6,8},{8,6},{10,12},{12,10},{14,0},{1,15},{3,5}... | collective-permute-start | bytes 49160 | tf_op jit(solution)/shard_map/ppermute | solution.py:358
  8.7 4.6 %collective-permute-start.3 = (f32[8,512]{1,0:T(8,128)S(1)}, f32[8,512]{1,0:T(8,128)S(1)}, u32[]{:S(2)}, u32[]{:S(2)}) collective-permute-start(f32[8,512]{1,0:T(8,128)S(1)} %get-tuple-element.31.payload_ref), channel_id=1, source_target_pairs={{0,8},{2,10},{4,12},{6,14},{8,0},{10,2},{12,4},{14,6},{1,9},{3,11}... | collective-permute-start | bytes 49160 | tf_op jit(solution)/shard_map/ppermute | solution.py:358
  8.7 4.6 %collective-permute-start.2 = (f32[8,512]{1,0:T(8,128)S(1)}, f32[8,512]{1,0:T(8,128)S(1)}, u32[]{:S(2)}, u32[]{:S(2)}) collective-permute-start(f32[8,512]{1,0:T(8,128)S(1)} %get-tuple-element.31.payload_ref), channel_id=1, source_target_pairs={{0,2},{2,0},{4,6},{6,4},{8,10},{10,8},{12,14},{14,12},{1,3},{3,1},... | collective-permute-start | bytes 49160 | tf_op jit(solution)/shard_map/ppermute | solution.py:358
  13.6 1.2 %collective-permute-start.5 = (f32[8,128]{1,0:T(8,128)S(1)}, f32[8,128]{1,0:T(8,128)S(1)}, u32[]{:S(2)}, u32[]{:S(2)}) collective-permute-start(f32[8,128]{1,0:T(8,128)S(1)} %get-tuple-element.35), channel_id=1, source_target_pairs={{0,1},{1,0},{2,3},{3,2},{4,5},{5,4},{6,7},{7,6},{8,9},{9,8},{10,11... | collective-permute-start | bytes 12296 | tf_op jit(solution)/shard_map/ppermute | solution.py:385
  14.8 3.9 %collective-permute-start.6 = (f32[8,128]{1,0:T(8,128)S(1)}, f32[8,128]{1,0:T(8,128)S(1)}, u32[]{:S(2)}, u32[]{:S(2)}) collective-permute-start(f32[8,128]{1,0:T(8,128)S(1)} %get-tuple-element.61.direction_ref), channel_id=1, source_target_pairs={{0,2},{1,17},{2,0},{3,5},{4,6},{5,3},{6,4},{7,9},{8,10},{9,7},{10,... | collective-permute-start | bytes 12296 | tf_op jit(solution)/shard_map/ppermute | solution.py:379
  15.0 2.0 %collective-permute-start.1 = (s32[4,8]{1,0:T(4,128)S(1)}, s32[4,8]{1,0:T(4,128)S(1)}, u32[]{:S(2)}, u32[]{:S(2)}) collective-permute-start(s32[4,8]{1,0:T(4,128)S(1)} %get-tuple-element.32.own_cols), channel_id=1, source_target_pairs={{0,1},{1,0},{2,3},{3,2},{4,5},{5,4},{6,7},{7,6},{8,9},{9,8},{10,11... | collective-permute-start | bytes 392 | tf_op jit(solution)/shard_map/ppermute | solution.py:385
  18.8 1.2 %collective-permute-start.7 = (f32[8,128]{1,0:T(8,128)S(1)}, f32[8,128]{1,0:T(8,128)S(1)}, u32[]{:S(2)}, u32[]{:S(2)}) collective-permute-start(f32[8,128]{1,0:T(8,128)S(1)} %collective-permute-done.6.mine_ref), channel_id=1, source_target_pairs={{0,1},{1,0},{2,3},{3,2},{4,5},{5,4},{6,7},{7,6},{8,9},{9,8},{10,11... | collective-permute-start | bytes 12296 | tf_op jit(solution)/shard_map/ppermute | solution.py:385
  20.6 3.7 %collective-permute-start.8 = (f32[8,128]{1,0:T(8,128)S(1)}, f32[8,128]{1,0:T(8,128)S(1)}, u32[]{:S(2)}, u32[]{:S(2)}) collective-permute-start(f32[8,128]{1,0:T(8,128)S(1)} %get-tuple-element.42.direction_in), channel_id=1, source_target_pairs={{0,2},{1,17},{2,0},{3,5},{4,6},{5,3},{6,4},{7,9},{8,10},{9,7},{10,... | collective-permute-start | bytes 12296 | tf_op jit(solution)/shard_map/ppermute | solution.py:379
  24.3 1.2 %collective-permute-start.9 = (f32[8,128]{1,0:T(8,128)S(1)}, f32[8,128]{1,0:T(8,128)S(1)}, u32[]{:S(2)}, u32[]{:S(2)}) collective-permute-start(f32[8,128]{1,0:T(8,128)S(1)} %collective-permute-done.8.mine_ref), channel_id=1, source_target_pairs={{0,1},{1,0},{2,3},{3,2},{4,5},{5,4},{6,7},{7,6},{8,9},{9,8},{10,11... | collective-permute-start | bytes 12296 | tf_op jit(solution)/shard_map/ppermute | solution.py:385
  26.0 3.7 %collective-permute-start.11 = (f32[8,128]{1,0:T(8,128)S(1)}, f32[8,128]{1,0:T(8,128)S(1)}, u32[]{:S(2)}, u32[]{:S(2)}) collective-permute-start(f32[8,128]{1,0:T(8,128)S(1)} %shard_map.99.own_estimate), channel_id=1, source_target_pairs={{0,2},{1,15},{2,0},{3,5},{4,6},{5,3},{6,4},{7,9},{8,10},{9,7},{10,... | collective-permute-start | bytes 12296 | tf_op jit(solution)/shard_map/ppermute | solution.py:379
  27.1 4.5 %collective-permute-start.10 = (f32[8,128]{1,0:T(8,128)S(1)}, f32[8,128]{1,0:T(8,128)S(1)}, u32[]{:S(2)}, u32[]{:S(2)}) collective-permute-start(f32[8,128]{1,0:T(8,128)S(1)} %shard_map.99.own_estimate), channel_id=1, source_target_pairs={{0,8},{2,10},{4,12},{6,14},{8,0},{10,2},{12,4},{14,6},{1,9},{3,11}... | collective-permute-start | bytes 12296 | tf_op jit(solution)/shard_map/ppermute | solution.py:358
  29.7 2.5 %collective-permute-start.12 = (f32[8,128]{1,0:T(8,128)S(1)}, f32[8,128]{1,0:T(8,128)S(1)}, u32[]{:S(2)}, u32[]{:S(2)}) collective-permute-start(f32[8,128]{1,0:T(8,128)S(1)} %collective-permute-done.11.mine_ref), channel_id=1, source_target_pairs={{0,1},{1,0},{2,3},{3,2},{4,5},{5,4},{6,7},{7,6},{8,9},{9,8},{10,11... | collective-permute-start | bytes 12296 | tf_op jit(solution)/shard_map/ppermute | solution.py:385
  33.2 1.5 %collective-permute-start.14 = (f32[8,128]{1,0:T(8,128)S(1)}, f32[8,128]{1,0:T(8,128)S(1)}, u32[]{:S(2)}, u32[]{:S(2)}) collective-permute-start(f32[8,128]{1,0:T(8,128)S(1)} %get-tuple-element.49), channel_id=1, source_target_pairs={{0,1},{1,0},{2,3},{3,2},{4,5},{5,4},{6,7},{7,6},{8,9},{9,8},{10,11... | collective-permute-start | bytes 12296 | tf_op jit(solution)/shard_map/ppermute | solution.py:385
  33.6 4.5 %collective-permute-start.13 = (f32[8,128]{1,0:T(8,128)S(1)}, f32[8,128]{1,0:T(8,128)S(1)}, u32[]{:S(2)}, u32[]{:S(2)}) collective-permute-start(f32[8,128]{1,0:T(8,128)S(1)} %get-tuple-element.47), channel_id=1, source_target_pairs={{0,8},{2,10},{4,12},{6,14},{8,0},{10,2},{12,4},{14,6},{1,9},{3,11}... | collective-permute-start | bytes 12296 | tf_op jit(solution)/shard_map/ppermute | solution.py:358
  34.7 3.6 %collective-permute-start.15 = (f32[8,128]{1,0:T(8,128)S(1)}, f32[8,128]{1,0:T(8,128)S(1)}, u32[]{:S(2)}, u32[]{:S(2)}) collective-permute-start(f32[8,128]{1,0:T(8,128)S(1)} %add.19), channel_id=1, source_target_pairs={{0,2},{1,15},{2,0},{3,5},{4,6},{5,3},{6,4},{7,9},{8,10},{9,7},{10,... | collective-permute-start | bytes 12296 | tf_op jit(solution)/shard_map/ppermute | solution.py:379
  38.3 2.5 %collective-permute-start.16 = (f32[8,128]{1,0:T(8,128)S(1)}, f32[8,128]{1,0:T(8,128)S(1)}, u32[]{:S(2)}, u32[]{:S(2)}) collective-permute-start(f32[8,128]{1,0:T(8,128)S(1)} %add_multiply_fusion), channel_id=1, source_target_pairs={{0,1},{1,0},{2,3},{3,2},{4,5},{5,4},{6,7},{7,6},{8,9},{9,8},{10,11... | collective-permute-start | bytes 12296 | tf_op jit(solution)/shard_map/ppermute | solution.py:385
  40.9 3.6 %collective-permute-start.17 = (f32[8,128]{1,0:T(8,128)S(1)}, f32[8,128]{1,0:T(8,128)S(1)}, u32[]{:S(2)}, u32[]{:S(2)}) collective-permute-start(f32[8,128]{1,0:T(8,128)S(1)} %get-tuple-element.59.direction_in), channel_id=1, source_target_pairs={{0,2},{1,17},{2,0},{3,5},{4,6},{5,3},{6,4},{7,9},{8,10},{9,7},{10,... | collective-permute-start | bytes 12296 | tf_op jit(solution)/shard_map/ppermute | solution.py:379
  44.5 1.2 %collective-permute-start.18 = (f32[8,128]{1,0:T(8,128)S(1)}, f32[8,128]{1,0:T(8,128)S(1)}, u32[]{:S(2)}, u32[]{:S(2)}) collective-permute-start(f32[8,128]{1,0:T(8,128)S(1)} %collective-permute-done.17.mine_ref), channel_id=1, source_target_pairs={{0,1},{1,0},{2,3},{3,2},{4,5},{5,4},{6,7},{7,6},{8,9},{9,8},{10,11... | collective-permute-start | bytes 12296 | tf_op jit(solution)/shard_map/ppermute | solution.py:385
  46.1 3.7 %collective-permute-start.19 = (f32[8,128]{1,0:T(8,128)S(1)}, f32[8,128]{1,0:T(8,128)S(1)}, u32[]{:S(2)}, u32[]{:S(2)}) collective-permute-start(f32[8,128]{1,0:T(8,128)S(1)} %get-tuple-element.50.direction_in), channel_id=1, source_target_pairs={{0,2},{1,17},{2,0},{3,5},{4,6},{5,3},{6,4},{7,9},{8,10},{9,7},{10,... | collective-permute-start | bytes 12296 | tf_op jit(solution)/shard_map/ppermute | solution.py:379
  49.8 1.2 %collective-permute-start.20 = (f32[8,128]{1,0:T(8,128)S(1)}, f32[8,128]{1,0:T(8,128)S(1)}, u32[]{:S(2)}, u32[]{:S(2)}) collective-permute-start(f32[8,128]{1,0:T(8,128)S(1)} %collective-permute-done.19.mine_ref), channel_id=1, source_target_pairs={{0,1},{1,0},{2,3},{3,2},{4,5},{5,4},{6,7},{7,6},{8,9},{9,8},{10,11... | collective-permute-start | bytes 12296 | tf_op jit(solution)/shard_map/ppermute | solution.py:385
  51.5 3.7 %collective-permute-start.22 = (f32[16,128]{1,0:T(8,128)S(1)}, f32[16,128]{1,0:T(8,128)S(1)}, u32[]{:S(2)}, u32[]{:S(2)}) collective-permute-start(f32[16,128]{1,0:T(8,128)S(1)} %get-tuple-element.53.packed_ref), channel_id=1, source_target_pairs={{0,2},{1,15},{2,0},{3,5},{4,6},{5,3},{6,4},{7,9},{8,10},{9,7},{10,... | collective-permute-start | bytes 24584 | tf_op jit(solution)/shard_map/ppermute | solution.py:379
  51.6 5.4 %collective-permute-start.21 = (f32[16,128]{1,0:T(8,128)S(1)}, f32[16,128]{1,0:T(8,128)S(1)}, u32[]{:S(2)}, u32[]{:S(2)}) collective-permute-start(f32[16,128]{1,0:T(8,128)S(1)} %get-tuple-element.53.packed_ref), channel_id=1, source_target_pairs={{0,8},{2,10},{4,12},{6,14},{8,0},{10,2},{12,4},{14,6},{1,9},{3,11}... | collective-permute-start | bytes 24584 | tf_op jit(solution)/shard_map/ppermute | solution.py:358
  55.2 2.5 %collective-permute-start.23 = (f32[16,128]{1,0:T(8,128)S(1)}, f32[16,128]{1,0:T(8,128)S(1)}, u32[]{:S(2)}, u32[]{:S(2)}) collective-permute-start(f32[16,128]{1,0:T(8,128)S(1)} %collective-permute-done.22.mine_ref), channel_id=1, source_target_pairs={{0,1},{1,0},{2,3},{3,2},{4,5},{5,4},{6,7},{7,6},{8,9},{9,8},{10,11... | collective-permute-start | bytes 24584 | tf_op jit(solution)/shard_map/ppermute | solution.py:385
  (5 other events, 24.1 us)

commit v10 on v9

--- a/solution.py
+++ b/solution.py
@@ -140,13 +140,9 @@
     return lax.rem(lax.axis_index("dom"), 2) == 0
 
 
-def meets_next():
-    return is_even() == (lax.axis_index("sub") == 0)
-
-
-def by_partner(mine, yours):
-    zero = lax.axis_index("sub") == 0
-    return jnp.where(zero, mine, yours), jnp.where(zero, yours, mine)
+def by_sibling(mine, yours):
+    ahead = lax.axis_index("sub") == 1
+    return jnp.where(ahead, mine, yours), jnp.where(ahead, yours, mine)
 
 
 def by_side(first, second):
@@ -159,10 +155,8 @@
     own, after, before, far = (
         scatter(outgoing[o : o + 1], maps[o : o + 1], torso) for o in range(maps.shape[0])
     )
-    ahead = meets_next()
     own_ref[...] = own
-    keep_ref[...] = jnp.where(ahead, after, before)
-    give_ref[...] = jnp.where(ahead, before, after)
+    keep_ref[...], give_ref[...] = by_sibling(after, before)
     far_ref[...] = far
 
 
@@ -265,7 +259,7 @@
     out_ref, own_ref, keep_ref, give_ref, far_ref,
 ):
     nodes, maps = nodes_ref[...], maps_ref[...]
-    after, before = by_side(*by_partner(mine_ref[...], yours_ref[...]))
+    after, before = by_sibling(mine_ref[...], yours_ref[...])
     estimates = [own_estimate[...], after, before, far_estimate[...]]
     feedback = feedback_of(estimates, nodes, maps, states_ref.shape[1])
     rows = [states_ref[i] for i in range(states_ref.shape[0])]
@@ -277,10 +271,10 @@
     spread_current(outgoing, maps, own_ref, keep_ref, give_ref, far_ref)
 
 
-def window_of(chain, direction, first, second):
+def window_of(chain, direction, mine, yours):
     torso = direction.shape[0]
     here = lax.axis_index("dom")
-    after, before = by_side(first, second)
+    after, before = by_sibling(mine, yours)
     before = jnp.where(here > 0, before[torso - HALO :], 0.0)
     after = jnp.where(here < chain - 1, after[0:HALO], 0.0)
     filler = jnp.zeros((torso - 2 * HALO, LANES), F32)
@@ -293,7 +287,7 @@
 ):
     diag = diag_ref[...]
     direction = direction_in[...]
-    window = window_of(chain, direction, *by_partner(mine_ref[...], yours_ref[...]))
+    window = window_of(chain, direction, mine_ref[...], yours_ref[...])
     moved = product(own_ref, other_ref, pick_ref, window)
     residual = forcing_ref[...] - (diag * direction + moved)
     estimate = direction
@@ -310,7 +304,7 @@
     torso = estimate_ref.shape[0]
     diag = diag_ref[...]
     direction = direction_in[...]
-    window = window_of(chain, direction, *by_partner(mine_ref[...], yours_ref[...]))
+    window = window_of(chain, direction, mine_ref[...], yours_ref[...])
     moved = product(own_ref, other_ref, pick_ref, window)
     residual = residual_in[...] - (diag * direction + moved)
     direction = KEEP[1] * direction + PULL[1] * (residual / diag)
@@ -332,8 +326,7 @@
     head, tail = slice(0, torso), slice(torso, 2 * torso)
     estimate, direction = packed_ref[head], packed_ref[tail]
     potential_ref[...] = estimate
-    first, second = by_partner(mine_ref[...], yours_ref[...])
-    after, before = by_side(first[head], second[head])
+    after, before = by_sibling(mine_ref[head], yours_ref[head])
     feedback = feedback_of(
         [estimate, after, before, far_ref[head]], nodes_ref[...], maps_ref[...],
         states_ref.shape[1],
@@ -342,7 +335,7 @@
     dense_ref[0] = states_ref[0] + TIME_STEP * FEEDBACK_RATE * feedback
     for k in range(states_ref.shape[1]):
         out_ref[:, k * LANES : (k + 1) * LANES] = dense_ref[:, k, :]
-    window = window_of(chain, direction, first[tail], second[tail])
+    window = window_of(chain, direction, mine_ref[tail], yours_ref[tail])
     moved = product(own_ref, other_ref, pick_ref, window)
     residual_ref[...] = residual_in[...] - (diag_ref[...] * direction + moved)
 
@@ -363,19 +356,17 @@
     def with_second(value):
         return swap(value, lambda i: ((i + 1) ^ 1) - 1)
 
-    def with_either(value, closed):
+    def with_near(value, closed):
         cases = lax.axis_size("case")
-        ends = () if closed or cases % 2 else (0, chain - 1)
+        ring = 2 * chain
         pairs = []
         for case in range(cases):
-            for i in range(chain):
-                me = (case * chain + i) * 2
-                pairs.append((me, (case * chain + (i ^ 1)) * 2))
-                if i in ends:
-                    pairs.append((me + 1, ((case ^ 1) * chain + i) * 2 + 1))
-                else:
-                    second = (((i + 1) ^ 1) - 1) % chain
-                    pairs.append((me + 1, (case * chain + second) * 2 + 1))
+            for me in range(ring):
+                other = (me + 1 if me % 2 else me - 1) % ring
+                beside = case
+                if me in (0, ring - 1) and not closed and cases % 2 == 0:
+                    other, beside = me, case ^ 1
+                pairs.append((case * ring + me, beside * ring + other))
         return lax.ppermute(value, ("case", "dom", "sub"), pairs)
 
     def with_far(value):
@@ -394,14 +385,15 @@
     counts = jnp.pad(send_count, ((0, 0), (0, slots - peers)))
     table = jnp.concatenate([send_node[0], recv_row[0], counts])
     index = shape(peers, slots, dtype=jnp.int32)
-    payload = shape(2 * peers, slots)
-    states, payload, nodes = call(begin, (dense, payload, index))(in_specs=[VMEM] * 2)(
+    payload_shape = shape(2 * peers, slots)
+    states, payload, nodes = call(begin, (dense, payload_shape, index))(in_specs=[VMEM] * 2)(
         states, table
     )
     columns, diag, own = call(
-        bring, (shape(*columns.shape[::-1], dtype=jnp.int32), field, payload)
+        bring, (shape(*columns.shape[::-1], dtype=jnp.int32), field, payload_shape)
     )(in_specs=[VMEM] * 3)(columns.T, diagonal.reshape(torso, LANES), payload)
     first, far, second = with_first(payload), with_far(payload), with_second(payload)
+    second, other_columns = lax.optimization_barrier((second, from_sibling(columns)))
     maps, forcing = call(first_forcing, (index, field))(in_specs=[VMEM] * 6)(
         nodes, table, own, first, far, second
     )
@@ -409,18 +401,18 @@
         last = time_step == 1
         forcing = forcing + from_sibling(forcing)
         direction = forcing / (CHEB_THETA * diag)
-        halo = with_either(direction, False)
+        halo = with_near(direction, False)
         if not last:
             choices = 2 * columns.shape[0] * torso
             direction, pick = call(bring_tiles, (field, shape(choices, 2 * torso)))(
                 in_specs=[VMEM] * 4
-            )(tile_values, columns, from_sibling(columns), direction)
+            )(tile_values, columns, other_columns, direction)
             halo, direction = lax.optimization_barrier((halo, direction))
             stored = (tile_values, other_tiles, pick)
         residual, direction, estimate = call(
             functools.partial(sweep_one, chain), (field,) * 3
         )(in_specs=[VMEM] * 8)(*stored, halo, from_sibling(halo), forcing, direction, diag)
-        halo = with_either(direction, False)
+        halo = with_near(direction, False)
         swept = call(
             functools.partial(sweep_two, chain, last), (packed, field) if last else field
         )(in_specs=[VMEM] * 9)(
@@ -428,13 +420,13 @@
         )
         estimate, residual = swept if last else (swept, None)
         far = with_far(estimate)
-        near = with_either(estimate, True)
+        near = with_near(estimate, True)
         if not last:
             states, own, keep, give, away = call(next_shares, (dense,) + (field,) * 4)(
                 in_specs=[VMEM] * 7
             )(states, estimate, far, near, from_sibling(near), nodes, maps)
             far = with_far(away)
-            near = with_either(keep + from_sibling(give), True)
+            near = with_near(keep + from_sibling(give), True)
             forcing = TORSO_COUPLING * (own + far + near)
     new_states, potential, residual = call(
         functools.partial(finish, chain),

time: 59.5 us -> 61.1 us (1.027)
  waiting for transfers between devices: 27.4 us -> 30.2 us
  starting transfers between devices: 21.2 us -> 20 us
    ppermute x11, starting transfers between devices: 7.73 us -> 0.81 us  [from_sibling(): return lax.ppermute(value, 'sub', [(0, 1), (1, 0)])]
    ppermute x7, starting transfers between devices: 3.08 us -> 8.1 us  [with_near(): return lax.ppermute(value, ('case', 'dom', 'sub'), pairs)]
    ppermute x7, waiting for transfers between devices: 13.7 us -> 16.4 us  [with_near(): return lax.ppermute(value, ('case', 'dom', 'sub'), pairs)]
    ppermute x11, waiting for transfers between devices: 8.63 us -> 10.6 us  [from_sibling(): return lax.ppermute(value, 'sub', [(0, 1), (1, 0)])]
    ppermute x6, waiting for transfers between devices: 5.03 us -> 3.2 us  [swap(): lax.ppermute(value, 'dom', [(i, partner(i) % chain) for i in range(chain)])]
    ppermute x6, starting transfers between devices: 10.4 us -> 11.1 us  [swap(): lax.ppermute(value, 'dom', [(i, partner(i) % chain) for i in range(chain)])]
  transfers between devices with their start and end apart: 24 -> 24, of which waited for: 18 -> 19; matrix products, arithmetic and copies ran while one was open for 1% -> 1% of each run, Pallas kernels for 1% -> 1%
where the time goes in v10:
time: 61.1 us; the launch traced here: 60.8 us
  waiting for transfers between devices  30.2 us (49%)
  starting transfers between devices  20 us (33%)
  Pallas kernels  5.23 us (9%)
  local copies, waits for them, and re-layouts  3.88 us (6%)
  other arithmetic  0.76 us (1%)
  between operations  0.71 us (1%)
    ppermute x7, waiting for transfers between devices, with_near(): return lax.ppermute(value, ('case', 'dom', 'sub'), pairs)  16.4 us
    ppermute x6, starting transfers between devices, swap(): lax.ppermute(value, 'dom', [(i, partner(i) % chain) for i in range(chain)])  11.1 us
    ppermute x11, waiting for transfers between devices, from_sibling(): return lax.ppermute(value, 'sub', [(0, 1), (1, 0)])  10.6 us
    ppermute x7, starting transfers between devices, with_near(): return lax.ppermute(value, ('case', 'dom', 'sub'), pairs)  8.1 us
    unnamed x10, local copies, waits for them, and re-layouts  3.88 us
    ppermute x6, waiting for transfers between devices, swap(): lax.ppermute(value, 'dom', [(i, partner(i) % chain) for i in range(chain)])  3.2 us
    pallas_call x1, Pallas kernels, on_device(): call(functools.partial(finish, chain), (shape(*dense.shape[:1], node_coun...  1.45 us
  transfers between devices with their start and end apart: 24, of which 19 were waited for; matrix products, arithmetic and copies ran while one was open for 1% of the time, Pallas kernels for 1%

profile of v10, /device:TPU:0, one launch (start us, length us, event | category | flops | bytes accessed | tf_op | source)
XLA Modules:
  0.0 60.8 jit_solution(13580752017890282212)
XLA Ops:
  3.1 5.6 %collective-permute-start.1 = (f32[8,512]{1,0:T(8,128)S(1)}, f32[8,512]{1,0:T(8,128)S(1)}, u32[]{:S(2)}, u32[]{:S(2)}) collective-permute-start(f32[8,512]{1,0:T(8,128)S(1)} %get-tuple-element.33.payload_ref), channel_id=1, source_target_pairs={{0,14},{2,4},{4,2},{6,8},{8,6},{10,12},{12,10},{14,0},{1,15},{3,5}... | collective-permute-start | bytes 49160 | tf_op jit(solution)/shard_map/ppermute | solution.py:351
  11.2 1.2 %collective-permute-done.2.other_cols = s32[4,8]{1,0:T(4,128)S(1)} collective-permute-done((s32[4,8]{1,0:T(4,128)S(1)}, s32[4,8]{1,0:T(4,128)S(1)}, u32[]{:S(2)}, u32[]{:S(2)}) %collective-permute-start.2) | collective-permute-done | bytes 160 | tf_op jit(solution)/shard_map/ppermute | solution.py:376
  14.8 1.5 %collective-permute-start.6 = (f32[8,128]{1,0:T(8,128)S(1)}, f32[8,128]{1,0:T(8,128)S(1)}, u32[]{:S(2)}, u32[]{:S(2)}) collective-permute-start(f32[8,128]{1,0:T(8,128)S(1)} %get-tuple-element.65.direction_ref), channel_id=1, source_target_pairs={{0,16},{1,2},{2,1},{3,4},{4,3},{5,6},{6,5},{7,8},{8,7},{9,10},{10,... | collective-permute-start | bytes 12296 | tf_op jit(solution)/shard_map/ppermute | solution.py:370
  16.4 1.6 %copy-done = f32[8,4,128,128]{3,2,1,0:T(8,128)S(1)} copy-done((f32[8,4,128,128]{3,2,1,0:T(8,128)S(1)}, f32[8,4,128,128]{3,2,1,0:T(8,128)}, u32[]{:S(2)}) %copy-start) | copy-done | bytes 2097176
  18.5 1.2 %collective-permute-done.7.yours_ref = f32[8,128]{1,0:T(8,128)S(1)} collective-permute-done((f32[8,128]{1,0:T(8,128)S(1)}, f32[8,128]{1,0:T(8,128)S(1)}, u32[]{:S(2)}, u32[]{:S(2)}) %collective-permute-start.7) | collective-permute-done | bytes 4128 | tf_op jit(solution)/shard_map/ppermute | solution.py:376
  20.2 1.6 %collective-permute-start.8 = (f32[8,128]{1,0:T(8,128)S(1)}, f32[8,128]{1,0:T(8,128)S(1)}, u32[]{:S(2)}, u32[]{:S(2)}) collective-permute-start(f32[8,128]{1,0:T(8,128)S(1)} %get-tuple-element.46.direction_in), channel_id=1, source_target_pairs={{0,16},{1,2},{2,1},{3,4},{4,3},{5,6},{6,5},{7,8},{8,7},{9,10},{10,... | collective-permute-start | bytes 12296 | tf_op jit(solution)/shard_map/ppermute | solution.py:370
  21.8 2.1 %collective-permute-done.8.mine_ref = f32[8,128]{1,0:T(8,128)S(1)} collective-permute-done((f32[8,128]{1,0:T(8,128)S(1)}, f32[8,128]{1,0:T(8,128)S(1)}, u32[]{:S(2)}, u32[]{:S(2)}) %collective-permute-start.8) | collective-permute-done | bytes 4128 | tf_op jit(solution)/shard_map/ppermute | solution.py:370
  23.9 1.2 %collective-permute-done.9.yours_ref = f32[8,128]{1,0:T(8,128)S(1)} collective-permute-done((f32[8,128]{1,0:T(8,128)S(1)}, f32[8,128]{1,0:T(8,128)S(1)}, u32[]{:S(2)}, u32[]{:S(2)}) %collective-permute-start.9) | collective-permute-done | bytes 4128 | tf_op jit(solution)/shard_map/ppermute | solution.py:376
  26.2 2.7 %collective-permute-start.10 = (f32[8,128]{1,0:T(8,128)S(1)}, f32[8,128]{1,0:T(8,128)S(1)}, u32[]{:S(2)}, u32[]{:S(2)}) collective-permute-start(f32[8,128]{1,0:T(8,128)S(1)} %shard_map.99.own_estimate), channel_id=1, source_target_pairs={{0,8},{2,10},{4,12},{6,14},{8,0},{10,2},{12,4},{14,6},{1,9},{3,11}... | collective-permute-start | bytes 12296 | tf_op jit(solution)/shard_map/ppermute | solution.py:351
  28.9 2.6 %collective-permute-done.11.mine_ref = f32[8,128]{1,0:T(8,128)S(1)} collective-permute-done((f32[8,128]{1,0:T(8,128)S(1)}, f32[8,128]{1,0:T(8,128)S(1)}, u32[]{:S(2)}, u32[]{:S(2)}) %collective-permute-start.11) | collective-permute-done | bytes 4128 | tf_op jit(solution)/shard_map/ppermute | solution.py:370
  31.5 1.2 %collective-permute-done.12.yours_ref = f32[8,128]{1,0:T(8,128)S(1)} collective-permute-done((f32[8,128]{1,0:T(8,128)S(1)}, f32[8,128]{1,0:T(8,128)S(1)}, u32[]{:S(2)}, u32[]{:S(2)}) %collective-permute-start.12) | collective-permute-done | bytes 4128 | tf_op jit(solution)/shard_map/ppermute | solution.py:376
  34.8 1.3 %collective-permute-start.15 = (f32[8,128]{1,0:T(8,128)S(1)}, f32[8,128]{1,0:T(8,128)S(1)}, u32[]{:S(2)}, u32[]{:S(2)}) collective-permute-start(f32[8,128]{1,0:T(8,128)S(1)} %add.19), channel_id=1, source_target_pairs={{0,15},{1,2},{2,1},{3,4},{4,3},{5,6},{6,5},{7,8},{8,7},{9,10},{10,... | collective-permute-start | bytes 12296 | tf_op jit(solution)/shard_map/ppermute | solution.py:370
  36.1 2.2 %collective-permute-done.13 = f32[8,128]{1,0:T(8,128)S(1)} collective-permute-done((f32[8,128]{1,0:T(8,128)S(1)}, f32[8,128]{1,0:T(8,128)S(1)}, u32[]{:S(2)}, u32[]{:S(2)}) %collective-permute-start.13) | collective-permute-done | bytes 4128 | tf_op jit(solution)/shard_map/ppermute | solution.py:351
  38.3 2.2 %collective-permute-done.15 = f32[8,128]{1,0:T(8,128)S(1)} collective-permute-done((f32[8,128]{1,0:T(8,128)S(1)}, f32[8,128]{1,0:T(8,128)S(1)}, u32[]{:S(2)}, u32[]{:S(2)}) %collective-permute-start.15) | collective-permute-done | bytes 4128 | tf_op jit(solution)/shard_map/ppermute | solution.py:370
  40.5 1.2 %collective-permute-done.16 = f32[8,128]{1,0:T(8,128)S(1)} collective-permute-done((f32[8,128]{1,0:T(8,128)S(1)}, f32[8,128]{1,0:T(8,128)S(1)}, u32[]{:S(2)}, u32[]{:S(2)}) %collective-permute-start.16) | collective-permute-done | bytes 4128 | tf_op jit(solution)/shard_map/ppermute | solution.py:376
  41.7 1.5 %collective-permute-start.17 = (f32[8,128]{1,0:T(8,128)S(1)}, f32[8,128]{1,0:T(8,128)S(1)}, u32[]{:S(2)}, u32[]{:S(2)}) collective-permute-start(f32[8,128]{1,0:T(8,128)S(1)} %get-tuple-element.63.direction_in), channel_id=1, source_target_pairs={{0,16},{1,2},{2,1},{3,4},{4,3},{5,6},{6,5},{7,8},{8,7},{9,10},{10,... | collective-permute-start | bytes 12296 | tf_op jit(solution)/shard_map/ppermute | solution.py:370
  43.2 2.1 %collective-permute-done.17.mine_ref = f32[8,128]{1,0:T(8,128)S(1)} collective-permute-done((f32[8,128]{1,0:T(8,128)S(1)}, f32[8,128]{1,0:T(8,128)S(1)}, u32[]{:S(2)}, u32[]{:S(2)}) %collective-permute-start.17) | collective-permute-done | bytes 4128 | tf_op jit(solution)/shard_map/ppermute | solution.py:370
  45.3 1.2 %collective-permute-done.18.yours_ref = f32[8,128]{1,0:T(8,128)S(1)} collective-permute-done((f32[8,128]{1,0:T(8,128)S(1)}, f32[8,128]{1,0:T(8,128)S(1)}, u32[]{:S(2)}, u32[]{:S(2)}) %collective-permute-start.18) | collective-permute-done | bytes 4128 | tf_op jit(solution)/shard_map/ppermute | solution.py:376
  47.0 1.6 %collective-permute-start.19 = (f32[8,128]{1,0:T(8,128)S(1)}, f32[8,128]{1,0:T(8,128)S(1)}, u32[]{:S(2)}, u32[]{:S(2)}) collective-permute-start(f32[8,128]{1,0:T(8,128)S(1)} %get-tuple-element.54.direction_in), channel_id=1, source_target_pairs={{0,16},{1,2},{2,1},{3,4},{4,3},{5,6},{6,5},{7,8},{8,7},{9,10},{10,... | collective-permute-start | bytes 12296 | tf_op jit(solution)/shard_map/ppermute | solution.py:370
  48.6 2.1 %collective-permute-done.19.mine_ref = f32[8,128]{1,0:T(8,128)S(1)} collective-permute-done((f32[8,128]{1,0:T(8,128)S(1)}, f32[8,128]{1,0:T(8,128)S(1)}, u32[]{:S(2)}, u32[]{:S(2)}) %collective-permute-start.19) | collective-permute-done | bytes 4128 | tf_op jit(solution)/shard_map/ppermute | solution.py:370
  50.7 1.2 %collective-permute-done.20.yours_ref = f32[8,128]{1,0:T(8,128)S(1)} collective-permute-done((f32[8,128]{1,0:T(8,128)S(1)}, f32[8,128]{1,0:T(8,128)S(1)}, u32[]{:S(2)}, u32[]{:S(2)}) %collective-permute-start.20) | collective-permute-done | bytes 4128 | tf_op jit(solution)/shard_map/ppermute | solution.py:376
  53.3 4.9 %collective-permute-done.22.mine_ref = f32[16,128]{1,0:T(8,128)S(1)} collective-permute-done((f32[16,128]{1,0:T(8,128)S(1)}, f32[16,128]{1,0:T(8,128)S(1)}, u32[]{:S(2)}, u32[]{:S(2)}) %collective-permute-start.22) | collective-permute-done | bytes 8224 | tf_op jit(solution)/shard_map/ppermute | solution.py:370
  58.2 1.2 %collective-permute-done.23.yours_ref = f32[16,128]{1,0:T(8,128)S(1)} collective-permute-done((f32[16,128]{1,0:T(8,128)S(1)}, f32[16,128]{1,0:T(8,128)S(1)}, u32[]{:S(2)}, u32[]{:S(2)}) %collective-permute-start.23) | collective-permute-done | bytes 8224 | tf_op jit(solution)/shard_map/ppermute | solution.py:376
  59.4 1.4 %shard_map.103 = (f32[19,2048]{1,0:T(8,128)}, f32[8,128]{1,0:T(8,128)}, f32[8,128]{1,0:T(8,128)}) custom-call(f32[8,4,128,128]{3,2,1,0:T(8,128)S(1)} %copy-done.1, f32[8,4,128,128]{3,2,1,0:T(8,128)S(1)} %collective-permute-done.other_ref, f32[64,16]{1,0:T(8,128)S(1)} %get-tuple-element.41.pick_ref, f32[16,128]{1,0:T(8,128)S(1)} %get-tuple-element.57.packed_ref, ...), custom_call_target="tpu_custom_call" | custom-call | flops 4000000 | bytes 262144 | tf_op jit(solution)/shard_map/pallas_call | solution.py:431
  (49 shorter events, 13.7 us)
Async XLA Ops:
  0.6 19.0 %collective-permute-start = (f32[8,4,128,128]{3,2,1,0:T(8,128)}, f32[8,4,128,128]{3,2,1,0:T(8,128)S(1)}, u32[]{:S(2)}, u32[]{:S(2)}) collective-permute-start(f32[8,4,128,128]{3,2,1,0:T(8,128)} %own_ref.9), channel_id=1, source_target_pairs={{0,1},{1,0},{2,3},{3,2},{4,5},{5,4},{6,7},{7,6},{8,9},{9,8},{10,11... | collective-permute-start | bytes 6291464 | tf_op jit(solution)/shard_map/ppermute | solution.py:376
  3.1 9.2 %collective-permute-start.1 = (f32[8,512]{1,0:T(8,128)S(1)}, f32[8,512]{1,0:T(8,128)S(1)}, u32[]{:S(2)}, u32[]{:S(2)}) collective-permute-start(f32[8,512]{1,0:T(8,128)S(1)} %get-tuple-element.33.payload_ref), channel_id=1, source_target_pairs={{0,14},{2,4},{4,2},{6,8},{8,6},{10,12},{12,10},{14,0},{1,15},{3,5}... | collective-permute-start | bytes 49160 | tf_op jit(solution)/shard_map/ppermute | solution.py:351
  8.7 4.6 %collective-permute-start.4 = (f32[8,512]{1,0:T(8,128)S(1)}, f32[8,512]{1,0:T(8,128)S(1)}, u32[]{:S(2)}, u32[]{:S(2)}) collective-permute-start(f32[8,512]{1,0:T(8,128)S(1)} %get-tuple-element.33.payload_ref), channel_id=1, source_target_pairs={{0,8},{2,10},{4,12},{6,14},{8,0},{10,2},{12,4},{14,6},{1,9},{3,11}... | collective-permute-start | bytes 49160 | tf_op jit(solution)/shard_map/ppermute | solution.py:351
  8.7 4.6 %collective-permute-start.3 = (f32[8,512]{1,0:T(8,128)S(1)}, f32[8,512]{1,0:T(8,128)S(1)}, u32[]{:S(2)}, u32[]{:S(2)}) collective-permute-start(f32[8,512]{1,0:T(8,128)S(1)} %get-tuple-element.33.payload_ref), channel_id=1, source_target_pairs={{0,2},{2,0},{4,6},{6,4},{8,10},{10,8},{12,14},{14,12},{1,3},{3,1},... | collective-permute-start | bytes 49160 | tf_op jit(solution)/shard_map/ppermute | solution.py:351
  11.2 1.2 %collective-permute-start.2 = (s32[4,8]{1,0:T(4,128)S(1)}, s32[4,8]{1,0:T(4,128)S(1)}, u32[]{:S(2)}, u32[]{:S(2)}) collective-permute-start(s32[4,8]{1,0:T(4,128)S(1)} %get-tuple-element.34.own_cols), channel_id=1, source_target_pairs={{0,1},{1,0},{2,3},{3,2},{4,5},{5,4},{6,7},{7,6},{8,9},{9,8},{10,11... | collective-permute-start | bytes 392 | tf_op jit(solution)/shard_map/ppermute | solution.py:376
  13.6 1.2 %collective-permute-start.5 = (f32[8,128]{1,0:T(8,128)S(1)}, f32[8,128]{1,0:T(8,128)S(1)}, u32[]{:S(2)}, u32[]{:S(2)}) collective-permute-start(f32[8,128]{1,0:T(8,128)S(1)} %get-tuple-element.39), channel_id=1, source_target_pairs={{0,1},{1,0},{2,3},{3,2},{4,5},{5,4},{6,7},{7,6},{8,9},{9,8},{10,11... | collective-permute-start | bytes 12296 | tf_op jit(solution)/shard_map/ppermute | solution.py:376
  14.8 3.6 %collective-permute-start.6 = (f32[8,128]{1,0:T(8,128)S(1)}, f32[8,128]{1,0:T(8,128)S(1)}, u32[]{:S(2)}, u32[]{:S(2)}) collective-permute-start(f32[8,128]{1,0:T(8,128)S(1)} %get-tuple-element.65.direction_ref), channel_id=1, source_target_pairs={{0,16},{1,2},{2,1},{3,4},{4,3},{5,6},{6,5},{7,8},{8,7},{9,10},{10,... | collective-permute-start | bytes 12296 | tf_op jit(solution)/shard_map/ppermute | solution.py:370
  18.5 1.2 %collective-permute-start.7 = (f32[8,128]{1,0:T(8,128)S(1)}, f32[8,128]{1,0:T(8,128)S(1)}, u32[]{:S(2)}, u32[]{:S(2)}) collective-permute-start(f32[8,128]{1,0:T(8,128)S(1)} %collective-permute-done.6.mine_ref), channel_id=1, source_target_pairs={{0,1},{1,0},{2,3},{3,2},{4,5},{5,4},{6,7},{7,6},{8,9},{9,8},{10,11... | collective-permute-start | bytes 12296 | tf_op jit(solution)/shard_map/ppermute | solution.py:376
  20.2 3.7 %collective-permute-start.8 = (f32[8,128]{1,0:T(8,128)S(1)}, f32[8,128]{1,0:T(8,128)S(1)}, u32[]{:S(2)}, u32[]{:S(2)}) collective-permute-start(f32[8,128]{1,0:T(8,128)S(1)} %get-tuple-element.46.direction_in), channel_id=1, source_target_pairs={{0,16},{1,2},{2,1},{3,4},{4,3},{5,6},{6,5},{7,8},{8,7},{9,10},{10,... | collective-permute-start | bytes 12296 | tf_op jit(solution)/shard_map/ppermute | solution.py:370
  23.9 1.2 %collective-permute-start.9 = (f32[8,128]{1,0:T(8,128)S(1)}, f32[8,128]{1,0:T(8,128)S(1)}, u32[]{:S(2)}, u32[]{:S(2)}) collective-permute-start(f32[8,128]{1,0:T(8,128)S(1)} %collective-permute-done.8.mine_ref), channel_id=1, source_target_pairs={{0,1},{1,0},{2,3},{3,2},{4,5},{5,4},{6,7},{7,6},{8,9},{9,8},{10,11... | collective-permute-start | bytes 12296 | tf_op jit(solution)/shard_map/ppermute | solution.py:376
  25.7 5.8 %collective-permute-start.11 = (f32[8,128]{1,0:T(8,128)S(1)}, f32[8,128]{1,0:T(8,128)S(1)}, u32[]{:S(2)}, u32[]{:S(2)}) collective-permute-start(f32[8,128]{1,0:T(8,128)S(1)} %shard_map.99.own_estimate), channel_id=1, source_target_pairs={{0,15},{1,2},{2,1},{3,4},{4,3},{5,6},{6,5},{7,8},{8,7},{9,10},{10,... | collective-permute-start | bytes 12296 | tf_op jit(solution)/shard_map/ppermute | solution.py:370
  26.2 5.3 %collective-permute-start.10 = (f32[8,128]{1,0:T(8,128)S(1)}, f32[8,128]{1,0:T(8,128)S(1)}, u32[]{:S(2)}, u32[]{:S(2)}) collective-permute-start(f32[8,128]{1,0:T(8,128)S(1)} %shard_map.99.own_estimate), channel_id=1, source_target_pairs={{0,8},{2,10},{4,12},{6,14},{8,0},{10,2},{12,4},{14,6},{1,9},{3,11}... | collective-permute-start | bytes 12296 | tf_op jit(solution)/shard_map/ppermute | solution.py:351
  31.5 1.2 %collective-permute-start.12 = (f32[8,128]{1,0:T(8,128)S(1)}, f32[8,128]{1,0:T(8,128)S(1)}, u32[]{:S(2)}, u32[]{:S(2)}) collective-permute-start(f32[8,128]{1,0:T(8,128)S(1)} %collective-permute-done.11.mine_ref), channel_id=1, source_target_pairs={{0,1},{1,0},{2,3},{3,2},{4,5},{5,4},{6,7},{7,6},{8,9},{9,8},{10,11... | collective-permute-start | bytes 12296 | tf_op jit(solution)/shard_map/ppermute | solution.py:376
  33.6 1.2 %collective-permute-start.14 = (f32[8,128]{1,0:T(8,128)S(1)}, f32[8,128]{1,0:T(8,128)S(1)}, u32[]{:S(2)}, u32[]{:S(2)}) collective-permute-start(f32[8,128]{1,0:T(8,128)S(1)} %get-tuple-element.53), channel_id=1, source_target_pairs={{0,1},{1,0},{2,3},{3,2},{4,5},{5,4},{6,7},{7,6},{8,9},{9,8},{10,11... | collective-permute-start | bytes 12296 | tf_op jit(solution)/shard_map/ppermute | solution.py:376
  33.8 4.5 %collective-permute-start.13 = (f32[8,128]{1,0:T(8,128)S(1)}, f32[8,128]{1,0:T(8,128)S(1)}, u32[]{:S(2)}, u32[]{:S(2)}) collective-permute-start(f32[8,128]{1,0:T(8,128)S(1)} %get-tuple-element.51), channel_id=1, source_target_pairs={{0,8},{2,10},{4,12},{6,14},{8,0},{10,2},{12,4},{14,6},{1,9},{3,11}... | collective-permute-start | bytes 12296 | tf_op jit(solution)/shard_map/ppermute | solution.py:351
  34.8 5.7 %collective-permute-start.15 = (f32[8,128]{1,0:T(8,128)S(1)}, f32[8,128]{1,0:T(8,128)S(1)}, u32[]{:S(2)}, u32[]{:S(2)}) collective-permute-start(f32[8,128]{1,0:T(8,128)S(1)} %add.19), channel_id=1, source_target_pairs={{0,15},{1,2},{2,1},{3,4},{4,3},{5,6},{6,5},{7,8},{8,7},{9,10},{10,... | collective-permute-start | bytes 12296 | tf_op jit(solution)/shard_map/ppermute | solution.py:370
  40.5 1.2 %collective-permute-start.16 = (f32[8,128]{1,0:T(8,128)S(1)}, f32[8,128]{1,0:T(8,128)S(1)}, u32[]{:S(2)}, u32[]{:S(2)}) collective-permute-start(f32[8,128]{1,0:T(8,128)S(1)} %add_multiply_fusion), channel_id=1, source_target_pairs={{0,1},{1,0},{2,3},{3,2},{4,5},{5,4},{6,7},{7,6},{8,9},{9,8},{10,11... | collective-permute-start | bytes 12296 | tf_op jit(solution)/shard_map/ppermute | solution.py:376
  41.7 3.6 %collective-permute-start.17 = (f32[8,128]{1,0:T(8,128)S(1)}, f32[8,128]{1,0:T(8,128)S(1)}, u32[]{:S(2)}, u32[]{:S(2)}) collective-permute-start(f32[8,128]{1,0:T(8,128)S(1)} %get-tuple-element.63.direction_in), channel_id=1, source_target_pairs={{0,16},{1,2},{2,1},{3,4},{4,3},{5,6},{6,5},{7,8},{8,7},{9,10},{10,... | collective-permute-start | bytes 12296 | tf_op jit(solution)/shard_map/ppermute | solution.py:370
  45.3 1.2 %collective-permute-start.18 = (f32[8,128]{1,0:T(8,128)S(1)}, f32[8,128]{1,0:T(8,128)S(1)}, u32[]{:S(2)}, u32[]{:S(2)}) collective-permute-start(f32[8,128]{1,0:T(8,128)S(1)} %collective-permute-done.17.mine_ref), channel_id=1, source_target_pairs={{0,1},{1,0},{2,3},{3,2},{4,5},{5,4},{6,7},{7,6},{8,9},{9,8},{10,11... | collective-permute-start | bytes 12296 | tf_op jit(solution)/shard_map/ppermute | solution.py:376
  47.0 3.7 %collective-permute-start.19 = (f32[8,128]{1,0:T(8,128)S(1)}, f32[8,128]{1,0:T(8,128)S(1)}, u32[]{:S(2)}, u32[]{:S(2)}) collective-permute-start(f32[8,128]{1,0:T(8,128)S(1)} %get-tuple-element.54.direction_in), channel_id=1, source_target_pairs={{0,16},{1,2},{2,1},{3,4},{4,3},{5,6},{6,5},{7,8},{8,7},{9,10},{10,... | collective-permute-start | bytes 12296 | tf_op jit(solution)/shard_map/ppermute | solution.py:370
  50.7 1.2 %collective-permute-start.20 = (f32[8,128]{1,0:T(8,128)S(1)}, f32[8,128]{1,0:T(8,128)S(1)}, u32[]{:S(2)}, u32[]{:S(2)}) collective-permute-start(f32[8,128]{1,0:T(8,128)S(1)} %collective-permute-done.19.mine_ref), channel_id=1, source_target_pairs={{0,1},{1,0},{2,3},{3,2},{4,5},{5,4},{6,7},{7,6},{8,9},{9,8},{10,11... | collective-permute-start | bytes 12296 | tf_op jit(solution)/shard_map/ppermute | solution.py:376
  52.3 5.8 %collective-permute-start.22 = (f32[16,128]{1,0:T(8,128)S(1)}, f32[16,128]{1,0:T(8,128)S(1)}, u32[]{:S(2)}, u32[]{:S(2)}) collective-permute-start(f32[16,128]{1,0:T(8,128)S(1)} %get-tuple-element.57.packed_ref), channel_id=1, source_target_pairs={{0,15},{1,2},{2,1},{3,4},{4,3},{5,6},{6,5},{7,8},{8,7},{9,10},{10,... | collective-permute-start | bytes 24584 | tf_op jit(solution)/shard_map/ppermute | solution.py:370
  52.4 5.8 %collective-permute-start.21 = (f32[16,128]{1,0:T(8,128)S(1)}, f32[16,128]{1,0:T(8,128)S(1)}, u32[]{:S(2)}, u32[]{:S(2)}) collective-permute-start(f32[16,128]{1,0:T(8,128)S(1)} %get-tuple-element.57.packed_ref), channel_id=1, source_target_pairs={{0,8},{2,10},{4,12},{6,14},{8,0},{10,2},{12,4},{14,6},{1,9},{3,11}... | collective-permute-start | bytes 24584 | tf_op jit(solution)/shard_map/ppermute | solution.py:351
  58.2 1.2 %collective-permute-start.23 = (f32[16,128]{1,0:T(8,128)S(1)}, f32[16,128]{1,0:T(8,128)S(1)}, u32[]{:S(2)}, u32[]{:S(2)}) collective-permute-start(f32[16,128]{1,0:T(8,128)S(1)} %collective-permute-done.22.mine_ref), channel_id=1, source_target_pairs={{0,1},{1,0},{2,3},{3,2},{4,5},{5,4},{6,7},{7,6},{8,9},{9,8},{10,11... | collective-permute-start | bytes 24584 | tf_op jit(solution)/shard_map/ppermute | solution.py:376
  (5 other events, 25.3 us)

commit v11 on v9

--- a/solution.py
+++ b/solution.py
@@ -229,8 +229,12 @@
     payload_out[...] = payload_ref[...]
 
 
-def bring_tiles(tiles_ref, own_cols, other_cols, direction_ref, direction_out, pick_ref):
+def bring_tiles(tiles_ref, direction_ref, direction_out):
     direction_out[...] = direction_ref[...]
+    del tiles_ref
+
+
+def choose(own_cols, other_cols, pick_ref):
     slots, tiles = own_cols.shape
     eye = lax.broadcasted_iota(jnp.int32, (tiles, tiles), 0) == lax.broadcasted_iota(
         jnp.int32, (tiles, tiles), 1
@@ -240,24 +244,39 @@
         row = own_cols[k : k + 1] if k < slots else other_cols[k - slots : k - slots + 1]
         column = jnp.sum(jnp.where(eye, row.astype(F32), 0.0), axis=1, keepdims=True)
         pick_ref[k * tiles : (k + 1) * tiles] = jnp.where(place == column.astype(jnp.int32), 1.0, 0.0)
-    del tiles_ref
-
-
-def first_forcing(
-    nodes_ref, table_ref, own_ref, first_ref, far_ref, second_ref,
-    maps_ref, forcing_ref,
-):
-    peers = nodes_ref.shape[0]
-    after, before = by_side(first_ref[...], second_ref[...])
-    come = [own_ref[0:1], before[1:2], after[2:3], far_ref[3:4]]
-    rows = [own_ref[peers : peers + 1], after[peers + 1 : peers + 2]]
-    rows += [before[peers + 2 : peers + 3], far_ref[peers + 3 : peers + 4]]
-    maps_ref[...] = jnp.where(nodes_ref[...] < 0, -1, jnp.concatenate(rows, axis=0).astype(jnp.int32))
+
+
+def first_forcing(own_ref, sibling_ref, near_ref, far_ref, base_ref, give_ref, forcing_ref):
+    peers = own_ref.shape[0] // 2
+    ahead = meets_next()
+    pairs = [(own_ref[0:1], own_ref[peers : peers + 1])]
+    pairs.append((far_ref[3:4], own_ref[peers + 3 : peers + 4]))
+    for k, mine in enumerate((own_ref, sibling_ref)):
+        at = 2 * peers * k
+        come = jnp.where(ahead, near_ref[at + 2 : at + 3], near_ref[at + 1 : at + 2])
+        rows = jnp.where(ahead, mine[peers + 2 : peers + 3], mine[peers + 1 : peers + 2])
+        pairs.append((come, rows))
     total = None
-    for o in range(peers):
-        part = scatter(come[o], table_ref[peers + o : peers + o + 1], forcing_ref.shape[0])
+    for come, rows in pairs:
+        part = scatter(come, rows.astype(jnp.int32), forcing_ref.shape[0])
         total = part if total is None else total + part
     forcing_ref[...] = TORSO_COUPLING * total
+    keep, give = (
+        jnp.where(ahead, near_ref[at + 1 : at + 2], near_ref[at + 2 : at + 3])
+        for at in (peers, 3 * peers)
+    )
+    give_ref[...] = give
+    base_ref[0:1] = own_ref[peers : peers + 1]
+    base_ref[1:2] = keep
+    base_ref[2:3] = far_ref[peers + 3 : peers + 4]
+
+
+def complete(base_ref, got_ref, nodes_ref, maps_ref):
+    ahead = meets_next()
+    keep, got = base_ref[1:2], got_ref[...]
+    after, before = jnp.where(ahead, keep, got), jnp.where(ahead, got, keep)
+    rows = jnp.concatenate([base_ref[0:1], after, before, base_ref[2:3]], axis=0)
+    maps_ref[...] = jnp.where(nodes_ref[...] < 0, -1, rows.astype(jnp.int32))
 
 
 def next_shares(
@@ -354,14 +373,8 @@
     heart = node_count // LANES
     torso = diagonal.shape[0] // LANES
 
-    def swap(value, partner):
-        return lax.ppermute(value, "dom", [(i, partner(i) % chain) for i in range(chain)])
-
-    def with_first(value):
-        return swap(value, lambda i: i ^ 1)
-
-    def with_second(value):
-        return swap(value, lambda i: ((i + 1) ^ 1) - 1)
+    def with_far(value):
+        return lax.ppermute(value, "dom", [(i, (i + chain // 2) % chain) for i in range(chain)])
 
     def with_either(value, closed):
         cases = lax.axis_size("case")
@@ -378,9 +391,6 @@
                     pairs.append((me + 1, (case * chain + second) * 2 + 1))
         return lax.ppermute(value, ("case", "dom", "sub"), pairs)
 
-    def with_far(value):
-        return swap(value, lambda i: i + chain // 2)
-
     def from_sibling(value):
         return lax.ppermute(value, "sub", [(0, 1), (1, 0)])
 
@@ -390,21 +400,25 @@
     dense = shape(states.shape[0], heart, LANES)
     field = shape(torso, LANES)
     packed = shape(2 * torso, LANES)
-    other_tiles = from_sibling(tile_values)
     counts = jnp.pad(send_count, ((0, 0), (0, slots - peers)))
     table = jnp.concatenate([send_node[0], recv_row[0], counts])
     index = shape(peers, slots, dtype=jnp.int32)
-    payload = shape(2 * peers, slots)
-    states, payload, nodes = call(begin, (dense, payload, index))(in_specs=[VMEM] * 2)(
+    payload_shape = shape(2 * peers, slots)
+    states, payload, nodes = call(begin, (dense, payload_shape, index))(in_specs=[VMEM] * 2)(
         states, table
     )
+    beside = from_sibling(payload)
+    tile_values, beside = lax.optimization_barrier((tile_values, beside))
+    other_tiles = from_sibling(tile_values)
+    far = with_far(payload)
+    near = with_either(jnp.concatenate([payload, beside]), True)
     columns, diag, own = call(
-        bring, (shape(*columns.shape[::-1], dtype=jnp.int32), field, payload)
+        bring, (shape(*columns.shape[::-1], dtype=jnp.int32), field, payload_shape)
     )(in_specs=[VMEM] * 3)(columns.T, diagonal.reshape(torso, LANES), payload)
-    first, far, second = with_first(payload), with_far(payload), with_second(payload)
-    maps, forcing = call(first_forcing, (index, field))(in_specs=[VMEM] * 6)(
-        nodes, table, own, first, far, second
-    )
+    base, give, forcing = call(first_forcing, (shape(3, slots), shape(1, slots), field))(
+        in_specs=[VMEM] * 4
+    )(own, beside, near, far)
+    maps = call(complete, index)(in_specs=[VMEM] * 3)(base, from_sibling(give), nodes)
     for time_step in range(2):
         last = time_step == 1
         forcing = forcing + from_sibling(forcing)
@@ -412,9 +426,10 @@
         halo = with_either(direction, False)
         if not last:
             choices = 2 * columns.shape[0] * torso
-            direction, pick = call(bring_tiles, (field, shape(choices, 2 * torso)))(
-                in_specs=[VMEM] * 4
-            )(tile_values, columns, from_sibling(columns), direction)
+            direction = call(bring_tiles, field)(in_specs=[VMEM] * 2)(tile_values, direction)
+            pick = call(choose, shape(choices, 2 * torso))(in_specs=[VMEM] * 2)(
+                columns, from_sibling(columns)
+            )
             halo, direction = lax.optimization_barrier((halo, direction))
             stored = (tile_values, other_tiles, pick)
         residual, direction, estimate = call(

time: 59.5 us -> 59.2 us (level)
  starting transfers between devices: 21.2 us -> 17.5 us
  waiting for transfers between devices: 27.4 us -> 31 us
    ppermute x6 -> x4, starting transfers between devices: 10.4 us -> 5.28 us  [with_far(): lax.ppermute(value, 'dom', [(i, (i + chain // 2) % chain) for i in range(...]
    ppermute x7 -> x8, waiting for transfers between devices: 13.7 us -> 17.2 us  [with_either(): return lax.ppermute(value, ('case', 'dom', 'sub'), pairs)]
    ppermute x11 -> x13, waiting for transfers between devices: 8.63 us -> 9.73 us  [from_sibling(): return lax.ppermute(value, 'sub', [(0, 1), (1, 0)])]
    ppermute x11 -> x13, starting transfers between devices: 7.73 us -> 8.79 us  [from_sibling(): return lax.ppermute(value, 'sub', [(0, 1), (1, 0)])]
    ppermute x6 -> x4, waiting for transfers between devices: 5.03 us -> 4.01 us  [with_far(): lax.ppermute(value, 'dom', [(i, (i + chain // 2) % chain) for i in range(...]
    ppermute x7 -> x8, starting transfers between devices: 3.08 us -> 3.39 us  [with_either(): return lax.ppermute(value, ('case', 'dom', 'sub'), pairs)]
  transfers between devices with their start and end apart: 24 -> 25, of which waited for: 18 -> 19; matrix products, arithmetic and copies ran while one was open for 1% -> 0% of each run, Pallas kernels for 1% -> 1%
where the time goes in v11:
time: 59.2 us; the launch traced here: 58.9 us
  waiting for transfers between devices  31 us (52%)
  starting transfers between devices  17.5 us (30%)
  Pallas kernels  5.06 us (9%)
  local copies, waits for them, and re-layouts  3.88 us (7%)
  other arithmetic  0.76 us (1%)
  between operations  0.76 us (1%)
    ppermute x8, waiting for transfers between devices, with_either(): return lax.ppermute(value, ('case', 'dom', 'sub'), pairs)  17.2 us
    ppermute x13, waiting for transfers between devices, from_sibling(): return lax.ppermute(value, 'sub', [(0, 1), (1, 0)])  9.73 us
    ppermute x13, starting transfers between devices, from_sibling(): return lax.ppermute(value, 'sub', [(0, 1), (1, 0)])  8.79 us
    ppermute x4, starting transfers between devices, with_far(): lax.ppermute(value, 'dom', [(i, (i + chain // 2) % chain) for i in range(...  5.28 us
    ppermute x4, waiting for transfers between devices, with_far(): lax.ppermute(value, 'dom', [(i, (i + chain // 2) % chain) for i in range(...  4.01 us
    unnamed x10, local copies, waits for them, and re-layouts  3.88 us
    ppermute x8, starting transfers between devices, with_either(): return lax.ppermute(value, ('case', 'dom', 'sub'), pairs)  3.39 us
    pallas_call x1, Pallas kernels, on_device(): call(functools.partial(finish, chain), (shape(*dense.shape[:1], node_coun...  1.45 us
  transfers between devices with their start and end apart: 25, of which 19 were waited for; matrix products, arithmetic and copies ran while one was open for 0% of the time, Pallas kernels for 1%

profile of v11, /device:TPU:0, one launch (start us, length us, event | category | flops | bytes accessed | tf_op | source)
XLA Modules:
  0.0 58.9 jit_solution(8880345661852372711)
XLA Ops:
  1.4 0.9 %copy-done.2 = f32[19,2048]{1,0:T(8,128)S(1)} copy-done((f32[19,2048]{1,0:T(8,128)S(1)}, f32[19,2048]{1,0:T(8,128)}, u32[]{:S(2)}) %copy-start.2) | copy-done | bytes 155672
  3.1 0.8 %collective-permute-done.sibling_ref = f32[8,512]{1,0:T(8,128)S(1)} collective-permute-done((f32[8,512]{1,0:T(8,128)S(1)}, f32[8,512]{1,0:T(8,128)S(1)}, u32[]{:S(2)}, u32[]{:S(2)}) %collective-permute-start) | collective-permute-done | bytes 16416 | tf_op jit(solution)/shard_map/ppermute | solution.py:395
  4.3 2.7 %collective-permute-start.3 = (f32[16,512]{1,0:T(8,128)S(1)}, f32[16,512]{1,0:T(8,128)S(1)}, u32[]{:S(2)}, u32[]{:S(2)}) collective-permute-start(f32[16,512]{1,0:T(8,128)S(1)} %pad_maximum_fusion), channel_id=1, source_target_pairs={{0,2},{1,15},{2,0},{3,5},{4,6},{5,3},{6,4},{7,9},{8,10},{9,7},{10,... | collective-permute-start | bytes 98312 | tf_op jit(solution)/shard_map/ppermute | solution.py:392
  7.0 2.6 %collective-permute-start.4 = (f32[8,512]{1,0:T(8,128)S(1)}, f32[8,512]{1,0:T(8,128)S(1)}, u32[]{:S(2)}, u32[]{:S(2)}) collective-permute-start(f32[8,512]{1,0:T(8,128)S(1)} %get-tuple-element.32.payload_ref), channel_id=1, source_target_pairs={{0,8},{2,10},{4,12},{6,14},{8,0},{10,2},{12,4},{14,6},{1,9},{3,11}... | collective-permute-start | bytes 49160 | tf_op jit(solution)/shard_map/ppermute | solution.py:377
  11.9 2.0 %collective-permute-start.5 = (f32[8,128]{1,0:T(8,128)S(1)}, f32[8,128]{1,0:T(8,128)S(1)}, u32[]{:S(2)}, u32[]{:S(2)}) collective-permute-start(f32[8,128]{1,0:T(8,128)S(1)} %get-tuple-element.38), channel_id=1, source_target_pairs={{0,1},{1,0},{2,3},{3,2},{4,5},{5,4},{6,7},{7,6},{8,9},{9,8},{10,11... | collective-permute-start | bytes 12296 | tf_op jit(solution)/shard_map/ppermute | solution.py:395
  14.7 1.6 %copy-done = f32[8,4,128,128]{3,2,1,0:T(8,128)S(1)} copy-done((f32[8,4,128,128]{3,2,1,0:T(8,128)S(1)}, f32[8,4,128,128]{3,2,1,0:T(8,128)}, u32[]{:S(2)}) %copy-start) | copy-done | bytes 2097176
  16.3 2.0 %collective-permute-done.6.mine_ref = f32[8,128]{1,0:T(8,128)S(1)} collective-permute-done((f32[8,128]{1,0:T(8,128)S(1)}, f32[8,128]{1,0:T(8,128)S(1)}, u32[]{:S(2)}, u32[]{:S(2)}) %collective-permute-start.6) | collective-permute-done | bytes 4128 | tf_op jit(solution)/shard_map/ppermute | solution.py:392
  20.5 3.5 %collective-permute-done.8.mine_ref = f32[8,128]{1,0:T(8,128)S(1)} collective-permute-done((f32[8,128]{1,0:T(8,128)S(1)}, f32[8,128]{1,0:T(8,128)S(1)}, u32[]{:S(2)}, u32[]{:S(2)}) %collective-permute-start.8) | collective-permute-done | bytes 4128 | tf_op jit(solution)/shard_map/ppermute | solution.py:392
  24.0 1.2 %collective-permute-done.9.yours_ref = f32[8,128]{1,0:T(8,128)S(1)} collective-permute-done((f32[8,128]{1,0:T(8,128)S(1)}, f32[8,128]{1,0:T(8,128)S(1)}, u32[]{:S(2)}, u32[]{:S(2)}) %collective-permute-start.9) | collective-permute-done | bytes 4128 | tf_op jit(solution)/shard_map/ppermute | solution.py:395
  25.8 2.0 %collective-permute-start.10 = (f32[8,128]{1,0:T(8,128)S(1)}, f32[8,128]{1,0:T(8,128)S(1)}, u32[]{:S(2)}, u32[]{:S(2)}) collective-permute-start(f32[8,128]{1,0:T(8,128)S(1)} %shard_map.100.own_estimate), channel_id=1, source_target_pairs={{0,8},{2,10},{4,12},{6,14},{8,0},{10,2},{12,4},{14,6},{1,9},{3,11}... | collective-permute-start | bytes 12296 | tf_op jit(solution)/shard_map/ppermute | solution.py:377
  27.8 1.5 %collective-permute-done.11.mine_ref = f32[8,128]{1,0:T(8,128)S(1)} collective-permute-done((f32[8,128]{1,0:T(8,128)S(1)}, f32[8,128]{1,0:T(8,128)S(1)}, u32[]{:S(2)}, u32[]{:S(2)}) %collective-permute-start.11) | collective-permute-done | bytes 4128 | tf_op jit(solution)/shard_map/ppermute | solution.py:392
  29.3 1.7 %collective-permute-start.12 = (f32[8,128]{1,0:T(8,128)S(1)}, f32[8,128]{1,0:T(8,128)S(1)}, u32[]{:S(2)}, u32[]{:S(2)}) collective-permute-start(f32[8,128]{1,0:T(8,128)S(1)} %collective-permute-done.11.mine_ref), channel_id=1, source_target_pairs={{0,1},{1,0},{2,3},{3,2},{4,5},{5,4},{6,7},{7,6},{8,9},{9,8},{10,11... | collective-permute-start | bytes 12296 | tf_op jit(solution)/shard_map/ppermute | solution.py:395
  31.0 1.2 %collective-permute-done.13.got_ref = f32[1,512]{1,0:T(1,128)S(1)} collective-permute-done((f32[1,512]{1,0:T(1,128)S(1)}, f32[1,512]{1,0:T(1,128)S(1)}, u32[]{:S(2)}, u32[]{:S(2)}) %collective-permute-start.13) | collective-permute-done | bytes 2080 | tf_op jit(solution)/shard_map/ppermute | solution.py:395
  32.2 0.9 %shard_map.102 = (f32[19,16,128]{2,1,0:T(8,128)S(1)}, f32[8,128]{1,0:T(8,128)S(1)}, f32[8,128]{1,0:T(8,128)S(1)}, f32[8,128]{1,0:T(8,128)S(1)}, f32[8,128]{1,0:T(8,128)S(1)}) custom-call(f32[19,16,128]{2,1,0:T(8,128)S(1)} %get-tuple-element.35.states_ref, f32[8,128]{1,0:T(8,128)S(1)} %shard_map.100.own_estimate, ...), custom_call_target="tpu_custom_call" | custom-call | flops 4000000 | bytes 262144 | tf_op jit(solution)/shard_map/pallas_call | solution.py:448
  33.4 0.9 %collective-permute-done.15 = f32[8,128]{1,0:T(8,128)S(1)} collective-permute-done((f32[8,128]{1,0:T(8,128)S(1)}, f32[8,128]{1,0:T(8,128)S(1)}, u32[]{:S(2)}, u32[]{:S(2)}) %collective-permute-start.15) | collective-permute-done | bytes 4128 | tf_op jit(solution)/shard_map/ppermute | solution.py:395
  34.6 3.3 %collective-permute-done.14 = f32[8,128]{1,0:T(8,128)S(1)} collective-permute-done((f32[8,128]{1,0:T(8,128)S(1)}, f32[8,128]{1,0:T(8,128)S(1)}, u32[]{:S(2)}, u32[]{:S(2)}) %collective-permute-start.14) | collective-permute-done | bytes 4128 | tf_op jit(solution)/shard_map/ppermute | solution.py:377
  38.0 1.7 %collective-permute-start.17 = (f32[8,128]{1,0:T(8,128)S(1)}, f32[8,128]{1,0:T(8,128)S(1)}, u32[]{:S(2)}, u32[]{:S(2)}) collective-permute-start(f32[8,128]{1,0:T(8,128)S(1)} %add_multiply_fusion), channel_id=1, source_target_pairs={{0,1},{1,0},{2,3},{3,2},{4,5},{5,4},{6,7},{7,6},{8,9},{9,8},{10,11... | collective-permute-start | bytes 12296 | tf_op jit(solution)/shard_map/ppermute | solution.py:395
  40.6 3.6 %collective-permute-done.18.mine_ref = f32[8,128]{1,0:T(8,128)S(1)} collective-permute-done((f32[8,128]{1,0:T(8,128)S(1)}, f32[8,128]{1,0:T(8,128)S(1)}, u32[]{:S(2)}, u32[]{:S(2)}) %collective-permute-start.18) | collective-permute-done | bytes 4128 | tf_op jit(solution)/shard_map/ppermute | solution.py:392
  44.2 1.2 %collective-permute-done.19.yours_ref = f32[8,128]{1,0:T(8,128)S(1)} collective-permute-done((f32[8,128]{1,0:T(8,128)S(1)}, f32[8,128]{1,0:T(8,128)S(1)}, u32[]{:S(2)}, u32[]{:S(2)}) %collective-permute-start.19) | collective-permute-done | bytes 4128 | tf_op jit(solution)/shard_map/ppermute | solution.py:395
  45.9 3.6 %collective-permute-done.20.mine_ref = f32[8,128]{1,0:T(8,128)S(1)} collective-permute-done((f32[8,128]{1,0:T(8,128)S(1)}, f32[8,128]{1,0:T(8,128)S(1)}, u32[]{:S(2)}, u32[]{:S(2)}) %collective-permute-start.20) | collective-permute-done | bytes 4128 | tf_op jit(solution)/shard_map/ppermute | solution.py:392
  49.5 1.2 %collective-permute-done.21.yours_ref = f32[8,128]{1,0:T(8,128)S(1)} collective-permute-done((f32[8,128]{1,0:T(8,128)S(1)}, f32[8,128]{1,0:T(8,128)S(1)}, u32[]{:S(2)}, u32[]{:S(2)}) %collective-permute-start.21) | collective-permute-done | bytes 4128 | tf_op jit(solution)/shard_map/ppermute | solution.py:395
  51.9 3.0 %collective-permute-done.23.mine_ref = f32[16,128]{1,0:T(8,128)S(1)} collective-permute-done((f32[16,128]{1,0:T(8,128)S(1)}, f32[16,128]{1,0:T(8,128)S(1)}, u32[]{:S(2)}, u32[]{:S(2)}) %collective-permute-start.23) | collective-permute-done | bytes 8224 | tf_op jit(solution)/shard_map/ppermute | solution.py:392
  54.9 1.7 %collective-permute-start.24 = (f32[16,128]{1,0:T(8,128)S(1)}, f32[16,128]{1,0:T(8,128)S(1)}, u32[]{:S(2)}, u32[]{:S(2)}) collective-permute-start(f32[16,128]{1,0:T(8,128)S(1)} %collective-permute-done.23.mine_ref), channel_id=1, source_target_pairs={{0,1},{1,0},{2,3},{3,2},{4,5},{5,4},{6,7},{7,6},{8,9},{9,8},{10,11... | collective-permute-start | bytes 24584 | tf_op jit(solution)/shard_map/ppermute | solution.py:395
  57.5 1.4 %shard_map.105 = (f32[19,2048]{1,0:T(8,128)}, f32[8,128]{1,0:T(8,128)}, f32[8,128]{1,0:T(8,128)}) custom-call(f32[8,4,128,128]{3,2,1,0:T(8,128)S(1)} %copy-done.1, f32[8,4,128,128]{3,2,1,0:T(8,128)S(1)} %collective-permute-done.1.other_ref, f32[64,16]{1,0:T(8,128)S(1)} %shard_map.96.pick_ref, f32[16,128]{1,0:T(8,128)S(1)} %get-tuple-element.55.packed_ref, ...), custom_call_target="tpu_custom_call" | custom-call | flops 4000000 | bytes 262144 | tf_op jit(solution)/shard_map/pallas_call | solution.py:454
  (54 shorter events, 11.9 us)
Async XLA Ops:
  2.6 1.4 %collective-permute-start = (f32[8,512]{1,0:T(8,128)S(1)}, f32[8,512]{1,0:T(8,128)S(1)}, u32[]{:S(2)}, u32[]{:S(2)}) collective-permute-start(f32[8,512]{1,0:T(8,128)S(1)} %get-tuple-element.32.payload_ref), channel_id=1, source_target_pairs={{0,1},{1,0},{2,3},{3,2},{4,5},{5,4},{6,7},{7,6},{8,9},{9,8},{10,11... | collective-permute-start | bytes 49160 | tf_op jit(solution)/shard_map/ppermute | solution.py:395
  4.0 15.8 %collective-permute-start.1 = (f32[8,4,128,128]{3,2,1,0:T(8,128)}, f32[8,4,128,128]{3,2,1,0:T(8,128)S(1)}, u32[]{:S(2)}, u32[]{:S(2)}) collective-permute-start(f32[8,4,128,128]{3,2,1,0:T(8,128)} %own_ref.4), channel_id=1, source_target_pairs={{0,1},{1,0},{2,3},{3,2},{4,5},{5,4},{6,7},{7,6},{8,9},{9,8},{10,11... | collective-permute-start | bytes 6291464 | tf_op jit(solution)/shard_map/ppermute | solution.py:395
  4.3 7.3 %collective-permute-start.3 = (f32[16,512]{1,0:T(8,128)S(1)}, f32[16,512]{1,0:T(8,128)S(1)}, u32[]{:S(2)}, u32[]{:S(2)}) collective-permute-start(f32[16,512]{1,0:T(8,128)S(1)} %pad_maximum_fusion), channel_id=1, source_target_pairs={{0,2},{1,15},{2,0},{3,5},{4,6},{5,3},{6,4},{7,9},{8,10},{9,7},{10,... | collective-permute-start | bytes 98312 | tf_op jit(solution)/shard_map/ppermute | solution.py:392
  7.0 4.6 %collective-permute-start.4 = (f32[8,512]{1,0:T(8,128)S(1)}, f32[8,512]{1,0:T(8,128)S(1)}, u32[]{:S(2)}, u32[]{:S(2)}) collective-permute-start(f32[8,512]{1,0:T(8,128)S(1)} %get-tuple-element.32.payload_ref), channel_id=1, source_target_pairs={{0,8},{2,10},{4,12},{6,14},{8,0},{10,2},{12,4},{14,6},{1,9},{3,11}... | collective-permute-start | bytes 49160 | tf_op jit(solution)/shard_map/ppermute | solution.py:377
  11.9 2.8 %collective-permute-start.5 = (f32[8,128]{1,0:T(8,128)S(1)}, f32[8,128]{1,0:T(8,128)S(1)}, u32[]{:S(2)}, u32[]{:S(2)}) collective-permute-start(f32[8,128]{1,0:T(8,128)S(1)} %get-tuple-element.38), channel_id=1, source_target_pairs={{0,1},{1,0},{2,3},{3,2},{4,5},{5,4},{6,7},{7,6},{8,9},{9,8},{10,11... | collective-permute-start | bytes 12296 | tf_op jit(solution)/shard_map/ppermute | solution.py:395
  14.7 3.6 %collective-permute-start.6 = (f32[8,128]{1,0:T(8,128)S(1)}, f32[8,128]{1,0:T(8,128)S(1)}, u32[]{:S(2)}, u32[]{:S(2)}) collective-permute-start(f32[8,128]{1,0:T(8,128)S(1)} %get-tuple-element.63.direction_ref), channel_id=1, source_target_pairs={{0,2},{1,17},{2,0},{3,5},{4,6},{5,3},{6,4},{7,9},{8,10},{9,7},{10,... | collective-permute-start | bytes 12296 | tf_op jit(solution)/shard_map/ppermute | solution.py:392
  18.3 1.4 %collective-permute-start.7 = (f32[8,128]{1,0:T(8,128)S(1)}, f32[8,128]{1,0:T(8,128)S(1)}, u32[]{:S(2)}, u32[]{:S(2)}) collective-permute-start(f32[8,128]{1,0:T(8,128)S(1)} %collective-permute-done.6.mine_ref), channel_id=1, source_target_pairs={{0,1},{1,0},{2,3},{3,2},{4,5},{5,4},{6,7},{7,6},{8,9},{9,8},{10,11... | collective-permute-start | bytes 12296 | tf_op jit(solution)/shard_map/ppermute | solution.py:395
  18.3 1.3 %collective-permute-start.2 = (s32[4,8]{1,0:T(4,128)S(1)}, s32[4,8]{1,0:T(4,128)S(1)}, u32[]{:S(2)}, u32[]{:S(2)}) collective-permute-start(s32[4,8]{1,0:T(4,128)S(1)} %get-tuple-element.34.own_cols), channel_id=1, source_target_pairs={{0,1},{1,0},{2,3},{3,2},{4,5},{5,4},{6,7},{7,6},{8,9},{9,8},{10,11... | collective-permute-start | bytes 392 | tf_op jit(solution)/shard_map/ppermute | solution.py:395
  20.3 3.7 %collective-permute-start.8 = (f32[8,128]{1,0:T(8,128)S(1)}, f32[8,128]{1,0:T(8,128)S(1)}, u32[]{:S(2)}, u32[]{:S(2)}) collective-permute-start(f32[8,128]{1,0:T(8,128)S(1)} %get-tuple-element.42.direction_in), channel_id=1, source_target_pairs={{0,2},{1,17},{2,0},{3,5},{4,6},{5,3},{6,4},{7,9},{8,10},{9,7},{10,... | collective-permute-start | bytes 12296 | tf_op jit(solution)/shard_map/ppermute | solution.py:392
  24.0 1.2 %collective-permute-start.9 = (f32[8,128]{1,0:T(8,128)S(1)}, f32[8,128]{1,0:T(8,128)S(1)}, u32[]{:S(2)}, u32[]{:S(2)}) collective-permute-start(f32[8,128]{1,0:T(8,128)S(1)} %collective-permute-done.8.mine_ref), channel_id=1, source_target_pairs={{0,1},{1,0},{2,3},{3,2},{4,5},{5,4},{6,7},{7,6},{8,9},{9,8},{10,11... | collective-permute-start | bytes 12296 | tf_op jit(solution)/shard_map/ppermute | solution.py:395
  25.6 3.7 %collective-permute-start.11 = (f32[8,128]{1,0:T(8,128)S(1)}, f32[8,128]{1,0:T(8,128)S(1)}, u32[]{:S(2)}, u32[]{:S(2)}) collective-permute-start(f32[8,128]{1,0:T(8,128)S(1)} %shard_map.100.own_estimate), channel_id=1, source_target_pairs={{0,2},{1,15},{2,0},{3,5},{4,6},{5,3},{6,4},{7,9},{8,10},{9,7},{10,... | collective-permute-start | bytes 12296 | tf_op jit(solution)/shard_map/ppermute | solution.py:392
  25.8 6.4 %collective-permute-start.10 = (f32[8,128]{1,0:T(8,128)S(1)}, f32[8,128]{1,0:T(8,128)S(1)}, u32[]{:S(2)}, u32[]{:S(2)}) collective-permute-start(f32[8,128]{1,0:T(8,128)S(1)} %shard_map.100.own_estimate), channel_id=1, source_target_pairs={{0,8},{2,10},{4,12},{6,14},{8,0},{10,2},{12,4},{14,6},{1,9},{3,11}... | collective-permute-start | bytes 12296 | tf_op jit(solution)/shard_map/ppermute | solution.py:377
  29.3 2.9 %collective-permute-start.12 = (f32[8,128]{1,0:T(8,128)S(1)}, f32[8,128]{1,0:T(8,128)S(1)}, u32[]{:S(2)}, u32[]{:S(2)}) collective-permute-start(f32[8,128]{1,0:T(8,128)S(1)} %collective-permute-done.11.mine_ref), channel_id=1, source_target_pairs={{0,1},{1,0},{2,3},{3,2},{4,5},{5,4},{6,7},{7,6},{8,9},{9,8},{10,11... | collective-permute-start | bytes 12296 | tf_op jit(solution)/shard_map/ppermute | solution.py:395
  33.2 1.2 %collective-permute-start.15 = (f32[8,128]{1,0:T(8,128)S(1)}, f32[8,128]{1,0:T(8,128)S(1)}, u32[]{:S(2)}, u32[]{:S(2)}) collective-permute-start(f32[8,128]{1,0:T(8,128)S(1)} %get-tuple-element.51), channel_id=1, source_target_pairs={{0,1},{1,0},{2,3},{3,2},{4,5},{5,4},{6,7},{7,6},{8,9},{9,8},{10,11... | collective-permute-start | bytes 12296 | tf_op jit(solution)/shard_map/ppermute | solution.py:395
  33.4 4.5 %collective-permute-start.14 = (f32[8,128]{1,0:T(8,128)S(1)}, f32[8,128]{1,0:T(8,128)S(1)}, u32[]{:S(2)}, u32[]{:S(2)}) collective-permute-start(f32[8,128]{1,0:T(8,128)S(1)} %get-tuple-element.49), channel_id=1, source_target_pairs={{0,8},{2,10},{4,12},{6,14},{8,0},{10,2},{12,4},{14,6},{1,9},{3,11}... | collective-permute-start | bytes 12296 | tf_op jit(solution)/shard_map/ppermute | solution.py:377
  34.4 3.6 %collective-permute-start.16 = (f32[8,128]{1,0:T(8,128)S(1)}, f32[8,128]{1,0:T(8,128)S(1)}, u32[]{:S(2)}, u32[]{:S(2)}) collective-permute-start(f32[8,128]{1,0:T(8,128)S(1)} %add.19), channel_id=1, source_target_pairs={{0,2},{1,15},{2,0},{3,5},{4,6},{5,3},{6,4},{7,9},{8,10},{9,7},{10,... | collective-permute-start | bytes 12296 | tf_op jit(solution)/shard_map/ppermute | solution.py:392
  38.0 2.5 %collective-permute-start.17 = (f32[8,128]{1,0:T(8,128)S(1)}, f32[8,128]{1,0:T(8,128)S(1)}, u32[]{:S(2)}, u32[]{:S(2)}) collective-permute-start(f32[8,128]{1,0:T(8,128)S(1)} %add_multiply_fusion), channel_id=1, source_target_pairs={{0,1},{1,0},{2,3},{3,2},{4,5},{5,4},{6,7},{7,6},{8,9},{9,8},{10,11... | collective-permute-start | bytes 12296 | tf_op jit(solution)/shard_map/ppermute | solution.py:395
  40.6 3.6 %collective-permute-start.18 = (f32[8,128]{1,0:T(8,128)S(1)}, f32[8,128]{1,0:T(8,128)S(1)}, u32[]{:S(2)}, u32[]{:S(2)}) collective-permute-start(f32[8,128]{1,0:T(8,128)S(1)} %get-tuple-element.61.direction_in), channel_id=1, source_target_pairs={{0,2},{1,17},{2,0},{3,5},{4,6},{5,3},{6,4},{7,9},{8,10},{9,7},{10,... | collective-permute-start | bytes 12296 | tf_op jit(solution)/shard_map/ppermute | solution.py:392
  44.2 1.2 %collective-permute-start.19 = (f32[8,128]{1,0:T(8,128)S(1)}, f32[8,128]{1,0:T(8,128)S(1)}, u32[]{:S(2)}, u32[]{:S(2)}) collective-permute-start(f32[8,128]{1,0:T(8,128)S(1)} %collective-permute-done.18.mine_ref), channel_id=1, source_target_pairs={{0,1},{1,0},{2,3},{3,2},{4,5},{5,4},{6,7},{7,6},{8,9},{9,8},{10,11... | collective-permute-start | bytes 12296 | tf_op jit(solution)/shard_map/ppermute | solution.py:395
  45.8 3.7 %collective-permute-start.20 = (f32[8,128]{1,0:T(8,128)S(1)}, f32[8,128]{1,0:T(8,128)S(1)}, u32[]{:S(2)}, u32[]{:S(2)}) collective-permute-start(f32[8,128]{1,0:T(8,128)S(1)} %get-tuple-element.52.direction_in), channel_id=1, source_target_pairs={{0,2},{1,17},{2,0},{3,5},{4,6},{5,3},{6,4},{7,9},{8,10},{9,7},{10,... | collective-permute-start | bytes 12296 | tf_op jit(solution)/shard_map/ppermute | solution.py:392
  49.5 1.2 %collective-permute-start.21 = (f32[8,128]{1,0:T(8,128)S(1)}, f32[8,128]{1,0:T(8,128)S(1)}, u32[]{:S(2)}, u32[]{:S(2)}) collective-permute-start(f32[8,128]{1,0:T(8,128)S(1)} %collective-permute-done.20.mine_ref), channel_id=1, source_target_pairs={{0,1},{1,0},{2,3},{3,2},{4,5},{5,4},{6,7},{7,6},{8,9},{9,8},{10,11... | collective-permute-start | bytes 12296 | tf_op jit(solution)/shard_map/ppermute | solution.py:395
  51.2 3.7 %collective-permute-start.23 = (f32[16,128]{1,0:T(8,128)S(1)}, f32[16,128]{1,0:T(8,128)S(1)}, u32[]{:S(2)}, u32[]{:S(2)}) collective-permute-start(f32[16,128]{1,0:T(8,128)S(1)} %get-tuple-element.55.packed_ref), channel_id=1, source_target_pairs={{0,2},{1,15},{2,0},{3,5},{4,6},{5,3},{6,4},{7,9},{8,10},{9,7},{10,... | collective-permute-start | bytes 24584 | tf_op jit(solution)/shard_map/ppermute | solution.py:392
  51.3 5.4 %collective-permute-start.22 = (f32[16,128]{1,0:T(8,128)S(1)}, f32[16,128]{1,0:T(8,128)S(1)}, u32[]{:S(2)}, u32[]{:S(2)}) collective-permute-start(f32[16,128]{1,0:T(8,128)S(1)} %get-tuple-element.55.packed_ref), channel_id=1, source_target_pairs={{0,8},{2,10},{4,12},{6,14},{8,0},{10,2},{12,4},{14,6},{1,9},{3,11}... | collective-permute-start | bytes 24584 | tf_op jit(solution)/shard_map/ppermute | solution.py:377
  54.9 2.5 %collective-permute-start.24 = (f32[16,128]{1,0:T(8,128)S(1)}, f32[16,128]{1,0:T(8,128)S(1)}, u32[]{:S(2)}, u32[]{:S(2)}) collective-permute-start(f32[16,128]{1,0:T(8,128)S(1)} %collective-permute-done.23.mine_ref), channel_id=1, source_target_pairs={{0,1},{1,0},{2,3},{3,2},{4,5},{5,4},{6,7},{7,6},{8,9},{9,8},{10,11... | collective-permute-start | bytes 24584 | tf_op jit(solution)/shard_map/ppermute | solution.py:395
  (6 other events, 8.5 us)

commit v12 on v11

--- a/solution.py
+++ b/solution.py
@@ -208,7 +208,9 @@
     return copies
 
 
-def begin(states_ref, table_ref, out_ref, payload_ref, nodes_ref):
+def begin(
+    states_ref, table_ref, out_ref, nodes_ref, own_ref, keep_ref, give_ref, far_ref
+):
     peers, slots = nodes_ref.shape
     for k in range(out_ref.shape[1]):
         out_ref[:, k, :] = states_ref[:, k * LANES : (k + 1) * LANES]
@@ -219,14 +221,24 @@
     rows, current = ionic_rows([out_ref[i] for i in range(out_ref.shape[0])])
     for i, row in enumerate(rows):
         out_ref[i] = row
-    payload_ref[0:peers] = pick_current(current, nodes_ref[...])
-    payload_ref[peers:] = table_ref[peers : 2 * peers].astype(F32)
-
-
-def bring(cols_ref, diag_ref, payload_ref, cols_out, diag_out, payload_out):
+    outgoing = pick_current(current, nodes_ref[...])
+    incoming = table_ref[peers : 2 * peers].astype(F32)
+
+    def pair(out, into):
+        return jnp.concatenate([outgoing[out : out + 1], incoming[into : into + 1]], axis=0)
+
+    to_next, to_prev = pair(1, 2), pair(2, 1)
+    ahead = meets_next()
+    own_ref[...] = pair(0, 0)
+    keep_ref[...] = jnp.where(ahead, to_next, to_prev)
+    give_ref[...] = jnp.where(ahead, to_prev, to_next)
+    far_ref[...] = pair(3, 3)
+
+
+def bring(cols_ref, diag_ref, own_ref, cols_out, diag_out, own_out):
     cols_out[...] = cols_ref[...]
     diag_out[...] = diag_ref[...]
-    payload_out[...] = payload_ref[...]
+    own_out[...] = own_ref[...]
 
 
 def bring_tiles(tiles_ref, direction_ref, direction_out):
@@ -246,36 +258,27 @@
         pick_ref[k * tiles : (k + 1) * tiles] = jnp.where(place == column.astype(jnp.int32), 1.0, 0.0)
 
 
-def first_forcing(own_ref, sibling_ref, near_ref, far_ref, base_ref, give_ref, forcing_ref):
-    peers = own_ref.shape[0] // 2
-    ahead = meets_next()
-    pairs = [(own_ref[0:1], own_ref[peers : peers + 1])]
-    pairs.append((far_ref[3:4], own_ref[peers + 3 : peers + 4]))
-    for k, mine in enumerate((own_ref, sibling_ref)):
-        at = 2 * peers * k
-        come = jnp.where(ahead, near_ref[at + 2 : at + 3], near_ref[at + 1 : at + 2])
-        rows = jnp.where(ahead, mine[peers + 2 : peers + 3], mine[peers + 1 : peers + 2])
-        pairs.append((come, rows))
+def first_forcing(
+    own_ref, keep_ref, got_ref, near_ref, to_far, far_ref, give_ref, forcing_ref
+):
     total = None
-    for come, rows in pairs:
+    for come, rows in (
+        (own_ref[0:1], own_ref[1:2]),
+        (far_ref[0:1], to_far[1:2]),
+        (near_ref[0:1], keep_ref[1:2]),
+        (near_ref[2:3], got_ref[1:2]),
+    ):
         part = scatter(come, rows.astype(jnp.int32), forcing_ref.shape[0])
         total = part if total is None else total + part
     forcing_ref[...] = TORSO_COUPLING * total
-    keep, give = (
-        jnp.where(ahead, near_ref[at + 1 : at + 2], near_ref[at + 2 : at + 3])
-        for at in (peers, 3 * peers)
-    )
-    give_ref[...] = give
-    base_ref[0:1] = own_ref[peers : peers + 1]
-    base_ref[1:2] = keep
-    base_ref[2:3] = far_ref[peers + 3 : peers + 4]
-
-
-def complete(base_ref, got_ref, nodes_ref, maps_ref):
+    give_ref[...] = near_ref[3:4]
+
+
+def complete(own_ref, near_ref, far_ref, got_ref, nodes_ref, maps_ref):
     ahead = meets_next()
-    keep, got = base_ref[1:2], got_ref[...]
+    keep, got = near_ref[1:2], got_ref[...]
     after, before = jnp.where(ahead, keep, got), jnp.where(ahead, got, keep)
-    rows = jnp.concatenate([base_ref[0:1], after, before, base_ref[2:3]], axis=0)
+    rows = jnp.concatenate([own_ref[1:2], after, before, far_ref[1:2]], axis=0)
     maps_ref[...] = jnp.where(nodes_ref[...] < 0, -1, rows.astype(jnp.int32))
 
 
@@ -403,32 +406,36 @@
     counts = jnp.pad(send_count, ((0, 0), (0, slots - peers)))
     table = jnp.concatenate([send_node[0], recv_row[0], counts])
     index = shape(peers, slots, dtype=jnp.int32)
-    payload_shape = shape(2 * peers, slots)
-    states, payload, nodes = call(begin, (dense, payload_shape, index))(in_specs=[VMEM] * 2)(
-        states, table
-    )
-    beside = from_sibling(payload)
-    tile_values, beside = lax.optimization_barrier((tile_values, beside))
+    double = shape(2, slots)
+    states, nodes, own, keep, give, to_far = call(begin, (dense, index) + (double,) * 4)(
+        in_specs=[VMEM] * 2
+    )(states, table)
+    got = from_sibling(give)
+    tile_values, got = lax.optimization_barrier((tile_values, got))
     other_tiles = from_sibling(tile_values)
-    far = with_far(payload)
-    near = with_either(jnp.concatenate([payload, beside]), True)
+    far = with_far(to_far)
+    near = with_either(jnp.concatenate([keep, got]), True)
     columns, diag, own = call(
-        bring, (shape(*columns.shape[::-1], dtype=jnp.int32), field, payload_shape)
-    )(in_specs=[VMEM] * 3)(columns.T, diagonal.reshape(torso, LANES), payload)
-    base, give, forcing = call(first_forcing, (shape(3, slots), shape(1, slots), field))(
-        in_specs=[VMEM] * 4
-    )(own, beside, near, far)
-    maps = call(complete, index)(in_specs=[VMEM] * 3)(base, from_sibling(give), nodes)
+        bring, (shape(*columns.shape[::-1], dtype=jnp.int32), field, double)
+    )(in_specs=[VMEM] * 3)(columns.T, diagonal.reshape(torso, LANES), own)
+    give, forcing = call(first_forcing, (shape(1, slots), field))(in_specs=[VMEM] * 6)(
+        own, keep, got, near, to_far, far
+    )
+    maps = call(complete, index)(in_specs=[VMEM] * 5)(own, near, far, from_sibling(give), nodes)
+    other_columns = from_sibling(columns)
     for time_step in range(2):
         last = time_step == 1
-        forcing = forcing + from_sibling(forcing)
+        others = from_sibling(forcing)
+        if not last:
+            others, other_columns = lax.optimization_barrier((others, other_columns))
+        forcing = forcing + others
         direction = forcing / (CHEB_THETA * diag)
         halo = with_either(direction, False)
         if not last:
             choices = 2 * columns.shape[0] * torso
             direction = call(bring_tiles, field)(in_specs=[VMEM] * 2)(tile_values, direction)
             pick = call(choose, shape(choices, 2 * torso))(in_specs=[VMEM] * 2)(
-                columns, from_sibling(columns)
+                columns, other_columns
             )
             halo, direction = lax.optimization_barrier((halo, direction))
             stored = (tile_values, other_tiles, pick)

time: 59.2 us -> 59.3 us (level)
  starting transfers between devices: 17.5 us -> 16.8 us
  waiting for transfers between devices: 31 us -> 31.7 us
    ppermute x4, starting transfers between devices: 5.28 us -> 4.53 us  [with_far(): lax.ppermute(value, 'dom', [(i, (i + chain // 2) % chain) for i in range(...]
where the time goes in v12:
time: 59.3 us; the launch traced here: 58.9 us
  waiting for transfers between devices  31.7 us (53%)
  starting transfers between devices  16.8 us (28%)
  Pallas kernels  5.08 us (9%)
  local copies, waits for them, and re-layouts  3.88 us (7%)
  other arithmetic  0.77 us (1%)
  between operations  0.75 us (1%)
    ppermute x8, waiting for transfers between devices, with_either(): return lax.ppermute(value, ('case', 'dom', 'sub'), pairs)  17.4 us
    ppermute x13, waiting for transfers between devices, from_sibling(): return lax.ppermute(value, 'sub', [(0, 1), (1, 0)])  10.3 us
    ppermute x13, starting transfers between devices, from_sibling(): return lax.ppermute(value, 'sub', [(0, 1), (1, 0)])  8.32 us
    ppermute x4, starting transfers between devices, with_far(): lax.ppermute(value, 'dom', [(i, (i + chain // 2) % chain) for i in range(...  4.53 us
    ppermute x4, waiting for transfers between devices, with_far(): lax.ppermute(value, 'dom', [(i, (i + chain // 2) % chain) for i in range(...  4.05 us
    ppermute x8, starting transfers between devices, with_either(): return lax.ppermute(value, ('case', 'dom', 'sub'), pairs)  3.92 us
    unnamed x10, local copies, waits for them, and re-layouts  3.88 us
    pallas_call x1, Pallas kernels, on_device(): call(functools.partial(finish, chain), (shape(*dense.shape[:1], node_coun...  1.45 us
  transfers between devices with their start and end apart: 25, of which 19 were waited for; matrix products, arithmetic and copies ran while one was open for 0% of the time, Pallas kernels for 1%

profile of v12, /device:TPU:0, one launch (start us, length us, event | category | flops | bytes accessed | tf_op | source)
XLA Modules:
  0.0 58.9 jit_solution(4810008135975870885)
XLA Ops:
  4.3 2.7 %collective-permute-start.2 = (f32[4,512]{1,0:T(4,128)S(1)}, f32[4,512]{1,0:T(4,128)S(1)}, u32[]{:S(2)}, u32[]{:S(2)}) collective-permute-start(f32[4,512]{1,0:T(4,128)S(1)} %pad_maximum_fusion), channel_id=1, source_target_pairs={{0,2},{1,15},{2,0},{3,5},{4,6},{5,3},{6,4},{7,9},{8,10},{9,7},{10,... | collective-permute-start | bytes 24584 | tf_op jit(solution)/shard_map/ppermute | solution.py:395
  7.0 2.6 %collective-permute-start.3 = (f32[2,512]{1,0:T(2,128)S(1)}, f32[2,512]{1,0:T(2,128)S(1)}, u32[]{:S(2)}, u32[]{:S(2)}) collective-permute-start(f32[2,512]{1,0:T(2,128)S(1)} %get-tuple-element.43.to_far), channel_id=1, source_target_pairs={{0,8},{2,10},{4,12},{6,14},{8,0},{10,2},{12,4},{14,6},{1,9},{3,11}... | collective-permute-start | bytes 12296 | tf_op jit(solution)/shard_map/ppermute | solution.py:380
  11.8 2.0 %collective-permute-start.4 = (f32[8,128]{1,0:T(8,128)S(1)}, f32[8,128]{1,0:T(8,128)S(1)}, u32[]{:S(2)}, u32[]{:S(2)}) collective-permute-start(f32[8,128]{1,0:T(8,128)S(1)} %get-tuple-element.44), channel_id=1, source_target_pairs={{0,1},{1,0},{2,3},{3,2},{4,5},{5,4},{6,7},{7,6},{8,9},{9,8},{10,11... | collective-permute-start | bytes 12296 | tf_op jit(solution)/shard_map/ppermute | solution.py:398
  13.9 1.1 %collective-permute-done.5.other_cols = s32[4,8]{1,0:T(4,128)S(1)} collective-permute-done((s32[4,8]{1,0:T(4,128)S(1)}, s32[4,8]{1,0:T(4,128)S(1)}, u32[]{:S(2)}, u32[]{:S(2)}) %collective-permute-start.5) | collective-permute-done | bytes 160 | tf_op jit(solution)/shard_map/ppermute | solution.py:398
  15.0 1.6 %copy-done = f32[8,4,128,128]{3,2,1,0:T(8,128)S(1)} copy-done((f32[8,4,128,128]{3,2,1,0:T(8,128)S(1)}, f32[8,4,128,128]{3,2,1,0:T(8,128)}, u32[]{:S(2)}) %copy-start) | copy-done | bytes 2097176
  16.6 2.0 %collective-permute-done.6.mine_ref = f32[8,128]{1,0:T(8,128)S(1)} collective-permute-done((f32[8,128]{1,0:T(8,128)S(1)}, f32[8,128]{1,0:T(8,128)S(1)}, u32[]{:S(2)}, u32[]{:S(2)}) %collective-permute-start.6) | collective-permute-done | bytes 4128 | tf_op jit(solution)/shard_map/ppermute | solution.py:395
  18.7 1.1 %collective-permute-done.7.yours_ref = f32[8,128]{1,0:T(8,128)S(1)} collective-permute-done((f32[8,128]{1,0:T(8,128)S(1)}, f32[8,128]{1,0:T(8,128)S(1)}, u32[]{:S(2)}, u32[]{:S(2)}) %collective-permute-start.7) | collective-permute-done | bytes 4128 | tf_op jit(solution)/shard_map/ppermute | solution.py:398
  20.8 3.2 %collective-permute-done.8.mine_ref = f32[8,128]{1,0:T(8,128)S(1)} collective-permute-done((f32[8,128]{1,0:T(8,128)S(1)}, f32[8,128]{1,0:T(8,128)S(1)}, u32[]{:S(2)}, u32[]{:S(2)}) %collective-permute-start.8) | collective-permute-done | bytes 4128 | tf_op jit(solution)/shard_map/ppermute | solution.py:395
  24.0 1.2 %collective-permute-done.9.yours_ref = f32[8,128]{1,0:T(8,128)S(1)} collective-permute-done((f32[8,128]{1,0:T(8,128)S(1)}, f32[8,128]{1,0:T(8,128)S(1)}, u32[]{:S(2)}, u32[]{:S(2)}) %collective-permute-start.9) | collective-permute-done | bytes 4128 | tf_op jit(solution)/shard_map/ppermute | solution.py:398
  26.1 1.3 %collective-permute-start.10 = (f32[8,128]{1,0:T(8,128)S(1)}, f32[8,128]{1,0:T(8,128)S(1)}, u32[]{:S(2)}, u32[]{:S(2)}) collective-permute-start(f32[8,128]{1,0:T(8,128)S(1)} %shard_map.100.own_estimate), channel_id=1, source_target_pairs={{0,8},{2,10},{4,12},{6,14},{8,0},{10,2},{12,4},{14,6},{1,9},{3,11}... | collective-permute-start | bytes 12296 | tf_op jit(solution)/shard_map/ppermute | solution.py:380
  27.4 1.9 %collective-permute-done.11.mine_ref = f32[8,128]{1,0:T(8,128)S(1)} collective-permute-done((f32[8,128]{1,0:T(8,128)S(1)}, f32[8,128]{1,0:T(8,128)S(1)}, u32[]{:S(2)}, u32[]{:S(2)}) %collective-permute-start.11) | collective-permute-done | bytes 4128 | tf_op jit(solution)/shard_map/ppermute | solution.py:395
  29.3 1.7 %collective-permute-start.12 = (f32[8,128]{1,0:T(8,128)S(1)}, f32[8,128]{1,0:T(8,128)S(1)}, u32[]{:S(2)}, u32[]{:S(2)}) collective-permute-start(f32[8,128]{1,0:T(8,128)S(1)} %collective-permute-done.11.mine_ref), channel_id=1, source_target_pairs={{0,1},{1,0},{2,3},{3,2},{4,5},{5,4},{6,7},{7,6},{8,9},{9,8},{10,11... | collective-permute-start | bytes 12296 | tf_op jit(solution)/shard_map/ppermute | solution.py:398
  31.1 1.2 %collective-permute-done.13.got_ref = f32[1,512]{1,0:T(1,128)S(1)} collective-permute-done((f32[1,512]{1,0:T(1,128)S(1)}, f32[1,512]{1,0:T(1,128)S(1)}, u32[]{:S(2)}, u32[]{:S(2)}) %collective-permute-start.13) | collective-permute-done | bytes 2080 | tf_op jit(solution)/shard_map/ppermute | solution.py:398
  32.2 0.9 %shard_map.102 = (f32[19,16,128]{2,1,0:T(8,128)S(1)}, f32[8,128]{1,0:T(8,128)S(1)}, f32[8,128]{1,0:T(8,128)S(1)}, f32[8,128]{1,0:T(8,128)S(1)}, f32[8,128]{1,0:T(8,128)S(1)}) custom-call(f32[19,16,128]{2,1,0:T(8,128)S(1)} %get-tuple-element.46.states_ref, f32[8,128]{1,0:T(8,128)S(1)} %shard_map.100.own_estimate, ...), custom_call_target="tpu_custom_call" | custom-call | flops 4000000 | bytes 262144 | tf_op jit(solution)/shard_map/pallas_call | solution.py:455
  33.4 1.0 %collective-permute-done.15 = f32[8,128]{1,0:T(8,128)S(1)} collective-permute-done((f32[8,128]{1,0:T(8,128)S(1)}, f32[8,128]{1,0:T(8,128)S(1)}, u32[]{:S(2)}, u32[]{:S(2)}) %collective-permute-start.15) | collective-permute-done | bytes 4128 | tf_op jit(solution)/shard_map/ppermute | solution.py:398
  34.4 3.5 %collective-permute-done.14 = f32[8,128]{1,0:T(8,128)S(1)} collective-permute-done((f32[8,128]{1,0:T(8,128)S(1)}, f32[8,128]{1,0:T(8,128)S(1)}, u32[]{:S(2)}, u32[]{:S(2)}) %collective-permute-start.14) | collective-permute-done | bytes 4128 | tf_op jit(solution)/shard_map/ppermute | solution.py:380
  38.0 1.7 %collective-permute-start.17 = (f32[8,128]{1,0:T(8,128)S(1)}, f32[8,128]{1,0:T(8,128)S(1)}, u32[]{:S(2)}, u32[]{:S(2)}) collective-permute-start(f32[8,128]{1,0:T(8,128)S(1)} %add_multiply_fusion), channel_id=1, source_target_pairs={{0,1},{1,0},{2,3},{3,2},{4,5},{5,4},{6,7},{7,6},{8,9},{9,8},{10,11... | collective-permute-start | bytes 12296 | tf_op jit(solution)/shard_map/ppermute | solution.py:398
  40.6 3.6 %collective-permute-done.18.mine_ref = f32[8,128]{1,0:T(8,128)S(1)} collective-permute-done((f32[8,128]{1,0:T(8,128)S(1)}, f32[8,128]{1,0:T(8,128)S(1)}, u32[]{:S(2)}, u32[]{:S(2)}) %collective-permute-start.18) | collective-permute-done | bytes 4128 | tf_op jit(solution)/shard_map/ppermute | solution.py:395
  44.2 1.2 %collective-permute-done.19.yours_ref = f32[8,128]{1,0:T(8,128)S(1)} collective-permute-done((f32[8,128]{1,0:T(8,128)S(1)}, f32[8,128]{1,0:T(8,128)S(1)}, u32[]{:S(2)}, u32[]{:S(2)}) %collective-permute-start.19) | collective-permute-done | bytes 4128 | tf_op jit(solution)/shard_map/ppermute | solution.py:398
  46.0 3.6 %collective-permute-done.20.mine_ref = f32[8,128]{1,0:T(8,128)S(1)} collective-permute-done((f32[8,128]{1,0:T(8,128)S(1)}, f32[8,128]{1,0:T(8,128)S(1)}, u32[]{:S(2)}, u32[]{:S(2)}) %collective-permute-start.20) | collective-permute-done | bytes 4128 | tf_op jit(solution)/shard_map/ppermute | solution.py:395
  49.5 1.2 %collective-permute-done.21.yours_ref = f32[8,128]{1,0:T(8,128)S(1)} collective-permute-done((f32[8,128]{1,0:T(8,128)S(1)}, f32[8,128]{1,0:T(8,128)S(1)}, u32[]{:S(2)}, u32[]{:S(2)}) %collective-permute-start.21) | collective-permute-done | bytes 4128 | tf_op jit(solution)/shard_map/ppermute | solution.py:398
  52.0 3.0 %collective-permute-done.23.mine_ref = f32[16,128]{1,0:T(8,128)S(1)} collective-permute-done((f32[16,128]{1,0:T(8,128)S(1)}, f32[16,128]{1,0:T(8,128)S(1)}, u32[]{:S(2)}, u32[]{:S(2)}) %collective-permute-start.23) | collective-permute-done | bytes 8224 | tf_op jit(solution)/shard_map/ppermute | solution.py:395
  54.9 1.7 %collective-permute-start.24 = (f32[16,128]{1,0:T(8,128)S(1)}, f32[16,128]{1,0:T(8,128)S(1)}, u32[]{:S(2)}, u32[]{:S(2)}) collective-permute-start(f32[16,128]{1,0:T(8,128)S(1)} %collective-permute-done.23.mine_ref), channel_id=1, source_target_pairs={{0,1},{1,0},{2,3},{3,2},{4,5},{5,4},{6,7},{7,6},{8,9},{9,8},{10,11... | collective-permute-start | bytes 24584 | tf_op jit(solution)/shard_map/ppermute | solution.py:398
  57.5 1.4 %shard_map.105 = (f32[19,2048]{1,0:T(8,128)}, f32[8,128]{1,0:T(8,128)}, f32[8,128]{1,0:T(8,128)}) custom-call(f32[8,4,128,128]{3,2,1,0:T(8,128)S(1)} %copy-done.1, f32[8,4,128,128]{3,2,1,0:T(8,128)S(1)} %collective-permute-done.1.other_ref, f32[64,16]{1,0:T(8,128)S(1)} %shard_map.97.pick_ref, f32[16,128]{1,0:T(8,128)S(1)} %get-tuple-element.63.packed_ref, ...), custom_call_target="tpu_custom_call" | custom-call | flops 4000000 | bytes 262144 | tf_op jit(solution)/shard_map/pallas_call | solution.py:461
  (54 shorter events, 12.0 us)
Async XLA Ops:
  2.6 1.3 %collective-permute-start = (f32[2,512]{1,0:T(2,128)S(1)}, f32[2,512]{1,0:T(2,128)S(1)}, u32[]{:S(2)}, u32[]{:S(2)}) collective-permute-start(f32[2,512]{1,0:T(2,128)S(1)} %get-tuple-element.36), channel_id=1, source_target_pairs={{0,1},{1,0},{2,3},{3,2},{4,5},{5,4},{6,7},{7,6},{8,9},{9,8},{10,11... | collective-permute-start | bytes 12296 | tf_op jit(solution)/shard_map/ppermute | solution.py:398
  3.9 15.9 %collective-permute-start.1 = (f32[8,4,128,128]{3,2,1,0:T(8,128)}, f32[8,4,128,128]{3,2,1,0:T(8,128)S(1)}, u32[]{:S(2)}, u32[]{:S(2)}) collective-permute-start(f32[8,4,128,128]{3,2,1,0:T(8,128)} %own_ref.4), channel_id=1, source_target_pairs={{0,1},{1,0},{2,3},{3,2},{4,5},{5,4},{6,7},{7,6},{8,9},{9,8},{10,11... | collective-permute-start | bytes 6291464 | tf_op jit(solution)/shard_map/ppermute | solution.py:398
  4.3 7.2 %collective-permute-start.2 = (f32[4,512]{1,0:T(4,128)S(1)}, f32[4,512]{1,0:T(4,128)S(1)}, u32[]{:S(2)}, u32[]{:S(2)}) collective-permute-start(f32[4,512]{1,0:T(4,128)S(1)} %pad_maximum_fusion), channel_id=1, source_target_pairs={{0,2},{1,15},{2,0},{3,5},{4,6},{5,3},{6,4},{7,9},{8,10},{9,7},{10,... | collective-permute-start | bytes 24584 | tf_op jit(solution)/shard_map/ppermute | solution.py:395
  7.0 4.5 %collective-permute-start.3 = (f32[2,512]{1,0:T(2,128)S(1)}, f32[2,512]{1,0:T(2,128)S(1)}, u32[]{:S(2)}, u32[]{:S(2)}) collective-permute-start(f32[2,512]{1,0:T(2,128)S(1)} %get-tuple-element.43.to_far), channel_id=1, source_target_pairs={{0,8},{2,10},{4,12},{6,14},{8,0},{10,2},{12,4},{14,6},{1,9},{3,11}... | collective-permute-start | bytes 12296 | tf_op jit(solution)/shard_map/ppermute | solution.py:380
  11.8 3.1 %collective-permute-start.4 = (f32[8,128]{1,0:T(8,128)S(1)}, f32[8,128]{1,0:T(8,128)S(1)}, u32[]{:S(2)}, u32[]{:S(2)}) collective-permute-start(f32[8,128]{1,0:T(8,128)S(1)} %get-tuple-element.44), channel_id=1, source_target_pairs={{0,1},{1,0},{2,3},{3,2},{4,5},{5,4},{6,7},{7,6},{8,9},{9,8},{10,11... | collective-permute-start | bytes 12296 | tf_op jit(solution)/shard_map/ppermute | solution.py:398
  13.8 1.2 %collective-permute-start.5 = (s32[4,8]{1,0:T(4,128)S(1)}, s32[4,8]{1,0:T(4,128)S(1)}, u32[]{:S(2)}, u32[]{:S(2)}) collective-permute-start(s32[4,8]{1,0:T(4,128)S(1)} %get-tuple-element.39.own_cols), channel_id=1, source_target_pairs={{0,1},{1,0},{2,3},{3,2},{4,5},{5,4},{6,7},{7,6},{8,9},{9,8},{10,11... | collective-permute-start | bytes 392 | tf_op jit(solution)/shard_map/ppermute | solution.py:398
  15.0 3.7 %collective-permute-start.6 = (f32[8,128]{1,0:T(8,128)S(1)}, f32[8,128]{1,0:T(8,128)S(1)}, u32[]{:S(2)}, u32[]{:S(2)}) collective-permute-start(f32[8,128]{1,0:T(8,128)S(1)} %get-tuple-element.71.direction_ref), channel_id=1, source_target_pairs={{0,2},{1,17},{2,0},{3,5},{4,6},{5,3},{6,4},{7,9},{8,10},{9,7},{10,... | collective-permute-start | bytes 12296 | tf_op jit(solution)/shard_map/ppermute | solution.py:395
  18.6 1.2 %collective-permute-start.7 = (f32[8,128]{1,0:T(8,128)S(1)}, f32[8,128]{1,0:T(8,128)S(1)}, u32[]{:S(2)}, u32[]{:S(2)}) collective-permute-start(f32[8,128]{1,0:T(8,128)S(1)} %collective-permute-done.6.mine_ref), channel_id=1, source_target_pairs={{0,1},{1,0},{2,3},{3,2},{4,5},{5,4},{6,7},{7,6},{8,9},{9,8},{10,11... | collective-permute-start | bytes 12296 | tf_op jit(solution)/shard_map/ppermute | solution.py:398
  20.3 3.7 %collective-permute-start.8 = (f32[8,128]{1,0:T(8,128)S(1)}, f32[8,128]{1,0:T(8,128)S(1)}, u32[]{:S(2)}, u32[]{:S(2)}) collective-permute-start(f32[8,128]{1,0:T(8,128)S(1)} %get-tuple-element.51.direction_in), channel_id=1, source_target_pairs={{0,2},{1,17},{2,0},{3,5},{4,6},{5,3},{6,4},{7,9},{8,10},{9,7},{10,... | collective-permute-start | bytes 12296 | tf_op jit(solution)/shard_map/ppermute | solution.py:395
  24.0 1.2 %collective-permute-start.9 = (f32[8,128]{1,0:T(8,128)S(1)}, f32[8,128]{1,0:T(8,128)S(1)}, u32[]{:S(2)}, u32[]{:S(2)}) collective-permute-start(f32[8,128]{1,0:T(8,128)S(1)} %collective-permute-done.8.mine_ref), channel_id=1, source_target_pairs={{0,1},{1,0},{2,3},{3,2},{4,5},{5,4},{6,7},{7,6},{8,9},{9,8},{10,11... | collective-permute-start | bytes 12296 | tf_op jit(solution)/shard_map/ppermute | solution.py:398
  25.7 3.7 %collective-permute-start.11 = (f32[8,128]{1,0:T(8,128)S(1)}, f32[8,128]{1,0:T(8,128)S(1)}, u32[]{:S(2)}, u32[]{:S(2)}) collective-permute-start(f32[8,128]{1,0:T(8,128)S(1)} %shard_map.100.own_estimate), channel_id=1, source_target_pairs={{0,2},{1,15},{2,0},{3,5},{4,6},{5,3},{6,4},{7,9},{8,10},{9,7},{10,... | collective-permute-start | bytes 12296 | tf_op jit(solution)/shard_map/ppermute | solution.py:395
  26.1 6.1 %collective-permute-start.10 = (f32[8,128]{1,0:T(8,128)S(1)}, f32[8,128]{1,0:T(8,128)S(1)}, u32[]{:S(2)}, u32[]{:S(2)}) collective-permute-start(f32[8,128]{1,0:T(8,128)S(1)} %shard_map.100.own_estimate), channel_id=1, source_target_pairs={{0,8},{2,10},{4,12},{6,14},{8,0},{10,2},{12,4},{14,6},{1,9},{3,11}... | collective-permute-start | bytes 12296 | tf_op jit(solution)/shard_map/ppermute | solution.py:380
  29.3 2.9 %collective-permute-start.12 = (f32[8,128]{1,0:T(8,128)S(1)}, f32[8,128]{1,0:T(8,128)S(1)}, u32[]{:S(2)}, u32[]{:S(2)}) collective-permute-start(f32[8,128]{1,0:T(8,128)S(1)} %collective-permute-done.11.mine_ref), channel_id=1, source_target_pairs={{0,1},{1,0},{2,3},{3,2},{4,5},{5,4},{6,7},{7,6},{8,9},{9,8},{10,11... | collective-permute-start | bytes 12296 | tf_op jit(solution)/shard_map/ppermute | solution.py:398
  33.2 1.2 %collective-permute-start.15 = (f32[8,128]{1,0:T(8,128)S(1)}, f32[8,128]{1,0:T(8,128)S(1)}, u32[]{:S(2)}, u32[]{:S(2)}) collective-permute-start(f32[8,128]{1,0:T(8,128)S(1)} %get-tuple-element.59), channel_id=1, source_target_pairs={{0,1},{1,0},{2,3},{3,2},{4,5},{5,4},{6,7},{7,6},{8,9},{9,8},{10,11... | collective-permute-start | bytes 12296 | tf_op jit(solution)/shard_map/ppermute | solution.py:398
  33.4 4.5 %collective-permute-start.14 = (f32[8,128]{1,0:T(8,128)S(1)}, f32[8,128]{1,0:T(8,128)S(1)}, u32[]{:S(2)}, u32[]{:S(2)}) collective-permute-start(f32[8,128]{1,0:T(8,128)S(1)} %get-tuple-element.57), channel_id=1, source_target_pairs={{0,8},{2,10},{4,12},{6,14},{8,0},{10,2},{12,4},{14,6},{1,9},{3,11}... | collective-permute-start | bytes 12296 | tf_op jit(solution)/shard_map/ppermute | solution.py:380
  34.4 3.6 %collective-permute-start.16 = (f32[8,128]{1,0:T(8,128)S(1)}, f32[8,128]{1,0:T(8,128)S(1)}, u32[]{:S(2)}, u32[]{:S(2)}) collective-permute-start(f32[8,128]{1,0:T(8,128)S(1)} %add.19), channel_id=1, source_target_pairs={{0,2},{1,15},{2,0},{3,5},{4,6},{5,3},{6,4},{7,9},{8,10},{9,7},{10,... | collective-permute-start | bytes 12296 | tf_op jit(solution)/shard_map/ppermute | solution.py:395
  38.0 2.5 %collective-permute-start.17 = (f32[8,128]{1,0:T(8,128)S(1)}, f32[8,128]{1,0:T(8,128)S(1)}, u32[]{:S(2)}, u32[]{:S(2)}) collective-permute-start(f32[8,128]{1,0:T(8,128)S(1)} %add_multiply_fusion), channel_id=1, source_target_pairs={{0,1},{1,0},{2,3},{3,2},{4,5},{5,4},{6,7},{7,6},{8,9},{9,8},{10,11... | collective-permute-start | bytes 12296 | tf_op jit(solution)/shard_map/ppermute | solution.py:398
  40.6 3.6 %collective-permute-start.18 = (f32[8,128]{1,0:T(8,128)S(1)}, f32[8,128]{1,0:T(8,128)S(1)}, u32[]{:S(2)}, u32[]{:S(2)}) collective-permute-start(f32[8,128]{1,0:T(8,128)S(1)} %get-tuple-element.69.direction_in), channel_id=1, source_target_pairs={{0,2},{1,17},{2,0},{3,5},{4,6},{5,3},{6,4},{7,9},{8,10},{9,7},{10,... | collective-permute-start | bytes 12296 | tf_op jit(solution)/shard_map/ppermute | solution.py:395
  44.2 1.2 %collective-permute-start.19 = (f32[8,128]{1,0:T(8,128)S(1)}, f32[8,128]{1,0:T(8,128)S(1)}, u32[]{:S(2)}, u32[]{:S(2)}) collective-permute-start(f32[8,128]{1,0:T(8,128)S(1)} %collective-permute-done.18.mine_ref), channel_id=1, source_target_pairs={{0,1},{1,0},{2,3},{3,2},{4,5},{5,4},{6,7},{7,6},{8,9},{9,8},{10,11... | collective-permute-start | bytes 12296 | tf_op jit(solution)/shard_map/ppermute | solution.py:398
  45.9 3.7 %collective-permute-start.20 = (f32[8,128]{1,0:T(8,128)S(1)}, f32[8,128]{1,0:T(8,128)S(1)}, u32[]{:S(2)}, u32[]{:S(2)}) collective-permute-start(f32[8,128]{1,0:T(8,128)S(1)} %get-tuple-element.60.direction_in), channel_id=1, source_target_pairs={{0,2},{1,17},{2,0},{3,5},{4,6},{5,3},{6,4},{7,9},{8,10},{9,7},{10,... | collective-permute-start | bytes 12296 | tf_op jit(solution)/shard_map/ppermute | solution.py:395
  49.5 1.2 %collective-permute-start.21 = (f32[8,128]{1,0:T(8,128)S(1)}, f32[8,128]{1,0:T(8,128)S(1)}, u32[]{:S(2)}, u32[]{:S(2)}) collective-permute-start(f32[8,128]{1,0:T(8,128)S(1)} %collective-permute-done.20.mine_ref), channel_id=1, source_target_pairs={{0,1},{1,0},{2,3},{3,2},{4,5},{5,4},{6,7},{7,6},{8,9},{9,8},{10,11... | collective-permute-start | bytes 12296 | tf_op jit(solution)/shard_map/ppermute | solution.py:398
  51.2 3.7 %collective-permute-start.23 = (f32[16,128]{1,0:T(8,128)S(1)}, f32[16,128]{1,0:T(8,128)S(1)}, u32[]{:S(2)}, u32[]{:S(2)}) collective-permute-start(f32[16,128]{1,0:T(8,128)S(1)} %get-tuple-element.63.packed_ref), channel_id=1, source_target_pairs={{0,2},{1,15},{2,0},{3,5},{4,6},{5,3},{6,4},{7,9},{8,10},{9,7},{10,... | collective-permute-start | bytes 24584 | tf_op jit(solution)/shard_map/ppermute | solution.py:395
  51.3 5.4 %collective-permute-start.22 = (f32[16,128]{1,0:T(8,128)S(1)}, f32[16,128]{1,0:T(8,128)S(1)}, u32[]{:S(2)}, u32[]{:S(2)}) collective-permute-start(f32[16,128]{1,0:T(8,128)S(1)} %get-tuple-element.63.packed_ref), channel_id=1, source_target_pairs={{0,8},{2,10},{4,12},{6,14},{8,0},{10,2},{12,4},{14,6},{1,9},{3,11}... | collective-permute-start | bytes 24584 | tf_op jit(solution)/shard_map/ppermute | solution.py:380
  54.9 2.5 %collective-permute-start.24 = (f32[16,128]{1,0:T(8,128)S(1)}, f32[16,128]{1,0:T(8,128)S(1)}, u32[]{:S(2)}, u32[]{:S(2)}) collective-permute-start(f32[16,128]{1,0:T(8,128)S(1)} %collective-permute-done.23.mine_ref), channel_id=1, source_target_pairs={{0,1},{1,0},{2,3},{3,2},{4,5},{5,4},{6,7},{7,6},{8,9},{9,8},{10,11... | collective-permute-start | bytes 24584 | tf_op jit(solution)/shard_map/ppermute | solution.py:398
  (6 other events, 8.2 us)

commit v13 on v12

--- a/solution.py
+++ b/solution.py
@@ -181,24 +181,33 @@
     return total
 
 
-def product(own_ref, other_ref, pick_ref, window):
-    tiles, slots = own_ref.shape[0], own_ref.shape[1]
+def tile_rows(count, slots, tile, pick, window):
     parts = jnp.concatenate(three_parts(window), axis=1).astype(jnp.bfloat16)
-    picked = jnp.dot(pick_ref[...].astype(jnp.bfloat16), parts, preferred_element_type=F32)
+    picked = jnp.dot(pick.astype(jnp.bfloat16), parts, preferred_element_type=F32)
     picked = picked[:, :LANES] + picked[:, LANES : 2 * LANES] + picked[:, 2 * LANES :]
     eye = lax.broadcasted_iota(jnp.int32, (LANES, LANES), 0) == lax.broadcasted_iota(
         jnp.int32, (LANES, LANES), 1
     )
     rows = []
-    for t in range(tiles):
+    for t in range(count):
         total = None
-        for k in range(2 * slots):
-            tile = own_ref[t, k] if k < slots else other_ref[t, k - slots]
-            term = tile * picked[k * tiles + t : k * tiles + t + 1]
+        for k in range(slots):
+            term = tile(t, k) * picked[k * count + t : k * count + t + 1]
             total = term if total is None else total + term
         column = jnp.sum(total, axis=1, keepdims=True)
         rows.append(jnp.sum(jnp.where(eye, column, 0.0), axis=0, keepdims=True))
     return jnp.concatenate(rows, axis=0)
+
+
+def product(own_ref, other_ref, pick_ref, window):
+    tiles, slots = own_ref.shape[0], own_ref.shape[1]
+    return tile_rows(
+        tiles,
+        2 * slots,
+        lambda t, k: own_ref[t, k] if k < slots else other_ref[t, k - slots],
+        pick_ref[...],
+        window,
+    )
 
 
 def fetch(pairs, sems):
@@ -326,24 +335,95 @@
 
 
 def sweep_two(
-    chain, last, own_ref, other_ref, pick_ref, mine_ref, yours_ref, direction_in, residual_in,
-    estimate_in, diag_ref, estimate_ref, *refs,
-):
-    torso = estimate_ref.shape[0]
+    chain, own_ref, other_ref, pick_ref, mine_ref, yours_ref, direction_in, residual_in,
+    estimate_in, diag_ref, estimate_ref,
+):
     diag = diag_ref[...]
     direction = direction_in[...]
     window = window_of(chain, direction, *by_partner(mine_ref[...], yours_ref[...]))
     moved = product(own_ref, other_ref, pick_ref, window)
     residual = residual_in[...] - (diag * direction + moved)
     direction = KEEP[1] * direction + PULL[1] * (residual / diag)
-    estimate = estimate_in[...] + direction
-    if last:
-        residual_ref, = refs
-        residual_ref[...] = residual
-        estimate_ref[0 : torso // 2] = estimate
-        estimate_ref[torso // 2 :] = direction
-    else:
-        estimate_ref[...] = estimate
+    estimate_ref[...] = estimate_in[...] + direction
+
+
+def pack_border(own_ref, other_ref, pick_ref, diag_ref, out_ref, sems):
+    tiles, slots = own_ref.shape[0], own_ref.shape[1]
+    ahead = meets_next()
+    first = jnp.where(ahead, tiles - HALO, 0)
+    copies = []
+    for j in range(HALO):
+        for i, ref in enumerate((own_ref, other_ref)):
+            at = (2 * j + i) * slots
+            copy = pltpu.make_async_copy(
+                ref.at[first + j], out_ref.at[pl.ds(at, slots)], sems.at[2 * j + i]
+            )
+            copy.start()
+            copies.append(copy)
+    last = 2 * HALO * slots
+    out_ref[last] = jnp.zeros((LANES, LANES), F32)
+    width = pick_ref.shape[1]
+    for k in range(2 * slots):
+        rows = pick_ref[k * tiles : (k + 1) * tiles]
+        out_ref[last, k * HALO : (k + 1) * HALO, 0:width] = jnp.where(
+            ahead, rows[tiles - HALO :], rows[:HALO]
+        )
+    at = 2 * slots * HALO
+    out_ref[last, at : at + HALO] = jnp.where(ahead, diag_ref[tiles - HALO :], diag_ref[:HALO])
+    for copy in copies:
+        copy.wait()
+
+
+def sweep_both(
+    chain, own_ref, other_ref, pick_ref, mine_border, yours_border, mine_ref, yours_ref, mine_two,
+    yours_two, forcing_ref, direction_ref, diag_ref, packed_ref, residual_ref,
+):
+    torso = diag_ref.shape[0]
+    slots = 2 * own_ref.shape[1]
+    here = lax.axis_index("dom")
+    ahead = meets_next()
+    diag = diag_ref[...]
+    direction = direction_ref[...]
+    after, before = by_side(*by_partner(mine_ref[...], yours_ref[...]))
+    after = jnp.where(here < chain - 1, after, 0.0)
+    before = jnp.where(here > 0, before, 0.0)
+    low, high = by_partner(mine_two[...], yours_two[...])
+    lower = lax.rem(here, 4) < 2
+    beyond_after = jnp.where(here < chain - 2, jnp.where(lower, low, high)[:HALO], 0.0)
+    beyond_before = jnp.where(here > 1, jnp.where(lower, high, low)[torso - HALO :], 0.0)
+    filler = jnp.zeros((torso - 2 * HALO, LANES), F32)
+    window = jnp.concatenate([before[torso - HALO :], direction, after[:HALO], filler], axis=0)
+    window_after = jnp.concatenate([direction[torso - HALO :], after, beyond_after, filler], axis=0)
+    window_before = jnp.concatenate([beyond_before, before, direction[:HALO], filler], axis=0)
+
+    moved = product(own_ref, other_ref, pick_ref, window)
+    residual = forcing_ref[...] - (diag * direction + moved)
+    second = KEEP[0] * direction + PULL[0] * (residual / diag)
+    rims = []
+    for border, is_next in ((mine_border, ahead), (yours_border, jnp.logical_not(ahead))):
+        last = HALO * slots
+        moved = tile_rows(
+            HALO,
+            slots,
+            lambda t, k, border=border: border[t * slots + k],
+            border[last, 0 : slots * HALO, 0 : pick_ref.shape[1]],
+            jnp.where(is_next, window_after, window_before),
+        )
+        rim_diag = border[last, slots * HALO : slots * HALO + HALO]
+        rim = jnp.where(is_next, after[:HALO], before[torso - HALO :])
+        left = CHEB_THETA * rim_diag * rim - (rim_diag * rim + moved)
+        outside = jnp.where(is_next, here == chain - 1, here == 0)
+        rims.append(jnp.where(outside, 0.0, KEEP[0] * rim + PULL[0] * (left / rim_diag)))
+    rim_after = jnp.where(ahead, rims[0], rims[1])
+    rim_before = jnp.where(ahead, rims[1], rims[0])
+
+    window = jnp.concatenate([rim_before, second, rim_after, filler], axis=0)
+    moved = product(own_ref, other_ref, pick_ref, window)
+    residual = residual - (diag * second + moved)
+    third = KEEP[1] * second + PULL[1] * (residual / diag)
+    residual_ref[...] = residual
+    packed_ref[0:torso] = direction + second + third
+    packed_ref[torso:] = third
 
 
 def finish(
@@ -375,6 +455,20 @@
     node_count = states.shape[1]
     heart = node_count // LANES
     torso = diagonal.shape[0] // LANES
+
+    def with_two(value):
+        cases = lax.axis_size("case")
+        pairs = []
+        for case in range(cases):
+            for i in range(chain):
+                me = (case * chain + i) * 2
+                pairs.append((me, (case * chain + (i ^ 2)) * 2))
+                if i in (0, 1, chain - 2, chain - 1) and cases % 2 == 0:
+                    pairs.append((me + 1, ((case ^ 1) * chain + i) * 2 + 1))
+                else:
+                    other = (((i - 2) ^ 2) + 2) % chain
+                    pairs.append((me + 1, (case * chain + other) * 2 + 1))
+        return lax.ppermute(value, ("case", "dom", "sub"), pairs)
 
     def with_far(value):
         return lax.ppermute(value, "dom", [(i, (i + chain // 2) % chain) for i in range(chain)])
@@ -423,47 +517,57 @@
     )
     maps = call(complete, index)(in_specs=[VMEM] * 5)(own, near, far, from_sibling(give), nodes)
     other_columns = from_sibling(columns)
-    for time_step in range(2):
-        last = time_step == 1
-        others = from_sibling(forcing)
-        if not last:
-            others, other_columns = lax.optimization_barrier((others, other_columns))
-        forcing = forcing + others
-        direction = forcing / (CHEB_THETA * diag)
-        halo = with_either(direction, False)
-        if not last:
-            choices = 2 * columns.shape[0] * torso
-            direction = call(bring_tiles, field)(in_specs=[VMEM] * 2)(tile_values, direction)
-            pick = call(choose, shape(choices, 2 * torso))(in_specs=[VMEM] * 2)(
-                columns, other_columns
-            )
-            halo, direction = lax.optimization_barrier((halo, direction))
-            stored = (tile_values, other_tiles, pick)
-        residual, direction, estimate = call(
-            functools.partial(sweep_one, chain), (field,) * 3
-        )(in_specs=[VMEM] * 8)(*stored, halo, from_sibling(halo), forcing, direction, diag)
-        halo = with_either(direction, False)
-        swept = call(
-            functools.partial(sweep_two, chain, last), (packed, field) if last else field
-        )(in_specs=[VMEM] * 9)(
-            *stored, halo, from_sibling(halo), direction, residual, estimate, diag
-        )
-        estimate, residual = swept if last else (swept, None)
-        far = with_far(estimate)
-        near = with_either(estimate, True)
-        if not last:
-            states, own, keep, give, away = call(next_shares, (dense,) + (field,) * 4)(
-                in_specs=[VMEM] * 7
-            )(states, estimate, far, near, from_sibling(near), nodes, maps)
-            far = with_far(away)
-            near = with_either(keep + from_sibling(give), True)
-            forcing = TORSO_COUPLING * (own + far + near)
+    others, other_columns = lax.optimization_barrier((from_sibling(forcing), other_columns))
+    forcing = forcing + others
+    direction = forcing / (CHEB_THETA * diag)
+    halo = with_either(direction, False)
+    direction = call(bring_tiles, field)(in_specs=[VMEM] * 2)(tile_values, direction)
+    choices = 2 * columns.shape[0] * torso
+    pick = call(choose, shape(choices, 2 * torso))(in_specs=[VMEM] * 2)(columns, other_columns)
+    halo, direction = lax.optimization_barrier((halo, direction))
+    stored = (tile_values, other_tiles, pick)
+    residual, direction, estimate = call(functools.partial(sweep_one, chain), (field,) * 3)(
+        in_specs=[VMEM] * 8
+    )(*stored, halo, from_sibling(halo), forcing, direction, diag)
+    halo = with_either(direction, False)
+    slots_all = 2 * columns.shape[0]
+    early, _ = lax.optimization_barrier((diag, halo))
+    border = call(
+        pack_border,
+        shape(HALO * slots_all + 1, LANES, LANES),
+        (pltpu.SemaphoreType.DMA((2 * HALO,)),),
+    )(in_specs=[VMEM] * 4)(*stored, early)
+    border = with_either(border, False)
+    estimate = call(functools.partial(sweep_two, chain), field)(in_specs=[VMEM] * 9)(
+        *stored, halo, from_sibling(halo), direction, residual, estimate, diag
+    )
+    far = with_far(estimate)
+    near = with_either(estimate, True)
+    states, own, keep, give, away = call(next_shares, (dense,) + (field,) * 4)(
+        in_specs=[VMEM] * 7
+    )(states, estimate, far, near, from_sibling(near), nodes, maps)
+
+    far = with_far(away)
+    near = with_either(keep + from_sibling(give), True)
+    forcing = TORSO_COUPLING * (own + far + near)
+    forcing = forcing + from_sibling(forcing)
+    direction = forcing / (CHEB_THETA * diag)
+    halo, two = with_either(direction, False), with_two(direction)
+    border, _ = lax.optimization_barrier((border, direction))
+    both, residual = call(functools.partial(sweep_both, chain), (packed, field))(
+        in_specs=[VMEM] * 12
+    )(
+        *stored, border, from_sibling(border), halo, from_sibling(halo), two, from_sibling(two),
+        forcing, direction, diag,
+    )
+    far = with_far(both)
+    near = with_either(both, True)
     new_states, potential, residual = call(
         functools.partial(finish, chain),
         (shape(*dense.shape[:1], node_count), field, field),
         (pltpu.VMEM(dense.shape, F32),),
     )(in_specs=[VMEM] * 12)(
-        *stored, estimate, far, near, from_sibling(near), residual, diag, states, nodes, maps
+        *stored, both, far, near, from_sibling(near), residual, diag, states, nodes, maps
     )
     return new_states, potential.reshape(-1), residual.reshape(-1)
 

time: 59.3 us -> 75.8 us (1.28)
  waiting for transfers between devices: 31.7 us -> 40.8 us
  starting transfers between devices: 16.8 us -> 23.9 us
    ppermute x8, waiting for transfers between devices: 17.4 us -> 28.7 us  [with_either(): return lax.ppermute(value, ('case', 'dom', 'sub'), pairs)]
    ppermute x4, starting transfers between devices: 4.53 us -> 9.17 us  [with_far(): lax.ppermute(value, 'dom', [(i, (i + chain // 2) % chain) for i in range(...]
    ppermute x0 -> x1, waiting for transfers between devices: none -> 3.31 us  [with_two(): return lax.ppermute(value, ('case', 'dom', 'sub'), pairs)]
    ppermute x4, waiting for transfers between devices: 4.05 us -> 1.23 us  [with_far(): lax.ppermute(value, 'dom', [(i, (i + chain // 2) % chain) for i in range(...]
    ppermute x8, starting transfers between devices: 3.92 us -> 6.73 us  [with_either(): return lax.ppermute(value, ('case', 'dom', 'sub'), pairs)]
    ppermute x13 -> x14, waiting for transfers between devices: 10.3 us -> 7.57 us  [from_sibling(): return lax.ppermute(value, 'sub', [(0, 1), (1, 0)])]
    pallas_call x2 -> x3, Pallas kernels: 1.01 us -> 1.84 us  [the longest x1 1.21 us: on_device(): call(functools.partial(sweep_both, chain), (packed, field))]
    ppermute x13 -> x14, starting transfers between devices: 8.32 us -> 7.67 us  [from_sibling(): return lax.ppermute(value, 'sub', [(0, 1), (1, 0)])]
  transfers between devices with their start and end apart: 25 -> 27, of which waited for: 19 -> 18; matrix products, arithmetic and copies ran while one was open for 0% -> 0% of each run, Pallas kernels for 1% -> 2%
where the time goes in v13:
time: 75.8 us; the launch traced here: 75.4 us
  waiting for transfers between devices  40.8 us (54%)
  starting transfers between devices  23.9 us (32%)
  Pallas kernels  5.43 us (7%)
  local copies, waits for them, and re-layouts  3.88 us (5%)
  other arithmetic  0.77 us (1%)
    ppermute x8, waiting for transfers between devices, with_either(): return lax.ppermute(value, ('case', 'dom', 'sub'), pairs)  28.7 us
    ppermute x4, starting transfers between devices, with_far(): lax.ppermute(value, 'dom', [(i, (i + chain // 2) % chain) for i in range(...  9.17 us
    ppermute x14, starting transfers between devices, from_sibling(): return lax.ppermute(value, 'sub', [(0, 1), (1, 0)])  7.67 us
    ppermute x14, waiting for transfers between devices, from_sibling(): return lax.ppermute(value, 'sub', [(0, 1), (1, 0)])  7.57 us
    ppermute x8, starting transfers between devices, with_either(): return lax.ppermute(value, ('case', 'dom', 'sub'), pairs)  6.73 us
    unnamed x10, local copies, waits for them, and re-layouts  3.88 us
    ppermute x1, waiting for transfers between devices, with_two(): return lax.ppermute(value, ('case', 'dom', 'sub'), pairs)  3.31 us
  transfers between devices with their start and end apart: 27, of which 18 were waited for; matrix products, arithmetic and copies ran while one was open for 0% of the time, Pallas kernels for 2%

profile of v13, /device:TPU:0, one launch (start us, length us, event | category | flops | bytes accessed | tf_op | source)
XLA Modules:
  0.0 75.4 jit_solution(14639330176723149062)
XLA Ops:
  1.4 0.9 %copy-done.2 = f32[19,2048]{1,0:T(8,128)S(1)} copy-done((f32[19,2048]{1,0:T(8,128)S(1)}, f32[19,2048]{1,0:T(8,128)}, u32[]{:S(2)}) %copy-start.2) | copy-done | bytes 155672
  4.3 2.7 %collective-permute-start.2 = (f32[4,512]{1,0:T(4,128)S(1)}, f32[4,512]{1,0:T(4,128)S(1)}, u32[]{:S(2)}, u32[]{:S(2)}) collective-permute-start(f32[4,512]{1,0:T(4,128)S(1)} %pad_maximum_fusion), channel_id=1, source_target_pairs={{0,2},{1,15},{2,0},{3,5},{4,6},{5,3},{6,4},{7,9},{8,10},{9,7},{10,... | collective-permute-start | bytes 24584 | tf_op jit(solution)/shard_map/ppermute | solution.py:489
  7.0 2.6 %collective-permute-start.3 = (f32[2,512]{1,0:T(2,128)S(1)}, f32[2,512]{1,0:T(2,128)S(1)}, u32[]{:S(2)}, u32[]{:S(2)}) collective-permute-start(f32[2,512]{1,0:T(2,128)S(1)} %get-tuple-element.42.to_far), channel_id=1, source_target_pairs={{0,8},{2,10},{4,12},{6,14},{8,0},{10,2},{12,4},{14,6},{1,9},{3,11}... | collective-permute-start | bytes 12296 | tf_op jit(solution)/shard_map/ppermute | solution.py:474
  11.8 2.0 %collective-permute-start.4 = (f32[8,128]{1,0:T(8,128)S(1)}, f32[8,128]{1,0:T(8,128)S(1)}, u32[]{:S(2)}, u32[]{:S(2)}) collective-permute-start(f32[8,128]{1,0:T(8,128)S(1)} %get-tuple-element.43), channel_id=1, source_target_pairs={{0,1},{1,0},{2,3},{3,2},{4,5},{5,4},{6,7},{7,6},{8,9},{9,8},{10,11... | collective-permute-start | bytes 12296 | tf_op jit(solution)/shard_map/ppermute | solution.py:492
  13.9 1.1 %collective-permute-done.5.other_cols = s32[4,8]{1,0:T(4,128)S(1)} collective-permute-done((s32[4,8]{1,0:T(4,128)S(1)}, s32[4,8]{1,0:T(4,128)S(1)}, u32[]{:S(2)}, u32[]{:S(2)}) %collective-permute-start.5) | collective-permute-done | bytes 160 | tf_op jit(solution)/shard_map/ppermute | solution.py:492
  15.0 1.6 %copy-done = f32[8,4,128,128]{3,2,1,0:T(8,128)S(1)} copy-done((f32[8,4,128,128]{3,2,1,0:T(8,128)S(1)}, f32[8,4,128,128]{3,2,1,0:T(8,128)}, u32[]{:S(2)}) %copy-start) | copy-done | bytes 2097176
  16.6 2.0 %collective-permute-done.6.mine_ref = f32[8,128]{1,0:T(8,128)S(1)} collective-permute-done((f32[8,128]{1,0:T(8,128)S(1)}, f32[8,128]{1,0:T(8,128)S(1)}, u32[]{:S(2)}, u32[]{:S(2)}) %collective-permute-start.6) | collective-permute-done | bytes 4128 | tf_op jit(solution)/shard_map/ppermute | solution.py:489
  18.7 1.1 %collective-permute-done.7.yours_ref = f32[8,128]{1,0:T(8,128)S(1)} collective-permute-done((f32[8,128]{1,0:T(8,128)S(1)}, f32[8,128]{1,0:T(8,128)S(1)}, u32[]{:S(2)}, u32[]{:S(2)}) %collective-permute-start.7) | collective-permute-done | bytes 4128 | tf_op jit(solution)/shard_map/ppermute | solution.py:492
  20.8 3.2 %collective-permute-done.8.mine_ref = f32[8,128]{1,0:T(8,128)S(1)} collective-permute-done((f32[8,128]{1,0:T(8,128)S(1)}, f32[8,128]{1,0:T(8,128)S(1)}, u32[]{:S(2)}, u32[]{:S(2)}) %collective-permute-start.8) | collective-permute-done | bytes 4128 | tf_op jit(solution)/shard_map/ppermute | solution.py:489
  24.6 1.2 %collective-permute-done.10.yours_ref = f32[8,128]{1,0:T(8,128)S(1)} collective-permute-done((f32[8,128]{1,0:T(8,128)S(1)}, f32[8,128]{1,0:T(8,128)S(1)}, u32[]{:S(2)}, u32[]{:S(2)}) %collective-permute-start.10) | collective-permute-done | bytes 4128 | tf_op jit(solution)/shard_map/ppermute | solution.py:492
  26.3 1.7 %collective-permute-start.12 = (f32[8,128]{1,0:T(8,128)S(1)}, f32[8,128]{1,0:T(8,128)S(1)}, u32[]{:S(2)}, u32[]{:S(2)}) collective-permute-start(f32[8,128]{1,0:T(8,128)S(1)} %shard_map.101.own_estimate), channel_id=1, source_target_pairs={{0,2},{1,15},{2,0},{3,5},{4,6},{5,3},{6,4},{7,9},{8,10},{9,7},{10,... | collective-permute-start | bytes 12296 | tf_op jit(solution)/shard_map/ppermute | solution.py:489
  28.0 1.1 %collective-permute-start.11 = (f32[8,128]{1,0:T(8,128)S(1)}, f32[8,128]{1,0:T(8,128)S(1)}, u32[]{:S(2)}, u32[]{:S(2)}) collective-permute-start(f32[8,128]{1,0:T(8,128)S(1)} %shard_map.101.own_estimate), channel_id=1, source_target_pairs={{0,8},{2,10},{4,12},{6,14},{8,0},{10,2},{12,4},{14,6},{1,9},{3,11}... | collective-permute-start | bytes 12296 | tf_op jit(solution)/shard_map/ppermute | solution.py:474
  29.1 20.0 %collective-permute-done.12.mine_ref = f32[8,128]{1,0:T(8,128)S(1)} collective-permute-done((f32[8,128]{1,0:T(8,128)S(1)}, f32[8,128]{1,0:T(8,128)S(1)}, u32[]{:S(2)}, u32[]{:S(2)}) %collective-permute-start.12) | collective-permute-done | bytes 4128 | tf_op jit(solution)/shard_map/ppermute | solution.py:489
  50.5 0.9 %shard_map.103 = (f32[19,16,128]{2,1,0:T(8,128)S(1)}, f32[8,128]{1,0:T(8,128)S(1)}, f32[8,128]{1,0:T(8,128)S(1)}, f32[8,128]{1,0:T(8,128)S(1)}, f32[8,128]{1,0:T(8,128)S(1)}) custom-call(f32[19,16,128]{2,1,0:T(8,128)S(1)} %get-tuple-element.51.states_ref, f32[8,128]{1,0:T(8,128)S(1)} %shard_map.101.own_estimate, ...), custom_call_target="tpu_custom_call" | custom-call | flops 4000000 | bytes 262144 | tf_op jit(solution)/shard_map/pallas_call | solution.py:546
  51.8 3.3 %collective-permute-start.15 = (f32[8,128]{1,0:T(8,128)S(1)}, f32[8,128]{1,0:T(8,128)S(1)}, u32[]{:S(2)}, u32[]{:S(2)}) collective-permute-start(f32[8,128]{1,0:T(8,128)S(1)} %get-tuple-element.57), channel_id=1, source_target_pairs={{0,8},{2,10},{4,12},{6,14},{8,0},{10,2},{12,4},{14,6},{1,9},{3,11}... | collective-permute-start | bytes 12296 | tf_op jit(solution)/shard_map/ppermute | solution.py:474
  55.1 0.9 %collective-permute-start.17 = (f32[8,128]{1,0:T(8,128)S(1)}, f32[8,128]{1,0:T(8,128)S(1)}, u32[]{:S(2)}, u32[]{:S(2)}) collective-permute-start(f32[8,128]{1,0:T(8,128)S(1)} %add.19), channel_id=1, source_target_pairs={{0,2},{1,15},{2,0},{3,5},{4,6},{5,3},{6,4},{7,9},{8,10},{9,7},{10,... | collective-permute-start | bytes 12296 | tf_op jit(solution)/shard_map/ppermute | solution.py:489
  56.7 2.0 %collective-permute-done.17 = f32[8,128]{1,0:T(8,128)S(1)} collective-permute-done((f32[8,128]{1,0:T(8,128)S(1)}, f32[8,128]{1,0:T(8,128)S(1)}, u32[]{:S(2)}, u32[]{:S(2)}) %collective-permute-start.17) | collective-permute-done | bytes 4128 | tf_op jit(solution)/shard_map/ppermute | solution.py:489
  58.7 1.4 %collective-permute-start.18 = (f32[8,128]{1,0:T(8,128)S(1)}, f32[8,128]{1,0:T(8,128)S(1)}, u32[]{:S(2)}, u32[]{:S(2)}) collective-permute-start(f32[8,128]{1,0:T(8,128)S(1)} %add_multiply_fusion), channel_id=1, source_target_pairs={{0,1},{1,0},{2,3},{3,2},{4,5},{5,4},{6,7},{7,6},{8,9},{9,8},{10,11... | collective-permute-start | bytes 12296 | tf_op jit(solution)/shard_map/ppermute | solution.py:492
  61.7 3.3 %collective-permute-done.22.mine_two = f32[8,128]{1,0:T(8,128)S(1)} collective-permute-done((f32[8,128]{1,0:T(8,128)S(1)}, f32[8,128]{1,0:T(8,128)S(1)}, u32[]{:S(2)}, u32[]{:S(2)}) %collective-permute-start.22) | collective-permute-done | bytes 4128 | tf_op jit(solution)/shard_map/ppermute | solution.py:471
  66.5 1.2 %shard_map.104 = (f32[16,128]{1,0:T(8,128)S(1)}, f32[8,128]{1,0:T(8,128)S(1)}) custom-call(f32[8,4,128,128]{3,2,1,0:T(8,128)S(1)} %copy-done.1, f32[8,4,128,128]{3,2,1,0:T(8,128)S(1)} %collective-permute-done.1.other_ref, f32[64,16]{1,0:T(8,128)S(1)} %shard_map.97.pick_ref, f32[17,128,128]{2,1,0:T(8,128)S(1)} %collective-permute-done.9.mine_border, ...), custom_call_target="tpu_custom_call" | custom-call | flops 4000000 | bytes 262144 | tf_op jit(solution)/shard_map/pallas_call | solution.py:557
  68.1 2.2 %collective-permute-start.24 = (f32[16,128]{1,0:T(8,128)S(1)}, f32[16,128]{1,0:T(8,128)S(1)}, u32[]{:S(2)}, u32[]{:S(2)}) collective-permute-start(f32[16,128]{1,0:T(8,128)S(1)} %get-tuple-element.61.packed_ref), channel_id=1, source_target_pairs={{0,8},{2,10},{4,12},{6,14},{8,0},{10,2},{12,4},{14,6},{1,9},{3,11}... | collective-permute-start | bytes 24584 | tf_op jit(solution)/shard_map/ppermute | solution.py:474
  70.3 1.1 %collective-permute-done.25.mine_ref = f32[16,128]{1,0:T(8,128)S(1)} collective-permute-done((f32[16,128]{1,0:T(8,128)S(1)}, f32[16,128]{1,0:T(8,128)S(1)}, u32[]{:S(2)}, u32[]{:S(2)}) %collective-permute-start.25) | collective-permute-done | bytes 8224 | tf_op jit(solution)/shard_map/ppermute | solution.py:489
  71.4 1.8 %collective-permute-start.26 = (f32[16,128]{1,0:T(8,128)S(1)}, f32[16,128]{1,0:T(8,128)S(1)}, u32[]{:S(2)}, u32[]{:S(2)}) collective-permute-start(f32[16,128]{1,0:T(8,128)S(1)} %collective-permute-done.25.mine_ref), channel_id=1, source_target_pairs={{0,1},{1,0},{2,3},{3,2},{4,5},{5,4},{6,7},{7,6},{8,9},{9,8},{10,11... | collective-permute-start | bytes 24584 | tf_op jit(solution)/shard_map/ppermute | solution.py:492
  74.0 1.5 %shard_map.105 = (f32[19,2048]{1,0:T(8,128)}, f32[8,128]{1,0:T(8,128)}, f32[8,128]{1,0:T(8,128)}) custom-call(f32[8,4,128,128]{3,2,1,0:T(8,128)S(1)} %copy-done.1, f32[8,4,128,128]{3,2,1,0:T(8,128)S(1)} %collective-permute-done.1.other_ref, f32[64,16]{1,0:T(8,128)S(1)} %shard_map.97.pick_ref, f32[16,128]{1,0:T(8,128)S(1)} %get-tuple-element.61.packed_ref, ...), custom_call_target="tpu_custom_call" | custom-call | flops 4000000 | bytes 262144 | tf_op jit(solution)/shard_map/pallas_call | solution.py:565
  (58 shorter events, 14.0 us)
Async XLA Ops:
  2.6 1.3 %collective-permute-start = (f32[2,512]{1,0:T(2,128)S(1)}, f32[2,512]{1,0:T(2,128)S(1)}, u32[]{:S(2)}, u32[]{:S(2)}) collective-permute-start(f32[2,512]{1,0:T(2,128)S(1)} %get-tuple-element.35), channel_id=1, source_target_pairs={{0,1},{1,0},{2,3},{3,2},{4,5},{5,4},{6,7},{7,6},{8,9},{9,8},{10,11... | collective-permute-start | bytes 12296 | tf_op jit(solution)/shard_map/ppermute | solution.py:492
  3.9 15.9 %collective-permute-start.1 = (f32[8,4,128,128]{3,2,1,0:T(8,128)}, f32[8,4,128,128]{3,2,1,0:T(8,128)S(1)}, u32[]{:S(2)}, u32[]{:S(2)}) collective-permute-start(f32[8,4,128,128]{3,2,1,0:T(8,128)} %own_ref.4), channel_id=1, source_target_pairs={{0,1},{1,0},{2,3},{3,2},{4,5},{5,4},{6,7},{7,6},{8,9},{9,8},{10,11... | collective-permute-start | bytes 6291464 | tf_op jit(solution)/shard_map/ppermute | solution.py:492
  4.3 7.2 %collective-permute-start.2 = (f32[4,512]{1,0:T(4,128)S(1)}, f32[4,512]{1,0:T(4,128)S(1)}, u32[]{:S(2)}, u32[]{:S(2)}) collective-permute-start(f32[4,512]{1,0:T(4,128)S(1)} %pad_maximum_fusion), channel_id=1, source_target_pairs={{0,2},{1,15},{2,0},{3,5},{4,6},{5,3},{6,4},{7,9},{8,10},{9,7},{10,... | collective-permute-start | bytes 24584 | tf_op jit(solution)/shard_map/ppermute | solution.py:489
  7.0 4.5 %collective-permute-start.3 = (f32[2,512]{1,0:T(2,128)S(1)}, f32[2,512]{1,0:T(2,128)S(1)}, u32[]{:S(2)}, u32[]{:S(2)}) collective-permute-start(f32[2,512]{1,0:T(2,128)S(1)} %get-tuple-element.42.to_far), channel_id=1, source_target_pairs={{0,8},{2,10},{4,12},{6,14},{8,0},{10,2},{12,4},{14,6},{1,9},{3,11}... | collective-permute-start | bytes 12296 | tf_op jit(solution)/shard_map/ppermute | solution.py:474
  11.8 3.1 %collective-permute-start.4 = (f32[8,128]{1,0:T(8,128)S(1)}, f32[8,128]{1,0:T(8,128)S(1)}, u32[]{:S(2)}, u32[]{:S(2)}) collective-permute-start(f32[8,128]{1,0:T(8,128)S(1)} %get-tuple-element.43), channel_id=1, source_target_pairs={{0,1},{1,0},{2,3},{3,2},{4,5},{5,4},{6,7},{7,6},{8,9},{9,8},{10,11... | collective-permute-start | bytes 12296 | tf_op jit(solution)/shard_map/ppermute | solution.py:492
  15.0 3.7 %collective-permute-start.6 = (f32[8,128]{1,0:T(8,128)S(1)}, f32[8,128]{1,0:T(8,128)S(1)}, u32[]{:S(2)}, u32[]{:S(2)}) collective-permute-start(f32[8,128]{1,0:T(8,128)S(1)} %get-tuple-element.69.direction_ref), channel_id=1, source_target_pairs={{0,2},{1,17},{2,0},{3,5},{4,6},{5,3},{6,4},{7,9},{8,10},{9,7},{10,... | collective-permute-start | bytes 12296 | tf_op jit(solution)/shard_map/ppermute | solution.py:489
  18.6 1.2 %collective-permute-start.7 = (f32[8,128]{1,0:T(8,128)S(1)}, f32[8,128]{1,0:T(8,128)S(1)}, u32[]{:S(2)}, u32[]{:S(2)}) collective-permute-start(f32[8,128]{1,0:T(8,128)S(1)} %collective-permute-done.6.mine_ref), channel_id=1, source_target_pairs={{0,1},{1,0},{2,3},{3,2},{4,5},{5,4},{6,7},{7,6},{8,9},{9,8},{10,11... | collective-permute-start | bytes 12296 | tf_op jit(solution)/shard_map/ppermute | solution.py:492
  20.3 3.7 %collective-permute-start.8 = (f32[8,128]{1,0:T(8,128)S(1)}, f32[8,128]{1,0:T(8,128)S(1)}, u32[]{:S(2)}, u32[]{:S(2)}) collective-permute-start(f32[8,128]{1,0:T(8,128)S(1)} %get-tuple-element.49.direction_in), channel_id=1, source_target_pairs={{0,2},{1,17},{2,0},{3,5},{4,6},{5,3},{6,4},{7,9},{8,10},{9,7},{10,... | collective-permute-start | bytes 12296 | tf_op jit(solution)/shard_map/ppermute | solution.py:489
  24.1 36.9 %collective-permute-start.9 = (f32[17,128,128]{2,1,0:T(8,128)S(1)}, f32[17,128,128]{2,1,0:T(8,128)S(1)}, u32[]{:S(2)}, u32[]{:S(2)}) collective-permute-start(f32[17,128,128]{2,1,0:T(8,128)S(1)} %shard_map.100), channel_id=1, source_target_pairs={{0,2},{1,17},{2,0},{3,5},{4,6},{5,3},{6,4},{7,9},{8,10},{9,7},{10,... | collective-permute-start | bytes 3342344 | tf_op jit(solution)/shard_map/ppermute | solution.py:489
  24.6 1.2 %collective-permute-start.10 = (f32[8,128]{1,0:T(8,128)S(1)}, f32[8,128]{1,0:T(8,128)S(1)}, u32[]{:S(2)}, u32[]{:S(2)}) collective-permute-start(f32[8,128]{1,0:T(8,128)S(1)} %collective-permute-done.8.mine_ref), channel_id=1, source_target_pairs={{0,1},{1,0},{2,3},{3,2},{4,5},{5,4},{6,7},{7,6},{8,9},{9,8},{10,11... | collective-permute-start | bytes 12296 | tf_op jit(solution)/shard_map/ppermute | solution.py:492
  26.3 22.8 %collective-permute-start.12 = (f32[8,128]{1,0:T(8,128)S(1)}, f32[8,128]{1,0:T(8,128)S(1)}, u32[]{:S(2)}, u32[]{:S(2)}) collective-permute-start(f32[8,128]{1,0:T(8,128)S(1)} %shard_map.101.own_estimate), channel_id=1, source_target_pairs={{0,2},{1,15},{2,0},{3,5},{4,6},{5,3},{6,4},{7,9},{8,10},{9,7},{10,... | collective-permute-start | bytes 12296 | tf_op jit(solution)/shard_map/ppermute | solution.py:489
  28.0 22.5 %collective-permute-start.11 = (f32[8,128]{1,0:T(8,128)S(1)}, f32[8,128]{1,0:T(8,128)S(1)}, u32[]{:S(2)}, u32[]{:S(2)}) collective-permute-start(f32[8,128]{1,0:T(8,128)S(1)} %shard_map.101.own_estimate), channel_id=1, source_target_pairs={{0,8},{2,10},{4,12},{6,14},{8,0},{10,2},{12,4},{14,6},{1,9},{3,11}... | collective-permute-start | bytes 12296 | tf_op jit(solution)/shard_map/ppermute | solution.py:474
  49.1 1.4 %collective-permute-start.13 = (f32[8,128]{1,0:T(8,128)S(1)}, f32[8,128]{1,0:T(8,128)S(1)}, u32[]{:S(2)}, u32[]{:S(2)}) collective-permute-start(f32[8,128]{1,0:T(8,128)S(1)} %collective-permute-done.12.mine_ref), channel_id=1, source_target_pairs={{0,1},{1,0},{2,3},{3,2},{4,5},{5,4},{6,7},{7,6},{8,9},{9,8},{10,11... | collective-permute-start | bytes 12296 | tf_op jit(solution)/shard_map/ppermute | solution.py:492
  49.1 1.3 %collective-permute-start.14 = (f32[1,512]{1,0:T(1,128)S(1)}, f32[1,512]{1,0:T(1,128)S(1)}, u32[]{:S(2)}, u32[]{:S(2)}) collective-permute-start(f32[1,512]{1,0:T(1,128)S(1)} %get-tuple-element.55), channel_id=1, source_target_pairs={{0,1},{1,0},{2,3},{3,2},{4,5},{5,4},{6,7},{7,6},{8,9},{9,8},{10,11... | collective-permute-start | bytes 6152 | tf_op jit(solution)/shard_map/ppermute | solution.py:492
  51.4 3.7 %collective-permute-start.16 = (f32[8,128]{1,0:T(8,128)S(1)}, f32[8,128]{1,0:T(8,128)S(1)}, u32[]{:S(2)}, u32[]{:S(2)}) collective-permute-start(f32[8,128]{1,0:T(8,128)S(1)} %get-tuple-element.59), channel_id=1, source_target_pairs={{0,1},{1,0},{2,3},{3,2},{4,5},{5,4},{6,7},{7,6},{8,9},{9,8},{10,11... | collective-permute-start | bytes 12296 | tf_op jit(solution)/shard_map/ppermute | solution.py:492
  51.8 4.9 %collective-permute-start.15 = (f32[8,128]{1,0:T(8,128)S(1)}, f32[8,128]{1,0:T(8,128)S(1)}, u32[]{:S(2)}, u32[]{:S(2)}) collective-permute-start(f32[8,128]{1,0:T(8,128)S(1)} %get-tuple-element.57), channel_id=1, source_target_pairs={{0,8},{2,10},{4,12},{6,14},{8,0},{10,2},{12,4},{14,6},{1,9},{3,11}... | collective-permute-start | bytes 12296 | tf_op jit(solution)/shard_map/ppermute | solution.py:474
  55.1 3.6 %collective-permute-start.17 = (f32[8,128]{1,0:T(8,128)S(1)}, f32[8,128]{1,0:T(8,128)S(1)}, u32[]{:S(2)}, u32[]{:S(2)}) collective-permute-start(f32[8,128]{1,0:T(8,128)S(1)} %add.19), channel_id=1, source_target_pairs={{0,2},{1,15},{2,0},{3,5},{4,6},{5,3},{6,4},{7,9},{8,10},{9,7},{10,... | collective-permute-start | bytes 12296 | tf_op jit(solution)/shard_map/ppermute | solution.py:489
  58.7 2.3 %collective-permute-start.18 = (f32[8,128]{1,0:T(8,128)S(1)}, f32[8,128]{1,0:T(8,128)S(1)}, u32[]{:S(2)}, u32[]{:S(2)}) collective-permute-start(f32[8,128]{1,0:T(8,128)S(1)} %add_multiply_fusion), channel_id=1, source_target_pairs={{0,1},{1,0},{2,3},{3,2},{4,5},{5,4},{6,7},{7,6},{8,9},{9,8},{10,11... | collective-permute-start | bytes 12296 | tf_op jit(solution)/shard_map/ppermute | solution.py:492
  61.0 5.5 %collective-permute-start.19 = (f32[17,128,128]{2,1,0:T(8,128)S(1)}, f32[17,128,128]{2,1,0:T(8,128)S(1)}, u32[]{:S(2)}, u32[]{:S(2)}) collective-permute-start(f32[17,128,128]{2,1,0:T(8,128)S(1)} %collective-permute-done.9.mine_border), channel_id=1, source_target_pairs={{0,1},{1,0},{2,3},{3,2},{4,5},{5,4},{6,7},{7,6},{8,9},{9,8},{10,11... | collective-permute-start | bytes 3342344 | tf_op jit(solution)/shard_map/ppermute | solution.py:492
  61.4 3.6 %collective-permute-start.22 = (f32[8,128]{1,0:T(8,128)S(1)}, f32[8,128]{1,0:T(8,128)S(1)}, u32[]{:S(2)}, u32[]{:S(2)}) collective-permute-start(f32[8,128]{1,0:T(8,128)S(1)} %get-tuple-element.67.direction_ref), channel_id=1, source_target_pairs={{0,4},{1,17},{2,6},{3,19},{4,0},{5,9},{6,2},{7,11},{8,12},{9,5},{1... | collective-permute-start | bytes 12296 | tf_op jit(solution)/shard_map/ppermute | solution.py:471
  61.7 3.6 %collective-permute-start.20 = (f32[8,128]{1,0:T(8,128)S(1)}, f32[8,128]{1,0:T(8,128)S(1)}, u32[]{:S(2)}, u32[]{:S(2)}) collective-permute-start(f32[8,128]{1,0:T(8,128)S(1)} %get-tuple-element.67.direction_ref), channel_id=1, source_target_pairs={{0,2},{1,17},{2,0},{3,5},{4,6},{5,3},{6,4},{7,9},{8,10},{9,7},{10,... | collective-permute-start | bytes 12296 | tf_op jit(solution)/shard_map/ppermute | solution.py:489
  67.7 3.7 %collective-permute-start.25 = (f32[16,128]{1,0:T(8,128)S(1)}, f32[16,128]{1,0:T(8,128)S(1)}, u32[]{:S(2)}, u32[]{:S(2)}) collective-permute-start(f32[16,128]{1,0:T(8,128)S(1)} %get-tuple-element.61.packed_ref), channel_id=1, source_target_pairs={{0,2},{1,15},{2,0},{3,5},{4,6},{5,3},{6,4},{7,9},{8,10},{9,7},{10,... | collective-permute-start | bytes 24584 | tf_op jit(solution)/shard_map/ppermute | solution.py:489
  68.1 5.1 %collective-permute-start.24 = (f32[16,128]{1,0:T(8,128)S(1)}, f32[16,128]{1,0:T(8,128)S(1)}, u32[]{:S(2)}, u32[]{:S(2)}) collective-permute-start(f32[16,128]{1,0:T(8,128)S(1)} %get-tuple-element.61.packed_ref), channel_id=1, source_target_pairs={{0,8},{2,10},{4,12},{6,14},{8,0},{10,2},{12,4},{14,6},{1,9},{3,11}... | collective-permute-start | bytes 24584 | tf_op jit(solution)/shard_map/ppermute | solution.py:474
  71.4 2.6 %collective-permute-start.26 = (f32[16,128]{1,0:T(8,128)S(1)}, f32[16,128]{1,0:T(8,128)S(1)}, u32[]{:S(2)}, u32[]{:S(2)}) collective-permute-start(f32[16,128]{1,0:T(8,128)S(1)} %collective-permute-done.25.mine_ref), channel_id=1, source_target_pairs={{0,1},{1,0},{2,3},{3,2},{4,5},{5,4},{6,7},{7,6},{8,9},{9,8},{10,11... | collective-permute-start | bytes 24584 | tf_op jit(solution)/shard_map/ppermute | solution.py:492
  (8 other events, 10.6 us)

commit v14 on v12

--- a/solution.py
+++ b/solution.py
@@ -406,13 +406,12 @@
     counts = jnp.pad(send_count, ((0, 0), (0, slots - peers)))
     table = jnp.concatenate([send_node[0], recv_row[0], counts])
     index = shape(peers, slots, dtype=jnp.int32)
+    other_tiles = from_sibling(tile_values)
     double = shape(2, slots)
     states, nodes, own, keep, give, to_far = call(begin, (dense, index) + (double,) * 4)(
         in_specs=[VMEM] * 2
     )(states, table)
     got = from_sibling(give)
-    tile_values, got = lax.optimization_barrier((tile_values, got))
-    other_tiles = from_sibling(tile_values)
     far = with_far(to_far)
     near = with_either(jnp.concatenate([keep, got]), True)
     columns, diag, own = call(

time: 59.3 us -> 59.9 us (1.010)
  waiting for transfers between devices: 31.7 us -> 32.3 us
    ppermute x13, waiting for transfers between devices: 10.3 us -> 11.1 us  [from_sibling(): return lax.ppermute(value, 'sub', [(0, 1), (1, 0)])]
  transfers between devices with their start and end apart: 25 -> 25, of which waited for: 19 -> 19; matrix products, arithmetic and copies ran while one was open for 0% -> 1% of each run, Pallas kernels for 1% -> 1%
where the time goes in v14:
time: 59.9 us; the launch traced here: 59.5 us
  waiting for transfers between devices  32.3 us (54%)
  starting transfers between devices  16.8 us (28%)
  Pallas kernels  5.08 us (8%)
  local copies, waits for them, and re-layouts  3.88 us (6%)
  other arithmetic  0.77 us (1%)
  between operations  0.75 us (1%)
    ppermute x8, waiting for transfers between devices, with_either(): return lax.ppermute(value, ('case', 'dom', 'sub'), pairs)  17.1 us
    ppermute x13, waiting for transfers between devices, from_sibling(): return lax.ppermute(value, 'sub', [(0, 1), (1, 0)])  11.1 us
    ppermute x13, starting transfers between devices, from_sibling(): return lax.ppermute(value, 'sub', [(0, 1), (1, 0)])  7.86 us
    ppermute x4, starting transfers between devices, with_far(): lax.ppermute(value, 'dom', [(i, (i + chain // 2) % chain) for i in range(...  4.78 us
    ppermute x8, starting transfers between devices, with_either(): return lax.ppermute(value, ('case', 'dom', 'sub'), pairs)  4.13 us
    ppermute x4, waiting for transfers between devices, with_far(): lax.ppermute(value, 'dom', [(i, (i + chain // 2) % chain) for i in range(...  4.04 us
    unnamed x10, local copies, waits for them, and re-layouts  3.88 us
    pallas_call x1, Pallas kernels, on_device(): call(functools.partial(finish, chain), (shape(*dense.shape[:1], node_coun...  1.44 us
  transfers between devices with their start and end apart: 25, of which 19 were waited for; matrix products, arithmetic and copies ran while one was open for 1% of the time, Pallas kernels for 1%

profile of v14, /device:TPU:0, one launch (start us, length us, event | category | flops | bytes accessed | tf_op | source)
XLA Modules:
  0.0 59.5 jit_solution(9468700675339473521)
XLA Ops:
  3.2 1.7 %collective-permute-done.1.got_ref = f32[2,512]{1,0:T(2,128)S(1)} collective-permute-done((f32[2,512]{1,0:T(2,128)S(1)}, f32[2,512]{1,0:T(2,128)S(1)}, u32[]{:S(2)}, u32[]{:S(2)}) %collective-permute-start.1) | collective-permute-done | bytes 4128 | tf_op jit(solution)/shard_map/ppermute | solution.py:398
  5.0 2.9 %collective-permute-start.2 = (f32[4,512]{1,0:T(4,128)S(1)}, f32[4,512]{1,0:T(4,128)S(1)}, u32[]{:S(2)}, u32[]{:S(2)}) collective-permute-start(f32[4,512]{1,0:T(4,128)S(1)} %pad_maximum_fusion), channel_id=1, source_target_pairs={{0,2},{1,15},{2,0},{3,5},{4,6},{5,3},{6,4},{7,9},{8,10},{9,7},{10,... | collective-permute-start | bytes 24584 | tf_op jit(solution)/shard_map/ppermute | solution.py:395
  7.9 2.6 %collective-permute-start.3 = (f32[2,512]{1,0:T(2,128)S(1)}, f32[2,512]{1,0:T(2,128)S(1)}, u32[]{:S(2)}, u32[]{:S(2)}) collective-permute-start(f32[2,512]{1,0:T(2,128)S(1)} %get-tuple-element.39.to_far), channel_id=1, source_target_pairs={{0,8},{2,10},{4,12},{6,14},{8,0},{10,2},{12,4},{14,6},{1,9},{3,11}... | collective-permute-start | bytes 12296 | tf_op jit(solution)/shard_map/ppermute | solution.py:380
  12.7 1.7 %collective-permute-start.4 = (f32[8,128]{1,0:T(8,128)S(1)}, f32[8,128]{1,0:T(8,128)S(1)}, u32[]{:S(2)}, u32[]{:S(2)}) collective-permute-start(f32[8,128]{1,0:T(8,128)S(1)} %get-tuple-element.40), channel_id=1, source_target_pairs={{0,1},{1,0},{2,3},{3,2},{4,5},{5,4},{6,7},{7,6},{8,9},{9,8},{10,11... | collective-permute-start | bytes 12296 | tf_op jit(solution)/shard_map/ppermute | solution.py:398
  14.5 1.1 %collective-permute-done.5.other_cols = s32[4,8]{1,0:T(4,128)S(1)} collective-permute-done((s32[4,8]{1,0:T(4,128)S(1)}, s32[4,8]{1,0:T(4,128)S(1)}, u32[]{:S(2)}, u32[]{:S(2)}) %collective-permute-start.5) | collective-permute-done | bytes 160 | tf_op jit(solution)/shard_map/ppermute | solution.py:398
  15.7 1.6 %copy-done = f32[8,4,128,128]{3,2,1,0:T(8,128)S(1)} copy-done((f32[8,4,128,128]{3,2,1,0:T(8,128)S(1)}, f32[8,4,128,128]{3,2,1,0:T(8,128)}, u32[]{:S(2)}) %copy-start) | copy-done | bytes 2097176
  17.3 2.0 %collective-permute-done.6.mine_ref = f32[8,128]{1,0:T(8,128)S(1)} collective-permute-done((f32[8,128]{1,0:T(8,128)S(1)}, f32[8,128]{1,0:T(8,128)S(1)}, u32[]{:S(2)}, u32[]{:S(2)}) %collective-permute-start.6) | collective-permute-done | bytes 4128 | tf_op jit(solution)/shard_map/ppermute | solution.py:395
  19.3 1.1 %collective-permute-done.7.yours_ref = f32[8,128]{1,0:T(8,128)S(1)} collective-permute-done((f32[8,128]{1,0:T(8,128)S(1)}, f32[8,128]{1,0:T(8,128)S(1)}, u32[]{:S(2)}, u32[]{:S(2)}) %collective-permute-start.7) | collective-permute-done | bytes 4128 | tf_op jit(solution)/shard_map/ppermute | solution.py:398
  21.4 3.2 %collective-permute-done.8.mine_ref = f32[8,128]{1,0:T(8,128)S(1)} collective-permute-done((f32[8,128]{1,0:T(8,128)S(1)}, f32[8,128]{1,0:T(8,128)S(1)}, u32[]{:S(2)}, u32[]{:S(2)}) %collective-permute-start.8) | collective-permute-done | bytes 4128 | tf_op jit(solution)/shard_map/ppermute | solution.py:395
  24.6 1.2 %collective-permute-done.9.yours_ref = f32[8,128]{1,0:T(8,128)S(1)} collective-permute-done((f32[8,128]{1,0:T(8,128)S(1)}, f32[8,128]{1,0:T(8,128)S(1)}, u32[]{:S(2)}, u32[]{:S(2)}) %collective-permute-start.9) | collective-permute-done | bytes 4128 | tf_op jit(solution)/shard_map/ppermute | solution.py:398
  26.8 1.5 %collective-permute-start.10 = (f32[8,128]{1,0:T(8,128)S(1)}, f32[8,128]{1,0:T(8,128)S(1)}, u32[]{:S(2)}, u32[]{:S(2)}) collective-permute-start(f32[8,128]{1,0:T(8,128)S(1)} %shard_map.100.own_estimate), channel_id=1, source_target_pairs={{0,8},{2,10},{4,12},{6,14},{8,0},{10,2},{12,4},{14,6},{1,9},{3,11}... | collective-permute-start | bytes 12296 | tf_op jit(solution)/shard_map/ppermute | solution.py:380
  28.3 1.7 %collective-permute-done.11.mine_ref = f32[8,128]{1,0:T(8,128)S(1)} collective-permute-done((f32[8,128]{1,0:T(8,128)S(1)}, f32[8,128]{1,0:T(8,128)S(1)}, u32[]{:S(2)}, u32[]{:S(2)}) %collective-permute-start.11) | collective-permute-done | bytes 4128 | tf_op jit(solution)/shard_map/ppermute | solution.py:395
  30.0 1.7 %collective-permute-start.12 = (f32[8,128]{1,0:T(8,128)S(1)}, f32[8,128]{1,0:T(8,128)S(1)}, u32[]{:S(2)}, u32[]{:S(2)}) collective-permute-start(f32[8,128]{1,0:T(8,128)S(1)} %collective-permute-done.11.mine_ref), channel_id=1, source_target_pairs={{0,1},{1,0},{2,3},{3,2},{4,5},{5,4},{6,7},{7,6},{8,9},{9,8},{10,11... | collective-permute-start | bytes 12296 | tf_op jit(solution)/shard_map/ppermute | solution.py:398
  31.7 1.2 %collective-permute-done.13.got_ref = f32[1,512]{1,0:T(1,128)S(1)} collective-permute-done((f32[1,512]{1,0:T(1,128)S(1)}, f32[1,512]{1,0:T(1,128)S(1)}, u32[]{:S(2)}, u32[]{:S(2)}) %collective-permute-start.13) | collective-permute-done | bytes 2080 | tf_op jit(solution)/shard_map/ppermute | solution.py:398
  34.1 1.0 %collective-permute-done.15 = f32[8,128]{1,0:T(8,128)S(1)} collective-permute-done((f32[8,128]{1,0:T(8,128)S(1)}, f32[8,128]{1,0:T(8,128)S(1)}, u32[]{:S(2)}, u32[]{:S(2)}) %collective-permute-start.15) | collective-permute-done | bytes 4128 | tf_op jit(solution)/shard_map/ppermute | solution.py:398
  35.1 3.5 %collective-permute-done.14 = f32[8,128]{1,0:T(8,128)S(1)} collective-permute-done((f32[8,128]{1,0:T(8,128)S(1)}, f32[8,128]{1,0:T(8,128)S(1)}, u32[]{:S(2)}, u32[]{:S(2)}) %collective-permute-start.14) | collective-permute-done | bytes 4128 | tf_op jit(solution)/shard_map/ppermute | solution.py:380
  38.7 1.7 %collective-permute-start.17 = (f32[8,128]{1,0:T(8,128)S(1)}, f32[8,128]{1,0:T(8,128)S(1)}, u32[]{:S(2)}, u32[]{:S(2)}) collective-permute-start(f32[8,128]{1,0:T(8,128)S(1)} %add_multiply_fusion), channel_id=1, source_target_pairs={{0,1},{1,0},{2,3},{3,2},{4,5},{5,4},{6,7},{7,6},{8,9},{9,8},{10,11... | collective-permute-start | bytes 12296 | tf_op jit(solution)/shard_map/ppermute | solution.py:398
  41.2 3.6 %collective-permute-done.18.mine_ref = f32[8,128]{1,0:T(8,128)S(1)} collective-permute-done((f32[8,128]{1,0:T(8,128)S(1)}, f32[8,128]{1,0:T(8,128)S(1)}, u32[]{:S(2)}, u32[]{:S(2)}) %collective-permute-start.18) | collective-permute-done | bytes 4128 | tf_op jit(solution)/shard_map/ppermute | solution.py:395
  44.8 1.2 %collective-permute-done.19.yours_ref = f32[8,128]{1,0:T(8,128)S(1)} collective-permute-done((f32[8,128]{1,0:T(8,128)S(1)}, f32[8,128]{1,0:T(8,128)S(1)}, u32[]{:S(2)}, u32[]{:S(2)}) %collective-permute-start.19) | collective-permute-done | bytes 4128 | tf_op jit(solution)/shard_map/ppermute | solution.py:398
  46.6 3.6 %collective-permute-done.20.mine_ref = f32[8,128]{1,0:T(8,128)S(1)} collective-permute-done((f32[8,128]{1,0:T(8,128)S(1)}, f32[8,128]{1,0:T(8,128)S(1)}, u32[]{:S(2)}, u32[]{:S(2)}) %collective-permute-start.20) | collective-permute-done | bytes 4128 | tf_op jit(solution)/shard_map/ppermute | solution.py:395
  50.2 1.2 %collective-permute-done.21.yours_ref = f32[8,128]{1,0:T(8,128)S(1)} collective-permute-done((f32[8,128]{1,0:T(8,128)S(1)}, f32[8,128]{1,0:T(8,128)S(1)}, u32[]{:S(2)}, u32[]{:S(2)}) %collective-permute-start.21) | collective-permute-done | bytes 4128 | tf_op jit(solution)/shard_map/ppermute | solution.py:398
  52.6 3.0 %collective-permute-done.23.mine_ref = f32[16,128]{1,0:T(8,128)S(1)} collective-permute-done((f32[16,128]{1,0:T(8,128)S(1)}, f32[16,128]{1,0:T(8,128)S(1)}, u32[]{:S(2)}, u32[]{:S(2)}) %collective-permute-start.23) | collective-permute-done | bytes 8224 | tf_op jit(solution)/shard_map/ppermute | solution.py:395
  55.6 1.7 %collective-permute-start.24 = (f32[16,128]{1,0:T(8,128)S(1)}, f32[16,128]{1,0:T(8,128)S(1)}, u32[]{:S(2)}, u32[]{:S(2)}) collective-permute-start(f32[16,128]{1,0:T(8,128)S(1)} %collective-permute-done.23.mine_ref), channel_id=1, source_target_pairs={{0,1},{1,0},{2,3},{3,2},{4,5},{5,4},{6,7},{7,6},{8,9},{9,8},{10,11... | collective-permute-start | bytes 24584 | tf_op jit(solution)/shard_map/ppermute | solution.py:398
  58.1 1.4 %shard_map.105 = (f32[19,2048]{1,0:T(8,128)}, f32[8,128]{1,0:T(8,128)}, f32[8,128]{1,0:T(8,128)}) custom-call(f32[8,4,128,128]{3,2,1,0:T(8,128)S(1)} %copy-done.1, f32[8,4,128,128]{3,2,1,0:T(8,128)S(1)} %collective-permute-done.other_ref, f32[64,16]{1,0:T(8,128)S(1)} %shard_map.97.pick_ref, f32[16,128]{1,0:T(8,128)S(1)} %get-tuple-element.59.packed_ref, ...), custom_call_target="tpu_custom_call" | custom-call | flops 4000000 | bytes 262144 | tf_op jit(solution)/shard_map/pallas_call | solution.py:460
  (54 shorter events, 11.8 us)
Async XLA Ops:
  0.6 19.8 %collective-permute-start = (f32[8,4,128,128]{3,2,1,0:T(8,128)}, f32[8,4,128,128]{3,2,1,0:T(8,128)S(1)}, u32[]{:S(2)}, u32[]{:S(2)}) collective-permute-start(f32[8,4,128,128]{3,2,1,0:T(8,128)} %own_ref.9), channel_id=1, source_target_pairs={{0,1},{1,0},{2,3},{3,2},{4,5},{5,4},{6,7},{7,6},{8,9},{9,8},{10,11... | collective-permute-start | bytes 6291464 | tf_op jit(solution)/shard_map/ppermute | solution.py:398
  3.1 1.8 %collective-permute-start.1 = (f32[2,512]{1,0:T(2,128)S(1)}, f32[2,512]{1,0:T(2,128)S(1)}, u32[]{:S(2)}, u32[]{:S(2)}) collective-permute-start(f32[2,512]{1,0:T(2,128)S(1)} %get-tuple-element.38), channel_id=1, source_target_pairs={{0,1},{1,0},{2,3},{3,2},{4,5},{5,4},{6,7},{7,6},{8,9},{9,8},{10,11... | collective-permute-start | bytes 12296 | tf_op jit(solution)/shard_map/ppermute | solution.py:398
  5.0 7.4 %collective-permute-start.2 = (f32[4,512]{1,0:T(4,128)S(1)}, f32[4,512]{1,0:T(4,128)S(1)}, u32[]{:S(2)}, u32[]{:S(2)}) collective-permute-start(f32[4,512]{1,0:T(4,128)S(1)} %pad_maximum_fusion), channel_id=1, source_target_pairs={{0,2},{1,15},{2,0},{3,5},{4,6},{5,3},{6,4},{7,9},{8,10},{9,7},{10,... | collective-permute-start | bytes 24584 | tf_op jit(solution)/shard_map/ppermute | solution.py:395
  7.9 4.5 %collective-permute-start.3 = (f32[2,512]{1,0:T(2,128)S(1)}, f32[2,512]{1,0:T(2,128)S(1)}, u32[]{:S(2)}, u32[]{:S(2)}) collective-permute-start(f32[2,512]{1,0:T(2,128)S(1)} %get-tuple-element.39.to_far), channel_id=1, source_target_pairs={{0,8},{2,10},{4,12},{6,14},{8,0},{10,2},{12,4},{14,6},{1,9},{3,11}... | collective-permute-start | bytes 12296 | tf_op jit(solution)/shard_map/ppermute | solution.py:380
  12.7 2.9 %collective-permute-start.4 = (f32[8,128]{1,0:T(8,128)S(1)}, f32[8,128]{1,0:T(8,128)S(1)}, u32[]{:S(2)}, u32[]{:S(2)}) collective-permute-start(f32[8,128]{1,0:T(8,128)S(1)} %get-tuple-element.40), channel_id=1, source_target_pairs={{0,1},{1,0},{2,3},{3,2},{4,5},{5,4},{6,7},{7,6},{8,9},{9,8},{10,11... | collective-permute-start | bytes 12296 | tf_op jit(solution)/shard_map/ppermute | solution.py:398
  14.4 1.2 %collective-permute-start.5 = (s32[4,8]{1,0:T(4,128)S(1)}, s32[4,8]{1,0:T(4,128)S(1)}, u32[]{:S(2)}, u32[]{:S(2)}) collective-permute-start(s32[4,8]{1,0:T(4,128)S(1)} %get-tuple-element.35.own_cols), channel_id=1, source_target_pairs={{0,1},{1,0},{2,3},{3,2},{4,5},{5,4},{6,7},{7,6},{8,9},{9,8},{10,11... | collective-permute-start | bytes 392 | tf_op jit(solution)/shard_map/ppermute | solution.py:398
  15.6 3.7 %collective-permute-start.6 = (f32[8,128]{1,0:T(8,128)S(1)}, f32[8,128]{1,0:T(8,128)S(1)}, u32[]{:S(2)}, u32[]{:S(2)}) collective-permute-start(f32[8,128]{1,0:T(8,128)S(1)} %get-tuple-element.67.direction_ref), channel_id=1, source_target_pairs={{0,2},{1,17},{2,0},{3,5},{4,6},{5,3},{6,4},{7,9},{8,10},{9,7},{10,... | collective-permute-start | bytes 12296 | tf_op jit(solution)/shard_map/ppermute | solution.py:395
  19.3 1.2 %collective-permute-start.7 = (f32[8,128]{1,0:T(8,128)S(1)}, f32[8,128]{1,0:T(8,128)S(1)}, u32[]{:S(2)}, u32[]{:S(2)}) collective-permute-start(f32[8,128]{1,0:T(8,128)S(1)} %collective-permute-done.6.mine_ref), channel_id=1, source_target_pairs={{0,1},{1,0},{2,3},{3,2},{4,5},{5,4},{6,7},{7,6},{8,9},{9,8},{10,11... | collective-permute-start | bytes 12296 | tf_op jit(solution)/shard_map/ppermute | solution.py:398
  20.9 3.7 %collective-permute-start.8 = (f32[8,128]{1,0:T(8,128)S(1)}, f32[8,128]{1,0:T(8,128)S(1)}, u32[]{:S(2)}, u32[]{:S(2)}) collective-permute-start(f32[8,128]{1,0:T(8,128)S(1)} %get-tuple-element.47.direction_in), channel_id=1, source_target_pairs={{0,2},{1,17},{2,0},{3,5},{4,6},{5,3},{6,4},{7,9},{8,10},{9,7},{10,... | collective-permute-start | bytes 12296 | tf_op jit(solution)/shard_map/ppermute | solution.py:395
  24.6 1.2 %collective-permute-start.9 = (f32[8,128]{1,0:T(8,128)S(1)}, f32[8,128]{1,0:T(8,128)S(1)}, u32[]{:S(2)}, u32[]{:S(2)}) collective-permute-start(f32[8,128]{1,0:T(8,128)S(1)} %collective-permute-done.8.mine_ref), channel_id=1, source_target_pairs={{0,1},{1,0},{2,3},{3,2},{4,5},{5,4},{6,7},{7,6},{8,9},{9,8},{10,11... | collective-permute-start | bytes 12296 | tf_op jit(solution)/shard_map/ppermute | solution.py:398
  26.3 3.7 %collective-permute-start.11 = (f32[8,128]{1,0:T(8,128)S(1)}, f32[8,128]{1,0:T(8,128)S(1)}, u32[]{:S(2)}, u32[]{:S(2)}) collective-permute-start(f32[8,128]{1,0:T(8,128)S(1)} %shard_map.100.own_estimate), channel_id=1, source_target_pairs={{0,2},{1,15},{2,0},{3,5},{4,6},{5,3},{6,4},{7,9},{8,10},{9,7},{10,... | collective-permute-start | bytes 12296 | tf_op jit(solution)/shard_map/ppermute | solution.py:395
  26.8 6.1 %collective-permute-start.10 = (f32[8,128]{1,0:T(8,128)S(1)}, f32[8,128]{1,0:T(8,128)S(1)}, u32[]{:S(2)}, u32[]{:S(2)}) collective-permute-start(f32[8,128]{1,0:T(8,128)S(1)} %shard_map.100.own_estimate), channel_id=1, source_target_pairs={{0,8},{2,10},{4,12},{6,14},{8,0},{10,2},{12,4},{14,6},{1,9},{3,11}... | collective-permute-start | bytes 12296 | tf_op jit(solution)/shard_map/ppermute | solution.py:380
  30.0 2.9 %collective-permute-start.12 = (f32[8,128]{1,0:T(8,128)S(1)}, f32[8,128]{1,0:T(8,128)S(1)}, u32[]{:S(2)}, u32[]{:S(2)}) collective-permute-start(f32[8,128]{1,0:T(8,128)S(1)} %collective-permute-done.11.mine_ref), channel_id=1, source_target_pairs={{0,1},{1,0},{2,3},{3,2},{4,5},{5,4},{6,7},{7,6},{8,9},{9,8},{10,11... | collective-permute-start | bytes 12296 | tf_op jit(solution)/shard_map/ppermute | solution.py:398
  33.8 1.2 %collective-permute-start.15 = (f32[8,128]{1,0:T(8,128)S(1)}, f32[8,128]{1,0:T(8,128)S(1)}, u32[]{:S(2)}, u32[]{:S(2)}) collective-permute-start(f32[8,128]{1,0:T(8,128)S(1)} %get-tuple-element.55), channel_id=1, source_target_pairs={{0,1},{1,0},{2,3},{3,2},{4,5},{5,4},{6,7},{7,6},{8,9},{9,8},{10,11... | collective-permute-start | bytes 12296 | tf_op jit(solution)/shard_map/ppermute | solution.py:398
  34.0 4.5 %collective-permute-start.14 = (f32[8,128]{1,0:T(8,128)S(1)}, f32[8,128]{1,0:T(8,128)S(1)}, u32[]{:S(2)}, u32[]{:S(2)}) collective-permute-start(f32[8,128]{1,0:T(8,128)S(1)} %get-tuple-element.53), channel_id=1, source_target_pairs={{0,8},{2,10},{4,12},{6,14},{8,0},{10,2},{12,4},{14,6},{1,9},{3,11}... | collective-permute-start | bytes 12296 | tf_op jit(solution)/shard_map/ppermute | solution.py:380
  35.0 3.6 %collective-permute-start.16 = (f32[8,128]{1,0:T(8,128)S(1)}, f32[8,128]{1,0:T(8,128)S(1)}, u32[]{:S(2)}, u32[]{:S(2)}) collective-permute-start(f32[8,128]{1,0:T(8,128)S(1)} %add.19), channel_id=1, source_target_pairs={{0,2},{1,15},{2,0},{3,5},{4,6},{5,3},{6,4},{7,9},{8,10},{9,7},{10,... | collective-permute-start | bytes 12296 | tf_op jit(solution)/shard_map/ppermute | solution.py:395
  38.7 2.5 %collective-permute-start.17 = (f32[8,128]{1,0:T(8,128)S(1)}, f32[8,128]{1,0:T(8,128)S(1)}, u32[]{:S(2)}, u32[]{:S(2)}) collective-permute-start(f32[8,128]{1,0:T(8,128)S(1)} %add_multiply_fusion), channel_id=1, source_target_pairs={{0,1},{1,0},{2,3},{3,2},{4,5},{5,4},{6,7},{7,6},{8,9},{9,8},{10,11... | collective-permute-start | bytes 12296 | tf_op jit(solution)/shard_map/ppermute | solution.py:398
  41.2 3.6 %collective-permute-start.18 = (f32[8,128]{1,0:T(8,128)S(1)}, f32[8,128]{1,0:T(8,128)S(1)}, u32[]{:S(2)}, u32[]{:S(2)}) collective-permute-start(f32[8,128]{1,0:T(8,128)S(1)} %get-tuple-element.65.direction_in), channel_id=1, source_target_pairs={{0,2},{1,17},{2,0},{3,5},{4,6},{5,3},{6,4},{7,9},{8,10},{9,7},{10,... | collective-permute-start | bytes 12296 | tf_op jit(solution)/shard_map/ppermute | solution.py:395
  44.8 1.2 %collective-permute-start.19 = (f32[8,128]{1,0:T(8,128)S(1)}, f32[8,128]{1,0:T(8,128)S(1)}, u32[]{:S(2)}, u32[]{:S(2)}) collective-permute-start(f32[8,128]{1,0:T(8,128)S(1)} %collective-permute-done.18.mine_ref), channel_id=1, source_target_pairs={{0,1},{1,0},{2,3},{3,2},{4,5},{5,4},{6,7},{7,6},{8,9},{9,8},{10,11... | collective-permute-start | bytes 12296 | tf_op jit(solution)/shard_map/ppermute | solution.py:398
  46.5 3.7 %collective-permute-start.20 = (f32[8,128]{1,0:T(8,128)S(1)}, f32[8,128]{1,0:T(8,128)S(1)}, u32[]{:S(2)}, u32[]{:S(2)}) collective-permute-start(f32[8,128]{1,0:T(8,128)S(1)} %get-tuple-element.56.direction_in), channel_id=1, source_target_pairs={{0,2},{1,17},{2,0},{3,5},{4,6},{5,3},{6,4},{7,9},{8,10},{9,7},{10,... | collective-permute-start | bytes 12296 | tf_op jit(solution)/shard_map/ppermute | solution.py:395
  50.2 1.2 %collective-permute-start.21 = (f32[8,128]{1,0:T(8,128)S(1)}, f32[8,128]{1,0:T(8,128)S(1)}, u32[]{:S(2)}, u32[]{:S(2)}) collective-permute-start(f32[8,128]{1,0:T(8,128)S(1)} %collective-permute-done.20.mine_ref), channel_id=1, source_target_pairs={{0,1},{1,0},{2,3},{3,2},{4,5},{5,4},{6,7},{7,6},{8,9},{9,8},{10,11... | collective-permute-start | bytes 12296 | tf_op jit(solution)/shard_map/ppermute | solution.py:398
  51.8 3.7 %collective-permute-start.23 = (f32[16,128]{1,0:T(8,128)S(1)}, f32[16,128]{1,0:T(8,128)S(1)}, u32[]{:S(2)}, u32[]{:S(2)}) collective-permute-start(f32[16,128]{1,0:T(8,128)S(1)} %get-tuple-element.59.packed_ref), channel_id=1, source_target_pairs={{0,2},{1,15},{2,0},{3,5},{4,6},{5,3},{6,4},{7,9},{8,10},{9,7},{10,... | collective-permute-start | bytes 24584 | tf_op jit(solution)/shard_map/ppermute | solution.py:395
  51.9 5.4 %collective-permute-start.22 = (f32[16,128]{1,0:T(8,128)S(1)}, f32[16,128]{1,0:T(8,128)S(1)}, u32[]{:S(2)}, u32[]{:S(2)}) collective-permute-start(f32[16,128]{1,0:T(8,128)S(1)} %get-tuple-element.59.packed_ref), channel_id=1, source_target_pairs={{0,8},{2,10},{4,12},{6,14},{8,0},{10,2},{12,4},{14,6},{1,9},{3,11}... | collective-permute-start | bytes 24584 | tf_op jit(solution)/shard_map/ppermute | solution.py:380
  55.6 2.5 %collective-permute-start.24 = (f32[16,128]{1,0:T(8,128)S(1)}, f32[16,128]{1,0:T(8,128)S(1)}, u32[]{:S(2)}, u32[]{:S(2)}) collective-permute-start(f32[16,128]{1,0:T(8,128)S(1)} %collective-permute-done.23.mine_ref), channel_id=1, source_target_pairs={{0,1},{1,0},{2,3},{3,2},{4,5},{5,4},{6,7},{7,6},{8,9},{9,8},{10,11... | collective-permute-start | bytes 24584 | tf_op jit(solution)/shard_map/ppermute | solution.py:398
  (6 other events, 8.2 us)

commit v15 on v14

--- a/solution.py
+++ b/solution.py
@@ -232,7 +232,8 @@
     own_ref[...] = pair(0, 0)
     keep_ref[...] = jnp.where(ahead, to_next, to_prev)
     give_ref[...] = jnp.where(ahead, to_prev, to_next)
-    far_ref[...] = pair(3, 3)
+    far_ref[...] = jnp.zeros_like(far_ref)
+    far_ref[0:2] = pair(3, 3)
 
 
 def bring(cols_ref, diag_ref, own_ref, cols_out, diag_out, own_out):
@@ -259,7 +260,7 @@
 
 
 def first_forcing(
-    own_ref, keep_ref, got_ref, near_ref, to_far, far_ref, give_ref, forcing_ref
+    own_ref, far_ref, near_ref, keep_ref, got_ref, to_far, give_ref, forcing_ref
 ):
     total = None
     for come, rows in (
@@ -408,7 +409,7 @@
     index = shape(peers, slots, dtype=jnp.int32)
     other_tiles = from_sibling(tile_values)
     double = shape(2, slots)
-    states, nodes, own, keep, give, to_far = call(begin, (dense, index) + (double,) * 4)(
+    states, nodes, own, keep, give, to_far = call(begin, (dense, index) + (double,) * 3 + (shape(8, slots),))(
         in_specs=[VMEM] * 2
     )(states, table)
     got = from_sibling(give)
@@ -418,7 +419,7 @@
         bring, (shape(*columns.shape[::-1], dtype=jnp.int32), field, double)
     )(in_specs=[VMEM] * 3)(columns.T, diagonal.reshape(torso, LANES), own)
     give, forcing = call(first_forcing, (shape(1, slots), field))(in_specs=[VMEM] * 6)(
-        own, keep, got, near, to_far, far
+        own, far, near, keep, got, to_far
     )
     maps = call(complete, index)(in_specs=[VMEM] * 5)(own, near, far, from_sibling(give), nodes)
     other_columns = from_sibling(columns)

time: 59.9 us -> 58.6 us (0.978)
  waiting for transfers between devices: 32.3 us -> 29.4 us
  starting transfers between devices: 16.8 us -> 18.4 us
    ppermute x13, waiting for transfers between devices: 11.1 us -> 8.62 us  [from_sibling(): return lax.ppermute(value, 'sub', [(0, 1), (1, 0)])]
    ppermute x4, starting transfers between devices: 4.78 us -> 7.12 us  [with_far(): lax.ppermute(value, 'dom', [(i, (i + chain // 2) % chain) for i in range(...]
    ppermute x8, starting transfers between devices: 4.13 us -> 3.25 us  [with_either(): return lax.ppermute(value, ('case', 'dom', 'sub'), pairs)]
  transfers between devices with their start and end apart: 25 -> 25, of which waited for: 19 -> 17; matrix products, arithmetic and copies ran while one was open for 1% -> 1% of each run, Pallas kernels for 1% -> 1%
where the time goes in v15:
time: 58.6 us; the launch traced here: 58.2 us
  waiting for transfers between devices  29.4 us (50%)
  starting transfers between devices  18.4 us (31%)
  Pallas kernels  5.07 us (9%)
  local copies, waits for them, and re-layouts  3.88 us (7%)
  other arithmetic  0.77 us (1%)
  between operations  0.74 us (1%)
    ppermute x8, waiting for transfers between devices, with_either(): return lax.ppermute(value, ('case', 'dom', 'sub'), pairs)  17.2 us
    ppermute x13, waiting for transfers between devices, from_sibling(): return lax.ppermute(value, 'sub', [(0, 1), (1, 0)])  8.62 us
    ppermute x13, starting transfers between devices, from_sibling(): return lax.ppermute(value, 'sub', [(0, 1), (1, 0)])  8.01 us
    ppermute x4, starting transfers between devices, with_far(): lax.ppermute(value, 'dom', [(i, (i + chain // 2) % chain) for i in range(...  7.12 us
    unnamed x10, local copies, waits for them, and re-layouts  3.88 us
    ppermute x4, waiting for transfers between devices, with_far(): lax.ppermute(value, 'dom', [(i, (i + chain // 2) % chain) for i in range(...  3.52 us
    ppermute x8, starting transfers between devices, with_either(): return lax.ppermute(value, ('case', 'dom', 'sub'), pairs)  3.25 us
    pallas_call x1, Pallas kernels, on_device(): call(functools.partial(finish, chain), (shape(*dense.shape[:1], node_coun...  1.45 us
  transfers between devices with their start and end apart: 25, of which 17 were waited for; matrix products, arithmetic and copies ran while one was open for 1% of the time, Pallas kernels for 1%

profile of v15, /device:TPU:0, one launch (start us, length us, event | category | flops | bytes accessed | tf_op | source)
XLA Modules:
  0.0 58.2 jit_solution(2507455985085181459)
XLA Ops:
  3.2 4.0 %collective-permute-start.1 = (f32[8,512]{1,0:T(8,128)S(1)}, f32[8,512]{1,0:T(8,128)S(1)}, u32[]{:S(2)}, u32[]{:S(2)}) collective-permute-start(f32[8,512]{1,0:T(8,128)S(1)} %get-tuple-element.37.to_far), channel_id=1, source_target_pairs={{0,8},{2,10},{4,12},{6,14},{8,0},{10,2},{12,4},{14,6},{1,9},{3,11}... | collective-permute-start | bytes 49160 | tf_op jit(solution)/shard_map/ppermute | solution.py:381
  7.3 1.6 %collective-permute-start.3 = (f32[4,512]{1,0:T(4,128)S(1)}, f32[4,512]{1,0:T(4,128)S(1)}, u32[]{:S(2)}, u32[]{:S(2)}) collective-permute-start(f32[4,512]{1,0:T(4,128)S(1)} %pad_maximum_fusion), channel_id=1, source_target_pairs={{0,2},{1,15},{2,0},{3,5},{4,6},{5,3},{6,4},{7,9},{8,10},{9,7},{10,... | collective-permute-start | bytes 24584 | tf_op jit(solution)/shard_map/ppermute | solution.py:396
  11.3 1.4 %collective-permute-start.4 = (f32[8,128]{1,0:T(8,128)S(1)}, f32[8,128]{1,0:T(8,128)S(1)}, u32[]{:S(2)}, u32[]{:S(2)}) collective-permute-start(f32[8,128]{1,0:T(8,128)S(1)} %get-tuple-element.40), channel_id=1, source_target_pairs={{0,1},{1,0},{2,3},{3,2},{4,5},{5,4},{6,7},{7,6},{8,9},{9,8},{10,11... | collective-permute-start | bytes 12296 | tf_op jit(solution)/shard_map/ppermute | solution.py:399
  12.7 1.1 %collective-permute-done.5.other_cols = s32[4,8]{1,0:T(4,128)S(1)} collective-permute-done((s32[4,8]{1,0:T(4,128)S(1)}, s32[4,8]{1,0:T(4,128)S(1)}, u32[]{:S(2)}, u32[]{:S(2)}) %collective-permute-start.5) | collective-permute-done | bytes 160 | tf_op jit(solution)/shard_map/ppermute | solution.py:399
  14.2 1.6 %copy-done = f32[8,4,128,128]{3,2,1,0:T(8,128)S(1)} copy-done((f32[8,4,128,128]{3,2,1,0:T(8,128)S(1)}, f32[8,4,128,128]{3,2,1,0:T(8,128)}, u32[]{:S(2)}) %copy-start) | copy-done | bytes 2097176
  15.8 1.7 %collective-permute-done.6.mine_ref = f32[8,128]{1,0:T(8,128)S(1)} collective-permute-done((f32[8,128]{1,0:T(8,128)S(1)}, f32[8,128]{1,0:T(8,128)S(1)}, u32[]{:S(2)}, u32[]{:S(2)}) %collective-permute-start.6) | collective-permute-done | bytes 4128 | tf_op jit(solution)/shard_map/ppermute | solution.py:396
  17.6 1.1 %collective-permute-done.7.yours_ref = f32[8,128]{1,0:T(8,128)S(1)} collective-permute-done((f32[8,128]{1,0:T(8,128)S(1)}, f32[8,128]{1,0:T(8,128)S(1)}, u32[]{:S(2)}, u32[]{:S(2)}) %collective-permute-start.7) | collective-permute-done | bytes 4128 | tf_op jit(solution)/shard_map/ppermute | solution.py:399
  19.7 3.2 %collective-permute-done.8.mine_ref = f32[8,128]{1,0:T(8,128)S(1)} collective-permute-done((f32[8,128]{1,0:T(8,128)S(1)}, f32[8,128]{1,0:T(8,128)S(1)}, u32[]{:S(2)}, u32[]{:S(2)}) %collective-permute-start.8) | collective-permute-done | bytes 4128 | tf_op jit(solution)/shard_map/ppermute | solution.py:396
  22.9 1.2 %collective-permute-done.9.yours_ref = f32[8,128]{1,0:T(8,128)S(1)} collective-permute-done((f32[8,128]{1,0:T(8,128)S(1)}, f32[8,128]{1,0:T(8,128)S(1)}, u32[]{:S(2)}, u32[]{:S(2)}) %collective-permute-start.9) | collective-permute-done | bytes 4128 | tf_op jit(solution)/shard_map/ppermute | solution.py:399
  25.1 1.5 %collective-permute-start.10 = (f32[8,128]{1,0:T(8,128)S(1)}, f32[8,128]{1,0:T(8,128)S(1)}, u32[]{:S(2)}, u32[]{:S(2)}) collective-permute-start(f32[8,128]{1,0:T(8,128)S(1)} %shard_map.100.own_estimate), channel_id=1, source_target_pairs={{0,8},{2,10},{4,12},{6,14},{8,0},{10,2},{12,4},{14,6},{1,9},{3,11}... | collective-permute-start | bytes 12296 | tf_op jit(solution)/shard_map/ppermute | solution.py:381
  26.6 1.7 %collective-permute-done.11.mine_ref = f32[8,128]{1,0:T(8,128)S(1)} collective-permute-done((f32[8,128]{1,0:T(8,128)S(1)}, f32[8,128]{1,0:T(8,128)S(1)}, u32[]{:S(2)}, u32[]{:S(2)}) %collective-permute-start.11) | collective-permute-done | bytes 4128 | tf_op jit(solution)/shard_map/ppermute | solution.py:396
  28.2 1.7 %collective-permute-start.12 = (f32[8,128]{1,0:T(8,128)S(1)}, f32[8,128]{1,0:T(8,128)S(1)}, u32[]{:S(2)}, u32[]{:S(2)}) collective-permute-start(f32[8,128]{1,0:T(8,128)S(1)} %collective-permute-done.11.mine_ref), channel_id=1, source_target_pairs={{0,1},{1,0},{2,3},{3,2},{4,5},{5,4},{6,7},{7,6},{8,9},{9,8},{10,11... | collective-permute-start | bytes 12296 | tf_op jit(solution)/shard_map/ppermute | solution.py:399
  29.9 1.2 %collective-permute-done.13.got_ref = f32[1,512]{1,0:T(1,128)S(1)} collective-permute-done((f32[1,512]{1,0:T(1,128)S(1)}, f32[1,512]{1,0:T(1,128)S(1)}, u32[]{:S(2)}, u32[]{:S(2)}) %collective-permute-start.13) | collective-permute-done | bytes 2080 | tf_op jit(solution)/shard_map/ppermute | solution.py:399
  31.1 0.9 %shard_map.102 = (f32[19,16,128]{2,1,0:T(8,128)S(1)}, f32[8,128]{1,0:T(8,128)S(1)}, f32[8,128]{1,0:T(8,128)S(1)}, f32[8,128]{1,0:T(8,128)S(1)}, f32[8,128]{1,0:T(8,128)S(1)}) custom-call(f32[19,16,128]{2,1,0:T(8,128)S(1)} %get-tuple-element.42.states_ref, f32[8,128]{1,0:T(8,128)S(1)} %shard_map.100.own_estimate, ...), custom_call_target="tpu_custom_call" | custom-call | flops 4000000 | bytes 262144 | tf_op jit(solution)/shard_map/pallas_call | solution.py:455
  33.7 3.5 %collective-permute-done.14 = f32[8,128]{1,0:T(8,128)S(1)} collective-permute-done((f32[8,128]{1,0:T(8,128)S(1)}, f32[8,128]{1,0:T(8,128)S(1)}, u32[]{:S(2)}, u32[]{:S(2)}) %collective-permute-start.14) | collective-permute-done | bytes 4128 | tf_op jit(solution)/shard_map/ppermute | solution.py:381
  37.2 1.8 %collective-permute-start.17 = (f32[8,128]{1,0:T(8,128)S(1)}, f32[8,128]{1,0:T(8,128)S(1)}, u32[]{:S(2)}, u32[]{:S(2)}) collective-permute-start(f32[8,128]{1,0:T(8,128)S(1)} %add_multiply_fusion), channel_id=1, source_target_pairs={{0,1},{1,0},{2,3},{3,2},{4,5},{5,4},{6,7},{7,6},{8,9},{9,8},{10,11... | collective-permute-start | bytes 12296 | tf_op jit(solution)/shard_map/ppermute | solution.py:399
  39.9 3.6 %collective-permute-done.18.mine_ref = f32[8,128]{1,0:T(8,128)S(1)} collective-permute-done((f32[8,128]{1,0:T(8,128)S(1)}, f32[8,128]{1,0:T(8,128)S(1)}, u32[]{:S(2)}, u32[]{:S(2)}) %collective-permute-start.18) | collective-permute-done | bytes 4128 | tf_op jit(solution)/shard_map/ppermute | solution.py:396
  43.5 1.2 %collective-permute-done.19.yours_ref = f32[8,128]{1,0:T(8,128)S(1)} collective-permute-done((f32[8,128]{1,0:T(8,128)S(1)}, f32[8,128]{1,0:T(8,128)S(1)}, u32[]{:S(2)}, u32[]{:S(2)}) %collective-permute-start.19) | collective-permute-done | bytes 4128 | tf_op jit(solution)/shard_map/ppermute | solution.py:399
  45.2 3.6 %collective-permute-done.20.mine_ref = f32[8,128]{1,0:T(8,128)S(1)} collective-permute-done((f32[8,128]{1,0:T(8,128)S(1)}, f32[8,128]{1,0:T(8,128)S(1)}, u32[]{:S(2)}, u32[]{:S(2)}) %collective-permute-start.20) | collective-permute-done | bytes 4128 | tf_op jit(solution)/shard_map/ppermute | solution.py:396
  48.8 1.2 %collective-permute-done.21.yours_ref = f32[8,128]{1,0:T(8,128)S(1)} collective-permute-done((f32[8,128]{1,0:T(8,128)S(1)}, f32[8,128]{1,0:T(8,128)S(1)}, u32[]{:S(2)}, u32[]{:S(2)}) %collective-permute-start.21) | collective-permute-done | bytes 4128 | tf_op jit(solution)/shard_map/ppermute | solution.py:399
  50.6 0.9 %collective-permute-start.22 = (f32[16,128]{1,0:T(8,128)S(1)}, f32[16,128]{1,0:T(8,128)S(1)}, u32[]{:S(2)}, u32[]{:S(2)}) collective-permute-start(f32[16,128]{1,0:T(8,128)S(1)} %get-tuple-element.59.packed_ref), channel_id=1, source_target_pairs={{0,8},{2,10},{4,12},{6,14},{8,0},{10,2},{12,4},{14,6},{1,9},{3,11}... | collective-permute-start | bytes 24584 | tf_op jit(solution)/shard_map/ppermute | solution.py:381
  51.5 2.7 %collective-permute-done.23.mine_ref = f32[16,128]{1,0:T(8,128)S(1)} collective-permute-done((f32[16,128]{1,0:T(8,128)S(1)}, f32[16,128]{1,0:T(8,128)S(1)}, u32[]{:S(2)}, u32[]{:S(2)}) %collective-permute-start.23) | collective-permute-done | bytes 8224 | tf_op jit(solution)/shard_map/ppermute | solution.py:396
  54.2 1.7 %collective-permute-start.24 = (f32[16,128]{1,0:T(8,128)S(1)}, f32[16,128]{1,0:T(8,128)S(1)}, u32[]{:S(2)}, u32[]{:S(2)}) collective-permute-start(f32[16,128]{1,0:T(8,128)S(1)} %collective-permute-done.23.mine_ref), channel_id=1, source_target_pairs={{0,1},{1,0},{2,3},{3,2},{4,5},{5,4},{6,7},{7,6},{8,9},{9,8},{10,11... | collective-permute-start | bytes 24584 | tf_op jit(solution)/shard_map/ppermute | solution.py:399
  56.8 1.4 %shard_map.105 = (f32[19,2048]{1,0:T(8,128)}, f32[8,128]{1,0:T(8,128)}, f32[8,128]{1,0:T(8,128)}) custom-call(f32[8,4,128,128]{3,2,1,0:T(8,128)S(1)} %copy-done.1, f32[8,4,128,128]{3,2,1,0:T(8,128)S(1)} %collective-permute-done.other_ref, f32[64,16]{1,0:T(8,128)S(1)} %shard_map.97.pick_ref, f32[16,128]{1,0:T(8,128)S(1)} %get-tuple-element.59.packed_ref, ...), custom_call_target="tpu_custom_call" | custom-call | flops 4000000 | bytes 262144 | tf_op jit(solution)/shard_map/pallas_call | solution.py:461
  (54 shorter events, 12.1 us)
Async XLA Ops:
  0.6 18.1 %collective-permute-start = (f32[8,4,128,128]{3,2,1,0:T(8,128)}, f32[8,4,128,128]{3,2,1,0:T(8,128)S(1)}, u32[]{:S(2)}, u32[]{:S(2)}) collective-permute-start(f32[8,4,128,128]{3,2,1,0:T(8,128)} %own_ref.9), channel_id=1, source_target_pairs={{0,1},{1,0},{2,3},{3,2},{4,5},{5,4},{6,7},{7,6},{8,9},{9,8},{10,11... | collective-permute-start | bytes 6291464 | tf_op jit(solution)/shard_map/ppermute | solution.py:399
  3.1 4.2 %collective-permute-start.2 = (f32[2,512]{1,0:T(2,128)S(1)}, f32[2,512]{1,0:T(2,128)S(1)}, u32[]{:S(2)}, u32[]{:S(2)}) collective-permute-start(f32[2,512]{1,0:T(2,128)S(1)} %get-tuple-element.39), channel_id=1, source_target_pairs={{0,1},{1,0},{2,3},{3,2},{4,5},{5,4},{6,7},{7,6},{8,9},{9,8},{10,11... | collective-permute-start | bytes 12296 | tf_op jit(solution)/shard_map/ppermute | solution.py:399
  3.2 7.8 %collective-permute-start.1 = (f32[8,512]{1,0:T(8,128)S(1)}, f32[8,512]{1,0:T(8,128)S(1)}, u32[]{:S(2)}, u32[]{:S(2)}) collective-permute-start(f32[8,512]{1,0:T(8,128)S(1)} %get-tuple-element.37.to_far), channel_id=1, source_target_pairs={{0,8},{2,10},{4,12},{6,14},{8,0},{10,2},{12,4},{14,6},{1,9},{3,11}... | collective-permute-start | bytes 49160 | tf_op jit(solution)/shard_map/ppermute | solution.py:381
  7.3 3.7 %collective-permute-start.3 = (f32[4,512]{1,0:T(4,128)S(1)}, f32[4,512]{1,0:T(4,128)S(1)}, u32[]{:S(2)}, u32[]{:S(2)}) collective-permute-start(f32[4,512]{1,0:T(4,128)S(1)} %pad_maximum_fusion), channel_id=1, source_target_pairs={{0,2},{1,15},{2,0},{3,5},{4,6},{5,3},{6,4},{7,9},{8,10},{9,7},{10,... | collective-permute-start | bytes 24584 | tf_op jit(solution)/shard_map/ppermute | solution.py:396
  11.3 2.5 %collective-permute-start.4 = (f32[8,128]{1,0:T(8,128)S(1)}, f32[8,128]{1,0:T(8,128)S(1)}, u32[]{:S(2)}, u32[]{:S(2)}) collective-permute-start(f32[8,128]{1,0:T(8,128)S(1)} %get-tuple-element.40), channel_id=1, source_target_pairs={{0,1},{1,0},{2,3},{3,2},{4,5},{5,4},{6,7},{7,6},{8,9},{9,8},{10,11... | collective-permute-start | bytes 12296 | tf_op jit(solution)/shard_map/ppermute | solution.py:399
  12.7 1.2 %collective-permute-start.5 = (s32[4,8]{1,0:T(4,128)S(1)}, s32[4,8]{1,0:T(4,128)S(1)}, u32[]{:S(2)}, u32[]{:S(2)}) collective-permute-start(s32[4,8]{1,0:T(4,128)S(1)} %get-tuple-element.35.own_cols), channel_id=1, source_target_pairs={{0,1},{1,0},{2,3},{3,2},{4,5},{5,4},{6,7},{7,6},{8,9},{9,8},{10,11... | collective-permute-start | bytes 392 | tf_op jit(solution)/shard_map/ppermute | solution.py:399
  13.8 3.7 %collective-permute-start.6 = (f32[8,128]{1,0:T(8,128)S(1)}, f32[8,128]{1,0:T(8,128)S(1)}, u32[]{:S(2)}, u32[]{:S(2)}) collective-permute-start(f32[8,128]{1,0:T(8,128)S(1)} %get-tuple-element.67.direction_ref), channel_id=1, source_target_pairs={{0,2},{1,17},{2,0},{3,5},{4,6},{5,3},{6,4},{7,9},{8,10},{9,7},{10,... | collective-permute-start | bytes 12296 | tf_op jit(solution)/shard_map/ppermute | solution.py:396
  17.5 1.2 %collective-permute-start.7 = (f32[8,128]{1,0:T(8,128)S(1)}, f32[8,128]{1,0:T(8,128)S(1)}, u32[]{:S(2)}, u32[]{:S(2)}) collective-permute-start(f32[8,128]{1,0:T(8,128)S(1)} %collective-permute-done.6.mine_ref), channel_id=1, source_target_pairs={{0,1},{1,0},{2,3},{3,2},{4,5},{5,4},{6,7},{7,6},{8,9},{9,8},{10,11... | collective-permute-start | bytes 12296 | tf_op jit(solution)/shard_map/ppermute | solution.py:399
  19.2 3.7 %collective-permute-start.8 = (f32[8,128]{1,0:T(8,128)S(1)}, f32[8,128]{1,0:T(8,128)S(1)}, u32[]{:S(2)}, u32[]{:S(2)}) collective-permute-start(f32[8,128]{1,0:T(8,128)S(1)} %get-tuple-element.47.direction_in), channel_id=1, source_target_pairs={{0,2},{1,17},{2,0},{3,5},{4,6},{5,3},{6,4},{7,9},{8,10},{9,7},{10,... | collective-permute-start | bytes 12296 | tf_op jit(solution)/shard_map/ppermute | solution.py:396
  22.9 1.2 %collective-permute-start.9 = (f32[8,128]{1,0:T(8,128)S(1)}, f32[8,128]{1,0:T(8,128)S(1)}, u32[]{:S(2)}, u32[]{:S(2)}) collective-permute-start(f32[8,128]{1,0:T(8,128)S(1)} %collective-permute-done.8.mine_ref), channel_id=1, source_target_pairs={{0,1},{1,0},{2,3},{3,2},{4,5},{5,4},{6,7},{7,6},{8,9},{9,8},{10,11... | collective-permute-start | bytes 12296 | tf_op jit(solution)/shard_map/ppermute | solution.py:399
  24.5 3.7 %collective-permute-start.11 = (f32[8,128]{1,0:T(8,128)S(1)}, f32[8,128]{1,0:T(8,128)S(1)}, u32[]{:S(2)}, u32[]{:S(2)}) collective-permute-start(f32[8,128]{1,0:T(8,128)S(1)} %shard_map.100.own_estimate), channel_id=1, source_target_pairs={{0,2},{1,15},{2,0},{3,5},{4,6},{5,3},{6,4},{7,9},{8,10},{9,7},{10,... | collective-permute-start | bytes 12296 | tf_op jit(solution)/shard_map/ppermute | solution.py:396
  25.1 6.0 %collective-permute-start.10 = (f32[8,128]{1,0:T(8,128)S(1)}, f32[8,128]{1,0:T(8,128)S(1)}, u32[]{:S(2)}, u32[]{:S(2)}) collective-permute-start(f32[8,128]{1,0:T(8,128)S(1)} %shard_map.100.own_estimate), channel_id=1, source_target_pairs={{0,8},{2,10},{4,12},{6,14},{8,0},{10,2},{12,4},{14,6},{1,9},{3,11}... | collective-permute-start | bytes 12296 | tf_op jit(solution)/shard_map/ppermute | solution.py:381
  28.2 2.9 %collective-permute-start.12 = (f32[8,128]{1,0:T(8,128)S(1)}, f32[8,128]{1,0:T(8,128)S(1)}, u32[]{:S(2)}, u32[]{:S(2)}) collective-permute-start(f32[8,128]{1,0:T(8,128)S(1)} %collective-permute-done.11.mine_ref), channel_id=1, source_target_pairs={{0,1},{1,0},{2,3},{3,2},{4,5},{5,4},{6,7},{7,6},{8,9},{9,8},{10,11... | collective-permute-start | bytes 12296 | tf_op jit(solution)/shard_map/ppermute | solution.py:399
  32.1 1.5 %collective-permute-start.15 = (f32[8,128]{1,0:T(8,128)S(1)}, f32[8,128]{1,0:T(8,128)S(1)}, u32[]{:S(2)}, u32[]{:S(2)}) collective-permute-start(f32[8,128]{1,0:T(8,128)S(1)} %get-tuple-element.55), channel_id=1, source_target_pairs={{0,1},{1,0},{2,3},{3,2},{4,5},{5,4},{6,7},{7,6},{8,9},{9,8},{10,11... | collective-permute-start | bytes 12296 | tf_op jit(solution)/shard_map/ppermute | solution.py:399
  32.7 4.5 %collective-permute-start.14 = (f32[8,128]{1,0:T(8,128)S(1)}, f32[8,128]{1,0:T(8,128)S(1)}, u32[]{:S(2)}, u32[]{:S(2)}) collective-permute-start(f32[8,128]{1,0:T(8,128)S(1)} %get-tuple-element.53), channel_id=1, source_target_pairs={{0,8},{2,10},{4,12},{6,14},{8,0},{10,2},{12,4},{14,6},{1,9},{3,11}... | collective-permute-start | bytes 12296 | tf_op jit(solution)/shard_map/ppermute | solution.py:381
  33.5 3.7 %collective-permute-start.16 = (f32[8,128]{1,0:T(8,128)S(1)}, f32[8,128]{1,0:T(8,128)S(1)}, u32[]{:S(2)}, u32[]{:S(2)}) collective-permute-start(f32[8,128]{1,0:T(8,128)S(1)} %add.19), channel_id=1, source_target_pairs={{0,2},{1,15},{2,0},{3,5},{4,6},{5,3},{6,4},{7,9},{8,10},{9,7},{10,... | collective-permute-start | bytes 12296 | tf_op jit(solution)/shard_map/ppermute | solution.py:396
  37.2 2.6 %collective-permute-start.17 = (f32[8,128]{1,0:T(8,128)S(1)}, f32[8,128]{1,0:T(8,128)S(1)}, u32[]{:S(2)}, u32[]{:S(2)}) collective-permute-start(f32[8,128]{1,0:T(8,128)S(1)} %add_multiply_fusion), channel_id=1, source_target_pairs={{0,1},{1,0},{2,3},{3,2},{4,5},{5,4},{6,7},{7,6},{8,9},{9,8},{10,11... | collective-permute-start | bytes 12296 | tf_op jit(solution)/shard_map/ppermute | solution.py:399
  39.9 3.6 %collective-permute-start.18 = (f32[8,128]{1,0:T(8,128)S(1)}, f32[8,128]{1,0:T(8,128)S(1)}, u32[]{:S(2)}, u32[]{:S(2)}) collective-permute-start(f32[8,128]{1,0:T(8,128)S(1)} %get-tuple-element.65.direction_in), channel_id=1, source_target_pairs={{0,2},{1,17},{2,0},{3,5},{4,6},{5,3},{6,4},{7,9},{8,10},{9,7},{10,... | collective-permute-start | bytes 12296 | tf_op jit(solution)/shard_map/ppermute | solution.py:396
  43.5 1.2 %collective-permute-start.19 = (f32[8,128]{1,0:T(8,128)S(1)}, f32[8,128]{1,0:T(8,128)S(1)}, u32[]{:S(2)}, u32[]{:S(2)}) collective-permute-start(f32[8,128]{1,0:T(8,128)S(1)} %collective-permute-done.18.mine_ref), channel_id=1, source_target_pairs={{0,1},{1,0},{2,3},{3,2},{4,5},{5,4},{6,7},{7,6},{8,9},{9,8},{10,11... | collective-permute-start | bytes 12296 | tf_op jit(solution)/shard_map/ppermute | solution.py:399
  45.2 3.7 %collective-permute-start.20 = (f32[8,128]{1,0:T(8,128)S(1)}, f32[8,128]{1,0:T(8,128)S(1)}, u32[]{:S(2)}, u32[]{:S(2)}) collective-permute-start(f32[8,128]{1,0:T(8,128)S(1)} %get-tuple-element.56.direction_in), channel_id=1, source_target_pairs={{0,2},{1,17},{2,0},{3,5},{4,6},{5,3},{6,4},{7,9},{8,10},{9,7},{10,... | collective-permute-start | bytes 12296 | tf_op jit(solution)/shard_map/ppermute | solution.py:396
  48.8 1.2 %collective-permute-start.21 = (f32[8,128]{1,0:T(8,128)S(1)}, f32[8,128]{1,0:T(8,128)S(1)}, u32[]{:S(2)}, u32[]{:S(2)}) collective-permute-start(f32[8,128]{1,0:T(8,128)S(1)} %collective-permute-done.20.mine_ref), channel_id=1, source_target_pairs={{0,1},{1,0},{2,3},{3,2},{4,5},{5,4},{6,7},{7,6},{8,9},{9,8},{10,11... | collective-permute-start | bytes 12296 | tf_op jit(solution)/shard_map/ppermute | solution.py:399
  50.5 3.7 %collective-permute-start.23 = (f32[16,128]{1,0:T(8,128)S(1)}, f32[16,128]{1,0:T(8,128)S(1)}, u32[]{:S(2)}, u32[]{:S(2)}) collective-permute-start(f32[16,128]{1,0:T(8,128)S(1)} %get-tuple-element.59.packed_ref), channel_id=1, source_target_pairs={{0,2},{1,15},{2,0},{3,5},{4,6},{5,3},{6,4},{7,9},{8,10},{9,7},{10,... | collective-permute-start | bytes 24584 | tf_op jit(solution)/shard_map/ppermute | solution.py:396
  50.6 5.4 %collective-permute-start.22 = (f32[16,128]{1,0:T(8,128)S(1)}, f32[16,128]{1,0:T(8,128)S(1)}, u32[]{:S(2)}, u32[]{:S(2)}) collective-permute-start(f32[16,128]{1,0:T(8,128)S(1)} %get-tuple-element.59.packed_ref), channel_id=1, source_target_pairs={{0,8},{2,10},{4,12},{6,14},{8,0},{10,2},{12,4},{14,6},{1,9},{3,11}... | collective-permute-start | bytes 24584 | tf_op jit(solution)/shard_map/ppermute | solution.py:381
  54.2 2.5 %collective-permute-start.24 = (f32[16,128]{1,0:T(8,128)S(1)}, f32[16,128]{1,0:T(8,128)S(1)}, u32[]{:S(2)}, u32[]{:S(2)}) collective-permute-start(f32[16,128]{1,0:T(8,128)S(1)} %collective-permute-done.23.mine_ref), channel_id=1, source_target_pairs={{0,1},{1,0},{2,3},{3,2},{4,5},{5,4},{6,7},{7,6},{8,9},{9,8},{10,11... | collective-permute-start | bytes 24584 | tf_op jit(solution)/shard_map/ppermute | solution.py:399
  (6 other events, 7.9 us)

commit v16 on v15

--- a/solution.py
+++ b/solution.py
@@ -116,13 +116,17 @@
     return first, second, rest - second
 
 
-def scatter(values, index, rows):
+def low_table(index):
+    spread = lax.broadcasted_iota(jnp.int32, (LANES, index.shape[1]), 0) == (index & (LANES - 1))
+    return jnp.where(spread, 1.0, 0.0).astype(jnp.bfloat16)
+
+
+def scatter(values, index, rows, table=None):
     slots = values.shape[1]
-    high, low = index >> 7, index & (LANES - 1)
+    high = index >> 7
     mine = lax.broadcasted_iota(jnp.int32, (rows, slots), 0) == high
     left = jnp.concatenate([jnp.where(mine, part, 0.0) for part in three_parts(values)], axis=0)
-    spread = lax.broadcasted_iota(jnp.int32, (LANES, slots), 0) == low
-    right = jnp.where(spread, 1.0, 0.0).astype(jnp.bfloat16)
+    right = low_table(index) if table is None else table
     sums = lax.dot_general(
         left.astype(jnp.bfloat16), right, (((1,), (1,)), ((), ())), preferred_element_type=F32
     )
@@ -154,10 +158,10 @@
     return jnp.where(even, first, second), jnp.where(even, second, first)
 
 
-def spread_current(outgoing, maps, own_ref, keep_ref, give_ref, far_ref):
+def spread_current(outgoing, maps, maps_low, own_ref, keep_ref, give_ref, far_ref):
     torso = own_ref.shape[0]
     own, after, before, far = (
-        scatter(outgoing[o : o + 1], maps[o : o + 1], torso) for o in range(maps.shape[0])
+        scatter(outgoing[o : o + 1], maps[o : o + 1], torso, maps_low[o]) for o in range(maps.shape[0])
     )
     ahead = meets_next()
     own_ref[...] = own
@@ -166,7 +170,7 @@
     far_ref[...] = far
 
 
-def feedback_of(estimates, nodes, maps, heart):
+def feedback_of(estimates, nodes, nodes_low, maps, heart):
     peers = nodes.shape[0]
     torso = estimates[0].shape[0]
 
@@ -177,7 +181,7 @@
     returned = gather(source, torso, maps)
     total = jnp.zeros((heart, LANES), F32)
     for o in range(peers):
-        total = total + scatter(returned[o : o + 1], nodes[o : o + 1], heart)
+        total = total + scatter(returned[o : o + 1], nodes[o : o + 1], heart, nodes_low[o])
     return total
 
 
@@ -283,21 +287,26 @@
     maps_ref[...] = jnp.where(nodes_ref[...] < 0, -1, rows.astype(jnp.int32))
 
 
+def spell(index_ref, low_ref):
+    for o in range(index_ref.shape[0]):
+        low_ref[o] = low_table(index_ref[o : o + 1])
+
+
 def next_shares(
     states_ref, own_estimate, far_estimate, mine_ref, yours_ref, nodes_ref, maps_ref,
-    out_ref, own_ref, keep_ref, give_ref, far_ref,
+    nodes_low, maps_low, out_ref, own_ref, keep_ref, give_ref, far_ref,
 ):
     nodes, maps = nodes_ref[...], maps_ref[...]
     after, before = by_side(*by_partner(mine_ref[...], yours_ref[...]))
     estimates = [own_estimate[...], after, before, far_estimate[...]]
-    feedback = feedback_of(estimates, nodes, maps, states_ref.shape[1])
+    feedback = feedback_of(estimates, nodes, nodes_low, maps, states_ref.shape[1])
     rows = [states_ref[i] for i in range(states_ref.shape[0])]
     rows[0] = rows[0] + TIME_STEP * FEEDBACK_RATE * feedback
     rows, current = ionic_rows(rows)
     for i, row in enumerate(rows):
         out_ref[i] = row
     outgoing = pick_current(current, nodes)
-    spread_current(outgoing, maps, own_ref, keep_ref, give_ref, far_ref)
+    spread_current(outgoing, maps, maps_low, own_ref, keep_ref, give_ref, far_ref)
 
 
 def window_of(chain, direction, first, second):
@@ -349,7 +358,7 @@
 
 def finish(
     chain, own_ref, other_ref, pick_ref, packed_ref, far_ref, mine_ref, yours_ref, residual_in,
-    diag_ref, states_ref, nodes_ref, maps_ref, out_ref, potential_ref, residual_ref, dense_ref,
+    diag_ref, states_ref, nodes_ref, nodes_low, maps_ref, out_ref, potential_ref, residual_ref, dense_ref,
 ):
     torso = residual_ref.shape[0]
     head, tail = slice(0, torso), slice(torso, 2 * torso)
@@ -358,7 +367,7 @@
     first, second = by_partner(mine_ref[...], yours_ref[...])
     after, before = by_side(first[head], second[head])
     feedback = feedback_of(
-        [estimate, after, before, far_ref[head]], nodes_ref[...], maps_ref[...],
+        [estimate, after, before, far_ref[head]], nodes_ref[...], nodes_low, maps_ref[...],
         states_ref.shape[1],
     )
     dense_ref[...] = states_ref[...]
@@ -423,6 +432,9 @@
     )
     maps = call(complete, index)(in_specs=[VMEM] * 5)(own, near, far, from_sibling(give), nodes)
     other_columns = from_sibling(columns)
+    low = shape(peers, LANES, slots, dtype=jnp.bfloat16)
+    nodes_low = call(spell, low)(in_specs=[VMEM])(nodes)
+    maps_low = call(spell, low)(in_specs=[VMEM])(maps)
     for time_step in range(2):
         last = time_step == 1
         others = from_sibling(forcing)
@@ -443,18 +455,21 @@
             functools.partial(sweep_one, chain), (field,) * 3
         )(in_specs=[VMEM] * 8)(*stored, halo, from_sibling(halo), forcing, direction, diag)
         halo = with_either(direction, False)
+        yours = from_sibling(halo)
+        if not last:
+            yours, maps = lax.optimization_barrier((yours, maps))
         swept = call(
             functools.partial(sweep_two, chain, last), (packed, field) if last else field
         )(in_specs=[VMEM] * 9)(
-            *stored, halo, from_sibling(halo), direction, residual, estimate, diag
+            *stored, halo, yours, direction, residual, estimate, diag
         )
         estimate, residual = swept if last else (swept, None)
         far = with_far(estimate)
         near = with_either(estimate, True)
         if not last:
             states, own, keep, give, away = call(next_shares, (dense,) + (field,) * 4)(
-                in_specs=[VMEM] * 7
-            )(states, estimate, far, near, from_sibling(near), nodes, maps)
+                in_specs=[VMEM] * 9
+            )(states, estimate, far, near, from_sibling(near), nodes, maps, nodes_low, maps_low)
             far = with_far(away)
             near = with_either(keep + from_sibling(give), True)
             forcing = TORSO_COUPLING * (own + far + near)
@@ -462,8 +477,8 @@
         functools.partial(finish, chain),
         (shape(*dense.shape[:1], node_count), field, field),
         (pltpu.VMEM(dense.shape, F32),),
-    )(in_specs=[VMEM] * 12)(
-        *stored, estimate, far, near, from_sibling(near), residual, diag, states, nodes, maps
+    )(in_specs=[VMEM] * 13)(
+        *stored, estimate, far, near, from_sibling(near), residual, diag, states, nodes, nodes_low, maps
     )
     return new_states, potential.reshape(-1), residual.reshape(-1)
 

time: 58.6 us -> 59 us (level)
  starting transfers between devices: 18.4 us -> 19.1 us
    ppermute x13, starting transfers between devices: 8.01 us -> 9.14 us  [from_sibling(): return lax.ppermute(value, 'sub', [(0, 1), (1, 0)])]
    ppermute x13, waiting for transfers between devices: 8.62 us -> 7.94 us  [from_sibling(): return lax.ppermute(value, 'sub', [(0, 1), (1, 0)])]
where the time goes in v16:
time: 59 us; the launch traced here: 58.7 us
  waiting for transfers between devices  28.9 us (49%)
  starting transfers between devices  19.1 us (32%)
  Pallas kernels  5.25 us (9%)
  local copies, waits for them, and re-layouts  3.88 us (7%)
  other arithmetic  0.77 us (1%)
  between operations  0.75 us (1%)
    ppermute x8, waiting for transfers between devices, with_either(): return lax.ppermute(value, ('case', 'dom', 'sub'), pairs)  17.4 us
    ppermute x13, starting transfers between devices, from_sibling(): return lax.ppermute(value, 'sub', [(0, 1), (1, 0)])  9.14 us
    ppermute x13, waiting for transfers between devices, from_sibling(): return lax.ppermute(value, 'sub', [(0, 1), (1, 0)])  7.94 us
    ppermute x4, starting transfers between devices, with_far(): lax.ppermute(value, 'dom', [(i, (i + chain // 2) % chain) for i in range(...  6.71 us
    unnamed x10, local copies, waits for them, and re-layouts  3.88 us
    ppermute x4, waiting for transfers between devices, with_far(): lax.ppermute(value, 'dom', [(i, (i + chain // 2) % chain) for i in range(...  3.52 us
    ppermute x8, starting transfers between devices, with_either(): return lax.ppermute(value, ('case', 'dom', 'sub'), pairs)  3.25 us
    pallas_call x1, Pallas kernels, on_device(): call(functools.partial(finish, chain), (shape(*dense.shape[:1], node_coun...  1.44 us
  transfers between devices with their start and end apart: 25, of which 17 were waited for; matrix products, arithmetic and copies ran while one was open for 1% of the time, Pallas kernels for 1%

profile of v16, /device:TPU:0, one launch (start us, length us, event | category | flops | bytes accessed | tf_op | source)
XLA Modules:
  0.0 58.7 jit_solution(4682514974748665234)
XLA Ops:
  1.9 0.9 %copy-done.2 = f32[19,2048]{1,0:T(8,128)S(1)} copy-done((f32[19,2048]{1,0:T(8,128)S(1)}, f32[19,2048]{1,0:T(8,128)}, u32[]{:S(2)}) %copy-start.2) | copy-done | bytes 155672
  3.2 4.0 %collective-permute-start.1 = (f32[8,512]{1,0:T(8,128)S(1)}, f32[8,512]{1,0:T(8,128)S(1)}, u32[]{:S(2)}, u32[]{:S(2)}) collective-permute-start(f32[8,512]{1,0:T(8,128)S(1)} %get-tuple-element.39.to_far), channel_id=1, source_target_pairs={{0,8},{2,10},{4,12},{6,14},{8,0},{10,2},{12,4},{14,6},{1,9},{3,11}... | collective-permute-start | bytes 49160 | tf_op jit(solution)/shard_map/ppermute | solution.py:390
  7.3 1.6 %collective-permute-start.3 = (f32[4,512]{1,0:T(4,128)S(1)}, f32[4,512]{1,0:T(4,128)S(1)}, u32[]{:S(2)}, u32[]{:S(2)}) collective-permute-start(f32[4,512]{1,0:T(4,128)S(1)} %pad_maximum_fusion), channel_id=1, source_target_pairs={{0,2},{1,15},{2,0},{3,5},{4,6},{5,3},{6,4},{7,9},{8,10},{9,7},{10,... | collective-permute-start | bytes 24584 | tf_op jit(solution)/shard_map/ppermute | solution.py:405
  11.3 1.4 %collective-permute-start.4 = (f32[8,128]{1,0:T(8,128)S(1)}, f32[8,128]{1,0:T(8,128)S(1)}, u32[]{:S(2)}, u32[]{:S(2)}) collective-permute-start(f32[8,128]{1,0:T(8,128)S(1)} %get-tuple-element.42), channel_id=1, source_target_pairs={{0,1},{1,0},{2,3},{3,2},{4,5},{5,4},{6,7},{7,6},{8,9},{9,8},{10,11... | collective-permute-start | bytes 12296 | tf_op jit(solution)/shard_map/ppermute | solution.py:408
  12.7 1.1 %collective-permute-done.5.other_cols = s32[4,8]{1,0:T(4,128)S(1)} collective-permute-done((s32[4,8]{1,0:T(4,128)S(1)}, s32[4,8]{1,0:T(4,128)S(1)}, u32[]{:S(2)}, u32[]{:S(2)}) %collective-permute-start.5) | collective-permute-done | bytes 160 | tf_op jit(solution)/shard_map/ppermute | solution.py:408
  14.2 1.6 %copy-done = f32[8,4,128,128]{3,2,1,0:T(8,128)S(1)} copy-done((f32[8,4,128,128]{3,2,1,0:T(8,128)S(1)}, f32[8,4,128,128]{3,2,1,0:T(8,128)}, u32[]{:S(2)}) %copy-start) | copy-done | bytes 2097176
  15.8 1.7 %collective-permute-done.6.mine_ref = f32[8,128]{1,0:T(8,128)S(1)} collective-permute-done((f32[8,128]{1,0:T(8,128)S(1)}, f32[8,128]{1,0:T(8,128)S(1)}, u32[]{:S(2)}, u32[]{:S(2)}) %collective-permute-start.6) | collective-permute-done | bytes 4128 | tf_op jit(solution)/shard_map/ppermute | solution.py:405
  17.6 1.1 %collective-permute-done.7.yours_ref = f32[8,128]{1,0:T(8,128)S(1)} collective-permute-done((f32[8,128]{1,0:T(8,128)S(1)}, f32[8,128]{1,0:T(8,128)S(1)}, u32[]{:S(2)}, u32[]{:S(2)}) %collective-permute-start.7) | collective-permute-done | bytes 4128 | tf_op jit(solution)/shard_map/ppermute | solution.py:408
  19.7 3.2 %collective-permute-done.8.mine_ref = f32[8,128]{1,0:T(8,128)S(1)} collective-permute-done((f32[8,128]{1,0:T(8,128)S(1)}, f32[8,128]{1,0:T(8,128)S(1)}, u32[]{:S(2)}, u32[]{:S(2)}) %collective-permute-start.8) | collective-permute-done | bytes 4128 | tf_op jit(solution)/shard_map/ppermute | solution.py:405
  25.3 1.5 %collective-permute-start.11 = (f32[8,128]{1,0:T(8,128)S(1)}, f32[8,128]{1,0:T(8,128)S(1)}, u32[]{:S(2)}, u32[]{:S(2)}) collective-permute-start(f32[8,128]{1,0:T(8,128)S(1)} %shard_map.101.own_estimate), channel_id=1, source_target_pairs={{0,8},{2,10},{4,12},{6,14},{8,0},{10,2},{12,4},{14,6},{1,9},{3,11}... | collective-permute-start | bytes 12296 | tf_op jit(solution)/shard_map/ppermute | solution.py:390
  26.8 1.7 %collective-permute-done.12.mine_ref = f32[8,128]{1,0:T(8,128)S(1)} collective-permute-done((f32[8,128]{1,0:T(8,128)S(1)}, f32[8,128]{1,0:T(8,128)S(1)}, u32[]{:S(2)}, u32[]{:S(2)}) %collective-permute-start.12) | collective-permute-done | bytes 4128 | tf_op jit(solution)/shard_map/ppermute | solution.py:405
  28.4 1.9 %collective-permute-start.13 = (f32[8,128]{1,0:T(8,128)S(1)}, f32[8,128]{1,0:T(8,128)S(1)}, u32[]{:S(2)}, u32[]{:S(2)}) collective-permute-start(f32[8,128]{1,0:T(8,128)S(1)} %collective-permute-done.12.mine_ref), channel_id=1, source_target_pairs={{0,1},{1,0},{2,3},{3,2},{4,5},{5,4},{6,7},{7,6},{8,9},{9,8},{10,11... | collective-permute-start | bytes 12296 | tf_op jit(solution)/shard_map/ppermute | solution.py:408
  31.1 0.9 %shard_map.104 = (f32[19,16,128]{2,1,0:T(8,128)S(1)}, f32[8,128]{1,0:T(8,128)S(1)}, f32[8,128]{1,0:T(8,128)S(1)}, f32[8,128]{1,0:T(8,128)S(1)}, f32[8,128]{1,0:T(8,128)S(1)}) custom-call(f32[19,16,128]{2,1,0:T(8,128)S(1)} %get-tuple-element.44.states_ref, f32[8,128]{1,0:T(8,128)S(1)} %shard_map.101.own_estimate, ...), custom_call_target="tpu_custom_call" | custom-call | flops 4000000 | bytes 262144 | tf_op jit(solution)/shard_map/pallas_call | solution.py:470
  32.1 1.0 %collective-permute-start.15 = (f32[8,128]{1,0:T(8,128)S(1)}, f32[8,128]{1,0:T(8,128)S(1)}, u32[]{:S(2)}, u32[]{:S(2)}) collective-permute-start(f32[8,128]{1,0:T(8,128)S(1)} %get-tuple-element.59), channel_id=1, source_target_pairs={{0,1},{1,0},{2,3},{3,2},{4,5},{5,4},{6,7},{7,6},{8,9},{9,8},{10,11... | collective-permute-start | bytes 12296 | tf_op jit(solution)/shard_map/ppermute | solution.py:408
  34.1 3.5 %collective-permute-done.14 = f32[8,128]{1,0:T(8,128)S(1)} collective-permute-done((f32[8,128]{1,0:T(8,128)S(1)}, f32[8,128]{1,0:T(8,128)S(1)}, u32[]{:S(2)}, u32[]{:S(2)}) %collective-permute-start.14) | collective-permute-done | bytes 4128 | tf_op jit(solution)/shard_map/ppermute | solution.py:390
  37.6 1.8 %collective-permute-start.17 = (f32[8,128]{1,0:T(8,128)S(1)}, f32[8,128]{1,0:T(8,128)S(1)}, u32[]{:S(2)}, u32[]{:S(2)}) collective-permute-start(f32[8,128]{1,0:T(8,128)S(1)} %add_multiply_fusion), channel_id=1, source_target_pairs={{0,1},{1,0},{2,3},{3,2},{4,5},{5,4},{6,7},{7,6},{8,9},{9,8},{10,11... | collective-permute-start | bytes 12296 | tf_op jit(solution)/shard_map/ppermute | solution.py:408
  40.3 3.6 %collective-permute-done.18.mine_ref = f32[8,128]{1,0:T(8,128)S(1)} collective-permute-done((f32[8,128]{1,0:T(8,128)S(1)}, f32[8,128]{1,0:T(8,128)S(1)}, u32[]{:S(2)}, u32[]{:S(2)}) %collective-permute-start.18) | collective-permute-done | bytes 4128 | tf_op jit(solution)/shard_map/ppermute | solution.py:405
  43.9 1.2 %collective-permute-done.19.yours_ref = f32[8,128]{1,0:T(8,128)S(1)} collective-permute-done((f32[8,128]{1,0:T(8,128)S(1)}, f32[8,128]{1,0:T(8,128)S(1)}, u32[]{:S(2)}, u32[]{:S(2)}) %collective-permute-start.19) | collective-permute-done | bytes 4128 | tf_op jit(solution)/shard_map/ppermute | solution.py:408
  45.6 3.6 %collective-permute-done.20.mine_ref = f32[8,128]{1,0:T(8,128)S(1)} collective-permute-done((f32[8,128]{1,0:T(8,128)S(1)}, f32[8,128]{1,0:T(8,128)S(1)}, u32[]{:S(2)}, u32[]{:S(2)}) %collective-permute-start.20) | collective-permute-done | bytes 4128 | tf_op jit(solution)/shard_map/ppermute | solution.py:405
  49.2 1.2 %collective-permute-done.21.yours_ref = f32[8,128]{1,0:T(8,128)S(1)} collective-permute-done((f32[8,128]{1,0:T(8,128)S(1)}, f32[8,128]{1,0:T(8,128)S(1)}, u32[]{:S(2)}, u32[]{:S(2)}) %collective-permute-start.21) | collective-permute-done | bytes 4128 | tf_op jit(solution)/shard_map/ppermute | solution.py:408
  51.7 2.9 %collective-permute-done.23.mine_ref = f32[16,128]{1,0:T(8,128)S(1)} collective-permute-done((f32[16,128]{1,0:T(8,128)S(1)}, f32[16,128]{1,0:T(8,128)S(1)}, u32[]{:S(2)}, u32[]{:S(2)}) %collective-permute-start.23) | collective-permute-done | bytes 8224 | tf_op jit(solution)/shard_map/ppermute | solution.py:405
  54.6 1.8 %collective-permute-start.24 = (f32[16,128]{1,0:T(8,128)S(1)}, f32[16,128]{1,0:T(8,128)S(1)}, u32[]{:S(2)}, u32[]{:S(2)}) collective-permute-start(f32[16,128]{1,0:T(8,128)S(1)} %collective-permute-done.23.mine_ref), channel_id=1, source_target_pairs={{0,1},{1,0},{2,3},{3,2},{4,5},{5,4},{6,7},{7,6},{8,9},{9,8},{10,11... | collective-permute-start | bytes 24584 | tf_op jit(solution)/shard_map/ppermute | solution.py:408
  56.4 0.8 %collective-permute-done.24.yours_ref = f32[16,128]{1,0:T(8,128)S(1)} collective-permute-done((f32[16,128]{1,0:T(8,128)S(1)}, f32[16,128]{1,0:T(8,128)S(1)}, u32[]{:S(2)}, u32[]{:S(2)}) %collective-permute-start.24) | collective-permute-done | bytes 8224 | tf_op jit(solution)/shard_map/ppermute | solution.py:408
  57.2 1.4 %shard_map.107 = (f32[19,2048]{1,0:T(8,128)}, f32[8,128]{1,0:T(8,128)}, f32[8,128]{1,0:T(8,128)}) custom-call(f32[8,4,128,128]{3,2,1,0:T(8,128)S(1)} %copy-done.1, f32[8,4,128,128]{3,2,1,0:T(8,128)S(1)} %collective-permute-done.other_ref, f32[64,16]{1,0:T(8,128)S(1)} %shard_map.97.pick_ref, f32[16,128]{1,0:T(8,128)S(1)} %get-tuple-element.63.packed_ref, ...), custom_call_target="tpu_custom_call" | custom-call | flops 4000000 | bytes 262144 | tf_op jit(solution)/shard_map/pallas_call | solution.py:476
  (56 shorter events, 12.6 us)
Async XLA Ops:
  0.6 18.1 %collective-permute-start = (f32[8,4,128,128]{3,2,1,0:T(8,128)}, f32[8,4,128,128]{3,2,1,0:T(8,128)S(1)}, u32[]{:S(2)}, u32[]{:S(2)}) collective-permute-start(f32[8,4,128,128]{3,2,1,0:T(8,128)} %own_ref.9), channel_id=1, source_target_pairs={{0,1},{1,0},{2,3},{3,2},{4,5},{5,4},{6,7},{7,6},{8,9},{9,8},{10,11... | collective-permute-start | bytes 6291464 | tf_op jit(solution)/shard_map/ppermute | solution.py:408
  3.1 4.2 %collective-permute-start.2 = (f32[2,512]{1,0:T(2,128)S(1)}, f32[2,512]{1,0:T(2,128)S(1)}, u32[]{:S(2)}, u32[]{:S(2)}) collective-permute-start(f32[2,512]{1,0:T(2,128)S(1)} %get-tuple-element.41), channel_id=1, source_target_pairs={{0,1},{1,0},{2,3},{3,2},{4,5},{5,4},{6,7},{7,6},{8,9},{9,8},{10,11... | collective-permute-start | bytes 12296 | tf_op jit(solution)/shard_map/ppermute | solution.py:408
  3.2 7.8 %collective-permute-start.1 = (f32[8,512]{1,0:T(8,128)S(1)}, f32[8,512]{1,0:T(8,128)S(1)}, u32[]{:S(2)}, u32[]{:S(2)}) collective-permute-start(f32[8,512]{1,0:T(8,128)S(1)} %get-tuple-element.39.to_far), channel_id=1, source_target_pairs={{0,8},{2,10},{4,12},{6,14},{8,0},{10,2},{12,4},{14,6},{1,9},{3,11}... | collective-permute-start | bytes 49160 | tf_op jit(solution)/shard_map/ppermute | solution.py:390
  7.3 3.7 %collective-permute-start.3 = (f32[4,512]{1,0:T(4,128)S(1)}, f32[4,512]{1,0:T(4,128)S(1)}, u32[]{:S(2)}, u32[]{:S(2)}) collective-permute-start(f32[4,512]{1,0:T(4,128)S(1)} %pad_maximum_fusion), channel_id=1, source_target_pairs={{0,2},{1,15},{2,0},{3,5},{4,6},{5,3},{6,4},{7,9},{8,10},{9,7},{10,... | collective-permute-start | bytes 24584 | tf_op jit(solution)/shard_map/ppermute | solution.py:405
  11.3 2.5 %collective-permute-start.4 = (f32[8,128]{1,0:T(8,128)S(1)}, f32[8,128]{1,0:T(8,128)S(1)}, u32[]{:S(2)}, u32[]{:S(2)}) collective-permute-start(f32[8,128]{1,0:T(8,128)S(1)} %get-tuple-element.42), channel_id=1, source_target_pairs={{0,1},{1,0},{2,3},{3,2},{4,5},{5,4},{6,7},{7,6},{8,9},{9,8},{10,11... | collective-permute-start | bytes 12296 | tf_op jit(solution)/shard_map/ppermute | solution.py:408
  13.8 3.7 %collective-permute-start.6 = (f32[8,128]{1,0:T(8,128)S(1)}, f32[8,128]{1,0:T(8,128)S(1)}, u32[]{:S(2)}, u32[]{:S(2)}) collective-permute-start(f32[8,128]{1,0:T(8,128)S(1)} %get-tuple-element.71.direction_ref), channel_id=1, source_target_pairs={{0,2},{1,17},{2,0},{3,5},{4,6},{5,3},{6,4},{7,9},{8,10},{9,7},{10,... | collective-permute-start | bytes 12296 | tf_op jit(solution)/shard_map/ppermute | solution.py:405
  17.5 1.2 %collective-permute-start.7 = (f32[8,128]{1,0:T(8,128)S(1)}, f32[8,128]{1,0:T(8,128)S(1)}, u32[]{:S(2)}, u32[]{:S(2)}) collective-permute-start(f32[8,128]{1,0:T(8,128)S(1)} %collective-permute-done.6.mine_ref), channel_id=1, source_target_pairs={{0,1},{1,0},{2,3},{3,2},{4,5},{5,4},{6,7},{7,6},{8,9},{9,8},{10,11... | collective-permute-start | bytes 12296 | tf_op jit(solution)/shard_map/ppermute | solution.py:408
  19.2 3.7 %collective-permute-start.8 = (f32[8,128]{1,0:T(8,128)S(1)}, f32[8,128]{1,0:T(8,128)S(1)}, u32[]{:S(2)}, u32[]{:S(2)}) collective-permute-start(f32[8,128]{1,0:T(8,128)S(1)} %get-tuple-element.49.direction_in), channel_id=1, source_target_pairs={{0,2},{1,17},{2,0},{3,5},{4,6},{5,3},{6,4},{7,9},{8,10},{9,7},{10,... | collective-permute-start | bytes 12296 | tf_op jit(solution)/shard_map/ppermute | solution.py:405
  22.9 1.4 %collective-permute-start.9 = (f32[8,128]{1,0:T(8,128)S(1)}, f32[8,128]{1,0:T(8,128)S(1)}, u32[]{:S(2)}, u32[]{:S(2)}) collective-permute-start(f32[8,128]{1,0:T(8,128)S(1)} %collective-permute-done.8.mine_ref), channel_id=1, source_target_pairs={{0,1},{1,0},{2,3},{3,2},{4,5},{5,4},{6,7},{7,6},{8,9},{9,8},{10,11... | collective-permute-start | bytes 12296 | tf_op jit(solution)/shard_map/ppermute | solution.py:408
  22.9 1.3 %collective-permute-start.10 = (f32[1,512]{1,0:T(1,128)S(1)}, f32[1,512]{1,0:T(1,128)S(1)}, u32[]{:S(2)}, u32[]{:S(2)}) collective-permute-start(f32[1,512]{1,0:T(1,128)S(1)} %get-tuple-element.50), channel_id=1, source_target_pairs={{0,1},{1,0},{2,3},{3,2},{4,5},{5,4},{6,7},{7,6},{8,9},{9,8},{10,11... | collective-permute-start | bytes 6152 | tf_op jit(solution)/shard_map/ppermute | solution.py:408
  24.7 3.7 %collective-permute-start.12 = (f32[8,128]{1,0:T(8,128)S(1)}, f32[8,128]{1,0:T(8,128)S(1)}, u32[]{:S(2)}, u32[]{:S(2)}) collective-permute-start(f32[8,128]{1,0:T(8,128)S(1)} %shard_map.101.own_estimate), channel_id=1, source_target_pairs={{0,2},{1,15},{2,0},{3,5},{4,6},{5,3},{6,4},{7,9},{8,10},{9,7},{10,... | collective-permute-start | bytes 12296 | tf_op jit(solution)/shard_map/ppermute | solution.py:405
  25.3 5.2 %collective-permute-start.11 = (f32[8,128]{1,0:T(8,128)S(1)}, f32[8,128]{1,0:T(8,128)S(1)}, u32[]{:S(2)}, u32[]{:S(2)}) collective-permute-start(f32[8,128]{1,0:T(8,128)S(1)} %shard_map.101.own_estimate), channel_id=1, source_target_pairs={{0,8},{2,10},{4,12},{6,14},{8,0},{10,2},{12,4},{14,6},{1,9},{3,11}... | collective-permute-start | bytes 12296 | tf_op jit(solution)/shard_map/ppermute | solution.py:390
  28.4 2.7 %collective-permute-start.13 = (f32[8,128]{1,0:T(8,128)S(1)}, f32[8,128]{1,0:T(8,128)S(1)}, u32[]{:S(2)}, u32[]{:S(2)}) collective-permute-start(f32[8,128]{1,0:T(8,128)S(1)} %collective-permute-done.12.mine_ref), channel_id=1, source_target_pairs={{0,1},{1,0},{2,3},{3,2},{4,5},{5,4},{6,7},{7,6},{8,9},{9,8},{10,11... | collective-permute-start | bytes 12296 | tf_op jit(solution)/shard_map/ppermute | solution.py:408
  32.1 1.9 %collective-permute-start.15 = (f32[8,128]{1,0:T(8,128)S(1)}, f32[8,128]{1,0:T(8,128)S(1)}, u32[]{:S(2)}, u32[]{:S(2)}) collective-permute-start(f32[8,128]{1,0:T(8,128)S(1)} %get-tuple-element.59), channel_id=1, source_target_pairs={{0,1},{1,0},{2,3},{3,2},{4,5},{5,4},{6,7},{7,6},{8,9},{9,8},{10,11... | collective-permute-start | bytes 12296 | tf_op jit(solution)/shard_map/ppermute | solution.py:408
  33.1 4.5 %collective-permute-start.14 = (f32[8,128]{1,0:T(8,128)S(1)}, f32[8,128]{1,0:T(8,128)S(1)}, u32[]{:S(2)}, u32[]{:S(2)}) collective-permute-start(f32[8,128]{1,0:T(8,128)S(1)} %get-tuple-element.57), channel_id=1, source_target_pairs={{0,8},{2,10},{4,12},{6,14},{8,0},{10,2},{12,4},{14,6},{1,9},{3,11}... | collective-permute-start | bytes 12296 | tf_op jit(solution)/shard_map/ppermute | solution.py:390
  33.9 3.7 %collective-permute-start.16 = (f32[8,128]{1,0:T(8,128)S(1)}, f32[8,128]{1,0:T(8,128)S(1)}, u32[]{:S(2)}, u32[]{:S(2)}) collective-permute-start(f32[8,128]{1,0:T(8,128)S(1)} %add.19), channel_id=1, source_target_pairs={{0,2},{1,15},{2,0},{3,5},{4,6},{5,3},{6,4},{7,9},{8,10},{9,7},{10,... | collective-permute-start | bytes 12296 | tf_op jit(solution)/shard_map/ppermute | solution.py:405
  37.6 2.6 %collective-permute-start.17 = (f32[8,128]{1,0:T(8,128)S(1)}, f32[8,128]{1,0:T(8,128)S(1)}, u32[]{:S(2)}, u32[]{:S(2)}) collective-permute-start(f32[8,128]{1,0:T(8,128)S(1)} %add_multiply_fusion), channel_id=1, source_target_pairs={{0,1},{1,0},{2,3},{3,2},{4,5},{5,4},{6,7},{7,6},{8,9},{9,8},{10,11... | collective-permute-start | bytes 12296 | tf_op jit(solution)/shard_map/ppermute | solution.py:408
  40.3 3.6 %collective-permute-start.18 = (f32[8,128]{1,0:T(8,128)S(1)}, f32[8,128]{1,0:T(8,128)S(1)}, u32[]{:S(2)}, u32[]{:S(2)}) collective-permute-start(f32[8,128]{1,0:T(8,128)S(1)} %get-tuple-element.69.direction_in), channel_id=1, source_target_pairs={{0,2},{1,17},{2,0},{3,5},{4,6},{5,3},{6,4},{7,9},{8,10},{9,7},{10,... | collective-permute-start | bytes 12296 | tf_op jit(solution)/shard_map/ppermute | solution.py:405
  43.9 1.2 %collective-permute-start.19 = (f32[8,128]{1,0:T(8,128)S(1)}, f32[8,128]{1,0:T(8,128)S(1)}, u32[]{:S(2)}, u32[]{:S(2)}) collective-permute-start(f32[8,128]{1,0:T(8,128)S(1)} %collective-permute-done.18.mine_ref), channel_id=1, source_target_pairs={{0,1},{1,0},{2,3},{3,2},{4,5},{5,4},{6,7},{7,6},{8,9},{9,8},{10,11... | collective-permute-start | bytes 12296 | tf_op jit(solution)/shard_map/ppermute | solution.py:408
  45.5 3.7 %collective-permute-start.20 = (f32[8,128]{1,0:T(8,128)S(1)}, f32[8,128]{1,0:T(8,128)S(1)}, u32[]{:S(2)}, u32[]{:S(2)}) collective-permute-start(f32[8,128]{1,0:T(8,128)S(1)} %get-tuple-element.60.direction_in), channel_id=1, source_target_pairs={{0,2},{1,17},{2,0},{3,5},{4,6},{5,3},{6,4},{7,9},{8,10},{9,7},{10,... | collective-permute-start | bytes 12296 | tf_op jit(solution)/shard_map/ppermute | solution.py:405
  49.2 1.2 %collective-permute-start.21 = (f32[8,128]{1,0:T(8,128)S(1)}, f32[8,128]{1,0:T(8,128)S(1)}, u32[]{:S(2)}, u32[]{:S(2)}) collective-permute-start(f32[8,128]{1,0:T(8,128)S(1)} %collective-permute-done.20.mine_ref), channel_id=1, source_target_pairs={{0,1},{1,0},{2,3},{3,2},{4,5},{5,4},{6,7},{7,6},{8,9},{9,8},{10,11... | collective-permute-start | bytes 12296 | tf_op jit(solution)/shard_map/ppermute | solution.py:408
  50.9 3.7 %collective-permute-start.23 = (f32[16,128]{1,0:T(8,128)S(1)}, f32[16,128]{1,0:T(8,128)S(1)}, u32[]{:S(2)}, u32[]{:S(2)}) collective-permute-start(f32[16,128]{1,0:T(8,128)S(1)} %get-tuple-element.63.packed_ref), channel_id=1, source_target_pairs={{0,2},{1,15},{2,0},{3,5},{4,6},{5,3},{6,4},{7,9},{8,10},{9,7},{10,... | collective-permute-start | bytes 24584 | tf_op jit(solution)/shard_map/ppermute | solution.py:405
  51.0 5.4 %collective-permute-start.22 = (f32[16,128]{1,0:T(8,128)S(1)}, f32[16,128]{1,0:T(8,128)S(1)}, u32[]{:S(2)}, u32[]{:S(2)}) collective-permute-start(f32[16,128]{1,0:T(8,128)S(1)} %get-tuple-element.63.packed_ref), channel_id=1, source_target_pairs={{0,8},{2,10},{4,12},{6,14},{8,0},{10,2},{12,4},{14,6},{1,9},{3,11}... | collective-permute-start | bytes 24584 | tf_op jit(solution)/shard_map/ppermute | solution.py:390
  54.6 2.6 %collective-permute-start.24 = (f32[16,128]{1,0:T(8,128)S(1)}, f32[16,128]{1,0:T(8,128)S(1)}, u32[]{:S(2)}, u32[]{:S(2)}) collective-permute-start(f32[16,128]{1,0:T(8,128)S(1)} %collective-permute-done.23.mine_ref), channel_id=1, source_target_pairs={{0,1},{1,0},{2,3},{3,2},{4,5},{5,4},{6,7},{7,6},{8,9},{9,8},{10,11... | collective-permute-start | bytes 24584 | tf_op jit(solution)/shard_map/ppermute | solution.py:408
  (6 other events, 7.9 us)

commit v17 on v15

--- a/solution.py
+++ b/solution.py
@@ -120,13 +120,28 @@
     slots = values.shape[1]
     high, low = index >> 7, index & (LANES - 1)
     mine = lax.broadcasted_iota(jnp.int32, (rows, slots), 0) == high
-    left = jnp.concatenate([jnp.where(mine, part, 0.0) for part in three_parts(values)], axis=0)
+    parts = [jnp.where(mine, part, 0.0) for part in three_parts(values)]
+    pieces = jnp.concatenate(parts + [jnp.zeros((rows, slots), F32)], axis=0)
     spread = lax.broadcasted_iota(jnp.int32, (LANES, slots), 0) == low
-    right = jnp.where(spread, 1.0, 0.0).astype(jnp.bfloat16)
-    sums = lax.dot_general(
-        left.astype(jnp.bfloat16), right, (((1,), (1,)), ((), ())), preferred_element_type=F32
-    )
-    return sums[:rows] + sums[rows : 2 * rows] + sums[2 * rows :]
+    return lax.dot_general(
+        jnp.where(spread, 1.0, 0.0).astype(jnp.bfloat16),
+        pieces.astype(jnp.bfloat16),
+        (((1,), (1,)), ((), ())),
+        preferred_element_type=F32,
+    )
+
+
+def turned(sums, rows):
+    whole = sums[0] if len(sums) == 1 else jnp.concatenate(sums, axis=1)
+    if whole.shape[1] < LANES:
+        filler = jnp.zeros((LANES, LANES - whole.shape[1]), F32)
+        whole = jnp.concatenate([whole, filler], axis=1)
+    whole = whole.T
+    out = []
+    for at in range(0, 4 * rows * len(sums), 4 * rows):
+        first, second, third = (whole[at + k * rows : at + (k + 1) * rows] for k in range(3))
+        out.append(first + second + third)
+    return out
 
 
 def pick_current(current, nodes):
@@ -156,8 +171,8 @@
 
 def spread_current(outgoing, maps, own_ref, keep_ref, give_ref, far_ref):
     torso = own_ref.shape[0]
-    own, after, before, far = (
-        scatter(outgoing[o : o + 1], maps[o : o + 1], torso) for o in range(maps.shape[0])
+    own, after, before, far = turned(
+        [scatter(outgoing[o : o + 1], maps[o : o + 1], torso) for o in range(maps.shape[0])], torso
     )
     ahead = meets_next()
     own_ref[...] = own
@@ -175,10 +190,11 @@
         return jnp.concatenate(rows * 2, axis=0)
 
     returned = gather(source, torso, maps)
-    total = jnp.zeros((heart, LANES), F32)
+    total = None
     for o in range(peers):
-        total = total + scatter(returned[o : o + 1], nodes[o : o + 1], heart)
-    return total
+        part = scatter(returned[o : o + 1], nodes[o : o + 1], heart)
+        total = part if total is None else total + part
+    return turned([total], heart)[0]
 
 
 def product(own_ref, other_ref, pick_ref, window):
@@ -271,7 +287,7 @@
     ):
         part = scatter(come, rows.astype(jnp.int32), forcing_ref.shape[0])
         total = part if total is None else total + part
-    forcing_ref[...] = TORSO_COUPLING * total
+    forcing_ref[...] = TORSO_COUPLING * turned([total], forcing_ref.shape[0])[0]
     give_ref[...] = near_ref[3:4]
 
 

time: 58.6 us -> 59.1 us (level)
  no operation moved by 1% of the time
where the time goes in v17:
time: 59.1 us; the launch traced here: 58.6 us
  waiting for transfers between devices  29.4 us (50%)
  starting transfers between devices  18.4 us (31%)
  Pallas kernels  5.47 us (9%)
  local copies, waits for them, and re-layouts  3.88 us (7%)
  other arithmetic  0.77 us (1%)
  between operations  0.74 us (1%)
    ppermute x8, waiting for transfers between devices, with_either(): return lax.ppermute(value, ('case', 'dom', 'sub'), pairs)  17.2 us
    ppermute x13, waiting for transfers between devices, from_sibling(): return lax.ppermute(value, 'sub', [(0, 1), (1, 0)])  8.61 us
    ppermute x13, starting transfers between devices, from_sibling(): return lax.ppermute(value, 'sub', [(0, 1), (1, 0)])  8.01 us
    ppermute x4, starting transfers between devices, with_far(): lax.ppermute(value, 'dom', [(i, (i + chain // 2) % chain) for i in range(...  7.14 us
    unnamed x10, local copies, waits for them, and re-layouts  3.88 us
    ppermute x4, waiting for transfers between devices, with_far(): lax.ppermute(value, 'dom', [(i, (i + chain // 2) % chain) for i in range(...  3.52 us
    ppermute x8, starting transfers between devices, with_either(): return lax.ppermute(value, ('case', 'dom', 'sub'), pairs)  3.25 us
    pallas_call x1, Pallas kernels, on_device(): call(functools.partial(finish, chain), (shape(*dense.shape[:1], node_coun...  1.49 us
  transfers between devices with their start and end apart: 25, of which 17 were waited for; matrix products, arithmetic and copies ran while one was open for 1% of the time, Pallas kernels for 1%

profile of v17, /device:TPU:0, one launch (start us, length us, event | category | flops | bytes accessed | tf_op | source)
XLA Modules:
  0.0 58.6 jit_solution(3551874119998626895)
XLA Ops:
  3.2 4.0 %collective-permute-start.1 = (f32[8,512]{1,0:T(8,128)S(1)}, f32[8,512]{1,0:T(8,128)S(1)}, u32[]{:S(2)}, u32[]{:S(2)}) collective-permute-start(f32[8,512]{1,0:T(8,128)S(1)} %get-tuple-element.37.to_far), channel_id=1, source_target_pairs={{0,8},{2,10},{4,12},{6,14},{8,0},{10,2},{12,4},{14,6},{1,9},{3,11}... | collective-permute-start | bytes 49160 | tf_op jit(solution)/shard_map/ppermute | solution.py:397
  7.3 1.6 %collective-permute-start.3 = (f32[4,512]{1,0:T(4,128)S(1)}, f32[4,512]{1,0:T(4,128)S(1)}, u32[]{:S(2)}, u32[]{:S(2)}) collective-permute-start(f32[4,512]{1,0:T(4,128)S(1)} %pad_maximum_fusion), channel_id=1, source_target_pairs={{0,2},{1,15},{2,0},{3,5},{4,6},{5,3},{6,4},{7,9},{8,10},{9,7},{10,... | collective-permute-start | bytes 24584 | tf_op jit(solution)/shard_map/ppermute | solution.py:412
  11.3 1.4 %collective-permute-start.4 = (f32[8,128]{1,0:T(8,128)S(1)}, f32[8,128]{1,0:T(8,128)S(1)}, u32[]{:S(2)}, u32[]{:S(2)}) collective-permute-start(f32[8,128]{1,0:T(8,128)S(1)} %get-tuple-element.40), channel_id=1, source_target_pairs={{0,1},{1,0},{2,3},{3,2},{4,5},{5,4},{6,7},{7,6},{8,9},{9,8},{10,11... | collective-permute-start | bytes 12296 | tf_op jit(solution)/shard_map/ppermute | solution.py:415
  12.8 1.1 %collective-permute-done.5.other_cols = s32[4,8]{1,0:T(4,128)S(1)} collective-permute-done((s32[4,8]{1,0:T(4,128)S(1)}, s32[4,8]{1,0:T(4,128)S(1)}, u32[]{:S(2)}, u32[]{:S(2)}) %collective-permute-start.5) | collective-permute-done | bytes 160 | tf_op jit(solution)/shard_map/ppermute | solution.py:415
  14.3 1.6 %copy-done = f32[8,4,128,128]{3,2,1,0:T(8,128)S(1)} copy-done((f32[8,4,128,128]{3,2,1,0:T(8,128)S(1)}, f32[8,4,128,128]{3,2,1,0:T(8,128)}, u32[]{:S(2)}) %copy-start) | copy-done | bytes 2097176
  15.9 1.7 %collective-permute-done.6.mine_ref = f32[8,128]{1,0:T(8,128)S(1)} collective-permute-done((f32[8,128]{1,0:T(8,128)S(1)}, f32[8,128]{1,0:T(8,128)S(1)}, u32[]{:S(2)}, u32[]{:S(2)}) %collective-permute-start.6) | collective-permute-done | bytes 4128 | tf_op jit(solution)/shard_map/ppermute | solution.py:412
  17.7 1.1 %collective-permute-done.7.yours_ref = f32[8,128]{1,0:T(8,128)S(1)} collective-permute-done((f32[8,128]{1,0:T(8,128)S(1)}, f32[8,128]{1,0:T(8,128)S(1)}, u32[]{:S(2)}, u32[]{:S(2)}) %collective-permute-start.7) | collective-permute-done | bytes 4128 | tf_op jit(solution)/shard_map/ppermute | solution.py:415
  19.7 3.2 %collective-permute-done.8.mine_ref = f32[8,128]{1,0:T(8,128)S(1)} collective-permute-done((f32[8,128]{1,0:T(8,128)S(1)}, f32[8,128]{1,0:T(8,128)S(1)}, u32[]{:S(2)}, u32[]{:S(2)}) %collective-permute-start.8) | collective-permute-done | bytes 4128 | tf_op jit(solution)/shard_map/ppermute | solution.py:412
  22.9 1.2 %collective-permute-done.9.yours_ref = f32[8,128]{1,0:T(8,128)S(1)} collective-permute-done((f32[8,128]{1,0:T(8,128)S(1)}, f32[8,128]{1,0:T(8,128)S(1)}, u32[]{:S(2)}, u32[]{:S(2)}) %collective-permute-start.9) | collective-permute-done | bytes 4128 | tf_op jit(solution)/shard_map/ppermute | solution.py:415
  25.1 1.5 %collective-permute-start.10 = (f32[8,128]{1,0:T(8,128)S(1)}, f32[8,128]{1,0:T(8,128)S(1)}, u32[]{:S(2)}, u32[]{:S(2)}) collective-permute-start(f32[8,128]{1,0:T(8,128)S(1)} %shard_map.100.own_estimate), channel_id=1, source_target_pairs={{0,8},{2,10},{4,12},{6,14},{8,0},{10,2},{12,4},{14,6},{1,9},{3,11}... | collective-permute-start | bytes 12296 | tf_op jit(solution)/shard_map/ppermute | solution.py:397
  26.6 1.7 %collective-permute-done.11.mine_ref = f32[8,128]{1,0:T(8,128)S(1)} collective-permute-done((f32[8,128]{1,0:T(8,128)S(1)}, f32[8,128]{1,0:T(8,128)S(1)}, u32[]{:S(2)}, u32[]{:S(2)}) %collective-permute-start.11) | collective-permute-done | bytes 4128 | tf_op jit(solution)/shard_map/ppermute | solution.py:412
  28.3 1.7 %collective-permute-start.12 = (f32[8,128]{1,0:T(8,128)S(1)}, f32[8,128]{1,0:T(8,128)S(1)}, u32[]{:S(2)}, u32[]{:S(2)}) collective-permute-start(f32[8,128]{1,0:T(8,128)S(1)} %collective-permute-done.11.mine_ref), channel_id=1, source_target_pairs={{0,1},{1,0},{2,3},{3,2},{4,5},{5,4},{6,7},{7,6},{8,9},{9,8},{10,11... | collective-permute-start | bytes 12296 | tf_op jit(solution)/shard_map/ppermute | solution.py:415
  30.0 1.2 %collective-permute-done.13.got_ref = f32[1,512]{1,0:T(1,128)S(1)} collective-permute-done((f32[1,512]{1,0:T(1,128)S(1)}, f32[1,512]{1,0:T(1,128)S(1)}, u32[]{:S(2)}, u32[]{:S(2)}) %collective-permute-start.13) | collective-permute-done | bytes 2080 | tf_op jit(solution)/shard_map/ppermute | solution.py:415
  31.2 1.2 %shard_map.102 = (f32[19,16,128]{2,1,0:T(8,128)S(1)}, f32[8,128]{1,0:T(8,128)S(1)}, f32[8,128]{1,0:T(8,128)S(1)}, f32[8,128]{1,0:T(8,128)S(1)}, f32[8,128]{1,0:T(8,128)S(1)}) custom-call(f32[19,16,128]{2,1,0:T(8,128)S(1)} %get-tuple-element.42.states_ref, f32[8,128]{1,0:T(8,128)S(1)} %shard_map.100.own_estimate, ...), custom_call_target="tpu_custom_call" | custom-call | flops 4000000 | bytes 262144 | tf_op jit(solution)/shard_map/pallas_call | solution.py:471
  34.1 3.5 %collective-permute-done.14 = f32[8,128]{1,0:T(8,128)S(1)} collective-permute-done((f32[8,128]{1,0:T(8,128)S(1)}, f32[8,128]{1,0:T(8,128)S(1)}, u32[]{:S(2)}, u32[]{:S(2)}) %collective-permute-start.14) | collective-permute-done | bytes 4128 | tf_op jit(solution)/shard_map/ppermute | solution.py:397
  37.6 1.8 %collective-permute-start.17 = (f32[8,128]{1,0:T(8,128)S(1)}, f32[8,128]{1,0:T(8,128)S(1)}, u32[]{:S(2)}, u32[]{:S(2)}) collective-permute-start(f32[8,128]{1,0:T(8,128)S(1)} %add_multiply_fusion), channel_id=1, source_target_pairs={{0,1},{1,0},{2,3},{3,2},{4,5},{5,4},{6,7},{7,6},{8,9},{9,8},{10,11... | collective-permute-start | bytes 12296 | tf_op jit(solution)/shard_map/ppermute | solution.py:415
  40.2 3.6 %collective-permute-done.18.mine_ref = f32[8,128]{1,0:T(8,128)S(1)} collective-permute-done((f32[8,128]{1,0:T(8,128)S(1)}, f32[8,128]{1,0:T(8,128)S(1)}, u32[]{:S(2)}, u32[]{:S(2)}) %collective-permute-start.18) | collective-permute-done | bytes 4128 | tf_op jit(solution)/shard_map/ppermute | solution.py:412
  43.9 1.2 %collective-permute-done.19.yours_ref = f32[8,128]{1,0:T(8,128)S(1)} collective-permute-done((f32[8,128]{1,0:T(8,128)S(1)}, f32[8,128]{1,0:T(8,128)S(1)}, u32[]{:S(2)}, u32[]{:S(2)}) %collective-permute-start.19) | collective-permute-done | bytes 4128 | tf_op jit(solution)/shard_map/ppermute | solution.py:415
  45.6 3.6 %collective-permute-done.20.mine_ref = f32[8,128]{1,0:T(8,128)S(1)} collective-permute-done((f32[8,128]{1,0:T(8,128)S(1)}, f32[8,128]{1,0:T(8,128)S(1)}, u32[]{:S(2)}, u32[]{:S(2)}) %collective-permute-start.20) | collective-permute-done | bytes 4128 | tf_op jit(solution)/shard_map/ppermute | solution.py:412
  49.2 1.2 %collective-permute-done.21.yours_ref = f32[8,128]{1,0:T(8,128)S(1)} collective-permute-done((f32[8,128]{1,0:T(8,128)S(1)}, f32[8,128]{1,0:T(8,128)S(1)}, u32[]{:S(2)}, u32[]{:S(2)}) %collective-permute-start.21) | collective-permute-done | bytes 4128 | tf_op jit(solution)/shard_map/ppermute | solution.py:415
  50.9 0.9 %collective-permute-start.22 = (f32[16,128]{1,0:T(8,128)S(1)}, f32[16,128]{1,0:T(8,128)S(1)}, u32[]{:S(2)}, u32[]{:S(2)}) collective-permute-start(f32[16,128]{1,0:T(8,128)S(1)} %get-tuple-element.59.packed_ref), channel_id=1, source_target_pairs={{0,8},{2,10},{4,12},{6,14},{8,0},{10,2},{12,4},{14,6},{1,9},{3,11}... | collective-permute-start | bytes 24584 | tf_op jit(solution)/shard_map/ppermute | solution.py:397
  51.9 2.7 %collective-permute-done.23.mine_ref = f32[16,128]{1,0:T(8,128)S(1)} collective-permute-done((f32[16,128]{1,0:T(8,128)S(1)}, f32[16,128]{1,0:T(8,128)S(1)}, u32[]{:S(2)}, u32[]{:S(2)}) %collective-permute-start.23) | collective-permute-done | bytes 8224 | tf_op jit(solution)/shard_map/ppermute | solution.py:412
  54.6 1.7 %collective-permute-start.24 = (f32[16,128]{1,0:T(8,128)S(1)}, f32[16,128]{1,0:T(8,128)S(1)}, u32[]{:S(2)}, u32[]{:S(2)}) collective-permute-start(f32[16,128]{1,0:T(8,128)S(1)} %collective-permute-done.23.mine_ref), channel_id=1, source_target_pairs={{0,1},{1,0},{2,3},{3,2},{4,5},{5,4},{6,7},{7,6},{8,9},{9,8},{10,11... | collective-permute-start | bytes 24584 | tf_op jit(solution)/shard_map/ppermute | solution.py:415
  57.1 1.5 %shard_map.105 = (f32[19,2048]{1,0:T(8,128)}, f32[8,128]{1,0:T(8,128)}, f32[8,128]{1,0:T(8,128)}) custom-call(f32[8,4,128,128]{3,2,1,0:T(8,128)S(1)} %copy-done.1, f32[8,4,128,128]{3,2,1,0:T(8,128)S(1)} %collective-permute-done.other_ref, f32[64,16]{1,0:T(8,128)S(1)} %shard_map.97.pick_ref, f32[16,128]{1,0:T(8,128)S(1)} %get-tuple-element.59.packed_ref, ...), custom_call_target="tpu_custom_call" | custom-call | flops 4000000 | bytes 262144 | tf_op jit(solution)/shard_map/pallas_call | solution.py:477
  (54 shorter events, 12.1 us)
Async XLA Ops:
  0.6 18.1 %collective-permute-start = (f32[8,4,128,128]{3,2,1,0:T(8,128)}, f32[8,4,128,128]{3,2,1,0:T(8,128)S(1)}, u32[]{:S(2)}, u32[]{:S(2)}) collective-permute-start(f32[8,4,128,128]{3,2,1,0:T(8,128)} %own_ref.9), channel_id=1, source_target_pairs={{0,1},{1,0},{2,3},{3,2},{4,5},{5,4},{6,7},{7,6},{8,9},{9,8},{10,11... | collective-permute-start | bytes 6291464 | tf_op jit(solution)/shard_map/ppermute | solution.py:415
  3.1 4.2 %collective-permute-start.2 = (f32[2,512]{1,0:T(2,128)S(1)}, f32[2,512]{1,0:T(2,128)S(1)}, u32[]{:S(2)}, u32[]{:S(2)}) collective-permute-start(f32[2,512]{1,0:T(2,128)S(1)} %get-tuple-element.39), channel_id=1, source_target_pairs={{0,1},{1,0},{2,3},{3,2},{4,5},{5,4},{6,7},{7,6},{8,9},{9,8},{10,11... | collective-permute-start | bytes 12296 | tf_op jit(solution)/shard_map/ppermute | solution.py:415
  3.2 7.8 %collective-permute-start.1 = (f32[8,512]{1,0:T(8,128)S(1)}, f32[8,512]{1,0:T(8,128)S(1)}, u32[]{:S(2)}, u32[]{:S(2)}) collective-permute-start(f32[8,512]{1,0:T(8,128)S(1)} %get-tuple-element.37.to_far), channel_id=1, source_target_pairs={{0,8},{2,10},{4,12},{6,14},{8,0},{10,2},{12,4},{14,6},{1,9},{3,11}... | collective-permute-start | bytes 49160 | tf_op jit(solution)/shard_map/ppermute | solution.py:397
  7.3 3.7 %collective-permute-start.3 = (f32[4,512]{1,0:T(4,128)S(1)}, f32[4,512]{1,0:T(4,128)S(1)}, u32[]{:S(2)}, u32[]{:S(2)}) collective-permute-start(f32[4,512]{1,0:T(4,128)S(1)} %pad_maximum_fusion), channel_id=1, source_target_pairs={{0,2},{1,15},{2,0},{3,5},{4,6},{5,3},{6,4},{7,9},{8,10},{9,7},{10,... | collective-permute-start | bytes 24584 | tf_op jit(solution)/shard_map/ppermute | solution.py:412
  11.3 2.5 %collective-permute-start.4 = (f32[8,128]{1,0:T(8,128)S(1)}, f32[8,128]{1,0:T(8,128)S(1)}, u32[]{:S(2)}, u32[]{:S(2)}) collective-permute-start(f32[8,128]{1,0:T(8,128)S(1)} %get-tuple-element.40), channel_id=1, source_target_pairs={{0,1},{1,0},{2,3},{3,2},{4,5},{5,4},{6,7},{7,6},{8,9},{9,8},{10,11... | collective-permute-start | bytes 12296 | tf_op jit(solution)/shard_map/ppermute | solution.py:415
  12.7 1.2 %collective-permute-start.5 = (s32[4,8]{1,0:T(4,128)S(1)}, s32[4,8]{1,0:T(4,128)S(1)}, u32[]{:S(2)}, u32[]{:S(2)}) collective-permute-start(s32[4,8]{1,0:T(4,128)S(1)} %get-tuple-element.35.own_cols), channel_id=1, source_target_pairs={{0,1},{1,0},{2,3},{3,2},{4,5},{5,4},{6,7},{7,6},{8,9},{9,8},{10,11... | collective-permute-start | bytes 392 | tf_op jit(solution)/shard_map/ppermute | solution.py:415
  13.9 3.7 %collective-permute-start.6 = (f32[8,128]{1,0:T(8,128)S(1)}, f32[8,128]{1,0:T(8,128)S(1)}, u32[]{:S(2)}, u32[]{:S(2)}) collective-permute-start(f32[8,128]{1,0:T(8,128)S(1)} %get-tuple-element.67.direction_ref), channel_id=1, source_target_pairs={{0,2},{1,17},{2,0},{3,5},{4,6},{5,3},{6,4},{7,9},{8,10},{9,7},{10,... | collective-permute-start | bytes 12296 | tf_op jit(solution)/shard_map/ppermute | solution.py:412
  17.6 1.2 %collective-permute-start.7 = (f32[8,128]{1,0:T(8,128)S(1)}, f32[8,128]{1,0:T(8,128)S(1)}, u32[]{:S(2)}, u32[]{:S(2)}) collective-permute-start(f32[8,128]{1,0:T(8,128)S(1)} %collective-permute-done.6.mine_ref), channel_id=1, source_target_pairs={{0,1},{1,0},{2,3},{3,2},{4,5},{5,4},{6,7},{7,6},{8,9},{9,8},{10,11... | collective-permute-start | bytes 12296 | tf_op jit(solution)/shard_map/ppermute | solution.py:415
  19.3 3.7 %collective-permute-start.8 = (f32[8,128]{1,0:T(8,128)S(1)}, f32[8,128]{1,0:T(8,128)S(1)}, u32[]{:S(2)}, u32[]{:S(2)}) collective-permute-start(f32[8,128]{1,0:T(8,128)S(1)} %get-tuple-element.47.direction_in), channel_id=1, source_target_pairs={{0,2},{1,17},{2,0},{3,5},{4,6},{5,3},{6,4},{7,9},{8,10},{9,7},{10,... | collective-permute-start | bytes 12296 | tf_op jit(solution)/shard_map/ppermute | solution.py:412
  22.9 1.2 %collective-permute-start.9 = (f32[8,128]{1,0:T(8,128)S(1)}, f32[8,128]{1,0:T(8,128)S(1)}, u32[]{:S(2)}, u32[]{:S(2)}) collective-permute-start(f32[8,128]{1,0:T(8,128)S(1)} %collective-permute-done.8.mine_ref), channel_id=1, source_target_pairs={{0,1},{1,0},{2,3},{3,2},{4,5},{5,4},{6,7},{7,6},{8,9},{9,8},{10,11... | collective-permute-start | bytes 12296 | tf_op jit(solution)/shard_map/ppermute | solution.py:415
  24.6 3.7 %collective-permute-start.11 = (f32[8,128]{1,0:T(8,128)S(1)}, f32[8,128]{1,0:T(8,128)S(1)}, u32[]{:S(2)}, u32[]{:S(2)}) collective-permute-start(f32[8,128]{1,0:T(8,128)S(1)} %shard_map.100.own_estimate), channel_id=1, source_target_pairs={{0,2},{1,15},{2,0},{3,5},{4,6},{5,3},{6,4},{7,9},{8,10},{9,7},{10,... | collective-permute-start | bytes 12296 | tf_op jit(solution)/shard_map/ppermute | solution.py:412
  25.1 6.0 %collective-permute-start.10 = (f32[8,128]{1,0:T(8,128)S(1)}, f32[8,128]{1,0:T(8,128)S(1)}, u32[]{:S(2)}, u32[]{:S(2)}) collective-permute-start(f32[8,128]{1,0:T(8,128)S(1)} %shard_map.100.own_estimate), channel_id=1, source_target_pairs={{0,8},{2,10},{4,12},{6,14},{8,0},{10,2},{12,4},{14,6},{1,9},{3,11}... | collective-permute-start | bytes 12296 | tf_op jit(solution)/shard_map/ppermute | solution.py:397
  28.3 2.9 %collective-permute-start.12 = (f32[8,128]{1,0:T(8,128)S(1)}, f32[8,128]{1,0:T(8,128)S(1)}, u32[]{:S(2)}, u32[]{:S(2)}) collective-permute-start(f32[8,128]{1,0:T(8,128)S(1)} %collective-permute-done.11.mine_ref), channel_id=1, source_target_pairs={{0,1},{1,0},{2,3},{3,2},{4,5},{5,4},{6,7},{7,6},{8,9},{9,8},{10,11... | collective-permute-start | bytes 12296 | tf_op jit(solution)/shard_map/ppermute | solution.py:415
  32.4 1.5 %collective-permute-start.15 = (f32[8,128]{1,0:T(8,128)S(1)}, f32[8,128]{1,0:T(8,128)S(1)}, u32[]{:S(2)}, u32[]{:S(2)}) collective-permute-start(f32[8,128]{1,0:T(8,128)S(1)} %get-tuple-element.55), channel_id=1, source_target_pairs={{0,1},{1,0},{2,3},{3,2},{4,5},{5,4},{6,7},{7,6},{8,9},{9,8},{10,11... | collective-permute-start | bytes 12296 | tf_op jit(solution)/shard_map/ppermute | solution.py:415
  33.1 4.5 %collective-permute-start.14 = (f32[8,128]{1,0:T(8,128)S(1)}, f32[8,128]{1,0:T(8,128)S(1)}, u32[]{:S(2)}, u32[]{:S(2)}) collective-permute-start(f32[8,128]{1,0:T(8,128)S(1)} %get-tuple-element.53), channel_id=1, source_target_pairs={{0,8},{2,10},{4,12},{6,14},{8,0},{10,2},{12,4},{14,6},{1,9},{3,11}... | collective-permute-start | bytes 12296 | tf_op jit(solution)/shard_map/ppermute | solution.py:397
  33.9 3.7 %collective-permute-start.16 = (f32[8,128]{1,0:T(8,128)S(1)}, f32[8,128]{1,0:T(8,128)S(1)}, u32[]{:S(2)}, u32[]{:S(2)}) collective-permute-start(f32[8,128]{1,0:T(8,128)S(1)} %add.19), channel_id=1, source_target_pairs={{0,2},{1,15},{2,0},{3,5},{4,6},{5,3},{6,4},{7,9},{8,10},{9,7},{10,... | collective-permute-start | bytes 12296 | tf_op jit(solution)/shard_map/ppermute | solution.py:412
  37.6 2.6 %collective-permute-start.17 = (f32[8,128]{1,0:T(8,128)S(1)}, f32[8,128]{1,0:T(8,128)S(1)}, u32[]{:S(2)}, u32[]{:S(2)}) collective-permute-start(f32[8,128]{1,0:T(8,128)S(1)} %add_multiply_fusion), channel_id=1, source_target_pairs={{0,1},{1,0},{2,3},{3,2},{4,5},{5,4},{6,7},{7,6},{8,9},{9,8},{10,11... | collective-permute-start | bytes 12296 | tf_op jit(solution)/shard_map/ppermute | solution.py:415
  40.2 3.6 %collective-permute-start.18 = (f32[8,128]{1,0:T(8,128)S(1)}, f32[8,128]{1,0:T(8,128)S(1)}, u32[]{:S(2)}, u32[]{:S(2)}) collective-permute-start(f32[8,128]{1,0:T(8,128)S(1)} %get-tuple-element.65.direction_in), channel_id=1, source_target_pairs={{0,2},{1,17},{2,0},{3,5},{4,6},{5,3},{6,4},{7,9},{8,10},{9,7},{10,... | collective-permute-start | bytes 12296 | tf_op jit(solution)/shard_map/ppermute | solution.py:412
  43.8 1.2 %collective-permute-start.19 = (f32[8,128]{1,0:T(8,128)S(1)}, f32[8,128]{1,0:T(8,128)S(1)}, u32[]{:S(2)}, u32[]{:S(2)}) collective-permute-start(f32[8,128]{1,0:T(8,128)S(1)} %collective-permute-done.18.mine_ref), channel_id=1, source_target_pairs={{0,1},{1,0},{2,3},{3,2},{4,5},{5,4},{6,7},{7,6},{8,9},{9,8},{10,11... | collective-permute-start | bytes 12296 | tf_op jit(solution)/shard_map/ppermute | solution.py:415
  45.5 3.7 %collective-permute-start.20 = (f32[8,128]{1,0:T(8,128)S(1)}, f32[8,128]{1,0:T(8,128)S(1)}, u32[]{:S(2)}, u32[]{:S(2)}) collective-permute-start(f32[8,128]{1,0:T(8,128)S(1)} %get-tuple-element.56.direction_in), channel_id=1, source_target_pairs={{0,2},{1,17},{2,0},{3,5},{4,6},{5,3},{6,4},{7,9},{8,10},{9,7},{10,... | collective-permute-start | bytes 12296 | tf_op jit(solution)/shard_map/ppermute | solution.py:412
  49.2 1.2 %collective-permute-start.21 = (f32[8,128]{1,0:T(8,128)S(1)}, f32[8,128]{1,0:T(8,128)S(1)}, u32[]{:S(2)}, u32[]{:S(2)}) collective-permute-start(f32[8,128]{1,0:T(8,128)S(1)} %collective-permute-done.20.mine_ref), channel_id=1, source_target_pairs={{0,1},{1,0},{2,3},{3,2},{4,5},{5,4},{6,7},{7,6},{8,9},{9,8},{10,11... | collective-permute-start | bytes 12296 | tf_op jit(solution)/shard_map/ppermute | solution.py:415
  50.9 3.7 %collective-permute-start.23 = (f32[16,128]{1,0:T(8,128)S(1)}, f32[16,128]{1,0:T(8,128)S(1)}, u32[]{:S(2)}, u32[]{:S(2)}) collective-permute-start(f32[16,128]{1,0:T(8,128)S(1)} %get-tuple-element.59.packed_ref), channel_id=1, source_target_pairs={{0,2},{1,15},{2,0},{3,5},{4,6},{5,3},{6,4},{7,9},{8,10},{9,7},{10,... | collective-permute-start | bytes 24584 | tf_op jit(solution)/shard_map/ppermute | solution.py:412
  50.9 5.4 %collective-permute-start.22 = (f32[16,128]{1,0:T(8,128)S(1)}, f32[16,128]{1,0:T(8,128)S(1)}, u32[]{:S(2)}, u32[]{:S(2)}) collective-permute-start(f32[16,128]{1,0:T(8,128)S(1)} %get-tuple-element.59.packed_ref), channel_id=1, source_target_pairs={{0,8},{2,10},{4,12},{6,14},{8,0},{10,2},{12,4},{14,6},{1,9},{3,11}... | collective-permute-start | bytes 24584 | tf_op jit(solution)/shard_map/ppermute | solution.py:397
  54.6 2.5 %collective-permute-start.24 = (f32[16,128]{1,0:T(8,128)S(1)}, f32[16,128]{1,0:T(8,128)S(1)}, u32[]{:S(2)}, u32[]{:S(2)}) collective-permute-start(f32[16,128]{1,0:T(8,128)S(1)} %collective-permute-done.23.mine_ref), channel_id=1, source_target_pairs={{0,1},{1,0},{2,3},{3,2},{4,5},{5,4},{6,7},{7,6},{8,9},{9,8},{10,11... | collective-permute-start | bytes 24584 | tf_op jit(solution)/shard_map/ppermute | solution.py:415
  (6 other events, 7.9 us)

commit v18 on v15

--- a/solution.py
+++ b/solution.py
@@ -109,24 +109,22 @@
     return jnp.concatenate(out, axis=1)
 
 
-def three_parts(value):
+def two_parts(value):
     first = value.astype(jnp.bfloat16).astype(F32)
-    rest = value - first
-    second = rest.astype(jnp.bfloat16).astype(F32)
-    return first, second, rest - second
+    return first, value - first
 
 
 def scatter(values, index, rows):
     slots = values.shape[1]
     high, low = index >> 7, index & (LANES - 1)
     mine = lax.broadcasted_iota(jnp.int32, (rows, slots), 0) == high
-    left = jnp.concatenate([jnp.where(mine, part, 0.0) for part in three_parts(values)], axis=0)
+    left = jnp.concatenate([jnp.where(mine, part, 0.0) for part in two_parts(values)], axis=0)
     spread = lax.broadcasted_iota(jnp.int32, (LANES, slots), 0) == low
     right = jnp.where(spread, 1.0, 0.0).astype(jnp.bfloat16)
     sums = lax.dot_general(
         left.astype(jnp.bfloat16), right, (((1,), (1,)), ((), ())), preferred_element_type=F32
     )
-    return sums[:rows] + sums[rows : 2 * rows] + sums[2 * rows :]
+    return sums[:rows] + sums[rows:]
 
 
 def pick_current(current, nodes):
@@ -183,9 +181,9 @@
 
 def product(own_ref, other_ref, pick_ref, window):
     tiles, slots = own_ref.shape[0], own_ref.shape[1]
-    parts = jnp.concatenate(three_parts(window), axis=1).astype(jnp.bfloat16)
+    parts = jnp.concatenate(two_parts(window), axis=1).astype(jnp.bfloat16)
     picked = jnp.dot(pick_ref[...].astype(jnp.bfloat16), parts, preferred_element_type=F32)
-    picked = picked[:, :LANES] + picked[:, LANES : 2 * LANES] + picked[:, 2 * LANES :]
+    picked = picked[:, :LANES] + picked[:, LANES:]
     eye = lax.broadcasted_iota(jnp.int32, (LANES, LANES), 0) == lax.broadcasted_iota(
         jnp.int32, (LANES, LANES), 1
     )

time: 58.6 us -> 58.6 us (level)
  no operation moved by 1% of the time
where the time goes in v18:
time: 58.6 us; the launch traced here: 58.1 us
  waiting for transfers between devices  29.4 us (50%)
  starting transfers between devices  18.3 us (31%)
  Pallas kernels  5.04 us (9%)
  local copies, waits for them, and re-layouts  3.88 us (7%)
  other arithmetic  0.77 us (1%)
  between operations  0.73 us (1%)
    ppermute x8, waiting for transfers between devices, with_either(): return lax.ppermute(value, ('case', 'dom', 'sub'), pairs)  17.2 us
    ppermute x13, waiting for transfers between devices, from_sibling(): return lax.ppermute(value, 'sub', [(0, 1), (1, 0)])  8.65 us
    ppermute x13, starting transfers between devices, from_sibling(): return lax.ppermute(value, 'sub', [(0, 1), (1, 0)])  7.92 us
    ppermute x4, starting transfers between devices, with_far(): lax.ppermute(value, 'dom', [(i, (i + chain // 2) % chain) for i in range(...  7.12 us
    unnamed x10, local copies, waits for them, and re-layouts  3.88 us
    ppermute x4, waiting for transfers between devices, with_far(): lax.ppermute(value, 'dom', [(i, (i + chain // 2) % chain) for i in range(...  3.52 us
    ppermute x8, starting transfers between devices, with_either(): return lax.ppermute(value, ('case', 'dom', 'sub'), pairs)  3.25 us
    pallas_call x1, Pallas kernels, on_device(): call(functools.partial(finish, chain), (shape(*dense.shape[:1], node_coun...  1.44 us
  transfers between devices with their start and end apart: 25, of which 17 were waited for; matrix products, arithmetic and copies ran while one was open for 1% of the time, Pallas kernels for 1%

profile of v18, /device:TPU:0, one launch (start us, length us, event | category | flops | bytes accessed | tf_op | source)
XLA Modules:
  0.0 58.1 jit_solution(7411827719698561999)
XLA Ops:
  3.2 4.0 %collective-permute-start.1 = (f32[8,512]{1,0:T(8,128)S(1)}, f32[8,512]{1,0:T(8,128)S(1)}, u32[]{:S(2)}, u32[]{:S(2)}) collective-permute-start(f32[8,512]{1,0:T(8,128)S(1)} %get-tuple-element.37.to_far), channel_id=1, source_target_pairs={{0,8},{2,10},{4,12},{6,14},{8,0},{10,2},{12,4},{14,6},{1,9},{3,11}... | collective-permute-start | bytes 49160 | tf_op jit(solution)/shard_map/ppermute | solution.py:379
  7.3 1.6 %collective-permute-start.3 = (f32[4,512]{1,0:T(4,128)S(1)}, f32[4,512]{1,0:T(4,128)S(1)}, u32[]{:S(2)}, u32[]{:S(2)}) collective-permute-start(f32[4,512]{1,0:T(4,128)S(1)} %pad_maximum_fusion), channel_id=1, source_target_pairs={{0,2},{1,15},{2,0},{3,5},{4,6},{5,3},{6,4},{7,9},{8,10},{9,7},{10,... | collective-permute-start | bytes 24584 | tf_op jit(solution)/shard_map/ppermute | solution.py:394
  11.3 1.4 %collective-permute-start.4 = (f32[8,128]{1,0:T(8,128)S(1)}, f32[8,128]{1,0:T(8,128)S(1)}, u32[]{:S(2)}, u32[]{:S(2)}) collective-permute-start(f32[8,128]{1,0:T(8,128)S(1)} %get-tuple-element.40), channel_id=1, source_target_pairs={{0,1},{1,0},{2,3},{3,2},{4,5},{5,4},{6,7},{7,6},{8,9},{9,8},{10,11... | collective-permute-start | bytes 12296 | tf_op jit(solution)/shard_map/ppermute | solution.py:397
  12.7 1.1 %collective-permute-done.5.other_cols = s32[4,8]{1,0:T(4,128)S(1)} collective-permute-done((s32[4,8]{1,0:T(4,128)S(1)}, s32[4,8]{1,0:T(4,128)S(1)}, u32[]{:S(2)}, u32[]{:S(2)}) %collective-permute-start.5) | collective-permute-done | bytes 160 | tf_op jit(solution)/shard_map/ppermute | solution.py:397
  14.2 1.6 %copy-done = f32[8,4,128,128]{3,2,1,0:T(8,128)S(1)} copy-done((f32[8,4,128,128]{3,2,1,0:T(8,128)S(1)}, f32[8,4,128,128]{3,2,1,0:T(8,128)}, u32[]{:S(2)}) %copy-start) | copy-done | bytes 2097176
  15.8 1.7 %collective-permute-done.6.mine_ref = f32[8,128]{1,0:T(8,128)S(1)} collective-permute-done((f32[8,128]{1,0:T(8,128)S(1)}, f32[8,128]{1,0:T(8,128)S(1)}, u32[]{:S(2)}, u32[]{:S(2)}) %collective-permute-start.6) | collective-permute-done | bytes 4128 | tf_op jit(solution)/shard_map/ppermute | solution.py:394
  17.5 1.1 %collective-permute-done.7.yours_ref = f32[8,128]{1,0:T(8,128)S(1)} collective-permute-done((f32[8,128]{1,0:T(8,128)S(1)}, f32[8,128]{1,0:T(8,128)S(1)}, u32[]{:S(2)}, u32[]{:S(2)}) %collective-permute-start.7) | collective-permute-done | bytes 4128 | tf_op jit(solution)/shard_map/ppermute | solution.py:397
  19.6 3.2 %collective-permute-done.8.mine_ref = f32[8,128]{1,0:T(8,128)S(1)} collective-permute-done((f32[8,128]{1,0:T(8,128)S(1)}, f32[8,128]{1,0:T(8,128)S(1)}, u32[]{:S(2)}, u32[]{:S(2)}) %collective-permute-start.8) | collective-permute-done | bytes 4128 | tf_op jit(solution)/shard_map/ppermute | solution.py:394
  22.8 1.2 %collective-permute-done.9.yours_ref = f32[8,128]{1,0:T(8,128)S(1)} collective-permute-done((f32[8,128]{1,0:T(8,128)S(1)}, f32[8,128]{1,0:T(8,128)S(1)}, u32[]{:S(2)}, u32[]{:S(2)}) %collective-permute-start.9) | collective-permute-done | bytes 4128 | tf_op jit(solution)/shard_map/ppermute | solution.py:397
  25.0 1.5 %collective-permute-start.10 = (f32[8,128]{1,0:T(8,128)S(1)}, f32[8,128]{1,0:T(8,128)S(1)}, u32[]{:S(2)}, u32[]{:S(2)}) collective-permute-start(f32[8,128]{1,0:T(8,128)S(1)} %shard_map.100.own_estimate), channel_id=1, source_target_pairs={{0,8},{2,10},{4,12},{6,14},{8,0},{10,2},{12,4},{14,6},{1,9},{3,11}... | collective-permute-start | bytes 12296 | tf_op jit(solution)/shard_map/ppermute | solution.py:379
  26.5 1.7 %collective-permute-done.11.mine_ref = f32[8,128]{1,0:T(8,128)S(1)} collective-permute-done((f32[8,128]{1,0:T(8,128)S(1)}, f32[8,128]{1,0:T(8,128)S(1)}, u32[]{:S(2)}, u32[]{:S(2)}) %collective-permute-start.11) | collective-permute-done | bytes 4128 | tf_op jit(solution)/shard_map/ppermute | solution.py:394
  28.2 1.7 %collective-permute-start.12 = (f32[8,128]{1,0:T(8,128)S(1)}, f32[8,128]{1,0:T(8,128)S(1)}, u32[]{:S(2)}, u32[]{:S(2)}) collective-permute-start(f32[8,128]{1,0:T(8,128)S(1)} %collective-permute-done.11.mine_ref), channel_id=1, source_target_pairs={{0,1},{1,0},{2,3},{3,2},{4,5},{5,4},{6,7},{7,6},{8,9},{9,8},{10,11... | collective-permute-start | bytes 12296 | tf_op jit(solution)/shard_map/ppermute | solution.py:397
  29.9 1.2 %collective-permute-done.13.got_ref = f32[1,512]{1,0:T(1,128)S(1)} collective-permute-done((f32[1,512]{1,0:T(1,128)S(1)}, f32[1,512]{1,0:T(1,128)S(1)}, u32[]{:S(2)}, u32[]{:S(2)}) %collective-permute-start.13) | collective-permute-done | bytes 2080 | tf_op jit(solution)/shard_map/ppermute | solution.py:397
  31.1 1.0 %shard_map.102 = (f32[19,16,128]{2,1,0:T(8,128)S(1)}, f32[8,128]{1,0:T(8,128)S(1)}, f32[8,128]{1,0:T(8,128)S(1)}, f32[8,128]{1,0:T(8,128)S(1)}, f32[8,128]{1,0:T(8,128)S(1)}) custom-call(f32[19,16,128]{2,1,0:T(8,128)S(1)} %get-tuple-element.42.states_ref, f32[8,128]{1,0:T(8,128)S(1)} %shard_map.100.own_estimate, ...), custom_call_target="tpu_custom_call" | custom-call | flops 4000000 | bytes 262144 | tf_op jit(solution)/shard_map/pallas_call | solution.py:453
  33.6 3.5 %collective-permute-done.14 = f32[8,128]{1,0:T(8,128)S(1)} collective-permute-done((f32[8,128]{1,0:T(8,128)S(1)}, f32[8,128]{1,0:T(8,128)S(1)}, u32[]{:S(2)}, u32[]{:S(2)}) %collective-permute-start.14) | collective-permute-done | bytes 4128 | tf_op jit(solution)/shard_map/ppermute | solution.py:379
  37.2 1.8 %collective-permute-start.17 = (f32[8,128]{1,0:T(8,128)S(1)}, f32[8,128]{1,0:T(8,128)S(1)}, u32[]{:S(2)}, u32[]{:S(2)}) collective-permute-start(f32[8,128]{1,0:T(8,128)S(1)} %add_multiply_fusion), channel_id=1, source_target_pairs={{0,1},{1,0},{2,3},{3,2},{4,5},{5,4},{6,7},{7,6},{8,9},{9,8},{10,11... | collective-permute-start | bytes 12296 | tf_op jit(solution)/shard_map/ppermute | solution.py:397
  39.8 3.6 %collective-permute-done.18.mine_ref = f32[8,128]{1,0:T(8,128)S(1)} collective-permute-done((f32[8,128]{1,0:T(8,128)S(1)}, f32[8,128]{1,0:T(8,128)S(1)}, u32[]{:S(2)}, u32[]{:S(2)}) %collective-permute-start.18) | collective-permute-done | bytes 4128 | tf_op jit(solution)/shard_map/ppermute | solution.py:394
  43.4 1.2 %collective-permute-done.19.yours_ref = f32[8,128]{1,0:T(8,128)S(1)} collective-permute-done((f32[8,128]{1,0:T(8,128)S(1)}, f32[8,128]{1,0:T(8,128)S(1)}, u32[]{:S(2)}, u32[]{:S(2)}) %collective-permute-start.19) | collective-permute-done | bytes 4128 | tf_op jit(solution)/shard_map/ppermute | solution.py:397
  45.2 3.6 %collective-permute-done.20.mine_ref = f32[8,128]{1,0:T(8,128)S(1)} collective-permute-done((f32[8,128]{1,0:T(8,128)S(1)}, f32[8,128]{1,0:T(8,128)S(1)}, u32[]{:S(2)}, u32[]{:S(2)}) %collective-permute-start.20) | collective-permute-done | bytes 4128 | tf_op jit(solution)/shard_map/ppermute | solution.py:394
  48.8 1.2 %collective-permute-done.21.yours_ref = f32[8,128]{1,0:T(8,128)S(1)} collective-permute-done((f32[8,128]{1,0:T(8,128)S(1)}, f32[8,128]{1,0:T(8,128)S(1)}, u32[]{:S(2)}, u32[]{:S(2)}) %collective-permute-start.21) | collective-permute-done | bytes 4128 | tf_op jit(solution)/shard_map/ppermute | solution.py:397
  50.5 0.9 %collective-permute-start.22 = (f32[16,128]{1,0:T(8,128)S(1)}, f32[16,128]{1,0:T(8,128)S(1)}, u32[]{:S(2)}, u32[]{:S(2)}) collective-permute-start(f32[16,128]{1,0:T(8,128)S(1)} %get-tuple-element.59.packed_ref), channel_id=1, source_target_pairs={{0,8},{2,10},{4,12},{6,14},{8,0},{10,2},{12,4},{14,6},{1,9},{3,11}... | collective-permute-start | bytes 24584 | tf_op jit(solution)/shard_map/ppermute | solution.py:379
  51.4 2.7 %collective-permute-done.23.mine_ref = f32[16,128]{1,0:T(8,128)S(1)} collective-permute-done((f32[16,128]{1,0:T(8,128)S(1)}, f32[16,128]{1,0:T(8,128)S(1)}, u32[]{:S(2)}, u32[]{:S(2)}) %collective-permute-start.23) | collective-permute-done | bytes 8224 | tf_op jit(solution)/shard_map/ppermute | solution.py:394
  54.1 1.7 %collective-permute-start.24 = (f32[16,128]{1,0:T(8,128)S(1)}, f32[16,128]{1,0:T(8,128)S(1)}, u32[]{:S(2)}, u32[]{:S(2)}) collective-permute-start(f32[16,128]{1,0:T(8,128)S(1)} %collective-permute-done.23.mine_ref), channel_id=1, source_target_pairs={{0,1},{1,0},{2,3},{3,2},{4,5},{5,4},{6,7},{7,6},{8,9},{9,8},{10,11... | collective-permute-start | bytes 24584 | tf_op jit(solution)/shard_map/ppermute | solution.py:397
  56.7 1.4 %shard_map.105 = (f32[19,2048]{1,0:T(8,128)}, f32[8,128]{1,0:T(8,128)}, f32[8,128]{1,0:T(8,128)}) custom-call(f32[8,4,128,128]{3,2,1,0:T(8,128)S(1)} %copy-done.1, f32[8,4,128,128]{3,2,1,0:T(8,128)S(1)} %collective-permute-done.other_ref, f32[64,16]{1,0:T(8,128)S(1)} %shard_map.97.pick_ref, f32[16,128]{1,0:T(8,128)S(1)} %get-tuple-element.59.packed_ref, ...), custom_call_target="tpu_custom_call" | custom-call | flops 4000000 | bytes 262144 | tf_op jit(solution)/shard_map/pallas_call | solution.py:459
  (54 shorter events, 12.0 us)
Async XLA Ops:
  0.6 18.0 %collective-permute-start = (f32[8,4,128,128]{3,2,1,0:T(8,128)}, f32[8,4,128,128]{3,2,1,0:T(8,128)S(1)}, u32[]{:S(2)}, u32[]{:S(2)}) collective-permute-start(f32[8,4,128,128]{3,2,1,0:T(8,128)} %own_ref.9), channel_id=1, source_target_pairs={{0,1},{1,0},{2,3},{3,2},{4,5},{5,4},{6,7},{7,6},{8,9},{9,8},{10,11... | collective-permute-start | bytes 6291464 | tf_op jit(solution)/shard_map/ppermute | solution.py:397
  3.1 4.2 %collective-permute-start.2 = (f32[2,512]{1,0:T(2,128)S(1)}, f32[2,512]{1,0:T(2,128)S(1)}, u32[]{:S(2)}, u32[]{:S(2)}) collective-permute-start(f32[2,512]{1,0:T(2,128)S(1)} %get-tuple-element.39), channel_id=1, source_target_pairs={{0,1},{1,0},{2,3},{3,2},{4,5},{5,4},{6,7},{7,6},{8,9},{9,8},{10,11... | collective-permute-start | bytes 12296 | tf_op jit(solution)/shard_map/ppermute | solution.py:397
  3.2 7.8 %collective-permute-start.1 = (f32[8,512]{1,0:T(8,128)S(1)}, f32[8,512]{1,0:T(8,128)S(1)}, u32[]{:S(2)}, u32[]{:S(2)}) collective-permute-start(f32[8,512]{1,0:T(8,128)S(1)} %get-tuple-element.37.to_far), channel_id=1, source_target_pairs={{0,8},{2,10},{4,12},{6,14},{8,0},{10,2},{12,4},{14,6},{1,9},{3,11}... | collective-permute-start | bytes 49160 | tf_op jit(solution)/shard_map/ppermute | solution.py:379
  7.3 3.7 %collective-permute-start.3 = (f32[4,512]{1,0:T(4,128)S(1)}, f32[4,512]{1,0:T(4,128)S(1)}, u32[]{:S(2)}, u32[]{:S(2)}) collective-permute-start(f32[4,512]{1,0:T(4,128)S(1)} %pad_maximum_fusion), channel_id=1, source_target_pairs={{0,2},{1,15},{2,0},{3,5},{4,6},{5,3},{6,4},{7,9},{8,10},{9,7},{10,... | collective-permute-start | bytes 24584 | tf_op jit(solution)/shard_map/ppermute | solution.py:394
  11.3 2.5 %collective-permute-start.4 = (f32[8,128]{1,0:T(8,128)S(1)}, f32[8,128]{1,0:T(8,128)S(1)}, u32[]{:S(2)}, u32[]{:S(2)}) collective-permute-start(f32[8,128]{1,0:T(8,128)S(1)} %get-tuple-element.40), channel_id=1, source_target_pairs={{0,1},{1,0},{2,3},{3,2},{4,5},{5,4},{6,7},{7,6},{8,9},{9,8},{10,11... | collective-permute-start | bytes 12296 | tf_op jit(solution)/shard_map/ppermute | solution.py:397
  12.6 1.2 %collective-permute-start.5 = (s32[4,8]{1,0:T(4,128)S(1)}, s32[4,8]{1,0:T(4,128)S(1)}, u32[]{:S(2)}, u32[]{:S(2)}) collective-permute-start(s32[4,8]{1,0:T(4,128)S(1)} %get-tuple-element.35.own_cols), channel_id=1, source_target_pairs={{0,1},{1,0},{2,3},{3,2},{4,5},{5,4},{6,7},{7,6},{8,9},{9,8},{10,11... | collective-permute-start | bytes 392 | tf_op jit(solution)/shard_map/ppermute | solution.py:397
  13.8 3.7 %collective-permute-start.6 = (f32[8,128]{1,0:T(8,128)S(1)}, f32[8,128]{1,0:T(8,128)S(1)}, u32[]{:S(2)}, u32[]{:S(2)}) collective-permute-start(f32[8,128]{1,0:T(8,128)S(1)} %get-tuple-element.67.direction_ref), channel_id=1, source_target_pairs={{0,2},{1,17},{2,0},{3,5},{4,6},{5,3},{6,4},{7,9},{8,10},{9,7},{10,... | collective-permute-start | bytes 12296 | tf_op jit(solution)/shard_map/ppermute | solution.py:394
  17.5 1.2 %collective-permute-start.7 = (f32[8,128]{1,0:T(8,128)S(1)}, f32[8,128]{1,0:T(8,128)S(1)}, u32[]{:S(2)}, u32[]{:S(2)}) collective-permute-start(f32[8,128]{1,0:T(8,128)S(1)} %collective-permute-done.6.mine_ref), channel_id=1, source_target_pairs={{0,1},{1,0},{2,3},{3,2},{4,5},{5,4},{6,7},{7,6},{8,9},{9,8},{10,11... | collective-permute-start | bytes 12296 | tf_op jit(solution)/shard_map/ppermute | solution.py:397
  19.1 3.7 %collective-permute-start.8 = (f32[8,128]{1,0:T(8,128)S(1)}, f32[8,128]{1,0:T(8,128)S(1)}, u32[]{:S(2)}, u32[]{:S(2)}) collective-permute-start(f32[8,128]{1,0:T(8,128)S(1)} %get-tuple-element.47.direction_in), channel_id=1, source_target_pairs={{0,2},{1,17},{2,0},{3,5},{4,6},{5,3},{6,4},{7,9},{8,10},{9,7},{10,... | collective-permute-start | bytes 12296 | tf_op jit(solution)/shard_map/ppermute | solution.py:394
  22.8 1.2 %collective-permute-start.9 = (f32[8,128]{1,0:T(8,128)S(1)}, f32[8,128]{1,0:T(8,128)S(1)}, u32[]{:S(2)}, u32[]{:S(2)}) collective-permute-start(f32[8,128]{1,0:T(8,128)S(1)} %collective-permute-done.8.mine_ref), channel_id=1, source_target_pairs={{0,1},{1,0},{2,3},{3,2},{4,5},{5,4},{6,7},{7,6},{8,9},{9,8},{10,11... | collective-permute-start | bytes 12296 | tf_op jit(solution)/shard_map/ppermute | solution.py:397
  24.5 3.7 %collective-permute-start.11 = (f32[8,128]{1,0:T(8,128)S(1)}, f32[8,128]{1,0:T(8,128)S(1)}, u32[]{:S(2)}, u32[]{:S(2)}) collective-permute-start(f32[8,128]{1,0:T(8,128)S(1)} %shard_map.100.own_estimate), channel_id=1, source_target_pairs={{0,2},{1,15},{2,0},{3,5},{4,6},{5,3},{6,4},{7,9},{8,10},{9,7},{10,... | collective-permute-start | bytes 12296 | tf_op jit(solution)/shard_map/ppermute | solution.py:394
  25.0 6.0 %collective-permute-start.10 = (f32[8,128]{1,0:T(8,128)S(1)}, f32[8,128]{1,0:T(8,128)S(1)}, u32[]{:S(2)}, u32[]{:S(2)}) collective-permute-start(f32[8,128]{1,0:T(8,128)S(1)} %shard_map.100.own_estimate), channel_id=1, source_target_pairs={{0,8},{2,10},{4,12},{6,14},{8,0},{10,2},{12,4},{14,6},{1,9},{3,11}... | collective-permute-start | bytes 12296 | tf_op jit(solution)/shard_map/ppermute | solution.py:379
  28.2 2.9 %collective-permute-start.12 = (f32[8,128]{1,0:T(8,128)S(1)}, f32[8,128]{1,0:T(8,128)S(1)}, u32[]{:S(2)}, u32[]{:S(2)}) collective-permute-start(f32[8,128]{1,0:T(8,128)S(1)} %collective-permute-done.11.mine_ref), channel_id=1, source_target_pairs={{0,1},{1,0},{2,3},{3,2},{4,5},{5,4},{6,7},{7,6},{8,9},{9,8},{10,11... | collective-permute-start | bytes 12296 | tf_op jit(solution)/shard_map/ppermute | solution.py:397
  32.0 1.4 %collective-permute-start.15 = (f32[8,128]{1,0:T(8,128)S(1)}, f32[8,128]{1,0:T(8,128)S(1)}, u32[]{:S(2)}, u32[]{:S(2)}) collective-permute-start(f32[8,128]{1,0:T(8,128)S(1)} %get-tuple-element.55), channel_id=1, source_target_pairs={{0,1},{1,0},{2,3},{3,2},{4,5},{5,4},{6,7},{7,6},{8,9},{9,8},{10,11... | collective-permute-start | bytes 12296 | tf_op jit(solution)/shard_map/ppermute | solution.py:397
  32.6 4.5 %collective-permute-start.14 = (f32[8,128]{1,0:T(8,128)S(1)}, f32[8,128]{1,0:T(8,128)S(1)}, u32[]{:S(2)}, u32[]{:S(2)}) collective-permute-start(f32[8,128]{1,0:T(8,128)S(1)} %get-tuple-element.53), channel_id=1, source_target_pairs={{0,8},{2,10},{4,12},{6,14},{8,0},{10,2},{12,4},{14,6},{1,9},{3,11}... | collective-permute-start | bytes 12296 | tf_op jit(solution)/shard_map/ppermute | solution.py:379
  33.5 3.7 %collective-permute-start.16 = (f32[8,128]{1,0:T(8,128)S(1)}, f32[8,128]{1,0:T(8,128)S(1)}, u32[]{:S(2)}, u32[]{:S(2)}) collective-permute-start(f32[8,128]{1,0:T(8,128)S(1)} %add.19), channel_id=1, source_target_pairs={{0,2},{1,15},{2,0},{3,5},{4,6},{5,3},{6,4},{7,9},{8,10},{9,7},{10,... | collective-permute-start | bytes 12296 | tf_op jit(solution)/shard_map/ppermute | solution.py:394
  37.2 2.6 %collective-permute-start.17 = (f32[8,128]{1,0:T(8,128)S(1)}, f32[8,128]{1,0:T(8,128)S(1)}, u32[]{:S(2)}, u32[]{:S(2)}) collective-permute-start(f32[8,128]{1,0:T(8,128)S(1)} %add_multiply_fusion), channel_id=1, source_target_pairs={{0,1},{1,0},{2,3},{3,2},{4,5},{5,4},{6,7},{7,6},{8,9},{9,8},{10,11... | collective-permute-start | bytes 12296 | tf_op jit(solution)/shard_map/ppermute | solution.py:397
  39.8 3.6 %collective-permute-start.18 = (f32[8,128]{1,0:T(8,128)S(1)}, f32[8,128]{1,0:T(8,128)S(1)}, u32[]{:S(2)}, u32[]{:S(2)}) collective-permute-start(f32[8,128]{1,0:T(8,128)S(1)} %get-tuple-element.65.direction_in), channel_id=1, source_target_pairs={{0,2},{1,17},{2,0},{3,5},{4,6},{5,3},{6,4},{7,9},{8,10},{9,7},{10,... | collective-permute-start | bytes 12296 | tf_op jit(solution)/shard_map/ppermute | solution.py:394
  43.4 1.2 %collective-permute-start.19 = (f32[8,128]{1,0:T(8,128)S(1)}, f32[8,128]{1,0:T(8,128)S(1)}, u32[]{:S(2)}, u32[]{:S(2)}) collective-permute-start(f32[8,128]{1,0:T(8,128)S(1)} %collective-permute-done.18.mine_ref), channel_id=1, source_target_pairs={{0,1},{1,0},{2,3},{3,2},{4,5},{5,4},{6,7},{7,6},{8,9},{9,8},{10,11... | collective-permute-start | bytes 12296 | tf_op jit(solution)/shard_map/ppermute | solution.py:397
  45.1 3.7 %collective-permute-start.20 = (f32[8,128]{1,0:T(8,128)S(1)}, f32[8,128]{1,0:T(8,128)S(1)}, u32[]{:S(2)}, u32[]{:S(2)}) collective-permute-start(f32[8,128]{1,0:T(8,128)S(1)} %get-tuple-element.56.direction_in), channel_id=1, source_target_pairs={{0,2},{1,17},{2,0},{3,5},{4,6},{5,3},{6,4},{7,9},{8,10},{9,7},{10,... | collective-permute-start | bytes 12296 | tf_op jit(solution)/shard_map/ppermute | solution.py:394
  48.8 1.2 %collective-permute-start.21 = (f32[8,128]{1,0:T(8,128)S(1)}, f32[8,128]{1,0:T(8,128)S(1)}, u32[]{:S(2)}, u32[]{:S(2)}) collective-permute-start(f32[8,128]{1,0:T(8,128)S(1)} %collective-permute-done.20.mine_ref), channel_id=1, source_target_pairs={{0,1},{1,0},{2,3},{3,2},{4,5},{5,4},{6,7},{7,6},{8,9},{9,8},{10,11... | collective-permute-start | bytes 12296 | tf_op jit(solution)/shard_map/ppermute | solution.py:397
  50.4 3.7 %collective-permute-start.23 = (f32[16,128]{1,0:T(8,128)S(1)}, f32[16,128]{1,0:T(8,128)S(1)}, u32[]{:S(2)}, u32[]{:S(2)}) collective-permute-start(f32[16,128]{1,0:T(8,128)S(1)} %get-tuple-element.59.packed_ref), channel_id=1, source_target_pairs={{0,2},{1,15},{2,0},{3,5},{4,6},{5,3},{6,4},{7,9},{8,10},{9,7},{10,... | collective-permute-start | bytes 24584 | tf_op jit(solution)/shard_map/ppermute | solution.py:394
  50.5 5.4 %collective-permute-start.22 = (f32[16,128]{1,0:T(8,128)S(1)}, f32[16,128]{1,0:T(8,128)S(1)}, u32[]{:S(2)}, u32[]{:S(2)}) collective-permute-start(f32[16,128]{1,0:T(8,128)S(1)} %get-tuple-element.59.packed_ref), channel_id=1, source_target_pairs={{0,8},{2,10},{4,12},{6,14},{8,0},{10,2},{12,4},{14,6},{1,9},{3,11}... | collective-permute-start | bytes 24584 | tf_op jit(solution)/shard_map/ppermute | solution.py:379
  54.1 2.5 %collective-permute-start.24 = (f32[16,128]{1,0:T(8,128)S(1)}, f32[16,128]{1,0:T(8,128)S(1)}, u32[]{:S(2)}, u32[]{:S(2)}) collective-permute-start(f32[16,128]{1,0:T(8,128)S(1)} %collective-permute-done.23.mine_ref), channel_id=1, source_target_pairs={{0,1},{1,0},{2,3},{3,2},{4,5},{5,4},{6,7},{7,6},{8,9},{9,8},{10,11... | collective-permute-start | bytes 24584 | tf_op jit(solution)/shard_map/ppermute | solution.py:397
  (6 other events, 7.9 us)

commit v19 on v15

--- a/solution.py
+++ b/solution.py
@@ -418,16 +418,14 @@
     columns, diag, own = call(
         bring, (shape(*columns.shape[::-1], dtype=jnp.int32), field, double)
     )(in_specs=[VMEM] * 3)(columns.T, diagonal.reshape(torso, LANES), own)
+    near, other_columns = lax.optimization_barrier((near, from_sibling(columns)))
     give, forcing = call(first_forcing, (shape(1, slots), field))(in_specs=[VMEM] * 6)(
         own, far, near, keep, got, to_far
     )
     maps = call(complete, index)(in_specs=[VMEM] * 5)(own, near, far, from_sibling(give), nodes)
-    other_columns = from_sibling(columns)
     for time_step in range(2):
         last = time_step == 1
         others = from_sibling(forcing)
-        if not last:
-            others, other_columns = lax.optimization_barrier((others, other_columns))
         forcing = forcing + others
         direction = forcing / (CHEB_THETA * diag)
         halo = with_either(direction, False)

time: 58.6 us -> 58.7 us (level)
  waiting for transfers between devices: 29.4 us -> 31.3 us
  starting transfers between devices: 18.4 us -> 16.6 us
    ppermute x4, starting transfers between devices: 7.12 us -> 5.61 us  [with_far(): lax.ppermute(value, 'dom', [(i, (i + chain // 2) % chain) for i in range(...]
    ppermute x13, waiting for transfers between devices: 8.62 us -> 9.87 us  [from_sibling(): return lax.ppermute(value, 'sub', [(0, 1), (1, 0)])]
    ppermute x8, waiting for transfers between devices: 17.2 us -> 17.9 us  [with_either(): return lax.ppermute(value, ('case', 'dom', 'sub'), pairs)]
  transfers between devices with their start and end apart: 25 -> 25, of which waited for: 17 -> 18; matrix products, arithmetic and copies ran while one was open for 1% -> 1% of each run, Pallas kernels for 1% -> 1%
where the time goes in v19:
time: 58.7 us; the launch traced here: 58.3 us
  waiting for transfers between devices  31.3 us (53%)
  starting transfers between devices  16.6 us (28%)
  Pallas kernels  5.08 us (9%)
  local copies, waits for them, and re-layouts  3.88 us (7%)
  other arithmetic  0.77 us (1%)
  between operations  0.74 us (1%)
    ppermute x8, waiting for transfers between devices, with_either(): return lax.ppermute(value, ('case', 'dom', 'sub'), pairs)  17.9 us
    ppermute x13, waiting for transfers between devices, from_sibling(): return lax.ppermute(value, 'sub', [(0, 1), (1, 0)])  9.87 us
    ppermute x13, starting transfers between devices, from_sibling(): return lax.ppermute(value, 'sub', [(0, 1), (1, 0)])  8.3 us
    ppermute x4, starting transfers between devices, with_far(): lax.ppermute(value, 'dom', [(i, (i + chain // 2) % chain) for i in range(...  5.61 us
    unnamed x10, local copies, waits for them, and re-layouts  3.88 us
    ppermute x4, waiting for transfers between devices, with_far(): lax.ppermute(value, 'dom', [(i, (i + chain // 2) % chain) for i in range(...  3.5 us
    ppermute x8, starting transfers between devices, with_either(): return lax.ppermute(value, ('case', 'dom', 'sub'), pairs)  2.7 us
    pallas_call x1, Pallas kernels, on_device(): call(functools.partial(finish, chain), (shape(*dense.shape[:1], node_coun...  1.45 us
  transfers between devices with their start and end apart: 25, of which 18 were waited for; matrix products, arithmetic and copies ran while one was open for 1% of the time, Pallas kernels for 1%

profile of v19, /device:TPU:0, one launch (start us, length us, event | category | flops | bytes accessed | tf_op | source)
XLA Modules:
  0.0 58.3 jit_solution(15452419829100602653)
XLA Ops:
  1.9 0.9 %copy-done.2 = f32[19,2048]{1,0:T(8,128)S(1)} copy-done((f32[19,2048]{1,0:T(8,128)S(1)}, f32[19,2048]{1,0:T(8,128)}, u32[]{:S(2)}) %copy-start.2) | copy-done | bytes 155672
  3.2 4.0 %collective-permute-start.4 = (f32[8,512]{1,0:T(8,128)S(1)}, f32[8,512]{1,0:T(8,128)S(1)}, u32[]{:S(2)}, u32[]{:S(2)}) collective-permute-start(f32[8,512]{1,0:T(8,128)S(1)} %get-tuple-element.41.to_far), channel_id=1, source_target_pairs={{0,8},{2,10},{4,12},{6,14},{8,0},{10,2},{12,4},{14,6},{1,9},{3,11}... | collective-permute-start | bytes 49160 | tf_op jit(solution)/shard_map/ppermute | solution.py:381
  7.3 1.6 %collective-permute-start.2 = (f32[4,512]{1,0:T(4,128)S(1)}, f32[4,512]{1,0:T(4,128)S(1)}, u32[]{:S(2)}, u32[]{:S(2)}) collective-permute-start(f32[4,512]{1,0:T(4,128)S(1)} %pad_maximum_fusion), channel_id=1, source_target_pairs={{0,2},{1,15},{2,0},{3,5},{4,6},{5,3},{6,4},{7,9},{8,10},{9,7},{10,... | collective-permute-start | bytes 24584 | tf_op jit(solution)/shard_map/ppermute | solution.py:396
  10.2 1.9 %collective-permute-start.3 = (s32[4,8]{1,0:T(4,128)S(1)}, s32[4,8]{1,0:T(4,128)S(1)}, u32[]{:S(2)}, u32[]{:S(2)}) collective-permute-start(s32[4,8]{1,0:T(4,128)S(1)} %get-tuple-element.35.own_cols), channel_id=1, source_target_pairs={{0,1},{1,0},{2,3},{3,2},{4,5},{5,4},{6,7},{7,6},{8,9},{9,8},{10,11... | collective-permute-start | bytes 392 | tf_op jit(solution)/shard_map/ppermute | solution.py:399
  13.6 0.8 %collective-permute-done.5 = f32[8,128]{1,0:T(8,128)S(1)} collective-permute-done((f32[8,128]{1,0:T(8,128)S(1)}, f32[8,128]{1,0:T(8,128)S(1)}, u32[]{:S(2)}, u32[]{:S(2)}) %collective-permute-start.5) | collective-permute-done | bytes 4128 | tf_op jit(solution)/shard_map/ppermute | solution.py:399
  14.4 1.6 %copy-done = f32[8,4,128,128]{3,2,1,0:T(8,128)S(1)} copy-done((f32[8,4,128,128]{3,2,1,0:T(8,128)S(1)}, f32[8,4,128,128]{3,2,1,0:T(8,128)}, u32[]{:S(2)}) %copy-start) | copy-done | bytes 2097176
  16.0 2.0 %collective-permute-done.6.mine_ref = f32[8,128]{1,0:T(8,128)S(1)} collective-permute-done((f32[8,128]{1,0:T(8,128)S(1)}, f32[8,128]{1,0:T(8,128)S(1)}, u32[]{:S(2)}, u32[]{:S(2)}) %collective-permute-start.6) | collective-permute-done | bytes 4128 | tf_op jit(solution)/shard_map/ppermute | solution.py:396
  18.1 1.1 %collective-permute-done.7.yours_ref = f32[8,128]{1,0:T(8,128)S(1)} collective-permute-done((f32[8,128]{1,0:T(8,128)S(1)}, f32[8,128]{1,0:T(8,128)S(1)}, u32[]{:S(2)}, u32[]{:S(2)}) %collective-permute-start.7) | collective-permute-done | bytes 4128 | tf_op jit(solution)/shard_map/ppermute | solution.py:399
  20.2 3.2 %collective-permute-done.8.mine_ref = f32[8,128]{1,0:T(8,128)S(1)} collective-permute-done((f32[8,128]{1,0:T(8,128)S(1)}, f32[8,128]{1,0:T(8,128)S(1)}, u32[]{:S(2)}, u32[]{:S(2)}) %collective-permute-start.8) | collective-permute-done | bytes 4128 | tf_op jit(solution)/shard_map/ppermute | solution.py:396
  23.4 1.2 %collective-permute-done.9.yours_ref = f32[8,128]{1,0:T(8,128)S(1)} collective-permute-done((f32[8,128]{1,0:T(8,128)S(1)}, f32[8,128]{1,0:T(8,128)S(1)}, u32[]{:S(2)}, u32[]{:S(2)}) %collective-permute-start.9) | collective-permute-done | bytes 4128 | tf_op jit(solution)/shard_map/ppermute | solution.py:399
  26.3 2.4 %collective-permute-done.11.mine_ref = f32[8,128]{1,0:T(8,128)S(1)} collective-permute-done((f32[8,128]{1,0:T(8,128)S(1)}, f32[8,128]{1,0:T(8,128)S(1)}, u32[]{:S(2)}, u32[]{:S(2)}) %collective-permute-start.11) | collective-permute-done | bytes 4128 | tf_op jit(solution)/shard_map/ppermute | solution.py:396
  28.7 1.7 %collective-permute-start.12 = (f32[8,128]{1,0:T(8,128)S(1)}, f32[8,128]{1,0:T(8,128)S(1)}, u32[]{:S(2)}, u32[]{:S(2)}) collective-permute-start(f32[8,128]{1,0:T(8,128)S(1)} %collective-permute-done.11.mine_ref), channel_id=1, source_target_pairs={{0,1},{1,0},{2,3},{3,2},{4,5},{5,4},{6,7},{7,6},{8,9},{9,8},{10,11... | collective-permute-start | bytes 12296 | tf_op jit(solution)/shard_map/ppermute | solution.py:399
  30.5 1.2 %collective-permute-done.13.got_ref = f32[1,512]{1,0:T(1,128)S(1)} collective-permute-done((f32[1,512]{1,0:T(1,128)S(1)}, f32[1,512]{1,0:T(1,128)S(1)}, u32[]{:S(2)}, u32[]{:S(2)}) %collective-permute-start.13) | collective-permute-done | bytes 2080 | tf_op jit(solution)/shard_map/ppermute | solution.py:399
  31.6 0.9 %shard_map.102 = (f32[19,16,128]{2,1,0:T(8,128)S(1)}, f32[8,128]{1,0:T(8,128)S(1)}, f32[8,128]{1,0:T(8,128)S(1)}, f32[8,128]{1,0:T(8,128)S(1)}, f32[8,128]{1,0:T(8,128)S(1)}) custom-call(f32[19,16,128]{2,1,0:T(8,128)S(1)} %get-tuple-element.39.states_ref, f32[8,128]{1,0:T(8,128)S(1)} %shard_map.100.own_estimate, ...), custom_call_target="tpu_custom_call" | custom-call | flops 4000000 | bytes 262144 | tf_op jit(solution)/shard_map/pallas_call | solution.py:453
  33.0 0.8 %collective-permute-done.15 = f32[8,128]{1,0:T(8,128)S(1)} collective-permute-done((f32[8,128]{1,0:T(8,128)S(1)}, f32[8,128]{1,0:T(8,128)S(1)}, u32[]{:S(2)}, u32[]{:S(2)}) %collective-permute-start.15) | collective-permute-done | bytes 4128 | tf_op jit(solution)/shard_map/ppermute | solution.py:399
  33.8 3.5 %collective-permute-done.14 = f32[8,128]{1,0:T(8,128)S(1)} collective-permute-done((f32[8,128]{1,0:T(8,128)S(1)}, f32[8,128]{1,0:T(8,128)S(1)}, u32[]{:S(2)}, u32[]{:S(2)}) %collective-permute-start.14) | collective-permute-done | bytes 4128 | tf_op jit(solution)/shard_map/ppermute | solution.py:381
  37.4 1.7 %collective-permute-start.17 = (f32[8,128]{1,0:T(8,128)S(1)}, f32[8,128]{1,0:T(8,128)S(1)}, u32[]{:S(2)}, u32[]{:S(2)}) collective-permute-start(f32[8,128]{1,0:T(8,128)S(1)} %add_multiply_fusion), channel_id=1, source_target_pairs={{0,1},{1,0},{2,3},{3,2},{4,5},{5,4},{6,7},{7,6},{8,9},{9,8},{10,11... | collective-permute-start | bytes 12296 | tf_op jit(solution)/shard_map/ppermute | solution.py:399
  40.0 3.6 %collective-permute-done.18.mine_ref = f32[8,128]{1,0:T(8,128)S(1)} collective-permute-done((f32[8,128]{1,0:T(8,128)S(1)}, f32[8,128]{1,0:T(8,128)S(1)}, u32[]{:S(2)}, u32[]{:S(2)}) %collective-permute-start.18) | collective-permute-done | bytes 4128 | tf_op jit(solution)/shard_map/ppermute | solution.py:396
  43.6 1.2 %collective-permute-done.19.yours_ref = f32[8,128]{1,0:T(8,128)S(1)} collective-permute-done((f32[8,128]{1,0:T(8,128)S(1)}, f32[8,128]{1,0:T(8,128)S(1)}, u32[]{:S(2)}, u32[]{:S(2)}) %collective-permute-start.19) | collective-permute-done | bytes 4128 | tf_op jit(solution)/shard_map/ppermute | solution.py:399
  45.4 3.6 %collective-permute-done.20.mine_ref = f32[8,128]{1,0:T(8,128)S(1)} collective-permute-done((f32[8,128]{1,0:T(8,128)S(1)}, f32[8,128]{1,0:T(8,128)S(1)}, u32[]{:S(2)}, u32[]{:S(2)}) %collective-permute-start.20) | collective-permute-done | bytes 4128 | tf_op jit(solution)/shard_map/ppermute | solution.py:396
  49.0 1.2 %collective-permute-done.21.yours_ref = f32[8,128]{1,0:T(8,128)S(1)} collective-permute-done((f32[8,128]{1,0:T(8,128)S(1)}, f32[8,128]{1,0:T(8,128)S(1)}, u32[]{:S(2)}, u32[]{:S(2)}) %collective-permute-start.21) | collective-permute-done | bytes 4128 | tf_op jit(solution)/shard_map/ppermute | solution.py:399
  51.4 3.0 %collective-permute-done.23.mine_ref = f32[16,128]{1,0:T(8,128)S(1)} collective-permute-done((f32[16,128]{1,0:T(8,128)S(1)}, f32[16,128]{1,0:T(8,128)S(1)}, u32[]{:S(2)}, u32[]{:S(2)}) %collective-permute-start.23) | collective-permute-done | bytes 8224 | tf_op jit(solution)/shard_map/ppermute | solution.py:396
  54.3 1.7 %collective-permute-start.24 = (f32[16,128]{1,0:T(8,128)S(1)}, f32[16,128]{1,0:T(8,128)S(1)}, u32[]{:S(2)}, u32[]{:S(2)}) collective-permute-start(f32[16,128]{1,0:T(8,128)S(1)} %collective-permute-done.23.mine_ref), channel_id=1, source_target_pairs={{0,1},{1,0},{2,3},{3,2},{4,5},{5,4},{6,7},{7,6},{8,9},{9,8},{10,11... | collective-permute-start | bytes 24584 | tf_op jit(solution)/shard_map/ppermute | solution.py:399
  56.9 1.4 %shard_map.105 = (f32[19,2048]{1,0:T(8,128)}, f32[8,128]{1,0:T(8,128)}, f32[8,128]{1,0:T(8,128)}) custom-call(f32[8,4,128,128]{3,2,1,0:T(8,128)S(1)} %copy-done.1, f32[8,4,128,128]{3,2,1,0:T(8,128)S(1)} %collective-permute-done.other_ref, f32[64,16]{1,0:T(8,128)S(1)} %shard_map.96.pick_ref, f32[16,128]{1,0:T(8,128)S(1)} %get-tuple-element.59.packed_ref, ...), custom_call_target="tpu_custom_call" | custom-call | flops 4000000 | bytes 262144 | tf_op jit(solution)/shard_map/pallas_call | solution.py:459
  (54 shorter events, 11.4 us)
Async XLA Ops:
  0.6 18.6 %collective-permute-start = (f32[8,4,128,128]{3,2,1,0:T(8,128)}, f32[8,4,128,128]{3,2,1,0:T(8,128)S(1)}, u32[]{:S(2)}, u32[]{:S(2)}) collective-permute-start(f32[8,4,128,128]{3,2,1,0:T(8,128)} %own_ref.9), channel_id=1, source_target_pairs={{0,1},{1,0},{2,3},{3,2},{4,5},{5,4},{6,7},{7,6},{8,9},{9,8},{10,11... | collective-permute-start | bytes 6291464 | tf_op jit(solution)/shard_map/ppermute | solution.py:399
  3.1 4.2 %collective-permute-start.1 = (f32[2,512]{1,0:T(2,128)S(1)}, f32[2,512]{1,0:T(2,128)S(1)}, u32[]{:S(2)}, u32[]{:S(2)}) collective-permute-start(f32[2,512]{1,0:T(2,128)S(1)} %get-tuple-element.37), channel_id=1, source_target_pairs={{0,1},{1,0},{2,3},{3,2},{4,5},{5,4},{6,7},{7,6},{8,9},{9,8},{10,11... | collective-permute-start | bytes 12296 | tf_op jit(solution)/shard_map/ppermute | solution.py:399
  3.2 9.7 %collective-permute-start.4 = (f32[8,512]{1,0:T(8,128)S(1)}, f32[8,512]{1,0:T(8,128)S(1)}, u32[]{:S(2)}, u32[]{:S(2)}) collective-permute-start(f32[8,512]{1,0:T(8,128)S(1)} %get-tuple-element.41.to_far), channel_id=1, source_target_pairs={{0,8},{2,10},{4,12},{6,14},{8,0},{10,2},{12,4},{14,6},{1,9},{3,11}... | collective-permute-start | bytes 49160 | tf_op jit(solution)/shard_map/ppermute | solution.py:381
  7.3 5.6 %collective-permute-start.2 = (f32[4,512]{1,0:T(4,128)S(1)}, f32[4,512]{1,0:T(4,128)S(1)}, u32[]{:S(2)}, u32[]{:S(2)}) collective-permute-start(f32[4,512]{1,0:T(4,128)S(1)} %pad_maximum_fusion), channel_id=1, source_target_pairs={{0,2},{1,15},{2,0},{3,5},{4,6},{5,3},{6,4},{7,9},{8,10},{9,7},{10,... | collective-permute-start | bytes 24584 | tf_op jit(solution)/shard_map/ppermute | solution.py:396
  10.2 2.7 %collective-permute-start.3 = (s32[4,8]{1,0:T(4,128)S(1)}, s32[4,8]{1,0:T(4,128)S(1)}, u32[]{:S(2)}, u32[]{:S(2)}) collective-permute-start(s32[4,8]{1,0:T(4,128)S(1)} %get-tuple-element.35.own_cols), channel_id=1, source_target_pairs={{0,1},{1,0},{2,3},{3,2},{4,5},{5,4},{6,7},{7,6},{8,9},{9,8},{10,11... | collective-permute-start | bytes 392 | tf_op jit(solution)/shard_map/ppermute | solution.py:399
  13.2 1.2 %collective-permute-start.5 = (f32[8,128]{1,0:T(8,128)S(1)}, f32[8,128]{1,0:T(8,128)S(1)}, u32[]{:S(2)}, u32[]{:S(2)}) collective-permute-start(f32[8,128]{1,0:T(8,128)S(1)} %get-tuple-element.43), channel_id=1, source_target_pairs={{0,1},{1,0},{2,3},{3,2},{4,5},{5,4},{6,7},{7,6},{8,9},{9,8},{10,11... | collective-permute-start | bytes 12296 | tf_op jit(solution)/shard_map/ppermute | solution.py:399
  14.4 3.6 %collective-permute-start.6 = (f32[8,128]{1,0:T(8,128)S(1)}, f32[8,128]{1,0:T(8,128)S(1)}, u32[]{:S(2)}, u32[]{:S(2)}) collective-permute-start(f32[8,128]{1,0:T(8,128)S(1)} %get-tuple-element.67.direction_ref), channel_id=1, source_target_pairs={{0,2},{1,17},{2,0},{3,5},{4,6},{5,3},{6,4},{7,9},{8,10},{9,7},{10,... | collective-permute-start | bytes 12296 | tf_op jit(solution)/shard_map/ppermute | solution.py:396
  18.0 1.2 %collective-permute-start.7 = (f32[8,128]{1,0:T(8,128)S(1)}, f32[8,128]{1,0:T(8,128)S(1)}, u32[]{:S(2)}, u32[]{:S(2)}) collective-permute-start(f32[8,128]{1,0:T(8,128)S(1)} %collective-permute-done.6.mine_ref), channel_id=1, source_target_pairs={{0,1},{1,0},{2,3},{3,2},{4,5},{5,4},{6,7},{7,6},{8,9},{9,8},{10,11... | collective-permute-start | bytes 12296 | tf_op jit(solution)/shard_map/ppermute | solution.py:399
  19.7 3.7 %collective-permute-start.8 = (f32[8,128]{1,0:T(8,128)S(1)}, f32[8,128]{1,0:T(8,128)S(1)}, u32[]{:S(2)}, u32[]{:S(2)}) collective-permute-start(f32[8,128]{1,0:T(8,128)S(1)} %get-tuple-element.47.direction_in), channel_id=1, source_target_pairs={{0,2},{1,17},{2,0},{3,5},{4,6},{5,3},{6,4},{7,9},{8,10},{9,7},{10,... | collective-permute-start | bytes 12296 | tf_op jit(solution)/shard_map/ppermute | solution.py:396
  23.4 1.2 %collective-permute-start.9 = (f32[8,128]{1,0:T(8,128)S(1)}, f32[8,128]{1,0:T(8,128)S(1)}, u32[]{:S(2)}, u32[]{:S(2)}) collective-permute-start(f32[8,128]{1,0:T(8,128)S(1)} %collective-permute-done.8.mine_ref), channel_id=1, source_target_pairs={{0,1},{1,0},{2,3},{3,2},{4,5},{5,4},{6,7},{7,6},{8,9},{9,8},{10,11... | collective-permute-start | bytes 12296 | tf_op jit(solution)/shard_map/ppermute | solution.py:399
  25.1 3.7 %collective-permute-start.11 = (f32[8,128]{1,0:T(8,128)S(1)}, f32[8,128]{1,0:T(8,128)S(1)}, u32[]{:S(2)}, u32[]{:S(2)}) collective-permute-start(f32[8,128]{1,0:T(8,128)S(1)} %shard_map.100.own_estimate), channel_id=1, source_target_pairs={{0,2},{1,15},{2,0},{3,5},{4,6},{5,3},{6,4},{7,9},{8,10},{9,7},{10,... | collective-permute-start | bytes 12296 | tf_op jit(solution)/shard_map/ppermute | solution.py:396
  25.6 6.1 %collective-permute-start.10 = (f32[8,128]{1,0:T(8,128)S(1)}, f32[8,128]{1,0:T(8,128)S(1)}, u32[]{:S(2)}, u32[]{:S(2)}) collective-permute-start(f32[8,128]{1,0:T(8,128)S(1)} %shard_map.100.own_estimate), channel_id=1, source_target_pairs={{0,8},{2,10},{4,12},{6,14},{8,0},{10,2},{12,4},{14,6},{1,9},{3,11}... | collective-permute-start | bytes 12296 | tf_op jit(solution)/shard_map/ppermute | solution.py:381
  28.7 2.9 %collective-permute-start.12 = (f32[8,128]{1,0:T(8,128)S(1)}, f32[8,128]{1,0:T(8,128)S(1)}, u32[]{:S(2)}, u32[]{:S(2)}) collective-permute-start(f32[8,128]{1,0:T(8,128)S(1)} %collective-permute-done.11.mine_ref), channel_id=1, source_target_pairs={{0,1},{1,0},{2,3},{3,2},{4,5},{5,4},{6,7},{7,6},{8,9},{9,8},{10,11... | collective-permute-start | bytes 12296 | tf_op jit(solution)/shard_map/ppermute | solution.py:399
  32.6 1.2 %collective-permute-start.15 = (f32[8,128]{1,0:T(8,128)S(1)}, f32[8,128]{1,0:T(8,128)S(1)}, u32[]{:S(2)}, u32[]{:S(2)}) collective-permute-start(f32[8,128]{1,0:T(8,128)S(1)} %get-tuple-element.55), channel_id=1, source_target_pairs={{0,1},{1,0},{2,3},{3,2},{4,5},{5,4},{6,7},{7,6},{8,9},{9,8},{10,11... | collective-permute-start | bytes 12296 | tf_op jit(solution)/shard_map/ppermute | solution.py:399
  32.8 4.5 %collective-permute-start.14 = (f32[8,128]{1,0:T(8,128)S(1)}, f32[8,128]{1,0:T(8,128)S(1)}, u32[]{:S(2)}, u32[]{:S(2)}) collective-permute-start(f32[8,128]{1,0:T(8,128)S(1)} %get-tuple-element.53), channel_id=1, source_target_pairs={{0,8},{2,10},{4,12},{6,14},{8,0},{10,2},{12,4},{14,6},{1,9},{3,11}... | collective-permute-start | bytes 12296 | tf_op jit(solution)/shard_map/ppermute | solution.py:381
  33.8 3.6 %collective-permute-start.16 = (f32[8,128]{1,0:T(8,128)S(1)}, f32[8,128]{1,0:T(8,128)S(1)}, u32[]{:S(2)}, u32[]{:S(2)}) collective-permute-start(f32[8,128]{1,0:T(8,128)S(1)} %add.19), channel_id=1, source_target_pairs={{0,2},{1,15},{2,0},{3,5},{4,6},{5,3},{6,4},{7,9},{8,10},{9,7},{10,... | collective-permute-start | bytes 12296 | tf_op jit(solution)/shard_map/ppermute | solution.py:396
  37.4 2.5 %collective-permute-start.17 = (f32[8,128]{1,0:T(8,128)S(1)}, f32[8,128]{1,0:T(8,128)S(1)}, u32[]{:S(2)}, u32[]{:S(2)}) collective-permute-start(f32[8,128]{1,0:T(8,128)S(1)} %add_multiply_fusion), channel_id=1, source_target_pairs={{0,1},{1,0},{2,3},{3,2},{4,5},{5,4},{6,7},{7,6},{8,9},{9,8},{10,11... | collective-permute-start | bytes 12296 | tf_op jit(solution)/shard_map/ppermute | solution.py:399
  40.0 3.6 %collective-permute-start.18 = (f32[8,128]{1,0:T(8,128)S(1)}, f32[8,128]{1,0:T(8,128)S(1)}, u32[]{:S(2)}, u32[]{:S(2)}) collective-permute-start(f32[8,128]{1,0:T(8,128)S(1)} %get-tuple-element.65.direction_in), channel_id=1, source_target_pairs={{0,2},{1,17},{2,0},{3,5},{4,6},{5,3},{6,4},{7,9},{8,10},{9,7},{10,... | collective-permute-start | bytes 12296 | tf_op jit(solution)/shard_map/ppermute | solution.py:396
  43.6 1.2 %collective-permute-start.19 = (f32[8,128]{1,0:T(8,128)S(1)}, f32[8,128]{1,0:T(8,128)S(1)}, u32[]{:S(2)}, u32[]{:S(2)}) collective-permute-start(f32[8,128]{1,0:T(8,128)S(1)} %collective-permute-done.18.mine_ref), channel_id=1, source_target_pairs={{0,1},{1,0},{2,3},{3,2},{4,5},{5,4},{6,7},{7,6},{8,9},{9,8},{10,11... | collective-permute-start | bytes 12296 | tf_op jit(solution)/shard_map/ppermute | solution.py:399
  45.3 3.7 %collective-permute-start.20 = (f32[8,128]{1,0:T(8,128)S(1)}, f32[8,128]{1,0:T(8,128)S(1)}, u32[]{:S(2)}, u32[]{:S(2)}) collective-permute-start(f32[8,128]{1,0:T(8,128)S(1)} %get-tuple-element.56.direction_in), channel_id=1, source_target_pairs={{0,2},{1,17},{2,0},{3,5},{4,6},{5,3},{6,4},{7,9},{8,10},{9,7},{10,... | collective-permute-start | bytes 12296 | tf_op jit(solution)/shard_map/ppermute | solution.py:396
  48.9 1.2 %collective-permute-start.21 = (f32[8,128]{1,0:T(8,128)S(1)}, f32[8,128]{1,0:T(8,128)S(1)}, u32[]{:S(2)}, u32[]{:S(2)}) collective-permute-start(f32[8,128]{1,0:T(8,128)S(1)} %collective-permute-done.20.mine_ref), channel_id=1, source_target_pairs={{0,1},{1,0},{2,3},{3,2},{4,5},{5,4},{6,7},{7,6},{8,9},{9,8},{10,11... | collective-permute-start | bytes 12296 | tf_op jit(solution)/shard_map/ppermute | solution.py:399
  50.6 3.7 %collective-permute-start.23 = (f32[16,128]{1,0:T(8,128)S(1)}, f32[16,128]{1,0:T(8,128)S(1)}, u32[]{:S(2)}, u32[]{:S(2)}) collective-permute-start(f32[16,128]{1,0:T(8,128)S(1)} %get-tuple-element.59.packed_ref), channel_id=1, source_target_pairs={{0,2},{1,15},{2,0},{3,5},{4,6},{5,3},{6,4},{7,9},{8,10},{9,7},{10,... | collective-permute-start | bytes 24584 | tf_op jit(solution)/shard_map/ppermute | solution.py:396
  50.7 5.4 %collective-permute-start.22 = (f32[16,128]{1,0:T(8,128)S(1)}, f32[16,128]{1,0:T(8,128)S(1)}, u32[]{:S(2)}, u32[]{:S(2)}) collective-permute-start(f32[16,128]{1,0:T(8,128)S(1)} %get-tuple-element.59.packed_ref), channel_id=1, source_target_pairs={{0,8},{2,10},{4,12},{6,14},{8,0},{10,2},{12,4},{14,6},{1,9},{3,11}... | collective-permute-start | bytes 24584 | tf_op jit(solution)/shard_map/ppermute | solution.py:381
  54.3 2.5 %collective-permute-start.24 = (f32[16,128]{1,0:T(8,128)S(1)}, f32[16,128]{1,0:T(8,128)S(1)}, u32[]{:S(2)}, u32[]{:S(2)}) collective-permute-start(f32[16,128]{1,0:T(8,128)S(1)} %collective-permute-done.23.mine_ref), channel_id=1, source_target_pairs={{0,1},{1,0},{2,3},{3,2},{4,5},{5,4},{6,7},{7,6},{8,9},{9,8},{10,11... | collective-permute-start | bytes 24584 | tf_op jit(solution)/shard_map/ppermute | solution.py:399
  (6 other events, 8.2 us)
